TPU v7x, 32 devices: a whole 2x2x4 slice. The times are simulated.
32 devices in a mesh: chan: 2 (over y), seqo: 4 (over z), seqi: 4 (over x, core).
Axes of the slice: x: 2, y: 2, z: 4, core: 2. Of those that a mesh axis runs over, the one named last changes fastest.
Arguments:
- gate_in: bfloat16 [32768, 4096], P(('seqo', 'seqi'), 'chan'), may hold values from -6 to 6
- value_in: bfloat16 [32768, 4096], P(('seqo', 'seqi'), 'chan'), may hold values from -6 to 6
- out_gate: bfloat16 [32768, 4096], P(('seqo', 'seqi'), 'chan'), may hold values from -6 to 6
- residual: bfloat16 [32768, 4096], P(('seqo', 'seqi'), 'chan'), may hold values from -200 to 200
- filters: bfloat16 [2, 16, 6, 32768], P('chan', ('seqo', 'seqi')), may hold values from -5 to 5
- kept_index: int32 [2, 64], P('chan'), may hold values from -1 to 2047, as said below
- kept_owner: int32 [2, 64], P('chan'), may hold values from -1 to 15, as said below
- skip_bias: float32 [4096], P('chan'), may hold values from -1 to 1
- norm_gain: float32 [4096], P('chan'), may hold values from 0.5 to 1.5
Outputs:
- hidden_out: bfloat16 [32768, 4096], P(('seqo', 'seqi'), 'chan')
- normed: bfloat16 [32768, 4096], P(('seqo', 'seqi'), 'chan')
Inputs may be any that keep to these rules, and one draw needn't show every extreme that they name: `kept_index`: row s lists the kept channels of slab s in rising order, distinct, between 32 and 64 of them, followed by -1 in the unused slots; some slab lists exactly 64. `kept_owner`: -1 exactly where kept_index is -1, else a device index along seqo+seqi. Within a slab no device owns more than 6 kept channels, and in every slab some device owns exactly 6.
All inputs are finite; a program needn't handle non-finite values.
Results may differ from a plain program's by a relative error of at most 0.005.
Values may be sent and summed in bfloat16 or wider, within the bound.
No kernel may reach another device: no remote copies, remote signals or barrier semaphores. Data moves between devices by JAX's collectives and lax.ppermute only.
A program may use at most 128 MiB of HBM per device.

v0:
```python
import jax
import jax.numpy as jnp
from jax import lax
from jax.sharding import PartitionSpec as P

FA = 512


norm_eps = 1e-06
highest = lax.Precision.HIGHEST


def owner_ranks(owners_row):
    is_live = owners_row >= 0
    slot_count = owners_row.shape[0]
    token_position = jnp.arange(slot_count, dtype=jnp.int32)
    earlier = (
        (owners_row[:, None] == owners_row[None, :])
        & is_live[None, :]
        & (token_position[None, :] < token_position[:, None])
    )
    return jnp.sum(earlier.astype(jnp.int32), axis=1)


def angle_table(first, second, modulus):
    product = first[:, None] * second[None, :] % modulus
    return 2.0 * jnp.pi / modulus * product.astype(jnp.float32)


def causal_convolve(signals, kernels, outer_len):
    channels, length = signals.shape
    inner_len = 2 * length // outer_len
    total_len = outer_len * inner_len
    outer_steps = jnp.arange(outer_len, dtype=jnp.int32)
    half_steps = jnp.arange(outer_len // 2, dtype=jnp.int32)
    inner_steps = jnp.arange(inner_len, dtype=jnp.int32)
    outer_angle = angle_table(outer_steps, half_steps, outer_len)
    twist_angle = angle_table(outer_steps, inner_steps, total_len)
    inner_angle = angle_table(inner_steps, inner_steps, inner_len)
    outer_cos = jnp.cos(outer_angle)
    outer_sin = jnp.sin(outer_angle)
    twist_cos = jnp.cos(twist_angle)
    twist_sin = jnp.sin(twist_angle)
    inner_cos = jnp.cos(inner_angle)
    inner_sin = jnp.sin(inner_angle)
    outer_fwd = jnp.concatenate([outer_cos, -outer_sin], axis=0)
    inner_fwd = jnp.concatenate(
        [
            jnp.concatenate([inner_cos, -inner_sin], axis=1),
            jnp.concatenate([inner_sin, inner_cos], axis=1),
        ],
        axis=0,
    )
    inner_back = jnp.concatenate(
        [
            jnp.concatenate([inner_cos, inner_sin], axis=1),
            jnp.concatenate([-inner_sin, inner_cos], axis=1),
        ],
        axis=0,
    )
    outer_back = jnp.concatenate([outer_cos, -outer_sin], axis=0)

    def forward(series):
        blocks = series.astype(jnp.float32).reshape(channels, outer_len // 2, inner_len)
        first = jnp.einsum("ka,cab->ckb", outer_fwd, blocks, precision=highest)
        first_re = first[:, :outer_len]
        first_im = first[:, outer_len:]
        turned_re = first_re * twist_cos + first_im * twist_sin
        turned_im = first_im * twist_cos - first_re * twist_sin
        stacked = jnp.concatenate([turned_re, turned_im], axis=2)
        spec = jnp.einsum("ckb,bj->ckj", stacked, inner_fwd, precision=highest)
        return (spec[:, :, :inner_len], spec[:, :, inner_len:])

    signal_re, signal_im = forward(signals)
    kernel_re, kernel_im = forward(kernels)
    joint_re = signal_re * kernel_re - signal_im * kernel_im
    joint_im = signal_re * kernel_im + signal_im * kernel_re
    joint = jnp.concatenate([joint_re, joint_im], axis=2)
    back = jnp.einsum("ckj,jb->ckb", joint, inner_back, precision=highest)
    back_re = back[:, :, :inner_len]
    back_im = back[:, :, inner_len:]
    untwist_re = back_re * twist_cos - back_im * twist_sin
    untwist_im = back_im * twist_cos + back_re * twist_sin
    untwisted = jnp.concatenate([untwist_re, untwist_im], axis=1)
    result = jnp.einsum("ka,ckb->cab", outer_back, untwisted, precision=highest)
    return (result / total_len).reshape(channels, length)


def local(
    gate_in, value_in, out_gate, residual, filters, kept_index, kept_owner, skip_bias, norm_gain
):
    tok_rows, slab_width = gate_in.shape
    own_slots = filters.shape[2]
    length = filters.shape[3]
    outer_devices = lax.axis_size("seqo")
    inner_devices = lax.axis_size("seqi")
    owner_count = outer_devices * inner_devices
    gated_prod = (gate_in.astype(jnp.float32) * value_in.astype(jnp.float32)).astype(jnp.bfloat16)
    index_row = kept_index[0]
    owners_row = kept_owner[0]
    is_live = owners_row >= 0
    slot_ranks = owner_ranks(owners_row)
    target = jnp.where(is_live, slot_ranks * owner_count + owners_row, -1)
    buffer_rows = jnp.arange(own_slots * owner_count, dtype=jnp.int32)
    select = (buffer_rows[:, None] == target[None, :]).astype(jnp.bfloat16)
    channel_pos = jnp.arange(slab_width, dtype=jnp.int32)
    spread = ((index_row[:, None] == channel_pos[None, :]) & is_live[:, None]).astype(jnp.bfloat16)
    picker = jnp.dot(select, spread, preferred_element_type=jnp.float32).astype(jnp.bfloat16)
    outgoing = lax.dot_general(
        picker, gated_prod, (((1,), (1,)), ((), ())), preferred_element_type=jnp.float32
    ).astype(jnp.bfloat16)
    incoming = lax.all_to_all(
        outgoing.reshape(own_slots, owner_count, tok_rows),
        ("seqo", "seqi"),
        split_axis=1,
        concat_axis=1,
        tiled=True,
    )
    convolved = causal_convolve(incoming.reshape(own_slots, length), filters[0, 0], FA)
    returned = lax.all_to_all(
        convolved.reshape(own_slots, owner_count, tok_rows),
        ("seqo", "seqi"),
        split_axis=1,
        concat_axis=1,
        tiled=True,
    )
    returned = returned.reshape(own_slots * owner_count, tok_rows)
    safe_target = jnp.where(is_live, target, 0)
    kept_rows = jnp.take(returned, safe_target, axis=0)
    put_at = jnp.where(is_live, index_row, slab_width)
    conv_cols = (
        jnp.zeros((tok_rows, slab_width), jnp.float32).at[:, put_at].set(kept_rows.T, mode="drop")
    )
    gated_wide = gated_prod.astype(jnp.float32)
    mixed_out = out_gate.astype(jnp.float32) * (conv_cols + skip_bias[None, :] * gated_wide)
    hidden_out = (residual.astype(jnp.float32) + mixed_out).astype(jnp.bfloat16)
    hidden_wide = hidden_out.astype(jnp.float32)
    squares = jnp.sum(hidden_wide * hidden_wide, axis=1)
    row_total = lax.psum(squares, "chan")
    width_all = slab_width * lax.axis_size("chan")
    scaling = lax.rsqrt(row_total / width_all + norm_eps)
    normed = (hidden_wide * scaling[:, None] * norm_gain[None, :]).astype(jnp.bfloat16)
    return (hidden_out, normed)


def solution(mesh):
    in_specs = (
        P(("seqo", "seqi"), "chan"),
        P(("seqo", "seqi"), "chan"),
        P(("seqo", "seqi"), "chan"),
        P(("seqo", "seqi"), "chan"),
        P("chan", ("seqo", "seqi"), None, None),
        P("chan", None),
        P("chan", None),
        P("chan"),
        P("chan"),
    )
    out_specs = (P(("seqo", "seqi"), "chan"), P(("seqo", "seqi"), "chan"))
    return jax.shard_map(local, mesh=mesh, in_specs=in_specs, out_specs=out_specs, check_vma=False)
```

profile of v0, /device:TPU:0, one launch (start us, length us, event | category | flops | bytes accessed | tf_op | source)
XLA Modules:
  0.0 180.5 jit_solution(1035144335705528502)
XLA Ops:
  0.6 0.7 compare_bitcast_fusion
  1.3 0.9 convert_reduce_fusion
  2.2 0.7 broadcast_compare_fusion
  2.9 0.7 fusion.78
  3.5 12.2 %copy.60 = bf16[2048,2048]{0,1:T(8,128)(2,1)} copy(bf16[2048,2048]{1,0:T(8,128)(2,1)} %param.9) | data formatting | bytes 16777216 | tf_op args[0]
  15.8 12.2 %copy.61 = bf16[2048,2048]{0,1:T(8,128)(2,1)} copy(bf16[2048,2048]{1,0:T(8,128)(2,1)} %param.10) | data formatting | bytes 16777216 | tf_op args[1]
  28.0 8.5 %fusion.22 = bf16[96,2048]{1,0:T(8,128)(2,1)S(1)} fusion(bf16[2048,2048]{0,1:T(8,128)(2,1)} %copy.61, bf16[2048,2048]{0,1:T(8,128)(2,1)} %copy.60, s32[64]{0:T(128)S(1)} %bitcast.71, pred[64]{0:T(512)(128)(4,1)S(1)} %get-tuple-element.24, s32[64]{0:T(128)S(1)} %fusion.78), kind=kOutput, calls=%fused_computation.29 | convolution fusion | flops 847910912 | bytes 17171008 | tf_op jit(solution)/shard_map/dot_general | solution.py:109
  36.5 1.0 copy.62
  37.5 7.4 %all-to-all-start = ((bf16[6,16,2048]{2,0,1:T(8,128)(2,1)}), bf16[6,16,2048]{2,0,1:T(8,128)(2,1)}, u32[]{:S(2)}, u32[]{:S(2)}) async-start(bf16[6,16,2048]{2,0,1:T(8,128)(2,1)} %copy.62), calls=%async_computation | async-start | bytes 1048576 | tf_op jit(solution)/shard_map/all_to_all | solution.py:112
  44.9 0.3 fusion.75
  45.2 0.1 copy.86
  45.3 0.9 copy.66
  46.2 0.9 fusion.72
  47.1 1.7 fusion.64
  48.8 2.1 %sine_negate_fusion = (f32[512,256]{1,0:T(8,128)S(1)}, f32[512,256]{1,0:T(8,128)S(1)}) fusion(), kind=kLoop, calls=%fused_computation.52 | loop fusion | flops 1966080 | bytes 1048576 | tf_op jit(solution)/shard_map/neg | solution.py:46
  50.9 0.0 copy-start
  50.9 0.0 copy-start.2
  50.9 0.8 copy-done
  51.7 0.2 copy-done.2
  51.9 2.5 %fusion.31 = f32[1024,768]{0,1:S(1)} fusion(bf16[256,768]{0,1:T(8,128)(2,1)} %bitcast.66, f32[512,256]{1,0:T(8,128)S(1)} %get-tuple-element.26, f32[512,256]{1,0:T(8,128)S(1)} %get-tuple-element.27), kind=kOutput, calls=%fused_computation.47 | convolution fusion | flops 2416181248 | bytes 4587520
  54.3 5.1 %all-to-all-done = bf16[6,16,2048]{2,0,1:T(8,128)(2,1)} async-done(((bf16[6,16,2048]{2,0,1:T(8,128)(2,1)}), bf16[6,16,2048]{2,0,1:T(8,128)(2,1)}, u32[]{:S(2)}, u32[]{:S(2)}) %all-to-all-start) | async-done | bytes 393248 | tf_op jit(solution)/shard_map/all_to_all | solution.py:112
  59.5 2.0 %copy.63 = bf16[6,16,2048]{2,1,0:T(8,128)(2,1)} copy(bf16[6,16,2048]{2,0,1:T(8,128)(2,1)} %all-to-all-done) | data formatting | bytes 786432 | tf_op jit(solution)/shard_map/all_to_all | solution.py:112
  61.5 1.9 %reshape.146 = bf16[6,256,128]{2,1,0:T(8,128)(2,1)} reshape(bf16[6,16,2048]{2,1,0:T(8,128)(2,1)} %copy.63) | data formatting | bytes 786432 | tf_op jit(solution)/shard_map/reshape | solution.py:64
  63.4 3.1 %convolution_bitcast_fusion = f32[6,1024,128]{1,2,0:T(8,128)S(1)} fusion(bf16[6,256,128]{2,1,0:T(8,128)(2,1)} %reshape.146, f32[512,256]{1,0:T(8,128)} %copy-done, f32[512,256]{1,0:T(8,128)} %copy-done.2), kind=kOutput, calls=%fused_computation.30 | convolution fusion | flops 2416181248 | bytes 4587520 | tf_op jit(solution)/shard_map/ka,cab->ckb/dot_general | solution.py:65
  66.5 1.0 multiply_add_fusion.3
  67.6 3.2 %fusion.6 = f32[6,512,256]{1,2,0:T(8,128)S(1)} fusion(f32[6,512,128]{1,2,0:T(8,128)S(1)} %get-tuple-element.17, f32[6,512,128]{1,2,0:T(8,128)S(1)} %get-tuple-element.16, f32[128,128]{0,1:T(8,128)S(1)} %copy-done.5, f32[128,128]{0,1:T(8,128)S(1)} %get-tuple-element.30, f32[128,128]{0,1:T(8,128)S(1)} %fusion.75), kind=kOutput, calls=%fused_computation.12 | convolution fusion | flops 2416902144 | bytes 6488064 | tf_op jit(solution)/shard_map/ckb,bj->ckj/dot_general | solution.py:71
  70.8 3.5 %fusion.10 = f32[6,512,256]{1,2,0:T(8,128)S(1)} fusion(f32[6,512,128]{1,2,0:T(8,128)S(1)} %get-tuple-element.20, f32[6,512,128]{1,2,0:T(8,128)S(1)} %get-tuple-element.21, f32[128,128]{0,1:T(8,128)S(1)} %copy-done.5, f32[128,128]{0,1:T(8,128)S(1)} %get-tuple-element.30, f32[128,128]{0,1:T(8,128)S(1)} %fusion.75), kind=kOutput, calls=%fused_computation.16 | convolution fusion | flops 2416902144 | bytes 6488064 | tf_op jit(solution)/shard_map/ckb,bj->ckj/dot_general | solution.py:71
  74.3 0.8 multiply_subtract_fusion.1
  75.1 3.4 %fusion.14 = f32[6,512,256]{1,2,0:T(8,128)S(1)} fusion(f32[6,512,128]{1,2,0:T(8,128)S(1)} %get-tuple-element.13, f32[6,512,128]{1,2,0:T(8,128)S(1)} %get-tuple-element.12, f32[128,128]{0,1:T(8,128)S(1)} %copy-done.5, f32[128,128]{0,1:T(8,128)S(1)} %fusion.75, f32[128,128]{0,1:T(8,128)S(1)} %get-tuple-element.30), kind=kOutput, calls=%fused_computation.20 | convolution fusion | flops 2416902144 | bytes 6488064 | tf_op jit(solution)/shard_map/ckj,jb->ckb/dot_general | solution.py:79
  78.5 0.5 multiply_subtract_fusion
  79.0 0.5 copy-done.1
  79.5 0.2 copy-done.3
  79.6 2.6 %fusion.26 = f32[6,256,128]{1,2,0:T(8,128)S(1)} fusion(f32[6,512,128]{1,2,0:T(8,128)S(1)} %get-tuple-element.15, f32[6,512,128]{1,2,0:T(8,128)S(1)} %get-tuple-element.14, f32[512,256]{1,0:T(8,128)S(1)} %copy-done.1, f32[512,256]{1,0:T(8,128)S(1)} %copy-done.3), kind=kOutput, calls=%fused_computation.40 | convolution fusion | flops 2417164288 | bytes 4980736 | tf_op jit(solution)/shard_map/ka,ckb->cab/dot_general | solution.py:85
  82.3 0.3 copy.72
  82.5 0.1 reshape_reshape.3
  82.6 1.4 copy.73
  84.1 4.1 %all-to-all-start.1 = ((f32[6,16,2048]{2,0,1:T(8,128)}), f32[6,16,2048]{2,0,1:T(8,128)S(1)}, u32[]{:S(2)}, u32[]{:S(2)}) async-start(f32[6,16,2048]{2,0,1:T(8,128)} %copy.73), calls=%async_computation.1 | async-start | bytes 2097152 | tf_op jit(solution)/shard_map/all_to_all | solution.py:120
  88.2 12.4 %copy.58 = bf16[2048,2048]{0,1:T(8,128)(2,1)} copy(bf16[2048,2048]{1,0:T(8,128)(2,1)} %param.12) | data formatting | bytes 16777216 | tf_op args[3]
  100.6 12.3 %copy.59 = bf16[2048,2048]{0,1:T(8,128)(2,1)} copy(bf16[2048,2048]{1,0:T(8,128)(2,1)} %param.11) | data formatting | bytes 16777216 | tf_op args[2]
  112.9 0.0 all-to-all-done.1
  113.0 0.5 copy.74
  113.4 0.0 copy-start.8
  113.4 8.2 %scatter_custom_fusion = f32[2048,2048]{0,1:T(8,128)} fusion(s32[64]{0:T(128)S(1)} %get-tuple-element.23, f32[]{:T(128)} %constant.64.clone.1, f32[]{:T(128)} %constant.81.clone.1, pred[64]{0:T(512)(128)(4,1)S(1)} %get-tuple-element.25, f32[96,2048]{1,0:T(8,128)S(1)} %bitcast.65, s32[1024]{0:T(1024)S(1)} %pad_clamp_fusion), kind=kCustom, calls=%fused_computation.9 | custom fusion | flops 131072 | bytes 17568264 | tf_op jit(solution)/shard_map/scatter | solution.py:132
  121.6 20.9 %fusion = (f32[2048]{0:T(1024)S(1)}, bf16[2048,2048]{0,1:T(8,128)(2,1)}) fusion(f32[2048,2048]{0,1:T(8,128)} %scatter_custom_fusion, bf16[2048,2048]{0,1:T(8,128)(2,1)} %copy.61, bf16[2048,2048]{0,1:T(8,128)(2,1)} %copy.60, f32[2048]{0:T(1024)S(1)} %copy-done.8, bf16[2048,2048]{0,1:T(8,128)(2,1)} %copy.59, bf16[2048,2048]{0,1:T(8,128)(2,1)} %copy.58), kind=kLoop, calls=%fused_computation.4 | loop fusion | flops 62912512 | bytes 58736640 | tf_op jit(solution)/shard_map/reduce_sum | solution.py:138
  142.5 5.0 %psum.7 = f32[2048]{0:T(1024)S(1)} all-reduce(f32[2048]{0:T(1024)S(1)} %get-tuple-element.10), channel_id=1, replica_groups=mesh['chan'=2,'seqo'=4,'seqi'=4] {'chan'}, use_global_device_ids=true, to_apply=%region_3.4 | all-reduce | flops 2048 | bytes 16384 | tf_op jit(solution)/shard_map/psum | solution.py:139
  147.5 12.2 %copy.75 = bf16[2048,2048]{1,0:T(8,128)(2,1)} copy(bf16[2048,2048]{0,1:T(8,128)(2,1)} %get-tuple-element.11) | data formatting | bytes 16777216
  159.7 8.5 %fusion.2 = bf16[2048,2048]{0,1:T(8,128)(2,1)} fusion(bf16[2048,2048]{0,1:T(8,128)(2,1)} %get-tuple-element.11, f32[2048]{0:T(1024)S(1)} %copy-done.7, f32[2048]{0:T(1024)S(1)} %add_rsqrt_fusion), kind=kLoop, calls=%fused_computation.6 | loop fusion | flops 16777216 | bytes 16793600 | tf_op jit(solution)/shard_map/convert_element_type | solution.py:142
  168.3 12.2 %copy.76 = bf16[2048,2048]{1,0:T(8,128)(2,1)} copy(bf16[2048,2048]{0,1:T(8,128)(2,1)} %fusion.2) | data formatting | bytes 16777216
  (18 shorter events, 0.1 us)
Async XLA Ops:
  15.8 12.2 %copy-start.10 = (s32[1,64]{1,0:T(1,128)S(1)}, s32[1,64]{1,0:T(1,128)}, u32[]{:S(2)}) copy-start(s32[1,64]{1,0:T(1,128)} %param.14) | copy-start | bytes 772
  28.0 17.2 %copy-start.6 = (bf16[1,1,6,32768]{3,2,1,0:T(8,128)(2,1)S(1)}, bf16[1,1,6,32768]{3,2,1,0:T(8,128)(2,1)}, u32[]{:S(2)}) copy-start(bf16[1,1,6,32768]{3,2,1,0:T(8,128)(2,1)} %param.13) | copy-start | bytes 1179652
  37.5 21.9 %all-to-all-start = ((bf16[6,16,2048]{2,0,1:T(8,128)(2,1)}), bf16[6,16,2048]{2,0,1:T(8,128)(2,1)}, u32[]{:S(2)}, u32[]{:S(2)}) async-start(bf16[6,16,2048]{2,0,1:T(8,128)(2,1)} %copy.62), calls=%async_computation | async-start | bytes 1048576 | tf_op jit(solution)/shard_map/all_to_all | solution.py:112
  50.9 0.8 copy-start
  50.9 1.0 copy-start.2
  63.4 3.1 %copy-start.4 = (f32[512,128]{0,1:T(8,128)S(1)}, f32[512,128]{0,1:T(8,128)}, u32[]{:S(2)}) copy-start(f32[512,128]{0,1:T(8,128)} %get-tuple-element.29) | copy-start | bytes 786436
  66.5 1.0 copy-start.5
  78.4 1.0 copy-start.1
  78.4 1.2 copy-start.3
  84.1 28.9 %all-to-all-start.1 = ((f32[6,16,2048]{2,0,1:T(8,128)}), f32[6,16,2048]{2,0,1:T(8,128)S(1)}, u32[]{:S(2)}, u32[]{:S(2)}) async-start(f32[6,16,2048]{2,0,1:T(8,128)} %copy.73), calls=%async_computation.1 | async-start | bytes 2097152 | tf_op jit(solution)/shard_map/all_to_all | solution.py:120
  100.6 12.3 %copy-start.9 = (s32[1,64]{1,0:T(1,128)S(1)}, s32[1,64]{1,0:T(1,128)}, u32[]{:S(2)}) copy-start(s32[1,64]{1,0:T(1,128)} %param.15) | copy-start | bytes 772
  113.4 8.2 %copy-start.8 = (f32[2048]{0:T(1024)S(1)}, f32[2048]{0:T(1024)}, u32[]{:S(2)}) copy-start(f32[2048]{0:T(1024)} %param.16) | copy-start | bytes 24580
  147.5 12.2 %copy-start.7 = (f32[2048]{0:T(1024)S(1)}, f32[2048]{0:T(1024)}, u32[]{:S(2)}) copy-start(f32[2048]{0:T(1024)} %param.17) | copy-start | bytes 24580
where the time goes:
time: 183 us; the launch traced here: 180 us
  local copies, waits for them, and re-layouts  83.5 us (46%)
  other arithmetic  47.7 us (26%)
  matrix products  26.8 us (15%)
  starting transfers between devices  11.5 us (6%)
  waiting for transfers between devices  5.13 us (3%)
  blocking collectives  4.98 us (3%)
    unnamed x29, local copies, waits for them, and re-layouts  75.3 us
    reduce_sum x1, other arithmetic, local(): squares = jnp.sum(hidden_wide * hidden_wide, axis=1)  20.9 us
    convert_element_type x1, other arithmetic, local(): (hidden_wide * scaling[:, None] * norm_gain[None, :]).astype(jnp.bfloat16)  8.53 us
    dot_general x1, matrix products, local(): lax.dot_general(picker, gated_prod, (((1,), (1,)), ((), ())), preferred_e...  8.5 us
    scatter x1, other arithmetic, local(): jnp.zeros((tok_rows, slab_width), jnp.float32).at[:, put_at]  8.18 us
    all_to_all x1, starting transfers between devices, local(): lax.all_to_all(outgoing.reshape(own_slots, owner_count, tok_rows), ('seqo...  7.4 us
    dot_general x2, matrix products, forward(): spec = jnp.einsum('ckb,bj->ckj', stacked, inner_fwd, precision=highest)  6.71 us
    all_to_all x1, waiting for transfers between devices, local(): lax.all_to_all(outgoing.reshape(own_slots, owner_count, tok_rows), ('seqo...  5.13 us
  transfers between devices with their start and end apart: 2, of which 1 were waited for; matrix products, arithmetic and copies ran while one was open for 18% of the time, Pallas kernels for 0%

commit v1 on v0

v1 whole, which is shorter than its diff:
```python
import functools

import jax
import jax.numpy as jnp
import numpy as np
from jax import lax
from jax.experimental import pallas as pl
from jax.experimental.pallas import tpu as pltpu
from jax.sharding import PartitionSpec as P

LANES = 128
TILE = 256
MIB = 1 << 20
norm_eps = 1e-06
f32 = jnp.float32
bf16 = jnp.bfloat16


def split_np(table):
    high = table.astype(jnp.bfloat16)
    low = (table - high.astype(np.float64)).astype(jnp.bfloat16)
    return high, low


def dft_tables(length):
    inner = LANES
    outer = length // inner
    a = np.arange(outer)
    b = np.arange(inner)
    quarter = np.arange(outer) + 0.25
    outer_angle = 2 * np.pi / outer * np.mod(quarter[:, None] * a[None, :], outer)
    turn_angle = 2 * np.pi / length * (quarter[:, None] * b[None, :])
    inner_angle = 2 * np.pi / inner * np.mod(b[:, None] * b[None, :], inner)
    outer_fwd = np.concatenate([np.cos(outer_angle), -np.sin(outer_angle)], axis=0)
    c, s = np.cos(inner_angle), np.sin(inner_angle)
    inner_fwd = np.concatenate(
        [np.concatenate([c, -s], axis=1), np.concatenate([s, c], axis=1)], axis=0
    )
    inner_back = np.concatenate(
        [np.concatenate([c, s], axis=1), np.concatenate([-s, c], axis=1)], axis=0
    )
    outer_back = np.concatenate([np.cos(outer_angle).T, -np.sin(outer_angle).T], axis=1) / length
    turn = np.concatenate([np.cos(turn_angle), np.sin(turn_angle)], axis=1).astype(np.float32)
    outer_fwd = np.concatenate(split_np(outer_fwd), axis=1)
    high, low = split_np(inner_fwd)
    inner_fwd = np.concatenate([high, high, low], axis=0)
    high, low = split_np(inner_back)
    inner_back = np.concatenate([high, high, low], axis=0)
    high, low = split_np(outer_back)
    outer_back = np.concatenate([high, high, low], axis=1)
    return outer_fwd, turn, inner_fwd, inner_back, outer_back


def split(value):
    high = value.astype(bf16)
    low = (value - high.astype(f32)).astype(bf16)
    return high, low


def dot(x, y):
    return jnp.dot(x, y, preferred_element_type=f32)


def dot_rows(x, y):
    return lax.dot_general(x, y, (((0,), (0,)), ((), ())), preferred_element_type=f32)


def to_spectrum(blocks, slots, outer_fwd, turn, inner_fwd):
    outer = blocks.shape[0]
    first = dot(outer_fwd[...], jnp.concatenate([blocks, blocks], axis=0))
    cos, sin = turn[:, :LANES], turn[:, LANES:]
    result = []
    for s in range(slots):
        re = first[:outer, s * LANES : (s + 1) * LANES]
        im = first[outer:, s * LANES : (s + 1) * LANES]
        turned = jnp.concatenate([re * cos + im * sin, im * cos - re * sin], axis=1)
        high, low = split(turned)
        result.append(dot(jnp.concatenate([high, low, high], axis=1), inner_fwd[...]))
    return result


def filter_kernel(filters, outer_fwd, turn, inner_fwd, spectra):
    slots, length = filters.shape
    outer = length // LANES
    wide = filters[...].astype(f32)
    blocks = [wide[s].reshape(outer, LANES) for s in range(slots)]
    blocks = jnp.concatenate(blocks, axis=1).astype(bf16)
    parts = to_spectrum(blocks, slots, outer_fwd, turn, inner_fwd)
    for s in range(slots):
        spectra[s] = parts[s]


def convolve_kernel(signals, spectra, outer_fwd, turn, inner_fwd, inner_back, outer_back, out):
    slots = spectra.shape[0]
    outer = spectra.shape[1]
    cos, sin = turn[:, :LANES], turn[:, LANES:]
    blocks = signals[...].reshape(outer, slots * LANES)
    parts = to_spectrum(blocks, slots, outer_fwd, turn, inner_fwd)
    for s in range(slots):
        sig_re, sig_im = parts[s][:, :LANES], parts[s][:, LANES:]
        ker_re, ker_im = spectra[s, :, :LANES], spectra[s, :, LANES:]
        joint = jnp.concatenate(
            [sig_re * ker_re - sig_im * ker_im, sig_re * ker_im + sig_im * ker_re], axis=1
        )
        high, low = split(joint)
        back = dot(jnp.concatenate([high, low, high], axis=1), inner_back[...])
        re, im = back[:, :LANES], back[:, LANES:]
        turned = jnp.concatenate([re * cos - im * sin, im * cos + re * sin], axis=0)
        high, low = split(turned)
        causal = dot(outer_back[...], jnp.concatenate([high, low, high], axis=0))
        out[:, :, s * LANES : (s + 1) * LANES] = causal.reshape(
            out.shape[0], out.shape[1], LANES
        ).astype(bf16)


def iota(shape, axis):
    return lax.broadcasted_iota(jnp.int32, shape, axis)


def to_column(row):
    size = row.shape[1]
    same = iota((size, size), 0) == iota((size, size), 1)
    return jnp.sum(jnp.where(same, row, 0), axis=1, keepdims=True)


def channel_of_row(index_row, owners_row, owner_count, rows):
    slots = owners_row.shape[1]
    owners_col = to_column(owners_row)
    index_col = to_column(index_row)
    earlier = (owners_col == owners_row) & (iota((slots, slots), 1) < iota((slots, slots), 0))
    rank_col = jnp.sum(earlier.astype(jnp.int32), axis=1, keepdims=True)
    target_col = jnp.where(owners_col >= 0, rank_col * owner_count + owners_col, -1)
    hit = target_col == iota((slots, rows), 1)
    return jnp.sum(jnp.where(hit, index_col + 1, 0), axis=0, keepdims=True) - 1


def pick_rows(tile, onehot_t, rows):
    picked = dot(tile, onehot_t).T
    return [picked[:rows, i : i + LANES] for i in range(0, tile.shape[0], LANES)]


def pick_kernel(
    owner_count, slots, index, owners, gate, value, payload, picked, channels, onehot_t, acc
):
    step = pl.program_id(0)
    rows = owner_count * slots

    @pl.when(step == 0)
    def _():
        row = channel_of_row(index[...], owners[...], owner_count, onehot_t.shape[1])
        channels[...] = jnp.broadcast_to(row, channels.shape)
        onehot_t[...] = (iota(onehot_t.shape, 0) == row).astype(f32).astype(bf16)

    gated = (gate[...].astype(f32) * value[...].astype(f32)).astype(bf16)
    blocks = gate.shape[0] // LANES
    for i, block in enumerate(pick_rows(gated, onehot_t[...], rows)):
        acc[step * blocks + i] = block
        picked[i] = block.astype(bf16)

    @pl.when(step == pl.num_programs(0) - 1)
    def _():
        for s in range(slots):
            part = acc[:, s * owner_count : (s + 1) * owner_count, :]
            payload[:, :, s * LANES : (s + 1) * LANES] = jnp.swapaxes(part, 0, 1).astype(bf16)


def base_kernel(
    channels,
    skip,
    gate,
    value,
    out_gate,
    residual,
    base,
    sums,
    picked_gate,
    picked_res,
    skip_wide,
    onehot,
    kept,
    onehot_t,
):
    rows = onehot.shape[0]

    @pl.when(pl.program_id(0) == 0)
    def _():
        row = channels[0:1, :]
        onehot_t[...] = (iota(onehot_t.shape, 0) == row).astype(f32).astype(bf16)
        hit = iota(onehot.shape, 1) == to_column(row)[:rows]
        onehot[...] = hit.astype(f32).astype(bf16)
        kept[...] = jnp.broadcast_to(jnp.max(hit.astype(f32), axis=0, keepdims=True), kept.shape)
        skip_col = jnp.sum(jnp.where(hit, skip[...], 0.0), axis=1, keepdims=True)
        skip_wide[...] = jnp.broadcast_to(skip_col, skip_wide.shape)

    gated = (gate[...].astype(f32) * value[...].astype(f32)).astype(bf16).astype(f32)
    mixed = out_gate[...].astype(f32) * (skip[...] * gated)
    hidden = (residual[...].astype(f32) + mixed).astype(bf16)
    base[...] = hidden
    wide = jnp.where(kept[0:1, :] > 0.0, 0.0, hidden.astype(f32))
    squares = wide * wide
    partial = squares[:, :LANES]
    for i in range(LANES, squares.shape[1], LANES):
        partial = partial + squares[:, i : i + LANES]
    total = jnp.sum(partial.T, axis=0, keepdims=True)
    for i in range(sums.shape[0]):
        sums[i] = total[:, i * LANES : (i + 1) * LANES]
    for i, block in enumerate(pick_rows(out_gate[...], onehot_t[...], rows)):
        picked_gate[i] = block.astype(bf16)
    for i, block in enumerate(pick_rows(residual[...], onehot_t[...], rows)):
        picked_res[i] = block.astype(bf16)


def kept_kernel(conv, picked, picked_gate, picked_res, skip_wide, sums, hidden, totals):
    owner_count, blocks = conv.shape[:2]
    total = jnp.zeros((blocks, LANES), f32)
    for s in range(conv.shape[2] // LANES):
        at = slice(s * owner_count, (s + 1) * owner_count)
        conv_rows = jnp.swapaxes(conv[:, :, s * LANES : (s + 1) * LANES].astype(f32), 0, 1)
        wide = conv_rows + skip_wide[at, :] * picked[:, at, :].astype(f32)
        value = picked_res[:, at, :].astype(f32) + picked_gate[:, at, :].astype(f32) * wide
        value = value.astype(bf16)
        hidden[:, at, :] = value
        value = value.astype(f32)
        total = total + jnp.sum(value * value, axis=1)
    for i in range(blocks):
        totals[i] = total[i : i + 1, :] + sums[i]


def final_kernel(width, count, *refs):
    parts = refs[:count]
    base, hidden_kept, onehot, kept, gain, hidden, normed = refs[count:]
    for i in range(base.shape[0] // LANES):
        at = slice(i * LANES, (i + 1) * LANES)
        total = parts[0][i]
        for part in parts[1:]:
            total = total + part[i]
        scale = lax.rsqrt(total / width + norm_eps)
        scale = jnp.broadcast_to(scale, (LANES, LANES)).T[:, 0:1]
        placed = dot_rows(hidden_kept[i], onehot[...])
        wide = jnp.where(kept[0:1, :] > 0.0, placed, base[at, :].astype(f32))
        hidden[at, :] = wide.astype(bf16)
        normed[at, :] = (wide * scale * gain[...]).astype(bf16)


def whole(shape):
    return pl.BlockSpec(shape, lambda *_: (0,) * len(shape))


def call(kernel, outs, ins, flops, moved, limit, scratch=(), grid=(), specs=None, out_specs=None):
    return pl.pallas_call(
        kernel,
        out_shape=outs,
        grid=grid,
        in_specs=specs if specs is not None else [whole(x.shape) for x in ins],
        out_specs=out_specs if out_specs is not None else [whole(x.shape) for x in outs],
        scratch_shapes=list(scratch),
        compiler_params=pltpu.CompilerParams(vmem_limit_bytes=limit),
        cost_estimate=pl.CostEstimate(flops=flops, bytes_accessed=moved, transcendentals=0),
    )(*ins)


def local(
    gate_in, value_in, out_gate, residual, filters, kept_index, kept_owner, skip_bias, norm_gain
):
    tok_rows, slab = gate_in.shape
    slots, length = filters.shape[2:]
    chan_devices = lax.axis_size("chan")
    owner_count = lax.axis_size("seqo") * lax.axis_size("seqi")
    rows = slots * owner_count
    lanes_rows = -(-rows // LANES) * LANES
    blocks = tok_rows // LANES
    outer = length // LANES
    tile = min(TILE, tok_rows)
    steps = tok_rows // tile
    dense = tok_rows * slab * 2
    sds = jax.ShapeDtypeStruct
    buffer = (owner_count, blocks, slots * LANES)
    tables = [jnp.asarray(x) for x in dft_tables(length)]
    outer_fwd, turn, inner_fwd, inner_back, outer_back = tables
    skip_row = skip_bias[None, :]
    gain_row = norm_gain[None, :]
    row_tile = pl.BlockSpec((tile, slab), lambda i: (i, 0))

    block_tile = tile // LANES
    picks_tile = pl.BlockSpec((block_tile, rows, LANES), lambda i: (i, 0, 0))
    sums_tile = pl.BlockSpec((block_tile, 1, LANES), lambda i: (i, 0, 0))
    picks = sds((blocks, rows, LANES), bf16)
    row_sums = sds((blocks, 1, LANES), f32)

    outs = [sds(buffer, bf16), picks, sds((8, lanes_rows), jnp.int32)]
    payload, picked, channels = call(
        functools.partial(pick_kernel, owner_count, slots),
        outs,
        [kept_index, kept_owner, gate_in, value_in],
        2 * tok_rows * slab * rows,
        2 * dense,
        32 * MIB,
        scratch=[
            pltpu.VMEM((slab, lanes_rows), bf16),
            pltpu.VMEM((blocks, rows, LANES), f32),
        ],
        grid=(steps,),
        specs=[whole(kept_index.shape), whole(kept_owner.shape), row_tile, row_tile],
        out_specs=[whole(buffer), picks_tile, whole(outs[2].shape)],
    )

    incoming = lax.all_to_all(payload, ("seqo", "seqi"), split_axis=0, concat_axis=0, tiled=True)

    spectrum = (slots, outer, 2 * LANES)
    (spectra,) = call(
        filter_kernel,
        [sds(spectrum, f32)],
        [filters[0, 0], outer_fwd, turn, inner_fwd],
        2 * slots * length * 2 * (2 * outer + 6 * LANES),
        8 * MIB,
        32 * MIB,
    )

    outs = [
        sds((tok_rows, slab), bf16),
        row_sums,
        picks,
        picks,
        sds((rows, LANES), f32),
        sds((rows, slab), bf16),
        sds((8, slab), f32),
    ]
    base, sums, picked_gate, picked_res, skip_wide, onehot, kept = call(
        base_kernel,
        outs,
        [channels, skip_row, gate_in, value_in, out_gate, residual],
        4 * tok_rows * slab * rows,
        5 * dense,
        32 * MIB,
        scratch=[pltpu.VMEM((slab, lanes_rows), bf16)],
        grid=(steps,),
        specs=[whole(channels.shape), whole(skip_row.shape)] + [row_tile] * 4,
        out_specs=[row_tile, sums_tile, picks_tile, picks_tile]
        + [whole(x.shape) for x in outs[4:]],
    )

    (convolved,) = call(
        convolve_kernel,
        [sds(buffer, bf16)],
        [incoming, spectra, outer_fwd, turn, inner_fwd, inner_back, outer_back],
        2 * slots * length * 2 * (5 * outer + 12 * LANES),
        8 * MIB,
        32 * MIB,
    )

    returned = lax.all_to_all(convolved, ("seqo", "seqi"), split_axis=0, concat_axis=0, tiled=True)

    hidden_kept, totals = call(
        kept_kernel,
        [picks, row_sums],
        [returned, picked, picked_gate, picked_res, skip_wide, sums],
        8 * rows * tok_rows,
        10 * rows * tok_rows,
        32 * MIB,
    )

    parts = [totals]
    for shift in range(1, chan_devices):
        ring = [(i, (i + shift) % chan_devices) for i in range(chan_devices)]
        parts.append(lax.ppermute(totals, "chan", ring))

    ins = parts + [base, hidden_kept, onehot, kept, gain_row]
    specs = [sums_tile] * len(parts) + [
        row_tile,
        picks_tile,
        whole(onehot.shape),
        whole(kept.shape),
        whole(gain_row.shape),
    ]
    hidden, normed = call(
        functools.partial(final_kernel, float(slab * chan_devices), len(parts)),
        [sds((tok_rows, slab), bf16)] * 2,
        ins,
        2 * tok_rows * slab * rows,
        3 * dense,
        32 * MIB,
        grid=(steps,),
        specs=specs,
        out_specs=[row_tile, row_tile],
    )
    return (hidden, normed)


def solution(mesh):
    positions = P(("seqo", "seqi"), "chan")
    in_specs = (
        positions,
        positions,
        positions,
        positions,
        P("chan", ("seqo", "seqi"), None, None),
        P("chan", None),
        P("chan", None),
        P("chan"),
        P("chan"),
    )
    return jax.shard_map(
        local, mesh=mesh, in_specs=in_specs, out_specs=(positions, positions), check_vma=False
    )
```

time: 183 us -> 85.4 us (0.47); the launches traced: 180 us -> 84.8 us
  local copies, waits for them, and re-layouts: 83.5 us -> 21.8 us
  other arithmetic: 47.7 us -> 0 us
  Pallas kernels: 0 us -> 38 us
  matrix products: 26.8 us -> 0 us
  waiting for transfers between devices: 5.13 us -> 11.6 us
  blocking collectives: 4.98 us -> 0 us
    unnamed x29 -> x34, local copies, waits for them, and re-layouts: 75.3 us -> 21.8 us
    pallas_call x0 -> x6, Pallas kernels: none -> 38 us  [call(): pl.pallas_call(kernel, out_shape=outs, grid=grid, in_specs=specs if specs...]
    dot_general x6 -> x0, matrix products: 24.3 us -> none  [the longest x1 8.5 us: local(): lax.dot_general(picker, gated_prod, (((1,), (1,)), ((), ())), preferred_e...]
    reduce_sum x2 -> x0, other arithmetic: 21.8 us -> none  [the longest x1 20.9 us: local(): squares = jnp.sum(hidden_wide * hidden_wide, axis=1)]
    convert_element_type x1 -> x0, other arithmetic: 8.53 us -> none  [local(): (hidden_wide * scaling[:, None] * norm_gain[None, :]).astype(jnp.bfloat16)]
    scatter x1 -> x0, other arithmetic: 8.18 us -> none  [local(): jnp.zeros((tok_rows, slab_width), jnp.float32).at[:, put_at]]
    psum x1 -> x0, blocking collectives: 4.98 us -> none  [local(): row_total = lax.psum(squares, 'chan')]
    all_to_all x2, waiting for transfers between devices: 5.13 us -> 9.44 us  [the longest x1 9.43 us: local(): lax.all_to_all(payload, ('seqo', 'seqi'), split_axis=0, concat_axis=0, ti...]
  transfers between devices with their start and end apart: 2 -> 3, of which waited for: 1 -> 2; matrix products, arithmetic and copies ran while one was open for 18% -> 0% of each run, Pallas kernels for 0% -> 21%
where the time goes in v1:
time: 85.4 us; the launch traced here: 84.8 us
  Pallas kernels  38 us (44%)
  local copies, waits for them, and re-layouts  21.8 us (26%)
  starting transfers between devices  12.6 us (15%)
  waiting for transfers between devices  11.6 us (14%)
    pallas_call x6, Pallas kernels, call(): pl.pallas_call(kernel, out_shape=outs, grid=grid, in_specs=specs if specs...  38 us
    unnamed x34, local copies, waits for them, and re-layouts  21.8 us
    all_to_all x1, waiting for transfers between devices, local(): lax.all_to_all(payload, ('seqo', 'seqi'), split_axis=0, concat_axis=0, ti...  9.43 us
    all_to_all x1, starting transfers between devices, local(): lax.all_to_all(payload, ('seqo', 'seqi'), split_axis=0, concat_axis=0, ti...  7.49 us
    all_to_all x1, starting transfers between devices, local(): lax.all_to_all(convolved, ('seqo', 'seqi'), split_axis=0, concat_axis=0,...  3.55 us
    ppermute x1, waiting for transfers between devices, local(): parts.append(lax.ppermute(totals, 'chan', ring))  2.13 us
  transfers between devices with their start and end apart: 3, of which 2 were waited for; matrix products, arithmetic and copies ran while one was open for 0% of the time, Pallas kernels for 21%

profile of v1, /device:TPU:0, one launch (start us, length us, event | category | flops | bytes accessed | tf_op | source)
XLA Modules:
  0.0 84.8 jit_solution(3757487271963746724)
XLA Ops:
  0.6 0.0 copy-start
  0.6 3.4 %copy-done = bf16[2048,2048]{1,0:T(8,128)(2,1)S(1)} copy-done((bf16[2048,2048]{1,0:T(8,128)(2,1)S(1)}, bf16[2048,2048]{1,0:T(8,128)(2,1)}, u32[]{:S(2)}) %copy-start) | copy-done | bytes 8388632
  4.0 0.0 copy-start.2
  4.0 3.4 %copy-done.2 = bf16[2048,2048]{1,0:T(8,128)(2,1)S(1)} copy-done((bf16[2048,2048]{1,0:T(8,128)(2,1)S(1)}, bf16[2048,2048]{1,0:T(8,128)(2,1)}, u32[]{:S(2)}) %copy-start.2) | copy-done | bytes 8388632
  7.4 0.0 copy-start.7
  7.4 0.7 copy-done.7
  8.1 0.0 copy-start.8
  8.1 0.7 copy-done.8
  8.7 0.0 copy-start.9
  8.7 0.0 copy-start.11
  8.7 0.0 copy-start.12
  8.7 0.0 copy-start.14
  8.7 0.0 copy-start.10
  8.7 5.4 %shard_map.149 = (bf16[16,16,768]{2,1,0:T(8,128)(2,1)}, bf16[16,96,128]{2,1,0:T(8,128)(2,1)S(1)}, s32[8,128]{1,0:T(8,128)S(1)}) custom-call(s32[1,64]{1,0:T(1,128)S(1)} %copy-done.7, s32[1,64]{1,0:T(1,128)S(1)} %copy-done.8, bf16[2048,2048]{1,0:T(8,128)(2,1)S(1)} %copy-done, bf16[2048,2048]{1,0:T(8,128)(2,1)S(1)} %copy-done.2), custom_call_target="tpu_custom_call" | custom-call | flops 805306368 | bytes 16777216 | tf_op jit(solution)/shard_map/pallas_call | solution.py:250
  14.2 0.0 copy-start.5
  14.2 7.5 %all-to-all-start = ((bf16[16,16,768]{2,1,0:T(8,128)(2,1)}), bf16[16,16,768]{2,1,0:T(8,128)(2,1)S(1)}, u32[]{:S(2)}, u32[]{:S(2)}) async-start(bf16[16,16,768]{2,1,0:T(8,128)(2,1)} %get-tuple-element.14), calls=%async_computation | async-start | bytes 786432 | tf_op jit(solution)/shard_map/all_to_all | solution.py:307
  21.7 0.0 copy-done.9
  21.7 0.0 copy-done.11
  21.7 0.0 copy-done.12
  21.7 0.0 copy-done.14
  21.7 1.6 %shard_map.150.spectra = f32[6,256,256]{2,1,0:T(8,128)S(1)} custom-call(bf16[6,32768]{1,0:T(8,128)(2,1)S(1)} %bitcast.5, bf16[512,512]{1,0:T(8,128)(2,1)S(1)} %copy-done.11, f32[256,256]{1,0:T(8,128)S(1)} %copy-done.14, bf16[768,256]{1,0:T(8,128)(2,1)S(1)} %copy-done.12), custom_call_target="tpu_custom_call" | custom-call | flops 1006632960 | bytes 8388608 | tf_op jit(solution)/shard_map/pallas_call | solution.py:250
  23.3 0.0 copy-start.15
  23.3 1.1 %copy-done.15 = f32[6,256,256]{2,1,0:T(8,128)} copy-done((f32[6,256,256]{2,1,0:T(8,128)}, f32[6,256,256]{2,1,0:T(8,128)S(1)}, u32[]{:S(2)}) %copy-start.15) | copy-done | bytes 1572888
  24.4 9.4 %all-to-all-done.signals = bf16[16,16,768]{2,1,0:T(8,128)(2,1)S(1)} async-done(((bf16[16,16,768]{2,1,0:T(8,128)(2,1)}), bf16[16,16,768]{2,1,0:T(8,128)(2,1)S(1)}, u32[]{:S(2)}, u32[]{:S(2)}) %all-to-all-start) | async-done | bytes 393248 | tf_op jit(solution)/shard_map/all_to_all | solution.py:307
  33.9 0.0 copy-done.10
  33.9 0.0 copy-start.13
  33.9 1.0 %copy-done.13 = bf16[768,256]{1,0:T(8,128)(2,1)S(1)} copy-done((bf16[768,256]{1,0:T(8,128)(2,1)S(1)}, bf16[768,256]{1,0:T(8,128)(2,1)}, u32[]{:S(2)}) %copy-start.13) | copy-done | bytes 393240
  34.9 0.0 copy-start.16
  34.9 1.4 %copy-done.16 = f32[6,256,256]{2,1,0:T(8,128)S(1)} copy-done((f32[6,256,256]{2,1,0:T(8,128)S(1)}, f32[6,256,256]{2,1,0:T(8,128)}, u32[]{:S(2)}) %copy-start.16) | copy-done | bytes 1572888
  36.3 5.7 %shard_map.151 = bf16[16,16,768]{2,1,0:T(8,128)(2,1)} custom-call(bf16[16,16,768]{2,1,0:T(8,128)(2,1)S(1)} %all-to-all-done.signals, f32[6,256,256]{2,1,0:T(8,128)S(1)} %copy-done.16, bf16[512,512]{1,0:T(8,128)(2,1)S(1)} %copy-done.11, f32[256,256]{1,0:T(8,128)S(1)} %copy-done.14, bf16[768,256]{1,0:T(8,128)(2,1)S(1)} %copy-done.12, ...), custom_call_target="tpu_custom_call" | custom-call | flops 2214592512 | bytes 8388608 | tf_op jit(solution)/shard_map/pallas_call | solution.py:250
  42.0 3.6 %all-to-all-start.1 = ((bf16[16,16,768]{2,1,0:T(8,128)(2,1)}), bf16[16,16,768]{2,1,0:T(8,128)(2,1)S(1)}, u32[]{:S(2)}, u32[]{:S(2)}) async-start(bf16[16,16,768]{2,1,0:T(8,128)(2,1)} %shard_map.151), calls=%async_computation.1 | async-start | bytes 786432 | tf_op jit(solution)/shard_map/all_to_all | solution.py:351
  45.5 0.0 copy-done.5
  45.5 0.0 copy-start.1
  45.6 3.4 %copy-done.1 = bf16[2048,2048]{1,0:T(8,128)(2,1)S(1)} copy-done((bf16[2048,2048]{1,0:T(8,128)(2,1)S(1)}, bf16[2048,2048]{1,0:T(8,128)(2,1)}, u32[]{:S(2)}) %copy-start.1) | copy-done | bytes 8388632
  48.9 0.0 copy-start.6
  48.9 16.6 %shard_map.152 = (bf16[2048,2048]{1,0:T(8,128)(2,1)S(1)}, f32[16,1,128]{2,1,0:T(1,128)S(1)}, bf16[16,96,128]{2,1,0:T(8,128)(2,1)S(1)}, bf16[16,96,128]{2,1,0:T(8...) custom-call(s32[8,128]{1,0:T(8,128)S(1)} %get-tuple-element.16.channels, ...), custom_call_target="tpu_custom_call" | custom-call | flops 1610612736 | bytes 41943040 | tf_op jit(solution)/shard_map/pallas_call | solution.py:250
  65.5 0.0 copy-start.3
  65.5 3.4 %copy-done.3 = bf16[2048,2048]{1,0:T(8,128)(2,1)} copy-done((bf16[2048,2048]{1,0:T(8,128)(2,1)}, bf16[2048,2048]{1,0:T(8,128)(2,1)S(1)}, u32[]{:S(2)}) %copy-start.3) | copy-done | bytes 8388632
  68.9 0.0 all-to-all-done.1.conv
  68.9 0.5 shard_map.153
  69.5 1.6 %collective-permute-start = (f32[16,1,128]{2,1,0:T(1,128)S(1)}, f32[16,1,128]{2,1,0:T(1,128)S(1)}, u32[]{:S(2)}, u32[]{:S(2)}) collective-permute-start(f32[16,1,128]{2,1,0:T(1,128)S(1)} %get-tuple-element.21.refs_0_), channel_id=1, source_target_pairs={{0,16},{16,0},{1,17},{17,1},{2,18},{18,2},{3,19},{19,3},{4,20},{20... | collective-permute-start | bytes 24584 | tf_op jit(solution)/shard_map/ppermute | solution.py:365
  71.0 2.1 %collective-permute-done.refs_1_ = f32[16,1,128]{2,1,0:T(1,128)S(1)} collective-permute-done((f32[16,1,128]{2,1,0:T(1,128)S(1)}, f32[16,1,128]{2,1,0:T(1,128)S(1)}, u32[]{:S(2)}, u32[]{:S(2)}) %collective-permute-start) | collective-permute-done | bytes 8224 | tf_op jit(solution)/shard_map/ppermute | solution.py:365
  73.2 0.0 copy-done.6
  73.2 0.0 copy-start.4
  73.2 3.4 %copy-done.4 = bf16[2048,2048]{1,0:T(8,128)(2,1)S(1)} copy-done((bf16[2048,2048]{1,0:T(8,128)(2,1)S(1)}, bf16[2048,2048]{1,0:T(8,128)(2,1)}, u32[]{:S(2)}) %copy-start.4) | copy-done | bytes 8388632
  76.6 8.2 %shard_map.154 = (bf16[2048,2048]{1,0:T(8,128)(2,1)}, bf16[2048,2048]{1,0:T(8,128)(2,1)}) custom-call(f32[16,1,128]{2,1,0:T(1,128)S(1)} %get-tuple-element.21.refs_0_, f32[16,1,128]{2,1,0:T(1,128)S(1)} %collective-permute-done.refs_1_, bf16[2048,2048]{1,0:T(8,128)(2,1)S(1)} %copy-done.4, bf16[16,96,128]{2,1,0:T(8,128)(2,1)S(1)} %get-tuple-element.23.refs_3_, ...), custom_call_target="tpu_custom_call" | custom-call | flops 805306368 | bytes 25165824 | tf_op jit(solution)/shard_map/pallas_call | solution.py:250
Async XLA Ops:
  0.6 3.4 %copy-start = (bf16[2048,2048]{1,0:T(8,128)(2,1)S(1)}, bf16[2048,2048]{1,0:T(8,128)(2,1)}, u32[]{:S(2)}) copy-start(bf16[2048,2048]{1,0:T(8,128)(2,1)} %gate.3) | copy-start | bytes 25165828
  4.0 3.4 %copy-start.2 = (bf16[2048,2048]{1,0:T(8,128)(2,1)S(1)}, bf16[2048,2048]{1,0:T(8,128)(2,1)}, u32[]{:S(2)}) copy-start(bf16[2048,2048]{1,0:T(8,128)(2,1)} %value.3) | copy-start | bytes 25165828
  7.4 0.7 copy-start.7
  8.1 0.7 copy-start.8
  8.7 13.0 %copy-start.9 = (bf16[1,1,6,32768]{3,2,1,0:T(8,128)(2,1)S(1)}, bf16[1,1,6,32768]{3,2,1,0:T(8,128)(2,1)}, u32[]{:S(2)}) copy-start(bf16[1,1,6,32768]{3,2,1,0:T(8,128)(2,1)} %param.18) | copy-start | bytes 1179652
  8.7 13.0 %copy-start.11 = (bf16[512,512]{1,0:T(8,128)(2,1)S(1)}, bf16[512,512]{1,0:T(8,128)(2,1)}, u32[]{:S(2)}) copy-start(bf16[512,512]{1,0:T(8,128)(2,1)} %constant.10.clone.outer_fwd) | copy-start | bytes 1572868
  8.7 13.0 %copy-start.12 = (bf16[768,256]{1,0:T(8,128)(2,1)S(1)}, bf16[768,256]{1,0:T(8,128)(2,1)}, u32[]{:S(2)}) copy-start(bf16[768,256]{1,0:T(8,128)(2,1)} %constant.12.clone.inner_fwd) | copy-start | bytes 1179652
  8.7 13.0 %copy-start.14 = (f32[256,256]{1,0:T(8,128)S(1)}, f32[256,256]{1,0:T(8,128)}, u32[]{:S(2)}) copy-start(f32[256,256]{1,0:T(8,128)} %constant.11.clone.turn) | copy-start | bytes 786436
  8.7 25.2 %copy-start.10 = (bf16[256,1536]{1,0:T(8,128)(2,1)S(1)}, bf16[256,1536]{1,0:T(8,128)(2,1)}, u32[]{:S(2)}) copy-start(bf16[256,1536]{1,0:T(8,128)(2,1)} %constant.14.clone.outer_back) | copy-start | bytes 2359300
  14.2 31.4 %copy-start.5 = (f32[2048]{0:T(1024)S(1)}, f32[2048]{0:T(1024)}, u32[]{:S(2)}) copy-start(f32[2048]{0:T(1024)} %param.21) | copy-start | bytes 24580
  14.2 19.7 %all-to-all-start = ((bf16[16,16,768]{2,1,0:T(8,128)(2,1)}), bf16[16,16,768]{2,1,0:T(8,128)(2,1)S(1)}, u32[]{:S(2)}, u32[]{:S(2)}) async-start(bf16[16,16,768]{2,1,0:T(8,128)(2,1)} %get-tuple-element.14), calls=%async_computation | async-start | bytes 786432 | tf_op jit(solution)/shard_map/all_to_all | solution.py:307
  23.3 1.1 %copy-start.15 = (f32[6,256,256]{2,1,0:T(8,128)}, f32[6,256,256]{2,1,0:T(8,128)S(1)}, u32[]{:S(2)}) copy-start(f32[6,256,256]{2,1,0:T(8,128)S(1)} %shard_map.150.spectra) | copy-start | bytes 4718596
  33.9 1.0 %copy-start.13 = (bf16[768,256]{1,0:T(8,128)(2,1)S(1)}, bf16[768,256]{1,0:T(8,128)(2,1)}, u32[]{:S(2)}) copy-start(bf16[768,256]{1,0:T(8,128)(2,1)} %constant.13.clone.inner_back) | copy-start | bytes 1179652
  34.9 1.4 %copy-start.16 = (f32[6,256,256]{2,1,0:T(8,128)S(1)}, f32[6,256,256]{2,1,0:T(8,128)}, u32[]{:S(2)}) copy-start(f32[6,256,256]{2,1,0:T(8,128)} %copy-done.15) | copy-start | bytes 4718596
  42.0 27.0 %all-to-all-start.1 = ((bf16[16,16,768]{2,1,0:T(8,128)(2,1)}), bf16[16,16,768]{2,1,0:T(8,128)(2,1)S(1)}, u32[]{:S(2)}, u32[]{:S(2)}) async-start(bf16[16,16,768]{2,1,0:T(8,128)(2,1)} %shard_map.151), calls=%async_computation.1 | async-start | bytes 786432 | tf_op jit(solution)/shard_map/all_to_all | solution.py:351
  45.5 3.4 %copy-start.1 = (bf16[2048,2048]{1,0:T(8,128)(2,1)S(1)}, bf16[2048,2048]{1,0:T(8,128)(2,1)}, u32[]{:S(2)}) copy-start(bf16[2048,2048]{1,0:T(8,128)(2,1)} %gate.3) | copy-start | bytes 25165828
  48.9 24.3 %copy-start.6 = (f32[2048]{0:T(1024)S(1)}, f32[2048]{0:T(1024)}, u32[]{:S(2)}) copy-start(f32[2048]{0:T(1024)} %param.22) | copy-start | bytes 24580
  65.5 3.4 %copy-start.3 = (bf16[2048,2048]{1,0:T(8,128)(2,1)}, bf16[2048,2048]{1,0:T(8,128)(2,1)S(1)}, u32[]{:S(2)}) copy-start(bf16[2048,2048]{1,0:T(8,128)(2,1)S(1)} %get-tuple-element.22.refs_2_) | copy-start | bytes 25165828
  69.5 3.7 %collective-permute-start = (f32[16,1,128]{2,1,0:T(1,128)S(1)}, f32[16,1,128]{2,1,0:T(1,128)S(1)}, u32[]{:S(2)}, u32[]{:S(2)}) collective-permute-start(f32[16,1,128]{2,1,0:T(1,128)S(1)} %get-tuple-element.21.refs_0_), channel_id=1, source_target_pairs={{0,16},{16,0},{1,17},{17,1},{2,18},{18,2},{3,19},{19,3},{4,20},{20... | collective-permute-start | bytes 24584 | tf_op jit(solution)/shard_map/ppermute | solution.py:365
  73.2 3.4 %copy-start.4 = (bf16[2048,2048]{1,0:T(8,128)(2,1)S(1)}, bf16[2048,2048]{1,0:T(8,128)(2,1)}, u32[]{:S(2)}) copy-start(bf16[2048,2048]{1,0:T(8,128)(2,1)} %copy-done.3) | copy-start | bytes 25165828

commit v2 on v1

--- a/solution.py
+++ b/solution.py
@@ -10,6 +10,7 @@
 
 LANES = 128
 TILE = 256
+HALVES = 2
 MIB = 1 << 20
 norm_eps = 1e-06
 f32 = jnp.float32
@@ -151,9 +152,8 @@
         channels[...] = jnp.broadcast_to(row, channels.shape)
         onehot_t[...] = (iota(onehot_t.shape, 0) == row).astype(f32).astype(bf16)
 
-    gated = (gate[...].astype(f32) * value[...].astype(f32)).astype(bf16)
     blocks = gate.shape[0] // LANES
-    for i, block in enumerate(pick_rows(gated, onehot_t[...], rows)):
+    for i, block in enumerate(pick_rows(gate[...] * value[...], onehot_t[...], rows)):
         acc[step * blocks + i] = block
         picked[i] = block.astype(bf16)
 
@@ -164,39 +164,22 @@
             payload[:, :, s * LANES : (s + 1) * LANES] = jnp.swapaxes(part, 0, 1).astype(bf16)
 
 
-def base_kernel(
-    channels,
-    skip,
-    gate,
-    value,
-    out_gate,
-    residual,
-    base,
-    sums,
-    picked_gate,
-    picked_res,
-    skip_wide,
-    onehot,
-    kept,
-    onehot_t,
-):
-    rows = onehot.shape[0]
-
-    @pl.when(pl.program_id(0) == 0)
-    def _():
-        row = channels[0:1, :]
-        onehot_t[...] = (iota(onehot_t.shape, 0) == row).astype(f32).astype(bf16)
-        hit = iota(onehot.shape, 1) == to_column(row)[:rows]
-        onehot[...] = hit.astype(f32).astype(bf16)
-        kept[...] = jnp.broadcast_to(jnp.max(hit.astype(f32), axis=0, keepdims=True), kept.shape)
-        skip_col = jnp.sum(jnp.where(hit, skip[...], 0.0), axis=1, keepdims=True)
-        skip_wide[...] = jnp.broadcast_to(skip_col, skip_wide.shape)
-
-    gated = (gate[...].astype(f32) * value[...].astype(f32)).astype(bf16).astype(f32)
+def place_kernel(channels, skip, onehot, others, skip_wide):
+    hit = iota(onehot.shape, 1) == to_column(channels[0:1, :])[: onehot.shape[0]]
+    onehot[...] = hit.astype(f32).astype(bf16)
+    others[...] = jnp.broadcast_to(1.0 - jnp.max(hit.astype(f32), axis=0, keepdims=True), others.shape)
+    skip_col = jnp.sum(jnp.where(hit, skip[...], 0.0), axis=1, keepdims=True)
+    skip_wide[...] = jnp.broadcast_to(skip_col, skip_wide.shape)
+
+
+def base_kernel(onehot_t, others, skip, gate, value, out_gate, residual, *refs):
+    base, sums, picked_gate, picked_res = refs[-4:]
+    rows = picked_gate.shape[1]
+    gated = (gate[...] * value[...]).astype(f32)
     mixed = out_gate[...].astype(f32) * (skip[...] * gated)
-    hidden = (residual[...].astype(f32) + mixed).astype(bf16)
+    hidden = ((residual[...].astype(f32) + mixed) * others[0:1, :]).astype(bf16)
     base[...] = hidden
-    wide = jnp.where(kept[0:1, :] > 0.0, 0.0, hidden.astype(f32))
+    wide = hidden.astype(f32)
     squares = wide * wide
     partial = squares[:, :LANES]
     for i in range(LANES, squares.shape[1], LANES):
@@ -210,43 +193,61 @@
         picked_res[i] = block.astype(bf16)
 
 
-def kept_kernel(conv, picked, picked_gate, picked_res, skip_wide, sums, hidden, totals):
+def kept_kernel(halves, conv, picked, skip_wide, *refs):
+    hidden, totals = refs[-2:]
     owner_count, blocks = conv.shape[:2]
-    total = jnp.zeros((blocks, LANES), f32)
-    for s in range(conv.shape[2] // LANES):
-        at = slice(s * owner_count, (s + 1) * owner_count)
-        conv_rows = jnp.swapaxes(conv[:, :, s * LANES : (s + 1) * LANES].astype(f32), 0, 1)
-        wide = conv_rows + skip_wide[at, :] * picked[:, at, :].astype(f32)
-        value = picked_res[:, at, :].astype(f32) + picked_gate[:, at, :].astype(f32) * wide
-        value = value.astype(bf16)
-        hidden[:, at, :] = value
-        value = value.astype(f32)
-        total = total + jnp.sum(value * value, axis=1)
-    for i in range(blocks):
-        totals[i] = total[i : i + 1, :] + sums[i]
-
-
-def final_kernel(width, count, *refs):
+    size = blocks // halves
+    for h in range(halves):
+        sums, picked_gate, picked_res = refs[3 * h : 3 * h + 3]
+        at_h = slice(h * size, (h + 1) * size)
+        total = jnp.zeros((size, LANES), f32)
+        for s in range(conv.shape[2] // LANES):
+            at = slice(s * owner_count, (s + 1) * owner_count)
+            conv_rows = conv[:, at_h, s * LANES : (s + 1) * LANES].astype(f32)
+            conv_rows = jnp.swapaxes(conv_rows, 0, 1)
+            wide = conv_rows + skip_wide[at, :] * picked[at_h, at, :].astype(f32)
+            value = picked_res[:, at, :].astype(f32) + picked_gate[:, at, :].astype(f32) * wide
+            value = value.astype(bf16)
+            hidden[at_h, at, :] = value
+            value = value.astype(f32)
+            total = total + jnp.sum(value * value, axis=1)
+        for i in range(size):
+            totals[h * size + i] = total[i : i + 1, :] + sums[i]
+
+
+def hidden_kernel(base, hidden_kept, onehot, hidden, held):
+    for i in range(hidden.shape[0] // LANES):
+        rows = slice(i * LANES, (i + 1) * LANES)
+        value = base[rows, :] + dot_rows(hidden_kept[i], onehot[...]).astype(bf16)
+        hidden[rows, :] = value
+        held[rows, :] = value
+
+
+def norm_kernel(width, count, *refs):
     parts = refs[:count]
-    base, hidden_kept, onehot, kept, gain, hidden, normed = refs[count:]
-    for i in range(base.shape[0] // LANES):
-        at = slice(i * LANES, (i + 1) * LANES)
+    held, gain, normed = refs[count:]
+    for i in range(normed.shape[0] // LANES):
         total = parts[0][i]
         for part in parts[1:]:
             total = total + part[i]
         scale = lax.rsqrt(total / width + norm_eps)
         scale = jnp.broadcast_to(scale, (LANES, LANES)).T[:, 0:1]
-        placed = dot_rows(hidden_kept[i], onehot[...])
-        wide = jnp.where(kept[0:1, :] > 0.0, placed, base[at, :].astype(f32))
-        hidden[at, :] = wide.astype(bf16)
-        normed[at, :] = (wide * scale * gain[...]).astype(bf16)
+        rows = slice(i * LANES, (i + 1) * LANES)
+        wide = held[rows, :].astype(f32)
+        normed[rows, :] = (wide * scale * gain[...]).astype(bf16)
 
 
 def whole(shape):
     return pl.BlockSpec(shape, lambda *_: (0,) * len(shape))
 
 
-def call(kernel, outs, ins, flops, moved, limit, scratch=(), grid=(), specs=None, out_specs=None):
+def in_hbm(x):
+    return pltpu.with_memory_space_constraint(x, pltpu.HBM)
+
+
+def call(
+    kernel, outs, ins, flops, moved, limit, scratch=(), grid=(), specs=None, out_specs=None, alias=None
+):
     return pl.pallas_call(
         kernel,
         out_shape=outs,
@@ -254,6 +255,7 @@
         in_specs=specs if specs is not None else [whole(x.shape) for x in ins],
         out_specs=out_specs if out_specs is not None else [whole(x.shape) for x in outs],
         scratch_shapes=list(scratch),
+        input_output_aliases=alias or {},
         compiler_params=pltpu.CompilerParams(vmem_limit_bytes=limit),
         cost_estimate=pl.CostEstimate(flops=flops, bytes_accessed=moved, transcendentals=0),
     )(*ins)
@@ -270,8 +272,9 @@
     lanes_rows = -(-rows // LANES) * LANES
     blocks = tok_rows // LANES
     outer = length // LANES
-    tile = min(TILE, tok_rows)
+    tile = min(TILE, tok_rows // HALVES)
     steps = tok_rows // tile
+    half = steps // HALVES
     dense = tok_rows * slab * 2
     sds = jax.ShapeDtypeStruct
     buffer = (owner_count, blocks, slots * LANES)
@@ -279,65 +282,83 @@
     outer_fwd, turn, inner_fwd, inner_back, outer_back = tables
     skip_row = skip_bias[None, :]
     gain_row = norm_gain[None, :]
+    gate_in, value_in, out_gate, residual = map(in_hbm, (gate_in, value_in, out_gate, residual))
     row_tile = pl.BlockSpec((tile, slab), lambda i: (i, 0))
-
     block_tile = tile // LANES
     picks_tile = pl.BlockSpec((block_tile, rows, LANES), lambda i: (i, 0, 0))
     sums_tile = pl.BlockSpec((block_tile, 1, LANES), lambda i: (i, 0, 0))
     picks = sds((blocks, rows, LANES), bf16)
     row_sums = sds((blocks, 1, LANES), f32)
 
-    outs = [sds(buffer, bf16), picks, sds((8, lanes_rows), jnp.int32)]
-    payload, picked, channels = call(
+    outs = [
+        sds(buffer, bf16),
+        picks,
+        sds((8, lanes_rows), jnp.int32),
+        sds((slab, lanes_rows), bf16),
+    ]
+    payload, picked, channels, onehot_t = call(
         functools.partial(pick_kernel, owner_count, slots),
         outs,
-        [kept_index, kept_owner, gate_in, value_in],
+        [in_hbm(kept_index), in_hbm(kept_owner), gate_in, value_in],
         2 * tok_rows * slab * rows,
         2 * dense,
-        32 * MIB,
-        scratch=[
-            pltpu.VMEM((slab, lanes_rows), bf16),
-            pltpu.VMEM((blocks, rows, LANES), f32),
-        ],
+        16 * MIB,
+        scratch=[pltpu.VMEM((blocks, rows, LANES), f32)],
         grid=(steps,),
         specs=[whole(kept_index.shape), whole(kept_owner.shape), row_tile, row_tile],
-        out_specs=[whole(buffer), picks_tile, whole(outs[2].shape)],
+        out_specs=[whole(buffer), picks_tile] + [whole(x.shape) for x in outs[2:]],
     )
 
     incoming = lax.all_to_all(payload, ("seqo", "seqi"), split_axis=0, concat_axis=0, tiled=True)
 
-    spectrum = (slots, outer, 2 * LANES)
     (spectra,) = call(
         filter_kernel,
-        [sds(spectrum, f32)],
+        [sds((slots, outer, 2 * LANES), f32)],
         [filters[0, 0], outer_fwd, turn, inner_fwd],
         2 * slots * length * 2 * (2 * outer + 6 * LANES),
         8 * MIB,
-        32 * MIB,
-    )
-
-    outs = [
-        sds((tok_rows, slab), bf16),
-        row_sums,
-        picks,
-        picks,
-        sds((rows, LANES), f32),
-        sds((rows, slab), bf16),
-        sds((8, slab), f32),
-    ]
-    base, sums, picked_gate, picked_res, skip_wide, onehot, kept = call(
-        base_kernel,
-        outs,
-        [channels, skip_row, gate_in, value_in, out_gate, residual],
-        4 * tok_rows * slab * rows,
-        5 * dense,
-        32 * MIB,
-        scratch=[pltpu.VMEM((slab, lanes_rows), bf16)],
-        grid=(steps,),
-        specs=[whole(channels.shape), whole(skip_row.shape)] + [row_tile] * 4,
-        out_specs=[row_tile, sums_tile, picks_tile, picks_tile]
-        + [whole(x.shape) for x in outs[4:]],
-    )
+        16 * MIB,
+    )
+    onehot, others, skip_wide = call(
+        place_kernel,
+        [sds((rows, slab), bf16), sds((8, slab), f32), sds((rows, LANES), f32)],
+        [channels, skip_row],
+        rows * slab * 8,
+        rows * slab * 2,
+        8 * MIB,
+    )
+
+    def base_half(h, onehot_t, base):
+        first = h * half
+        place = pl.BlockSpec((tile, slab), lambda i: (first + i, 0))
+        outs = [
+            pltpu.VMEM((tok_rows, slab), bf16),
+            sds((blocks // HALVES, 1, LANES), f32),
+            sds((blocks // HALVES, rows, LANES), bf16),
+            sds((blocks // HALVES, rows, LANES), bf16),
+        ]
+        ins = [onehot_t, others, skip_row, gate_in, value_in, out_gate, residual]
+        specs = [whole(x.shape) for x in ins[:3]] + [place] * 4
+        alias = None
+        if base is not None:
+            alias = {len(ins): 0}
+            ins = ins + [base]
+            specs = specs + [pl.BlockSpec(memory_space=pl.ANY)]
+        return call(
+            base_kernel,
+            outs,
+            ins,
+            4 * tok_rows * slab * rows // HALVES,
+            5 * dense // HALVES,
+            20 * MIB,
+            grid=(half,),
+            specs=specs,
+            out_specs=[place, sums_tile, picks_tile, picks_tile],
+            alias=alias,
+        )
+
+    base, *half_picks = base_half(0, onehot_t, None)
+    spectra, base = lax.optimization_barrier((spectra, base))
 
     (convolved,) = call(
         convolve_kernel,
@@ -345,18 +366,21 @@
         [incoming, spectra, outer_fwd, turn, inner_fwd, inner_back, outer_back],
         2 * slots * length * 2 * (5 * outer + 12 * LANES),
         8 * MIB,
-        32 * MIB,
-    )
+        20 * MIB,
+    )
+    convolved, onehot_t = lax.optimization_barrier((convolved, onehot_t))
 
     returned = lax.all_to_all(convolved, ("seqo", "seqi"), split_axis=0, concat_axis=0, tiled=True)
 
+    base, *more_picks = base_half(1, onehot_t, base)
+
     hidden_kept, totals = call(
-        kept_kernel,
+        functools.partial(kept_kernel, HALVES),
         [picks, row_sums],
-        [returned, picked, picked_gate, picked_res, skip_wide, sums],
+        [returned, picked, skip_wide, *half_picks, *more_picks],
         8 * rows * tok_rows,
         10 * rows * tok_rows,
-        32 * MIB,
+        16 * MIB,
     )
 
     parts = [totals]
@@ -364,24 +388,27 @@
         ring = [(i, (i + shift) % chan_devices) for i in range(chan_devices)]
         parts.append(lax.ppermute(totals, "chan", ring))
 
-    ins = parts + [base, hidden_kept, onehot, kept, gain_row]
-    specs = [sums_tile] * len(parts) + [
-        row_tile,
-        picks_tile,
-        whole(onehot.shape),
-        whole(kept.shape),
-        whole(gain_row.shape),
-    ]
-    hidden, normed = call(
-        functools.partial(final_kernel, float(slab * chan_devices), len(parts)),
-        [sds((tok_rows, slab), bf16)] * 2,
-        ins,
+    hidden, held = call(
+        hidden_kernel,
+        [sds((tok_rows, slab), bf16), pltpu.VMEM((tok_rows, slab), bf16)],
+        [base, hidden_kept, onehot],
         2 * tok_rows * slab * rows,
-        3 * dense,
-        32 * MIB,
+        dense,
+        16 * MIB,
         grid=(steps,),
-        specs=specs,
+        specs=[row_tile, picks_tile, whole(onehot.shape)],
         out_specs=[row_tile, row_tile],
+    )
+    (normed,) = call(
+        functools.partial(norm_kernel, float(slab * chan_devices), len(parts)),
+        [sds((tok_rows, slab), bf16)],
+        parts + [held, gain_row],
+        4 * tok_rows * slab,
+        dense,
+        16 * MIB,
+        grid=(steps,),
+        specs=[sums_tile] * len(parts) + [row_tile, whole(gain_row.shape)],
+        out_specs=[row_tile],
     )
     return (hidden, normed)
 

time: 85.4 us -> 83.2 us (0.974)
  waiting for transfers between devices: 11.6 us -> 0.01 us
  Pallas kernels: 38 us -> 47.8 us
  local copies, waits for them, and re-layouts: 21.8 us -> 19.1 us
  starting transfers between devices: 12.6 us -> 14.9 us
    pallas_call x6 -> x9, Pallas kernels: 38 us -> 47.8 us  [call(): pl.pallas_call(kernel, out_shape=outs, grid=grid, in_specs=specs if specs...]
    all_to_all x1, waiting for transfers between devices: 9.43 us -> 0.01 us  [local(): lax.all_to_all(payload, ('seqo', 'seqi'), split_axis=0, concat_axis=0, ti...]
    unnamed x34 -> x32, local copies, waits for them, and re-layouts: 21.8 us -> 19.1 us
    all_to_all x1, starting transfers between devices: 3.55 us -> 6 us  [local(): lax.all_to_all(convolved, ('seqo', 'seqi'), split_axis=0, concat_axis=0,...]
    ppermute x1, waiting for transfers between devices: 2.13 us -> 0.01 us  [local(): parts.append(lax.ppermute(totals, 'chan', ring))]
  transfers between devices with their start and end apart: 3 -> 3, of which waited for: 2 -> 0; matrix products, arithmetic and copies ran while one was open for 0% -> 0% of each run, Pallas kernels for 21% -> 31%
where the time goes in v2:
time: 83.2 us; the launch traced here: 82.6 us
  Pallas kernels  47.8 us (57%)
  local copies, waits for them, and re-layouts  19.1 us (23%)
  starting transfers between devices  14.9 us (18%)
    pallas_call x9, Pallas kernels, call(): pl.pallas_call(kernel, out_shape=outs, grid=grid, in_specs=specs if specs...  47.8 us
    unnamed x32, local copies, waits for them, and re-layouts  19.1 us
    all_to_all x1, starting transfers between devices, local(): lax.all_to_all(payload, ('seqo', 'seqi'), split_axis=0, concat_axis=0, ti...  7.36 us
    all_to_all x1, starting transfers between devices, local(): lax.all_to_all(convolved, ('seqo', 'seqi'), split_axis=0, concat_axis=0,...  6 us
  transfers between devices with their start and end apart: 3, of which 0 were waited for; matrix products, arithmetic and copies ran while one was open for 0% of the time, Pallas kernels for 31%

profile of v2, /device:TPU:0, one launch (start us, length us, event | category | flops | bytes accessed | tf_op | source)
XLA Modules:
  0.0 82.6 jit_solution(9006007778168573305)
XLA Ops:
  0.6 0.0 copy-start.4
  0.6 10.6 %shard_map.149 = (bf16[16,16,768]{2,1,0:T(8,128)(2,1)}, bf16[16,96,128]{2,1,0:T(8,128)(2,1)S(1)}, s32[8,128]{1,0:T(8,128)S(1)}, bf16[2048,128]{1,0:T(8,128)(2,1)S(1)}) custom-call(s32[1,64]{1,0:T(1,128)} %index.1, s32[1,64]{1,0:T(1,128)} %owners.1, bf16[2048,2048]{1,0:T(8,128)(2,1)} %gate.5, bf16[2048,2048]{1,0:T(8,128)(2,1)} %value.5), custom_call_target="tpu_custom_call" | custom-call | flops 805306368 | bytes 16777216 | tf_op jit(solution)/shard_map/pallas_call | solution.py:251
  11.2 7.4 %all-to-all-start = ((bf16[16,16,768]{2,1,0:T(8,128)(2,1)}), bf16[16,16,768]{2,1,0:T(8,128)(2,1)S(1)}, u32[]{:S(2)}, u32[]{:S(2)}) async-start(bf16[16,16,768]{2,1,0:T(8,128)(2,1)} %get-tuple-element.25), calls=%async_computation | async-start | bytes 786432 | tf_op jit(solution)/shard_map/all_to_all | solution.py:312
  18.6 0.0 copy-done.4
  18.6 0.4 shard_map.151
  19.0 0.0 copy-start.6
  19.0 0.0 copy-start.8
  19.0 0.0 copy-start.10
  19.0 0.0 copy-start.12
  19.0 0.0 copy-start.7
  19.0 8.7 %shard_map.152 = (bf16[2048,2048]{1,0:T(8,128)(2,1)S(1)}, f32[8,1,128]{2,1,0:T(1,128)S(1)}, bf16[8,96,128]{2,1,0:T(8,128)(2,1)S(1)}, bf16[8,96,128]{2,1,0:T(8,128)(2,1)S(1)}) custom-call(bf16[2048,128]{1,0:T(8,128)(2,1)S(1)} %get-tuple-element.31.onehot_t, f32[8,2048]{1,0:T(8,128)S(1)} %get-tuple-element.28.others, f32[1,2048]{1,0:T(1,128)S(1)} %bitcast.4, ...), custom_call_target="tpu_custom_call" | custom-call | flops 805306368 | bytes 20971520 | tf_op jit(solution)/shard_map/pallas_call | solution.py:251
  27.7 0.0 copy-start
  27.7 3.4 %copy-done = bf16[2048,2048]{1,0:T(8,128)(2,1)} copy-done((bf16[2048,2048]{1,0:T(8,128)(2,1)}, bf16[2048,2048]{1,0:T(8,128)(2,1)S(1)}, u32[]{:S(2)}) %copy-start) | copy-done | bytes 8388632
  31.1 0.0 copy-done.6
  31.1 0.0 copy-done.8
  31.1 0.0 copy-done.10
  31.1 0.0 copy-done.12
  31.1 1.5 %shard_map.150.spectra = f32[6,256,256]{2,1,0:T(8,128)S(1)} custom-call(bf16[6,32768]{1,0:T(8,128)(2,1)S(1)} %bitcast.7, bf16[512,512]{1,0:T(8,128)(2,1)S(1)} %copy-done.8, f32[256,256]{1,0:T(8,128)S(1)} %copy-done.12, bf16[768,256]{1,0:T(8,128)(2,1)S(1)} %copy-done.10), custom_call_target="tpu_custom_call" | custom-call | flops 1006632960 | bytes 8388608 | tf_op jit(solution)/shard_map/pallas_call | solution.py:251
  32.6 0.0 copy-start.14
  32.6 1.1 %copy-done.14 = f32[6,256,256]{2,1,0:T(8,128)} copy-done((f32[6,256,256]{2,1,0:T(8,128)}, f32[6,256,256]{2,1,0:T(8,128)S(1)}, u32[]{:S(2)}) %copy-start.14) | copy-done | bytes 1572888
  33.8 0.0 all-to-all-done.signals
  33.8 0.0 copy-done.7
  33.8 0.0 copy-start.9
  33.8 1.0 %copy-done.9 = bf16[512,512]{1,0:T(8,128)(2,1)S(1)} copy-done((bf16[512,512]{1,0:T(8,128)(2,1)S(1)}, bf16[512,512]{1,0:T(8,128)(2,1)}, u32[]{:S(2)}) %copy-start.9) | copy-done | bytes 524312
  34.8 0.0 copy-start.11
  34.8 1.0 %copy-done.11 = bf16[768,256]{1,0:T(8,128)(2,1)S(1)} copy-done((bf16[768,256]{1,0:T(8,128)(2,1)S(1)}, bf16[768,256]{1,0:T(8,128)(2,1)}, u32[]{:S(2)}) %copy-start.11) | copy-done | bytes 393240
  35.8 0.0 copy-start.13
  35.8 0.9 %copy-done.13 = f32[256,256]{1,0:T(8,128)S(1)} copy-done((f32[256,256]{1,0:T(8,128)S(1)}, f32[256,256]{1,0:T(8,128)}, u32[]{:S(2)}) %copy-start.13) | copy-done | bytes 262168
  36.8 0.0 copy-start.15
  36.8 1.4 %copy-done.15 = f32[6,256,256]{2,1,0:T(8,128)S(1)} copy-done((f32[6,256,256]{2,1,0:T(8,128)S(1)}, f32[6,256,256]{2,1,0:T(8,128)}, u32[]{:S(2)}) %copy-start.15) | copy-done | bytes 1572888
  38.2 5.6 %shard_map.153 = bf16[16,16,768]{2,1,0:T(8,128)(2,1)} custom-call(bf16[16,16,768]{2,1,0:T(8,128)(2,1)S(1)} %all-to-all-done.signals, f32[6,256,256]{2,1,0:T(8,128)S(1)} %copy-done.15, bf16[512,512]{1,0:T(8,128)(2,1)S(1)} %copy-done.9, f32[256,256]{1,0:T(8,128)S(1)} %copy-done.13, bf16[768,256]{1,0:T(8,128)(2,1)S(1)} %copy-done.10, ...), custom_call_target="tpu_custom_call" | custom-call | flops 2214592512 | bytes 8388608 | tf_op jit(solution)/shard_map/pallas_call | solution.py:251
  43.8 6.0 %all-to-all-start.1 = ((bf16[16,16,768]{2,1,0:T(8,128)(2,1)}), bf16[16,16,768]{2,1,0:T(8,128)(2,1)S(1)}, u32[]{:S(2)}, u32[]{:S(2)}) async-start(bf16[16,16,768]{2,1,0:T(8,128)(2,1)} %shard_map.153), calls=%async_computation.1 | async-start | bytes 786432 | tf_op jit(solution)/shard_map/all_to_all | solution.py:373
  49.8 0.0 copy-start.1
  49.8 3.4 %copy-done.1 = bf16[2048,2048]{1,0:T(8,128)(2,1)S(1)} copy-done((bf16[2048,2048]{1,0:T(8,128)(2,1)S(1)}, bf16[2048,2048]{1,0:T(8,128)(2,1)}, u32[]{:S(2)}) %copy-start.1) | copy-done | bytes 8388632
  53.2 8.5 %shard_map.154 = (bf16[2048,2048]{1,0:T(8,128)(2,1)S(1)}, f32[8,1,128]{2,1,0:T(1,128)S(1)}, bf16[8,96,128]{2,1,0:T(8,128)(2,1)S(1)}, bf16[8,96,128]{2,1,0:T(8,128)(2,1)S(1)}) custom-call(bf16[2048,128]{1,0:T(8,128)(2,1)S(1)} %get-tuple-element.31.onehot_t, f32[8,2048]{1,0:T(8,128)S(1)} %get-tuple-element.28.others, ...), custom_call_target="tpu_custom_call", output_to_operand_aliasing={{0}: (7, {})} | custom-call | flops 805306368 | bytes 20971520 | tf_op jit(solution)/shard_map/pallas_call | solution.py:251
  61.7 0.0 copy-start.2
  61.7 3.4 %copy-done.2 = bf16[2048,2048]{1,0:T(8,128)(2,1)} copy-done((bf16[2048,2048]{1,0:T(8,128)(2,1)}, bf16[2048,2048]{1,0:T(8,128)(2,1)S(1)}, u32[]{:S(2)}) %copy-start.2) | copy-done | bytes 8388632
  65.1 0.0 copy-start.5
  65.1 0.0 all-to-all-done.1.conv
  65.1 0.5 shard_map.155
  65.6 1.6 %collective-permute-start = (f32[16,1,128]{2,1,0:T(1,128)S(1)}, f32[16,1,128]{2,1,0:T(1,128)S(1)}, u32[]{:S(2)}, u32[]{:S(2)}) collective-permute-start(f32[16,1,128]{2,1,0:T(1,128)S(1)} %get-tuple-element.46.refs_0_), channel_id=1, source_target_pairs={{0,16},{16,0},{1,17},{17,1},{2,18},{18,2},{3,19},{19,3},{4,20},{20... | collective-permute-start | bytes 24584 | tf_op jit(solution)/shard_map/ppermute | solution.py:389
  67.2 0.0 copy-start.3
  67.2 3.4 %copy-done.3 = bf16[2048,2048]{1,0:T(8,128)(2,1)S(1)} copy-done((bf16[2048,2048]{1,0:T(8,128)(2,1)S(1)}, bf16[2048,2048]{1,0:T(8,128)(2,1)}, u32[]{:S(2)}) %copy-start.3) | copy-done | bytes 8388632
  70.6 6.2 %shard_map.156 = (bf16[2048,2048]{1,0:T(8,128)(2,1)}, bf16[2048,2048]{1,0:T(8,128)(2,1)S(1)}) custom-call(bf16[2048,2048]{1,0:T(8,128)(2,1)S(1)} %copy-done.3, bf16[16,96,128]{2,1,0:T(8,128)(2,1)S(1)} %get-tuple-element.43.hidden_kept, bf16[96,2048]{1,0:T(8,128)(2,1)S(1)} %get-tuple-element.44.onehot), custom_call_target="tpu_custom_call" | custom-call | flops 805306368 | bytes 8388608 | tf_op jit(solution)/shard_map/pallas_call | solution.py:251
  76.8 0.0 collective-permute-done.refs_1_
  76.8 0.0 copy-done.5
  76.8 5.8 %shard_map.157 = bf16[2048,2048]{1,0:T(8,128)(2,1)} custom-call(f32[16,1,128]{2,1,0:T(1,128)S(1)} %get-tuple-element.46.refs_0_, f32[16,1,128]{2,1,0:T(1,128)S(1)} %collective-permute-done.refs_1_, bf16[2048,2048]{1,0:T(8,128)(2,1)S(1)} %get-tuple-element.47.refs_2_, f32[1,2048]{1,0:T(1,128)S(1)} %bitcast.6), custom_call_target="tpu_custom_call" | custom-call | flops 16777216 | bytes 8388608 | tf_op jit(solution)/shard_map/pallas_call | solution.py:251
Async XLA Ops:
  0.6 17.9 %copy-start.4 = (f32[2048]{0:T(1024)S(1)}, f32[2048]{0:T(1024)}, u32[]{:S(2)}) copy-start(f32[2048]{0:T(1024)} %param.21) | copy-start | bytes 24580
  11.2 22.6 %all-to-all-start = ((bf16[16,16,768]{2,1,0:T(8,128)(2,1)}), bf16[16,16,768]{2,1,0:T(8,128)(2,1)S(1)}, u32[]{:S(2)}, u32[]{:S(2)}) async-start(bf16[16,16,768]{2,1,0:T(8,128)(2,1)} %get-tuple-element.25), calls=%async_computation | async-start | bytes 786432 | tf_op jit(solution)/shard_map/all_to_all | solution.py:312
  19.0 12.1 %copy-start.6 = (bf16[1,1,6,32768]{3,2,1,0:T(8,128)(2,1)S(1)}, bf16[1,1,6,32768]{3,2,1,0:T(8,128)(2,1)}, u32[]{:S(2)}) copy-start(bf16[1,1,6,32768]{3,2,1,0:T(8,128)(2,1)} %param.18) | copy-start | bytes 1179652
  19.0 12.1 %copy-start.8 = (bf16[512,512]{1,0:T(8,128)(2,1)S(1)}, bf16[512,512]{1,0:T(8,128)(2,1)}, u32[]{:S(2)}) copy-start(bf16[512,512]{1,0:T(8,128)(2,1)} %constant.10.clone.outer_fwd) | copy-start | bytes 1572868
  19.0 12.1 %copy-start.10 = (bf16[768,256]{1,0:T(8,128)(2,1)S(1)}, bf16[768,256]{1,0:T(8,128)(2,1)}, u32[]{:S(2)}) copy-start(bf16[768,256]{1,0:T(8,128)(2,1)} %constant.12.clone.inner_fwd) | copy-start | bytes 1179652
  19.0 12.1 %copy-start.12 = (f32[256,256]{1,0:T(8,128)S(1)}, f32[256,256]{1,0:T(8,128)}, u32[]{:S(2)}) copy-start(f32[256,256]{1,0:T(8,128)} %constant.11.clone.turn) | copy-start | bytes 786436
  19.0 14.8 %copy-start.7 = (bf16[256,1536]{1,0:T(8,128)(2,1)S(1)}, bf16[256,1536]{1,0:T(8,128)(2,1)}, u32[]{:S(2)}) copy-start(bf16[256,1536]{1,0:T(8,128)(2,1)} %constant.14.clone.outer_back) | copy-start | bytes 2359300
  27.7 3.4 %copy-start = (bf16[2048,2048]{1,0:T(8,128)(2,1)}, bf16[2048,2048]{1,0:T(8,128)(2,1)S(1)}, u32[]{:S(2)}) copy-start(bf16[2048,2048]{1,0:T(8,128)(2,1)S(1)} %get-tuple-element.32.refs_0_) | copy-start | bytes 25165828
  32.6 1.1 %copy-start.14 = (f32[6,256,256]{2,1,0:T(8,128)}, f32[6,256,256]{2,1,0:T(8,128)S(1)}, u32[]{:S(2)}) copy-start(f32[6,256,256]{2,1,0:T(8,128)S(1)} %shard_map.150.spectra) | copy-start | bytes 4718596
  33.8 1.0 %copy-start.9 = (bf16[512,512]{1,0:T(8,128)(2,1)S(1)}, bf16[512,512]{1,0:T(8,128)(2,1)}, u32[]{:S(2)}) copy-start(bf16[512,512]{1,0:T(8,128)(2,1)} %constant.10.clone.outer_fwd) | copy-start | bytes 1572868
  34.8 1.0 %copy-start.11 = (bf16[768,256]{1,0:T(8,128)(2,1)S(1)}, bf16[768,256]{1,0:T(8,128)(2,1)}, u32[]{:S(2)}) copy-start(bf16[768,256]{1,0:T(8,128)(2,1)} %constant.13.clone.inner_back) | copy-start | bytes 1179652
  35.8 0.9 %copy-start.13 = (f32[256,256]{1,0:T(8,128)S(1)}, f32[256,256]{1,0:T(8,128)}, u32[]{:S(2)}) copy-start(f32[256,256]{1,0:T(8,128)} %constant.11.clone.turn) | copy-start | bytes 786436
  36.8 1.4 %copy-start.15 = (f32[6,256,256]{2,1,0:T(8,128)S(1)}, f32[6,256,256]{2,1,0:T(8,128)}, u32[]{:S(2)}) copy-start(f32[6,256,256]{2,1,0:T(8,128)} %copy-done.14) | copy-start | bytes 4718596
  43.8 21.3 %all-to-all-start.1 = ((bf16[16,16,768]{2,1,0:T(8,128)(2,1)}), bf16[16,16,768]{2,1,0:T(8,128)(2,1)S(1)}, u32[]{:S(2)}, u32[]{:S(2)}) async-start(bf16[16,16,768]{2,1,0:T(8,128)(2,1)} %shard_map.153), calls=%async_computation.1 | async-start | bytes 786432 | tf_op jit(solution)/shard_map/all_to_all | solution.py:373
  49.8 3.4 %copy-start.1 = (bf16[2048,2048]{1,0:T(8,128)(2,1)S(1)}, bf16[2048,2048]{1,0:T(8,128)(2,1)}, u32[]{:S(2)}) copy-start(bf16[2048,2048]{1,0:T(8,128)(2,1)} %copy-done) | copy-start | bytes 25165828
  61.7 3.4 %copy-start.2 = (bf16[2048,2048]{1,0:T(8,128)(2,1)}, bf16[2048,2048]{1,0:T(8,128)(2,1)S(1)}, u32[]{:S(2)}) copy-start(bf16[2048,2048]{1,0:T(8,128)(2,1)S(1)} %get-tuple-element.33.base) | copy-start | bytes 25165828
  65.1 11.7 %copy-start.5 = (f32[2048]{0:T(1024)S(1)}, f32[2048]{0:T(1024)}, u32[]{:S(2)}) copy-start(f32[2048]{0:T(1024)} %param.22) | copy-start | bytes 24580
  65.6 11.2 %collective-permute-start = (f32[16,1,128]{2,1,0:T(1,128)S(1)}, f32[16,1,128]{2,1,0:T(1,128)S(1)}, u32[]{:S(2)}, u32[]{:S(2)}) collective-permute-start(f32[16,1,128]{2,1,0:T(1,128)S(1)} %get-tuple-element.46.refs_0_), channel_id=1, source_target_pairs={{0,16},{16,0},{1,17},{17,1},{2,18},{18,2},{3,19},{19,3},{4,20},{20... | collective-permute-start | bytes 24584 | tf_op jit(solution)/shard_map/ppermute | solution.py:389
  67.2 3.4 %copy-start.3 = (bf16[2048,2048]{1,0:T(8,128)(2,1)S(1)}, bf16[2048,2048]{1,0:T(8,128)(2,1)}, u32[]{:S(2)}) copy-start(bf16[2048,2048]{1,0:T(8,128)(2,1)} %copy-done.2) | copy-start | bytes 25165828

commit v3 on v2

v3 whole, which is shorter than its diff:
```python
import functools

import jax
import jax.numpy as jnp
import numpy as np
from jax import lax
from jax.experimental import pallas as pl
from jax.experimental.pallas import tpu as pltpu
from jax.sharding import PartitionSpec as P

LANES = 128
TILE = 256
CHUNK = 16
MIB = 1 << 20
norm_eps = 1e-06
f32 = jnp.float32
bf16 = jnp.bfloat16


def split_np(table):
    high = table.astype(jnp.bfloat16)
    low = (table - high.astype(np.float64)).astype(jnp.bfloat16)
    return high, low


def dft_tables(length):
    inner = LANES
    outer = length // inner
    a = np.arange(outer)
    b = np.arange(inner)
    quarter = np.arange(outer) + 0.25
    outer_angle = 2 * np.pi / outer * np.mod(quarter[:, None] * a[None, :], outer)
    turn_angle = 2 * np.pi / length * (quarter[:, None] * b[None, :])
    inner_angle = 2 * np.pi / inner * np.mod(b[:, None] * b[None, :], inner)
    outer_fwd = np.concatenate([np.cos(outer_angle), -np.sin(outer_angle)], axis=0)
    c, s = np.cos(inner_angle), np.sin(inner_angle)
    inner_fwd = np.concatenate(
        [np.concatenate([c, -s], axis=1), np.concatenate([s, c], axis=1)], axis=0
    )
    inner_back = np.concatenate(
        [np.concatenate([c, s], axis=1), np.concatenate([-s, c], axis=1)], axis=0
    )
    outer_back = np.concatenate([np.cos(outer_angle).T, -np.sin(outer_angle).T], axis=1) / length
    turn = np.concatenate([np.cos(turn_angle), np.sin(turn_angle)], axis=1).astype(np.float32)
    outer_fwd = np.concatenate(split_np(outer_fwd), axis=1)
    high, low = split_np(inner_fwd)
    inner_fwd = np.concatenate([high, high, low], axis=0)
    high, low = split_np(inner_back)
    inner_back = np.concatenate([high, high, low], axis=0)
    high, low = split_np(outer_back)
    outer_back = np.concatenate([high, high, low], axis=1)
    return outer_fwd, turn, inner_fwd, inner_back, outer_back


def split(value):
    high = value.astype(bf16)
    low = (value - high.astype(f32)).astype(bf16)
    return high, low


def dot(x, y):
    return jnp.dot(x, y, preferred_element_type=f32)


def dot_rows(x, y):
    return lax.dot_general(x, y, (((0,), (0,)), ((), ())), preferred_element_type=f32)


def to_spectrum(blocks, slots, outer_fwd, turn, inner_fwd):
    outer = blocks.shape[0]
    first = dot(outer_fwd[...], jnp.concatenate([blocks, blocks], axis=0))
    cos, sin = turn[:, :LANES], turn[:, LANES:]
    result = []
    for s in range(slots):
        re = first[:outer, s * LANES : (s + 1) * LANES]
        im = first[outer:, s * LANES : (s + 1) * LANES]
        turned = jnp.concatenate([re * cos + im * sin, im * cos - re * sin], axis=1)
        high, low = split(turned)
        result.append(dot(jnp.concatenate([high, low, high], axis=1), inner_fwd[...]))
    return result


def filter_kernel(filters, outer_fwd, turn, inner_fwd, spectra):
    slots, length = filters.shape
    outer = length // LANES
    wide = filters[...].astype(f32)
    blocks = [wide[s].reshape(outer, LANES) for s in range(slots)]
    blocks = jnp.concatenate(blocks, axis=1).astype(bf16)
    parts = to_spectrum(blocks, slots, outer_fwd, turn, inner_fwd)
    for s in range(slots):
        spectra[s] = parts[s]


def convolve_kernel(owner_count, *refs):
    signals = refs[:owner_count]
    spectra, outer_fwd, turn, inner_fwd, inner_back, outer_back = refs[owner_count : owner_count + 6]
    outs = refs[owner_count + 6 : 2 * owner_count + 6]
    blocks, result = refs[2 * owner_count + 6 :]
    slots, outer = spectra.shape[:2]
    piece = outer // owner_count
    me = my_place()
    places = [
        pl.ds(pl.multiple_of(partner(me, d, owner_count, -1) * piece, piece), piece)
        for d in range(owner_count)
    ]
    for d in range(owner_count):
        blocks[places[d], :] = signals[d][...]
    cos, sin = turn[:, :LANES], turn[:, LANES:]
    parts = to_spectrum(blocks[...], slots, outer_fwd, turn, inner_fwd)
    for s in range(slots):
        sig_re, sig_im = parts[s][:, :LANES], parts[s][:, LANES:]
        ker_re, ker_im = spectra[s, :, :LANES], spectra[s, :, LANES:]
        joint = jnp.concatenate(
            [sig_re * ker_re - sig_im * ker_im, sig_re * ker_im + sig_im * ker_re], axis=1
        )
        high, low = split(joint)
        back = dot(jnp.concatenate([high, low, high], axis=1), inner_back[...])
        re, im = back[:, :LANES], back[:, LANES:]
        turned = jnp.concatenate([re * cos - im * sin, im * cos + re * sin], axis=0)
        high, low = split(turned)
        causal = dot(outer_back[...], jnp.concatenate([high, low, high], axis=0))
        result[:, s * LANES : (s + 1) * LANES] = causal.astype(bf16)
    for d in range(owner_count):
        outs[d][...] = result[places[d], :]


def my_place():
    return lax.axis_index("seqo") * lax.axis_size("seqi") + lax.axis_index("seqi")


def partner(place, d, count, sign=1):
    if count & (count - 1) == 0:
        return lax.bitwise_xor(place, d) if not isinstance(place, int) else place ^ d
    return (place + sign * d + count) % count


def relative(owner, me, count):
    if count & (count - 1) == 0:
        return lax.bitwise_xor(owner, me)
    return lax.rem(owner - me + count, count)


def iota(shape, axis):
    return lax.broadcasted_iota(jnp.int32, shape, axis)


def to_column(row):
    size = row.shape[1]
    same = iota((size, size), 0) == iota((size, size), 1)
    return jnp.sum(jnp.where(same, row, 0), axis=1, keepdims=True)


def channel_of_row(index_row, owners_row, owner_count, rows):
    slots = owners_row.shape[1]
    owners_col = to_column(owners_row)
    index_col = to_column(index_row)
    earlier = (owners_col == owners_row) & (iota((slots, slots), 1) < iota((slots, slots), 0))
    rank_col = jnp.sum(earlier.astype(jnp.int32), axis=1, keepdims=True)
    place_col = relative(owners_col, jnp.full_like(owners_col, my_place()), owner_count)
    target_col = jnp.where(owners_col >= 0, rank_col * owner_count + place_col, -1)
    hit = target_col == iota((slots, rows), 1)
    return jnp.sum(jnp.where(hit, index_col + 1, 0), axis=0, keepdims=True) - 1


def pick_rows(tile, onehot_t, rows):
    picked = dot(tile, onehot_t).T
    return [picked[:rows, i : i + LANES] for i in range(0, tile.shape[0], LANES)]


def fetch(sources, stages, sems):
    tile = TILE if sources[0].shape[0] % TILE == 0 else LANES
    count = sources[0].shape[0] // tile

    def copies(i):
        rows = pl.ds(pl.multiple_of(i * tile, tile), tile)
        return [
            pltpu.make_async_copy(source.at[rows, :], stage.at[rows, :], sems.at[n, i])
            for n, (source, stage) in enumerate(zip(sources, stages))
        ]

    for i in range(count):
        for copy in copies(i):
            copy.start()

    def wait(i):
        for copy in copies(i):
            copy.wait()
        return pl.multiple_of(i * tile, tile)

    return wait, tile, count


def pick_kernel(owner_count, slots, index, owners, gate, value, *refs):
    gated, picked, channels, onehot_t = refs[:4]
    payload = refs[4 : 4 + owner_count]
    acc, gate_stage, value_stage, lists, list_sems, sems = refs[4 + owner_count :]
    rows = owner_count * slots
    list_copies = [
        pltpu.make_async_copy(source, lists.at[n], list_sems.at[n])
        for n, source in enumerate((index, owners))
    ]
    for copy in list_copies:
        copy.start()
    wait, tile, count = fetch((gate, value), (gate_stage, value_stage), sems)
    for copy in list_copies:
        copy.wait()
    row = channel_of_row(lists[0], lists[1], owner_count, onehot_t.shape[1])
    channels[...] = jnp.broadcast_to(row, channels.shape)
    onehot_t[...] = (iota(onehot_t.shape, 0) == row).astype(f32).astype(bf16)

    def step(i, _):
        first = wait(i)
        at = pl.ds(first, tile)
        gated[at, :] = gate_stage[at, :] * value_stage[at, :]
        for n, block in enumerate(pick_rows(gated[at, :], onehot_t[...], rows)):
            acc[i * (tile // LANES) + n] = block
            picked[i * (tile // LANES) + n] = block.astype(bf16)
        return 0

    lax.fori_loop(0, count, step, 0)
    for s in range(slots):
        part = jnp.swapaxes(acc[:, s * owner_count : (s + 1) * owner_count, :], 0, 1)
        part = part.astype(bf16)
        for d in range(owner_count):
            payload[d][:, s * LANES : (s + 1) * LANES] = part[d]


def place_kernel(channels, skip, onehot, others, skip_wide):
    hit = iota(onehot.shape, 1) == to_column(channels[0:1, :])[: onehot.shape[0]]
    onehot[...] = hit.astype(f32).astype(bf16)
    others[...] = jnp.broadcast_to(1.0 - jnp.max(hit.astype(f32), axis=0, keepdims=True), others.shape)
    skip_col = jnp.sum(jnp.where(hit, skip[...], 0.0), axis=1, keepdims=True)
    skip_wide[...] = jnp.broadcast_to(skip_col, skip_wide.shape)


def base_kernel(onehot_t, others, skip, gated, out_gate, residual, *refs):
    base, sums, picked_gate, picked_res, gate_stage, res_stage, partial, sems = refs
    rows = picked_gate.shape[1]
    slab = gated.shape[1]
    wait, tile, count = fetch((out_gate, residual), (gate_stage, res_stage), sems)

    def step(i, _):
        first = wait(i)
        for c in range(0, tile, CHUNK):
            at = pl.ds(first + c, CHUNK)
            total = jnp.zeros((CHUNK, LANES), f32)
            for j in range(0, slab, LANES):
                lanes = slice(j, j + LANES)
                mixed = skip[:, lanes] * gated[at, lanes].astype(f32)
                mixed = gate_stage[at, lanes].astype(f32) * mixed
                hidden = (res_stage[at, lanes].astype(f32) + mixed) * others[0:1, lanes]
                hidden = hidden.astype(bf16)
                base[at, lanes] = hidden
                hidden = hidden.astype(f32)
                total = total + hidden * hidden
            partial[c : c + CHUNK, :] = total
        total = jnp.sum(partial[...].T, axis=0, keepdims=True)
        at = pl.ds(first, tile)
        picks_gate = pick_rows(gate_stage[at, :], onehot_t[...], rows)
        picks_res = pick_rows(res_stage[at, :], onehot_t[...], rows)
        for n in range(tile // LANES):
            block = i * (tile // LANES) + n
            sums[block] = total[:, n * LANES : (n + 1) * LANES]
            picked_gate[block] = picks_gate[n].astype(bf16)
            picked_res[block] = picks_res[n].astype(bf16)
        return 0

    lax.fori_loop(0, count, step, 0)


def kept_kernel(owner_count, *refs):
    conv = refs[:owner_count]
    picked, skip_wide, sums, picked_gate, picked_res, hidden, totals, wide_conv = refs[owner_count:]
    blocks, rows = picked.shape[:2]
    for d in range(owner_count):
        wide_conv[d] = conv[d][...].astype(f32)
    total = jnp.zeros((blocks, LANES), f32)
    for s in range(rows // owner_count):
        at = slice(s * owner_count, (s + 1) * owner_count)
        wide = jnp.swapaxes(wide_conv[:, :, s * LANES : (s + 1) * LANES], 0, 1)
        wide = wide + skip_wide[at, :] * picked[:, at, :].astype(f32)
        value = picked_res[:, at, :].astype(f32) + picked_gate[:, at, :].astype(f32) * wide
        value = value.astype(bf16)
        hidden[:, at, :] = value
        value = value.astype(f32)
        total = total + jnp.sum(value * value, axis=1)
    for i in range(blocks):
        totals[i] = total[i : i + 1, :] + sums[i]


def hidden_kernel(base, hidden_kept, onehot, hidden, held, sems):
    slab = held.shape[1]
    wide = min(slab, 2 * LANES)

    def copy(i):
        rows = pl.ds(pl.multiple_of(i * LANES, LANES), LANES)
        return pltpu.make_async_copy(held.at[rows, :], hidden.at[rows, :], sems.at[i])

    def step(i, _):
        rows = pl.ds(pl.multiple_of(i * LANES, LANES), LANES)
        kept = hidden_kept[i].astype(f32).T.astype(bf16)
        for j in range(0, slab, wide):
            lanes = slice(j, j + wide)
            held[rows, lanes] = base[rows, lanes] + dot(kept, onehot[:, lanes]).astype(bf16)
        copy(i).start()
        return 0

    lax.fori_loop(0, sems.shape[0], step, 0)
    lax.fori_loop(0, sems.shape[0], lambda i, _: (copy(i).wait(), 0)[1], 0)


def norm_kernel(width, count, *refs):
    parts = refs[:count]
    held, gain, normed, stage, turned, sems = refs[count:]
    slab = held.shape[1]

    def copy(i):
        rows = pl.ds(pl.multiple_of(i * LANES, LANES), LANES)
        return pltpu.make_async_copy(stage.at[rows, :], normed.at[rows, :], sems.at[i])

    def step(i, _):
        total = parts[0][i]
        for part in parts[1:]:
            total = total + part[i]
        scale = lax.rsqrt(total / width + norm_eps)
        turned[...] = jnp.broadcast_to(scale, (LANES, LANES)).T
        first = pl.multiple_of(i * LANES, LANES)
        for c in range(0, LANES, CHUNK):
            at = pl.ds(first + c, CHUNK)
            scales = turned[c : c + CHUNK, :]
            for j in range(0, slab, LANES):
                lanes = slice(j, j + LANES)
                value = held[at, lanes].astype(f32) * scales * gain[:, lanes]
                stage[at, lanes] = value.astype(bf16)
        copy(i).start()
        return 0

    lax.fori_loop(0, sems.shape[0], step, 0)
    lax.fori_loop(0, sems.shape[0], lambda i, _: (copy(i).wait(), 0)[1], 0)


def in_hbm(x):
    return pltpu.with_memory_space_constraint(x, pltpu.HBM)


def in_vmem(x):
    return pltpu.with_memory_space_constraint(x, pltpu.VMEM)


def call(kernel, outs, ins, flops, moved, limit, scratch=(), far=(), far_outs=()):
    near = pl.BlockSpec(memory_space=pltpu.VMEM)
    away = pl.BlockSpec(memory_space=pl.ANY)
    return pl.pallas_call(
        kernel,
        out_shape=outs,
        in_specs=[away if n in far else near for n in range(len(ins))],
        out_specs=[away if n in far_outs else near for n in range(len(outs))],
        scratch_shapes=list(scratch),
        compiler_params=pltpu.CompilerParams(vmem_limit_bytes=limit),
        cost_estimate=pl.CostEstimate(flops=flops, bytes_accessed=moved, transcendentals=0),
    )(*ins)


def exchange(pieces, sign):
    count = len(pieces)
    result = [pieces[0]]
    for d in range(1, count):
        pairs = [(i, partner(i, d, count, sign)) for i in range(count)]
        result.append(lax.ppermute(pieces[d], ("seqo", "seqi"), pairs))
    return result


def local(
    gate_in, value_in, out_gate, residual, filters, kept_index, kept_owner, skip_bias, norm_gain
):
    tok_rows, slab = gate_in.shape
    slots, length = filters.shape[2:]
    chan_devices = lax.axis_size("chan")
    owner_count = lax.axis_size("seqo") * lax.axis_size("seqi")
    rows = slots * owner_count
    lanes_rows = -(-rows // LANES) * LANES
    blocks = tok_rows // LANES
    outer = length // LANES
    tiles = tok_rows // (TILE if tok_rows % TILE == 0 else LANES)
    dense = tok_rows * slab * 2
    sds = jax.ShapeDtypeStruct
    tables = [jnp.asarray(x) for x in dft_tables(length)]
    outer_fwd, turn, inner_fwd, inner_back, outer_back = tables
    skip_row = skip_bias[None, :]
    gain_row = norm_gain[None, :]
    gate_in, value_in, out_gate, residual = map(in_hbm, (gate_in, value_in, out_gate, residual))
    picks = sds((blocks, rows, LANES), bf16)
    row_sums = sds((blocks, 1, LANES), f32)
    piece = sds((blocks, slots * LANES), bf16)
    whole = (tok_rows, slab)

    outs = [
        pltpu.VMEM(whole, bf16),
        picks,
        sds((8, lanes_rows), jnp.int32),
        sds((slab, lanes_rows), bf16),
    ] + [piece] * owner_count
    gated, picked, channels, onehot_t, *payload = call(
        functools.partial(pick_kernel, owner_count, slots),
        outs,
        [in_hbm(kept_index), in_hbm(kept_owner), gate_in, value_in],
        2 * tok_rows * slab * rows,
        2 * dense,
        24 * MIB,
        scratch=[
            pltpu.VMEM((blocks, rows, LANES), f32),
            pltpu.VMEM(whole, bf16),
            pltpu.VMEM(whole, bf16),
            pltpu.VMEM((2,) + kept_index.shape, jnp.int32),
            pltpu.SemaphoreType.DMA((2,)),
            pltpu.SemaphoreType.DMA((2, tiles)),
        ],
        far=(0, 1, 2, 3),
    )

    incoming = exchange(payload, 1)

    (spectra,) = call(
        filter_kernel,
        [sds((slots, outer, 2 * LANES), f32)],
        [filters[0, 0], outer_fwd, turn, inner_fwd],
        2 * slots * length * 2 * (2 * outer + 6 * LANES),
        8 * MIB,
        16 * MIB,
    )
    onehot, others, skip_wide = call(
        place_kernel,
        [sds((rows, slab), bf16), sds((8, slab), f32), sds((rows, LANES), f32)],
        [channels, skip_row],
        rows * slab * 8,
        rows * slab * 2,
        8 * MIB,
    )
    base, sums, picked_gate, picked_res = call(
        base_kernel,
        [pltpu.VMEM(whole, bf16), row_sums, picks, picks],
        [onehot_t, others, skip_row, in_vmem(gated), out_gate, residual],
        4 * tok_rows * slab * rows,
        4 * dense,
        24 * MIB,
        scratch=[
            pltpu.VMEM(whole, bf16),
            pltpu.VMEM(whole, bf16),
            pltpu.VMEM((tok_rows // tiles, LANES), f32),
            pltpu.SemaphoreType.DMA((2, tiles)),
        ],
        far=(4, 5),
    )
    spectra, base = lax.optimization_barrier((spectra, base))

    convolved = call(
        functools.partial(convolve_kernel, owner_count),
        [piece] * owner_count,
        incoming + [spectra, outer_fwd, turn, inner_fwd, inner_back, outer_back],
        2 * slots * length * 2 * (5 * outer + 12 * LANES),
        8 * MIB,
        20 * MIB,
        scratch=[pltpu.VMEM((outer, slots * LANES), bf16)] * 2,
    )
    returned = exchange(list(convolved), -1)

    hidden_kept, totals = call(
        functools.partial(kept_kernel, owner_count),
        [picks, row_sums],
        returned + [picked, skip_wide, sums, picked_gate, picked_res],
        8 * rows * tok_rows,
        10 * rows * tok_rows,
        16 * MIB,
        scratch=[pltpu.VMEM((owner_count, blocks, slots * LANES), f32)],
    )

    parts = [totals]
    for shift in range(1, chan_devices):
        ring = [(i, (i + shift) % chan_devices) for i in range(chan_devices)]
        parts.append(lax.ppermute(totals, "chan", ring))

    hidden, held = call(
        hidden_kernel,
        [pltpu.HBM(whole, bf16), pltpu.VMEM(whole, bf16)],
        [in_vmem(base), hidden_kept, onehot],
        2 * tok_rows * slab * rows,
        2 * dense,
        8 * MIB,
        scratch=[pltpu.SemaphoreType.DMA((blocks,))],
        far_outs=(0,),
    )
    (normed,) = call(
        functools.partial(norm_kernel, float(slab * chan_devices), len(parts)),
        [pltpu.HBM(whole, bf16)],
        parts + [in_vmem(held), gain_row],
        4 * tok_rows * slab,
        2 * dense,
        16 * MIB,
        scratch=[
            pltpu.VMEM(whole, bf16),
            pltpu.VMEM((LANES, LANES), f32),
            pltpu.SemaphoreType.DMA((blocks,)),
        ],
        far_outs=(0,),
    )
    return (hidden, normed)


def solution(mesh):
    positions = P(("seqo", "seqi"), "chan")
    in_specs = (
        positions,
        positions,
        positions,
        positions,
        P("chan", ("seqo", "seqi"), None, None),
        P("chan", None),
        P("chan", None),
        P("chan"),
        P("chan"),
    )
    return jax.shard_map(
        local, mesh=mesh, in_specs=in_specs, out_specs=(positions, positions), check_vma=False
    )
```

time: 83.2 us -> 92.8 us (1.12)
  starting transfers between devices: 14.9 us -> 44.2 us
  local copies, waits for them, and re-layouts: 19.1 us -> 0.04 us
  Pallas kernels: 47.8 us -> 40.4 us
  waiting for transfers between devices: 0.01 us -> 7.29 us
    ppermute x0 -> x30, starting transfers between devices: none -> 42.6 us  [exchange(): result.append(lax.ppermute(pieces[d], ('seqo', 'seqi'), pairs))]
    unnamed x32 -> x16, local copies, waits for them, and re-layouts: 19.1 us -> 0.04 us
    all_to_all x2 -> x0, starting transfers between devices: 13.4 us -> none  [the longest x1 7.36 us: local(): lax.all_to_all(payload, ('seqo', 'seqi'), split_axis=0, concat_axis=0, ti...]
    pallas_call x9 -> x8, Pallas kernels: 47.8 us -> 40.4 us  [call(): pl.pallas_call(kernel, out_shape=outs, in_specs=[away if n in far else ne...]
    ppermute x0 -> x30, waiting for transfers between devices: none -> 7.29 us  [exchange(): result.append(lax.ppermute(pieces[d], ('seqo', 'seqi'), pairs))]
  transfers between devices with their start and end apart: 3 -> 31, of which waited for: 0 -> 5; matrix products, arithmetic and copies ran while one was open for 0% -> 0% of each run, Pallas kernels for 31% -> 22%
where the time goes in v3:
time: 92.8 us; the launch traced here: 92.6 us
  starting transfers between devices  44.2 us (48%)
  Pallas kernels  40.4 us (44%)
  waiting for transfers between devices  7.29 us (8%)
    ppermute x30, starting transfers between devices, exchange(): result.append(lax.ppermute(pieces[d], ('seqo', 'seqi'), pairs))  42.6 us
    pallas_call x8, Pallas kernels, call(): pl.pallas_call(kernel, out_shape=outs, in_specs=[away if n in far else ne...  40.4 us
    ppermute x30, waiting for transfers between devices, exchange(): result.append(lax.ppermute(pieces[d], ('seqo', 'seqi'), pairs))  7.29 us
  transfers between devices with their start and end apart: 31, of which 5 were waited for; matrix products, arithmetic and copies ran while one was open for 0% of the time, Pallas kernels for 22%

profile of v3, /device:TPU:0, one launch (start us, length us, event | category | flops | bytes accessed | tf_op | source)
XLA Modules:
  0.0 92.6 jit_solution(3251139242545282059)
XLA Ops:
  0.6 10.0 %shard_map.150 = (bf16[2048,2048]{1,0:T(8,128)(2,1)S(1)}, bf16[16,96,128]{2,1,0:T(8,128)(2,1)S(1)}, s32[8,128]{1,0:T(8,128)S(1)}, bf16[2048,128]{1,0:T(8,128)(2,...) custom-call(s32[1,64]{1,0:T(1,128)} %index.1, ...), custom_call_target="tpu_custom_call" | custom-call | flops 805306368 | bytes 16777216 | tf_op jit(solution)/shard_map/pallas_call | solution.py:353
  10.6 0.5 collective-permute-start
  11.1 2.6 %collective-permute-start.1 = (bf16[16,768]{1,0:T(8,128)(2,1)S(1)}, bf16[16,768]{1,0:T(8,128)(2,1)S(1)}, u32[]{:S(2)}, u32[]{:S(2)}) collective-permute-start(bf16[16,768]{1,0:T(8,128)(2,1)S(1)} %get-tuple-element.59), channel_id=1, source_target_pairs={{0,2},{1,3},{2,0},{3,1},{4,6},{5,7},{6,4},{7,5},{8,10},{9,11},{10,... | collective-permute-start | bytes 73736 | tf_op jit(solution)/shard_map/ppermute | solution.py:369
  13.7 2.3 %collective-permute-start.10 = (bf16[16,768]{1,0:T(8,128)(2,1)S(1)}, bf16[16,768]{1,0:T(8,128)(2,1)S(1)}, u32[]{:S(2)}, u32[]{:S(2)}) collective-permute-start(bf16[16,768]{1,0:T(8,128)(2,1)S(1)} %get-tuple-element.68), channel_id=1, source_target_pairs={{0,11},{1,10},{2,9},{3,8},{4,15},{5,14},{6,13},{7,12},{8,3},{9,2},... | collective-permute-start | bytes 73736 | tf_op jit(solution)/shard_map/ppermute | solution.py:369
  16.0 1.4 %collective-permute-start.11 = (bf16[16,768]{1,0:T(8,128)(2,1)S(1)}, bf16[16,768]{1,0:T(8,128)(2,1)S(1)}, u32[]{:S(2)}, u32[]{:S(2)}) collective-permute-start(bf16[16,768]{1,0:T(8,128)(2,1)S(1)} %get-tuple-element.69), channel_id=1, source_target_pairs={{0,12},{1,13},{2,14},{3,15},{4,8},{5,9},{6,10},{7,11},{8,4},{9,5},... | collective-permute-start | bytes 73736 | tf_op jit(solution)/shard_map/ppermute | solution.py:369
  17.4 2.1 %collective-permute-start.12 = (bf16[16,768]{1,0:T(8,128)(2,1)S(1)}, bf16[16,768]{1,0:T(8,128)(2,1)S(1)}, u32[]{:S(2)}, u32[]{:S(2)}) collective-permute-start(bf16[16,768]{1,0:T(8,128)(2,1)S(1)} %get-tuple-element.70), channel_id=1, source_target_pairs={{0,13},{1,12},{2,15},{3,14},{4,9},{5,8},{6,11},{7,10},{8,5},{9,4},... | collective-permute-start | bytes 73736 | tf_op jit(solution)/shard_map/ppermute | solution.py:369
  19.5 0.4 shard_map.151
  19.9 0.0 collective-permute-done.refs_1_
  19.9 2.3 %collective-permute-start.13 = (bf16[16,768]{1,0:T(8,128)(2,1)S(1)}, bf16[16,768]{1,0:T(8,128)(2,1)S(1)}, u32[]{:S(2)}, u32[]{:S(2)}) collective-permute-start(bf16[16,768]{1,0:T(8,128)(2,1)S(1)} %get-tuple-element.71), channel_id=1, source_target_pairs={{0,14},{1,15},{2,12},{3,13},{4,10},{5,11},{6,8},{7,9},{8,6},{9,7},... | collective-permute-start | bytes 73736 | tf_op jit(solution)/shard_map/ppermute | solution.py:369
  22.2 0.0 collective-permute-done.1.refs_2_
  22.2 2.2 %collective-permute-start.14 = (bf16[16,768]{1,0:T(8,128)(2,1)S(1)}, bf16[16,768]{1,0:T(8,128)(2,1)S(1)}, u32[]{:S(2)}, u32[]{:S(2)}) collective-permute-start(bf16[16,768]{1,0:T(8,128)(2,1)S(1)} %get-tuple-element.72), channel_id=1, source_target_pairs={{0,15},{1,14},{2,13},{3,12},{4,11},{5,10},{6,9},{7,8},{8,7},{9,6},... | collective-permute-start | bytes 73736 | tf_op jit(solution)/shard_map/ppermute | solution.py:369
  24.4 0.0 collective-permute-done.10.refs_11_
  24.4 1.4 %collective-permute-start.2 = (bf16[16,768]{1,0:T(8,128)(2,1)S(1)}, bf16[16,768]{1,0:T(8,128)(2,1)S(1)}, u32[]{:S(2)}, u32[]{:S(2)}) collective-permute-start(bf16[16,768]{1,0:T(8,128)(2,1)S(1)} %get-tuple-element.60), channel_id=1, source_target_pairs={{0,3},{1,2},{2,1},{3,0},{4,7},{5,6},{6,5},{7,4},{8,11},{9,10},{10,... | collective-permute-start | bytes 73736 | tf_op jit(solution)/shard_map/ppermute | solution.py:369
  25.9 1.5 %collective-permute-start.4 = (bf16[16,768]{1,0:T(8,128)(2,1)S(1)}, bf16[16,768]{1,0:T(8,128)(2,1)S(1)}, u32[]{:S(2)}, u32[]{:S(2)}) collective-permute-start(bf16[16,768]{1,0:T(8,128)(2,1)S(1)} %get-tuple-element.62), channel_id=1, source_target_pairs={{0,5},{1,4},{2,7},{3,6},{4,1},{5,0},{6,3},{7,2},{8,13},{9,12},{10,... | collective-permute-start | bytes 73736 | tf_op jit(solution)/shard_map/ppermute | solution.py:369
  27.4 0.0 copy-start.3
  27.4 0.0 copy-start.6
  27.4 11.9 %shard_map.152 = (bf16[2048,2048]{1,0:T(8,128)(2,1)S(1)}, f32[16,1,128]{2,1,0:T(1,128)S(1)}, bf16[16,96,128]{2,1,0:T(8,128)(2,1)S(1)}, bf16[16,96,128]{2,1,0:T(8,128)(2,1)S(1)}) custom-call(bf16[2048,128]{1,0:T(8,128)(2,1)S(1)} %get-tuple-element.51.onehot_t, f32[8,2048]{1,0:T(8,128)S(1)} %get-tuple-element.53.others, f32[1,2048]{1,0:T(1,128)S(1)} %bitcast.4, ...), custom_call_target="tpu_custom_call" | custom-call | flops 1610612736 | bytes 33554432 | tf_op jit(solution)/shard_map/pallas_call | solution.py:353
  39.4 0.0 collective-permute-done.13.refs_14_
  39.4 0.6 collective-permute-start.5
  39.9 2.4 %collective-permute-start.6 = (bf16[16,768]{1,0:T(8,128)(2,1)S(1)}, bf16[16,768]{1,0:T(8,128)(2,1)S(1)}, u32[]{:S(2)}, u32[]{:S(2)}) collective-permute-start(bf16[16,768]{1,0:T(8,128)(2,1)S(1)} %get-tuple-element.64), channel_id=1, source_target_pairs={{0,7},{1,6},{2,5},{3,4},{4,3},{5,2},{6,1},{7,0},{8,15},{9,14},{10,... | collective-permute-start | bytes 73736 | tf_op jit(solution)/shard_map/ppermute | solution.py:369
  42.3 2.4 %collective-permute-start.8 = (bf16[16,768]{1,0:T(8,128)(2,1)S(1)}, bf16[16,768]{1,0:T(8,128)(2,1)S(1)}, u32[]{:S(2)}, u32[]{:S(2)}) collective-permute-start(bf16[16,768]{1,0:T(8,128)(2,1)S(1)} %get-tuple-element.66), channel_id=1, source_target_pairs={{0,9},{1,8},{2,11},{3,10},{4,13},{5,12},{6,15},{7,14},{8,1},{9,0},... | collective-permute-start | bytes 73736 | tf_op jit(solution)/shard_map/ppermute | solution.py:369
  44.7 0.5 collective-permute-start.9
  45.3 1.6 %shard_map.149.refs_16_ = f32[6,256,256]{2,1,0:T(8,128)S(1)} custom-call(bf16[6,32768]{1,0:T(8,128)(2,1)S(1)} %bitcast.6, bf16[512,512]{1,0:T(8,128)(2,1)S(1)} %copy-done.4, f32[256,256]{1,0:T(8,128)S(1)} %copy-done.7, bf16[768,256]{1,0:T(8,128)(2,1)S(1)} %copy-done.5), custom_call_target="tpu_custom_call" | custom-call | flops 1006632960 | bytes 8388608 | tf_op jit(solution)/shard_map/pallas_call | solution.py:353
  46.9 0.3 collective-permute-done.7.refs_8_
  47.3 3.3 %collective-permute-done.9.refs_10_ = bf16[16,768]{1,0:T(8,128)(2,1)S(1)} collective-permute-done((bf16[16,768]{1,0:T(8,128)(2,1)S(1)}, bf16[16,768]{1,0:T(8,128)(2,1)S(1)}, u32[]{:S(2)}, u32[]{:S(2)}) %collective-permute-start.9) | collective-permute-done | bytes 24608 | tf_op jit(solution)/shard_map/ppermute | solution.py:369
  50.6 5.1 %shard_map.153 = (bf16[16,768]{1,0:T(8,128)(2,1)S(1)}, bf16[16,768]{1,0:T(8,128)(2,1)S(1)}, bf16[16,768]{1,0:T(8,128)(2,1)S(1)}, bf16[16,768]{1,0:T(8,128)(2,1)S...) custom-call(bf16[16,768]{1,0:T(8,128)(2,1)S(1)} %get-tuple-element.5, ...), custom_call_target="tpu_custom_call" | custom-call | flops 2214592512 | bytes 8388608 | tf_op jit(solution)/shard_map/pallas_call | solution.py:353
  55.7 0.1 collective-permute-start.15
  55.8 0.6 collective-permute-start.16
  56.4 1.2 %collective-permute-start.17 = (bf16[16,768]{1,0:T(8,128)(2,1)S(1)}, bf16[16,768]{1,0:T(8,128)(2,1)S(1)}, u32[]{:S(2)}, u32[]{:S(2)}) collective-permute-start(bf16[16,768]{1,0:T(8,128)(2,1)S(1)} %get-tuple-element.77), channel_id=1, source_target_pairs={{0,3},{1,2},{2,1},{3,0},{4,7},{5,6},{6,5},{7,4},{8,11},{9,10},{10,... | collective-permute-start | bytes 73736 | tf_op jit(solution)/shard_map/ppermute | solution.py:369
  57.6 0.3 collective-permute-start.18
  58.0 1.4 %collective-permute-start.19 = (bf16[16,768]{1,0:T(8,128)(2,1)S(1)}, bf16[16,768]{1,0:T(8,128)(2,1)S(1)}, u32[]{:S(2)}, u32[]{:S(2)}) collective-permute-start(bf16[16,768]{1,0:T(8,128)(2,1)S(1)} %get-tuple-element.79), channel_id=1, source_target_pairs={{0,5},{1,4},{2,7},{3,6},{4,1},{5,0},{6,3},{7,2},{8,13},{9,12},{10,... | collective-permute-start | bytes 73736 | tf_op jit(solution)/shard_map/ppermute | solution.py:369
  59.3 0.4 collective-permute-start.20
  59.7 0.2 collective-permute-done.16.refs_2_
  59.9 2.1 %collective-permute-start.21 = (bf16[16,768]{1,0:T(8,128)(2,1)S(1)}, bf16[16,768]{1,0:T(8,128)(2,1)S(1)}, u32[]{:S(2)}, u32[]{:S(2)}) collective-permute-start(bf16[16,768]{1,0:T(8,128)(2,1)S(1)} %get-tuple-element.81), channel_id=1, source_target_pairs={{0,7},{1,6},{2,5},{3,4},{4,3},{5,2},{6,1},{7,0},{8,15},{9,14},{10,... | collective-permute-start | bytes 73736 | tf_op jit(solution)/shard_map/ppermute | solution.py:369
  62.1 0.4 collective-permute-start.22
  62.5 2.2 %collective-permute-start.23 = (bf16[16,768]{1,0:T(8,128)(2,1)S(1)}, bf16[16,768]{1,0:T(8,128)(2,1)S(1)}, u32[]{:S(2)}, u32[]{:S(2)}) collective-permute-start(bf16[16,768]{1,0:T(8,128)(2,1)S(1)} %get-tuple-element.83), channel_id=1, source_target_pairs={{0,9},{1,8},{2,11},{3,10},{4,13},{5,12},{6,15},{7,14},{8,1},{9,0},... | collective-permute-start | bytes 73736 | tf_op jit(solution)/shard_map/ppermute | solution.py:369
  64.6 0.8 collective-permute-start.24
  65.4 2.8 %collective-permute-start.25 = (bf16[16,768]{1,0:T(8,128)(2,1)S(1)}, bf16[16,768]{1,0:T(8,128)(2,1)S(1)}, u32[]{:S(2)}, u32[]{:S(2)}) collective-permute-start(bf16[16,768]{1,0:T(8,128)(2,1)S(1)} %get-tuple-element.85), channel_id=1, source_target_pairs={{0,11},{1,10},{2,9},{3,8},{4,15},{5,14},{6,13},{7,12},{8,3},{9,2},... | collective-permute-start | bytes 73736 | tf_op jit(solution)/shard_map/ppermute | solution.py:369
  68.3 1.3 %collective-permute-start.26 = (bf16[16,768]{1,0:T(8,128)(2,1)S(1)}, bf16[16,768]{1,0:T(8,128)(2,1)S(1)}, u32[]{:S(2)}, u32[]{:S(2)}) collective-permute-start(bf16[16,768]{1,0:T(8,128)(2,1)S(1)} %get-tuple-element.86), channel_id=1, source_target_pairs={{0,12},{1,13},{2,14},{3,15},{4,8},{5,9},{6,10},{7,11},{8,4},{9,5},... | collective-permute-start | bytes 73736 | tf_op jit(solution)/shard_map/ppermute | solution.py:369
  69.6 2.1 %collective-permute-start.27 = (bf16[16,768]{1,0:T(8,128)(2,1)S(1)}, bf16[16,768]{1,0:T(8,128)(2,1)S(1)}, u32[]{:S(2)}, u32[]{:S(2)}) collective-permute-start(bf16[16,768]{1,0:T(8,128)(2,1)S(1)} %get-tuple-element.87), channel_id=1, source_target_pairs={{0,13},{1,12},{2,15},{3,14},{4,9},{5,8},{6,11},{7,10},{8,5},{9,4},... | collective-permute-start | bytes 73736 | tf_op jit(solution)/shard_map/ppermute | solution.py:369
  71.7 1.9 %collective-permute-start.28 = (bf16[16,768]{1,0:T(8,128)(2,1)S(1)}, bf16[16,768]{1,0:T(8,128)(2,1)S(1)}, u32[]{:S(2)}, u32[]{:S(2)}) collective-permute-start(bf16[16,768]{1,0:T(8,128)(2,1)S(1)} %get-tuple-element.88), channel_id=1, source_target_pairs={{0,14},{1,15},{2,12},{3,13},{4,10},{5,11},{6,8},{7,9},{8,6},{9,7},... | collective-permute-start | bytes 73736 | tf_op jit(solution)/shard_map/ppermute | solution.py:369
  73.7 2.6 %collective-permute-start.29 = (bf16[16,768]{1,0:T(8,128)(2,1)S(1)}, bf16[16,768]{1,0:T(8,128)(2,1)S(1)}, u32[]{:S(2)}, u32[]{:S(2)}) collective-permute-start(bf16[16,768]{1,0:T(8,128)(2,1)S(1)} %get-tuple-element.89), channel_id=1, source_target_pairs={{0,15},{1,14},{2,13},{3,12},{4,11},{5,10},{6,9},{7,8},{8,7},{9,6},... | collective-permute-start | bytes 73736 | tf_op jit(solution)/shard_map/ppermute | solution.py:369
  76.3 2.0 %collective-permute-done.28.refs_14_ = bf16[16,768]{1,0:T(8,128)(2,1)S(1)} collective-permute-done((bf16[16,768]{1,0:T(8,128)(2,1)S(1)}, bf16[16,768]{1,0:T(8,128)(2,1)S(1)}, u32[]{:S(2)}, u32[]{:S(2)}) %collective-permute-start.28) | collective-permute-done | bytes 24608 | tf_op jit(solution)/shard_map/ppermute | solution.py:369
  78.3 1.3 %collective-permute-done.29.refs_15_ = bf16[16,768]{1,0:T(8,128)(2,1)S(1)} collective-permute-done((bf16[16,768]{1,0:T(8,128)(2,1)S(1)}, bf16[16,768]{1,0:T(8,128)(2,1)S(1)}, u32[]{:S(2)}, u32[]{:S(2)}) %collective-permute-start.29) | collective-permute-done | bytes 24608 | tf_op jit(solution)/shard_map/ppermute | solution.py:369
  79.6 0.5 shard_map.154
  80.1 1.6 %collective-permute-start.30 = (f32[16,1,128]{2,1,0:T(1,128)S(1)}, f32[16,1,128]{2,1,0:T(1,128)S(1)}, u32[]{:S(2)}, u32[]{:S(2)}) collective-permute-start(f32[16,1,128]{2,1,0:T(1,128)S(1)} %get-tuple-element.98.refs_0_), channel_id=1, source_target_pairs={{0,16},{16,0},{1,17},{17,1},{2,18},{18,2},{3,19},{19,3},{4,20},{20... | collective-permute-start | bytes 24584 | tf_op jit(solution)/shard_map/ppermute | solution.py:480
  81.7 6.5 %shard_map.155 = (bf16[2048,2048]{1,0:T(8,128)(2,1)}, bf16[2048,2048]{1,0:T(8,128)(2,1)S(1)}) custom-call(bf16[2048,2048]{1,0:T(8,128)(2,1)S(1)} %get-tuple-element.56.base, bf16[16,96,128]{2,1,0:T(8,128)(2,1)S(1)} %get-tuple-element.95.hidden_kept, bf16[96,2048]{1,0:T(8,128)(2,1)S(1)} %get-tuple-element.96.onehot), custom_call_target="tpu_custom_call" | custom-call | flops 805306368 | bytes 16777216 | tf_op jit(solution)/shard_map/pallas_call | solution.py:353
  88.3 4.4 %shard_map.156 = bf16[2048,2048]{1,0:T(8,128)(2,1)} custom-call(f32[16,1,128]{2,1,0:T(1,128)S(1)} %get-tuple-element.98.refs_0_, f32[16,1,128]{2,1,0:T(1,128)S(1)} %collective-permute-done.30.refs_1_, bf16[2048,2048]{1,0:T(8,128)(2,1)S(1)} %get-tuple-element.99.refs_2_, f32[1,2048]{1,0:T(1,128)S(1)} %bitcast.5), custom_call_target="tpu_custom_call" | custom-call | flops 16777216 | bytes 16777216 | tf_op jit(solution)/shard_map/pallas_call | solution.py:353
  (38 shorter events, 0.1 us)
Async XLA Ops:
  0.6 18.9 %copy-start = (f32[2048]{0:T(1024)S(1)}, f32[2048]{0:T(1024)}, u32[]{:S(2)}) copy-start(f32[2048]{0:T(1024)} %param.21) | copy-start | bytes 24580
  10.6 9.3 %collective-permute-start = (bf16[16,768]{1,0:T(8,128)(2,1)S(1)}, bf16[16,768]{1,0:T(8,128)(2,1)S(1)}, u32[]{:S(2)}, u32[]{:S(2)}) collective-permute-start(bf16[16,768]{1,0:T(8,128)(2,1)S(1)} %get-tuple-element.58), channel_id=1, source_target_pairs={{0,1},{1,0},{2,3},{3,2},{4,5},{5,4},{6,7},{7,6},{8,9},{9,8},{10,11... | collective-permute-start | bytes 73736 | tf_op jit(solution)/shard_map/ppermute | solution.py:369
  11.1 11.1 %collective-permute-start.1 = (bf16[16,768]{1,0:T(8,128)(2,1)S(1)}, bf16[16,768]{1,0:T(8,128)(2,1)S(1)}, u32[]{:S(2)}, u32[]{:S(2)}) collective-permute-start(bf16[16,768]{1,0:T(8,128)(2,1)S(1)} %get-tuple-element.59), channel_id=1, source_target_pairs={{0,2},{1,3},{2,0},{3,1},{4,6},{5,7},{6,4},{7,5},{8,10},{9,11},{10,... | collective-permute-start | bytes 73736 | tf_op jit(solution)/shard_map/ppermute | solution.py:369
  13.7 10.7 %collective-permute-start.10 = (bf16[16,768]{1,0:T(8,128)(2,1)S(1)}, bf16[16,768]{1,0:T(8,128)(2,1)S(1)}, u32[]{:S(2)}, u32[]{:S(2)}) collective-permute-start(bf16[16,768]{1,0:T(8,128)(2,1)S(1)} %get-tuple-element.68), channel_id=1, source_target_pairs={{0,11},{1,10},{2,9},{3,8},{4,15},{5,14},{6,13},{7,12},{8,3},{9,2},... | collective-permute-start | bytes 73736 | tf_op jit(solution)/shard_map/ppermute | solution.py:369
  16.0 9.8 %collective-permute-start.11 = (bf16[16,768]{1,0:T(8,128)(2,1)S(1)}, bf16[16,768]{1,0:T(8,128)(2,1)S(1)}, u32[]{:S(2)}, u32[]{:S(2)}) collective-permute-start(bf16[16,768]{1,0:T(8,128)(2,1)S(1)} %get-tuple-element.69), channel_id=1, source_target_pairs={{0,12},{1,13},{2,14},{3,15},{4,8},{5,9},{6,10},{7,11},{8,4},{9,5},... | collective-permute-start | bytes 73736 | tf_op jit(solution)/shard_map/ppermute | solution.py:369
  17.4 8.5 %collective-permute-start.12 = (bf16[16,768]{1,0:T(8,128)(2,1)S(1)}, bf16[16,768]{1,0:T(8,128)(2,1)S(1)}, u32[]{:S(2)}, u32[]{:S(2)}) collective-permute-start(bf16[16,768]{1,0:T(8,128)(2,1)S(1)} %get-tuple-element.70), channel_id=1, source_target_pairs={{0,13},{1,12},{2,15},{3,14},{4,9},{5,8},{6,11},{7,10},{8,5},{9,4},... | collective-permute-start | bytes 73736 | tf_op jit(solution)/shard_map/ppermute | solution.py:369
  19.9 19.4 %collective-permute-start.13 = (bf16[16,768]{1,0:T(8,128)(2,1)S(1)}, bf16[16,768]{1,0:T(8,128)(2,1)S(1)}, u32[]{:S(2)}, u32[]{:S(2)}) collective-permute-start(bf16[16,768]{1,0:T(8,128)(2,1)S(1)} %get-tuple-element.71), channel_id=1, source_target_pairs={{0,14},{1,15},{2,12},{3,13},{4,10},{5,11},{6,8},{7,9},{8,6},{9,7},... | collective-permute-start | bytes 73736 | tf_op jit(solution)/shard_map/ppermute | solution.py:369
  22.2 17.7 %collective-permute-start.14 = (bf16[16,768]{1,0:T(8,128)(2,1)S(1)}, bf16[16,768]{1,0:T(8,128)(2,1)S(1)}, u32[]{:S(2)}, u32[]{:S(2)}) collective-permute-start(bf16[16,768]{1,0:T(8,128)(2,1)S(1)} %get-tuple-element.72), channel_id=1, source_target_pairs={{0,15},{1,14},{2,13},{3,12},{4,11},{5,10},{6,9},{7,8},{8,7},{9,6},... | collective-permute-start | bytes 73736 | tf_op jit(solution)/shard_map/ppermute | solution.py:369
  24.4 17.9 %collective-permute-start.2 = (bf16[16,768]{1,0:T(8,128)(2,1)S(1)}, bf16[16,768]{1,0:T(8,128)(2,1)S(1)}, u32[]{:S(2)}, u32[]{:S(2)}) collective-permute-start(bf16[16,768]{1,0:T(8,128)(2,1)S(1)} %get-tuple-element.60), channel_id=1, source_target_pairs={{0,3},{1,2},{2,1},{3,0},{4,7},{5,6},{6,5},{7,4},{8,11},{9,10},{10,... | collective-permute-start | bytes 73736 | tf_op jit(solution)/shard_map/ppermute | solution.py:369
  25.9 16.4 %collective-permute-start.3 = (bf16[16,768]{1,0:T(8,128)(2,1)S(1)}, bf16[16,768]{1,0:T(8,128)(2,1)S(1)}, u32[]{:S(2)}, u32[]{:S(2)}) collective-permute-start(bf16[16,768]{1,0:T(8,128)(2,1)S(1)} %get-tuple-element.61), channel_id=1, source_target_pairs={{0,4},{1,5},{2,6},{3,7},{4,0},{5,1},{6,2},{7,3},{8,12},{9,13},{10,... | collective-permute-start | bytes 73736 | tf_op jit(solution)/shard_map/ppermute | solution.py:369
  25.9 18.8 %collective-permute-start.4 = (bf16[16,768]{1,0:T(8,128)(2,1)S(1)}, bf16[16,768]{1,0:T(8,128)(2,1)S(1)}, u32[]{:S(2)}, u32[]{:S(2)}) collective-permute-start(bf16[16,768]{1,0:T(8,128)(2,1)S(1)} %get-tuple-element.62), channel_id=1, source_target_pairs={{0,5},{1,4},{2,7},{3,6},{4,1},{5,0},{6,3},{7,2},{8,13},{9,12},{10,... | collective-permute-start | bytes 73736 | tf_op jit(solution)/shard_map/ppermute | solution.py:369
  27.4 17.9 %copy-start.2 = (bf16[1,1,6,32768]{3,2,1,0:T(8,128)(2,1)S(1)}, bf16[1,1,6,32768]{3,2,1,0:T(8,128)(2,1)}, u32[]{:S(2)}) copy-start(bf16[1,1,6,32768]{3,2,1,0:T(8,128)(2,1)} %param.18) | copy-start | bytes 1179652
  27.4 17.9 %copy-start.4 = (bf16[512,512]{1,0:T(8,128)(2,1)S(1)}, bf16[512,512]{1,0:T(8,128)(2,1)}, u32[]{:S(2)}) copy-start(bf16[512,512]{1,0:T(8,128)(2,1)} %constant.10.clone.outer_fwd.refs_17_) | copy-start | bytes 1572868
  27.4 17.9 %copy-start.5 = (bf16[768,256]{1,0:T(8,128)(2,1)S(1)}, bf16[768,256]{1,0:T(8,128)(2,1)}, u32[]{:S(2)}) copy-start(bf16[768,256]{1,0:T(8,128)(2,1)} %constant.12.clone.inner_fwd.refs_19_) | copy-start | bytes 1179652
  27.4 17.9 %copy-start.7 = (f32[256,256]{1,0:T(8,128)S(1)}, f32[256,256]{1,0:T(8,128)}, u32[]{:S(2)}) copy-start(f32[256,256]{1,0:T(8,128)} %constant.11.clone.turn.refs_18_) | copy-start | bytes 786436
  27.4 23.2 %copy-start.3 = (bf16[256,1536]{1,0:T(8,128)(2,1)S(1)}, bf16[256,1536]{1,0:T(8,128)(2,1)}, u32[]{:S(2)}) copy-start(bf16[256,1536]{1,0:T(8,128)(2,1)} %constant.14.clone.refs_21_) | copy-start | bytes 2359300
  27.4 23.2 %copy-start.6 = (bf16[768,256]{1,0:T(8,128)(2,1)S(1)}, bf16[768,256]{1,0:T(8,128)(2,1)}, u32[]{:S(2)}) copy-start(bf16[768,256]{1,0:T(8,128)(2,1)} %constant.13.clone.refs_20_) | copy-start | bytes 1179652
  39.4 7.5 %collective-permute-start.5 = (bf16[16,768]{1,0:T(8,128)(2,1)S(1)}, bf16[16,768]{1,0:T(8,128)(2,1)S(1)}, u32[]{:S(2)}, u32[]{:S(2)}) collective-permute-start(bf16[16,768]{1,0:T(8,128)(2,1)S(1)} %get-tuple-element.63), channel_id=1, source_target_pairs={{0,6},{1,7},{2,4},{3,5},{4,2},{5,3},{6,0},{7,1},{8,14},{9,15},{10,... | collective-permute-start | bytes 73736 | tf_op jit(solution)/shard_map/ppermute | solution.py:369
  39.9 7.0 %collective-permute-start.6 = (bf16[16,768]{1,0:T(8,128)(2,1)S(1)}, bf16[16,768]{1,0:T(8,128)(2,1)S(1)}, u32[]{:S(2)}, u32[]{:S(2)}) collective-permute-start(bf16[16,768]{1,0:T(8,128)(2,1)S(1)} %get-tuple-element.64), channel_id=1, source_target_pairs={{0,7},{1,6},{2,5},{3,4},{4,3},{5,2},{6,1},{7,0},{8,15},{9,14},{10,... | collective-permute-start | bytes 73736 | tf_op jit(solution)/shard_map/ppermute | solution.py:369
  42.3 5.0 %collective-permute-start.7 = (bf16[16,768]{1,0:T(8,128)(2,1)S(1)}, bf16[16,768]{1,0:T(8,128)(2,1)S(1)}, u32[]{:S(2)}, u32[]{:S(2)}) collective-permute-start(bf16[16,768]{1,0:T(8,128)(2,1)S(1)} %get-tuple-element.65), channel_id=1, source_target_pairs={{0,8},{1,9},{2,10},{3,11},{4,12},{5,13},{6,14},{7,15},{8,0},{9,1},... | collective-permute-start | bytes 73736 | tf_op jit(solution)/shard_map/ppermute | solution.py:369
  42.3 5.0 %collective-permute-start.8 = (bf16[16,768]{1,0:T(8,128)(2,1)S(1)}, bf16[16,768]{1,0:T(8,128)(2,1)S(1)}, u32[]{:S(2)}, u32[]{:S(2)}) collective-permute-start(bf16[16,768]{1,0:T(8,128)(2,1)S(1)} %get-tuple-element.66), channel_id=1, source_target_pairs={{0,9},{1,8},{2,11},{3,10},{4,13},{5,12},{6,15},{7,14},{8,1},{9,0},... | collective-permute-start | bytes 73736 | tf_op jit(solution)/shard_map/ppermute | solution.py:369
  44.7 5.9 %collective-permute-start.9 = (bf16[16,768]{1,0:T(8,128)(2,1)S(1)}, bf16[16,768]{1,0:T(8,128)(2,1)S(1)}, u32[]{:S(2)}, u32[]{:S(2)}) collective-permute-start(bf16[16,768]{1,0:T(8,128)(2,1)S(1)} %get-tuple-element.67), channel_id=1, source_target_pairs={{0,10},{1,11},{2,8},{3,9},{4,14},{5,15},{6,12},{7,13},{8,2},{9,3},... | collective-permute-start | bytes 73736 | tf_op jit(solution)/shard_map/ppermute | solution.py:369
  50.6 37.6 %copy-start.1 = (f32[2048]{0:T(1024)S(1)}, f32[2048]{0:T(1024)}, u32[]{:S(2)}) copy-start(f32[2048]{0:T(1024)} %param.22) | copy-start | bytes 24580
  55.7 3.6 %collective-permute-start.15 = (bf16[16,768]{1,0:T(8,128)(2,1)S(1)}, bf16[16,768]{1,0:T(8,128)(2,1)S(1)}, u32[]{:S(2)}, u32[]{:S(2)}) collective-permute-start(bf16[16,768]{1,0:T(8,128)(2,1)S(1)} %get-tuple-element.75), channel_id=1, source_target_pairs={{0,1},{1,0},{2,3},{3,2},{4,5},{5,4},{6,7},{7,6},{8,9},{9,8},{10,11... | collective-permute-start | bytes 73736 | tf_op jit(solution)/shard_map/ppermute | solution.py:369
  55.8 4.1 %collective-permute-start.16 = (bf16[16,768]{1,0:T(8,128)(2,1)S(1)}, bf16[16,768]{1,0:T(8,128)(2,1)S(1)}, u32[]{:S(2)}, u32[]{:S(2)}) collective-permute-start(bf16[16,768]{1,0:T(8,128)(2,1)S(1)} %get-tuple-element.76), channel_id=1, source_target_pairs={{0,2},{1,3},{2,0},{3,1},{4,6},{5,7},{6,4},{7,5},{8,10},{9,11},{10,... | collective-permute-start | bytes 73736 | tf_op jit(solution)/shard_map/ppermute | solution.py:369
  56.4 5.7 %collective-permute-start.17 = (bf16[16,768]{1,0:T(8,128)(2,1)S(1)}, bf16[16,768]{1,0:T(8,128)(2,1)S(1)}, u32[]{:S(2)}, u32[]{:S(2)}) collective-permute-start(bf16[16,768]{1,0:T(8,128)(2,1)S(1)} %get-tuple-element.77), channel_id=1, source_target_pairs={{0,3},{1,2},{2,1},{3,0},{4,7},{5,6},{6,5},{7,4},{8,11},{9,10},{10,... | collective-permute-start | bytes 73736 | tf_op jit(solution)/shard_map/ppermute | solution.py:369
  57.6 4.8 %collective-permute-start.18 = (bf16[16,768]{1,0:T(8,128)(2,1)S(1)}, bf16[16,768]{1,0:T(8,128)(2,1)S(1)}, u32[]{:S(2)}, u32[]{:S(2)}) collective-permute-start(bf16[16,768]{1,0:T(8,128)(2,1)S(1)} %get-tuple-element.78), channel_id=1, source_target_pairs={{0,4},{1,5},{2,6},{3,7},{4,0},{5,1},{6,2},{7,3},{8,12},{9,13},{10,... | collective-permute-start | bytes 73736 | tf_op jit(solution)/shard_map/ppermute | solution.py:369
  58.0 6.7 %collective-permute-start.19 = (bf16[16,768]{1,0:T(8,128)(2,1)S(1)}, bf16[16,768]{1,0:T(8,128)(2,1)S(1)}, u32[]{:S(2)}, u32[]{:S(2)}) collective-permute-start(bf16[16,768]{1,0:T(8,128)(2,1)S(1)} %get-tuple-element.79), channel_id=1, source_target_pairs={{0,5},{1,4},{2,7},{3,6},{4,1},{5,0},{6,3},{7,2},{8,13},{9,12},{10,... | collective-permute-start | bytes 73736 | tf_op jit(solution)/shard_map/ppermute | solution.py:369
  59.3 6.1 %collective-permute-start.20 = (bf16[16,768]{1,0:T(8,128)(2,1)S(1)}, bf16[16,768]{1,0:T(8,128)(2,1)S(1)}, u32[]{:S(2)}, u32[]{:S(2)}) collective-permute-start(bf16[16,768]{1,0:T(8,128)(2,1)S(1)} %get-tuple-element.80), channel_id=1, source_target_pairs={{0,6},{1,7},{2,4},{3,5},{4,2},{5,3},{6,0},{7,1},{8,14},{9,15},{10,... | collective-permute-start | bytes 73736 | tf_op jit(solution)/shard_map/ppermute | solution.py:369
  59.9 8.4 %collective-permute-start.21 = (bf16[16,768]{1,0:T(8,128)(2,1)S(1)}, bf16[16,768]{1,0:T(8,128)(2,1)S(1)}, u32[]{:S(2)}, u32[]{:S(2)}) collective-permute-start(bf16[16,768]{1,0:T(8,128)(2,1)S(1)} %get-tuple-element.81), channel_id=1, source_target_pairs={{0,7},{1,6},{2,5},{3,4},{4,3},{5,2},{6,1},{7,0},{8,15},{9,14},{10,... | collective-permute-start | bytes 73736 | tf_op jit(solution)/shard_map/ppermute | solution.py:369
  62.1 7.5 %collective-permute-start.22 = (bf16[16,768]{1,0:T(8,128)(2,1)S(1)}, bf16[16,768]{1,0:T(8,128)(2,1)S(1)}, u32[]{:S(2)}, u32[]{:S(2)}) collective-permute-start(bf16[16,768]{1,0:T(8,128)(2,1)S(1)} %get-tuple-element.82), channel_id=1, source_target_pairs={{0,8},{1,9},{2,10},{3,11},{4,12},{5,13},{6,14},{7,15},{8,0},{9,1},... | collective-permute-start | bytes 73736 | tf_op jit(solution)/shard_map/ppermute | solution.py:369
  62.5 9.3 %collective-permute-start.23 = (bf16[16,768]{1,0:T(8,128)(2,1)S(1)}, bf16[16,768]{1,0:T(8,128)(2,1)S(1)}, u32[]{:S(2)}, u32[]{:S(2)}) collective-permute-start(bf16[16,768]{1,0:T(8,128)(2,1)S(1)} %get-tuple-element.83), channel_id=1, source_target_pairs={{0,9},{1,8},{2,11},{3,10},{4,13},{5,12},{6,15},{7,14},{8,1},{9,0},... | collective-permute-start | bytes 73736 | tf_op jit(solution)/shard_map/ppermute | solution.py:369
  64.6 9.0 %collective-permute-start.24 = (bf16[16,768]{1,0:T(8,128)(2,1)S(1)}, bf16[16,768]{1,0:T(8,128)(2,1)S(1)}, u32[]{:S(2)}, u32[]{:S(2)}) collective-permute-start(bf16[16,768]{1,0:T(8,128)(2,1)S(1)} %get-tuple-element.84), channel_id=1, source_target_pairs={{0,10},{1,11},{2,8},{3,9},{4,14},{5,15},{6,12},{7,13},{8,2},{9,3},... | collective-permute-start | bytes 73736 | tf_op jit(solution)/shard_map/ppermute | solution.py:369
  65.4 10.8 %collective-permute-start.25 = (bf16[16,768]{1,0:T(8,128)(2,1)S(1)}, bf16[16,768]{1,0:T(8,128)(2,1)S(1)}, u32[]{:S(2)}, u32[]{:S(2)}) collective-permute-start(bf16[16,768]{1,0:T(8,128)(2,1)S(1)} %get-tuple-element.85), channel_id=1, source_target_pairs={{0,11},{1,10},{2,9},{3,8},{4,15},{5,14},{6,13},{7,12},{8,3},{9,2},... | collective-permute-start | bytes 73736 | tf_op jit(solution)/shard_map/ppermute | solution.py:369
  68.3 8.0 %collective-permute-start.26 = (bf16[16,768]{1,0:T(8,128)(2,1)S(1)}, bf16[16,768]{1,0:T(8,128)(2,1)S(1)}, u32[]{:S(2)}, u32[]{:S(2)}) collective-permute-start(bf16[16,768]{1,0:T(8,128)(2,1)S(1)} %get-tuple-element.86), channel_id=1, source_target_pairs={{0,12},{1,13},{2,14},{3,15},{4,8},{5,9},{6,10},{7,11},{8,4},{9,5},... | collective-permute-start | bytes 73736 | tf_op jit(solution)/shard_map/ppermute | solution.py:369
  69.6 6.7 %collective-permute-start.27 = (bf16[16,768]{1,0:T(8,128)(2,1)S(1)}, bf16[16,768]{1,0:T(8,128)(2,1)S(1)}, u32[]{:S(2)}, u32[]{:S(2)}) collective-permute-start(bf16[16,768]{1,0:T(8,128)(2,1)S(1)} %get-tuple-element.87), channel_id=1, source_target_pairs={{0,13},{1,12},{2,15},{3,14},{4,9},{5,8},{6,11},{7,10},{8,5},{9,4},... | collective-permute-start | bytes 73736 | tf_op jit(solution)/shard_map/ppermute | solution.py:369
  71.7 6.5 %collective-permute-start.28 = (bf16[16,768]{1,0:T(8,128)(2,1)S(1)}, bf16[16,768]{1,0:T(8,128)(2,1)S(1)}, u32[]{:S(2)}, u32[]{:S(2)}) collective-permute-start(bf16[16,768]{1,0:T(8,128)(2,1)S(1)} %get-tuple-element.88), channel_id=1, source_target_pairs={{0,14},{1,15},{2,12},{3,13},{4,10},{5,11},{6,8},{7,9},{8,6},{9,7},... | collective-permute-start | bytes 73736 | tf_op jit(solution)/shard_map/ppermute | solution.py:369
  73.7 5.9 %collective-permute-start.29 = (bf16[16,768]{1,0:T(8,128)(2,1)S(1)}, bf16[16,768]{1,0:T(8,128)(2,1)S(1)}, u32[]{:S(2)}, u32[]{:S(2)}) collective-permute-start(bf16[16,768]{1,0:T(8,128)(2,1)S(1)} %get-tuple-element.89), channel_id=1, source_target_pairs={{0,15},{1,14},{2,13},{3,12},{4,11},{5,10},{6,9},{7,8},{8,7},{9,6},... | collective-permute-start | bytes 73736 | tf_op jit(solution)/shard_map/ppermute | solution.py:369
  80.1 8.1 %collective-permute-start.30 = (f32[16,1,128]{2,1,0:T(1,128)S(1)}, f32[16,1,128]{2,1,0:T(1,128)S(1)}, u32[]{:S(2)}, u32[]{:S(2)}) collective-permute-start(f32[16,1,128]{2,1,0:T(1,128)S(1)} %get-tuple-element.98.refs_0_), channel_id=1, source_target_pairs={{0,16},{16,0},{1,17},{17,1},{2,18},{18,2},{3,19},{19,3},{4,20},{20... | collective-permute-start | bytes 24584 | tf_op jit(solution)/shard_map/ppermute | solution.py:480

commit v4 on v3

v4 whole, which is shorter than its diff:
```python
import functools

import jax
import jax.numpy as jnp
import numpy as np
from jax import lax
from jax.experimental import pallas as pl
from jax.experimental.pallas import tpu as pltpu
from jax.sharding import PartitionSpec as P

LANES = 128
TILE = 256
CHUNK = 16
AHEAD = 3
HALVES = 2
MIB = 1 << 20
norm_eps = 1e-06
f32 = jnp.float32
bf16 = jnp.bfloat16


def split_np(table):
    high = table.astype(jnp.bfloat16)
    low = (table - high.astype(np.float64)).astype(jnp.bfloat16)
    return high, low


def dft_tables(length):
    inner = LANES
    outer = length // inner
    a = np.arange(outer)
    b = np.arange(inner)
    quarter = np.arange(outer) + 0.25
    outer_angle = 2 * np.pi / outer * np.mod(quarter[:, None] * a[None, :], outer)
    turn_angle = 2 * np.pi / length * (quarter[:, None] * b[None, :])
    inner_angle = 2 * np.pi / inner * np.mod(b[:, None] * b[None, :], inner)
    outer_fwd = np.concatenate([np.cos(outer_angle), -np.sin(outer_angle)], axis=0)
    c, s = np.cos(inner_angle), np.sin(inner_angle)
    inner_fwd = np.concatenate(
        [np.concatenate([c, -s], axis=1), np.concatenate([s, c], axis=1)], axis=0
    )
    inner_back = np.concatenate(
        [np.concatenate([c, s], axis=1), np.concatenate([-s, c], axis=1)], axis=0
    )
    outer_back = np.concatenate([np.cos(outer_angle).T, -np.sin(outer_angle).T], axis=1) / length
    turn = np.concatenate([np.cos(turn_angle), np.sin(turn_angle)], axis=1).astype(np.float32)
    outer_fwd = np.concatenate(split_np(outer_fwd), axis=1)
    inner = np.concatenate(split_np(inner_fwd) + split_np(inner_back), axis=0)
    outer_back = np.concatenate(split_np(outer_back), axis=1)
    return outer_fwd, turn, inner, outer_back


def split(value):
    high = value.astype(bf16)
    low = (value - high.astype(f32)).astype(bf16)
    return high, low


def dot(x, y):
    return jnp.dot(x, y, preferred_element_type=f32)


def dot_rows(x, y):
    return lax.dot_general(x, y, (((0,), (0,)), ((), ())), preferred_element_type=f32)


def times_table(value, table):
    high, low = split(value)
    depth = value.shape[1]
    stacked = jnp.concatenate([table, table[:depth]], axis=0)
    return dot(jnp.concatenate([high, high, low], axis=1), stacked)


def table_times(table, value):
    high, low = split(value)
    depth = value.shape[0]
    stacked = jnp.concatenate([table, table[:, :depth]], axis=1)
    return dot(stacked, jnp.concatenate([high, high, low], axis=0))


def to_spectrum(blocks, slots, outer_fwd, turn, inner_fwd):
    outer = blocks.shape[0]
    first = dot(outer_fwd, jnp.concatenate([blocks, blocks], axis=0))
    turn, inner_fwd = turn(), inner_fwd()
    cos, sin = turn[:, :LANES], turn[:, LANES:]
    result = []
    for s in range(slots):
        re = first[:outer, s * LANES : (s + 1) * LANES]
        im = first[outer:, s * LANES : (s + 1) * LANES]
        turned = jnp.concatenate([re * cos + im * sin, im * cos - re * sin], axis=1)
        result.append(times_table(turned, inner_fwd))
    return result


def filter_kernel(filters, outer_fwd, turn, inner, spectra):
    slots, length = filters.shape
    outer = length // LANES
    wide = filters[...].astype(f32)
    blocks = [wide[s].reshape(outer, LANES) for s in range(slots)]
    blocks = jnp.concatenate(blocks, axis=1).astype(bf16)
    parts = to_spectrum(
        blocks, slots, outer_fwd[...], lambda: turn[...], lambda: inner[: 4 * LANES, :]
    )
    for s in range(slots):
        spectra[s] = parts[s]


def convolve_kernel(
    signals_far, outer_fwd_far, turn_far, inner_far, spectra_far, outer_back_far, out, *scratch
):
    sources = (signals_far, outer_fwd_far, turn_far, inner_far, spectra_far, outer_back_far)
    signals, outer_fwd, turn_ref, inner, spectra, outer_back, sems = scratch
    copies = [
        pltpu.make_async_copy(source, scratch[n], sems.at[n]) for n, source in enumerate(sources)
    ]
    for copy in copies[:4]:
        copy.start()
    slots, outer = spectra.shape[:2]

    def turn_now():
        copies[2].wait()
        return turn_ref[...]

    def inner_now():
        copies[3].wait()
        return inner[: 4 * LANES, :]

    copies[0].wait()
    copies[1].wait()
    for copy in copies[4:]:
        copy.start()
    blocks = signals[...].reshape(outer, slots * LANES)
    parts = to_spectrum(blocks, slots, outer_fwd[...], turn_now, inner_now)
    turn = turn_ref[...]
    cos, sin = turn[:, :LANES], turn[:, LANES:]
    copies[4].wait()
    turned = []
    for s in range(slots):
        sig_re, sig_im = parts[s][:, :LANES], parts[s][:, LANES:]
        ker_re, ker_im = spectra[s, :, :LANES], spectra[s, :, LANES:]
        joint = jnp.concatenate(
            [sig_re * ker_re - sig_im * ker_im, sig_re * ker_im + sig_im * ker_re], axis=1
        )
        back = times_table(joint, inner[4 * LANES :, :])
        re, im = back[:, :LANES], back[:, LANES:]
        turned.append(jnp.concatenate([re * cos - im * sin, im * cos + re * sin], axis=0))
    copies[5].wait()
    for s in range(0, slots, 2):
        pair = turned[s : s + 2]
        causal = table_times(outer_back[...], jnp.concatenate(pair, axis=1)).astype(bf16)
        lanes = slice(s * LANES, (s + len(pair)) * LANES)
        out[:, :, lanes] = causal.reshape(out.shape[:2] + (len(pair) * LANES,))


def iota(shape, axis):
    return lax.broadcasted_iota(jnp.int32, shape, axis)


def to_column(row):
    size = row.shape[1]
    same = iota((size, size), 0) == iota((size, size), 1)
    return jnp.sum(jnp.where(same, row, 0), axis=1, keepdims=True)


def channel_of_row(index_row, owners_row, owner_count, rows):
    slots = owners_row.shape[1]
    owners_col = to_column(owners_row)
    index_col = to_column(index_row)
    earlier = (owners_col == owners_row) & (iota((slots, slots), 1) < iota((slots, slots), 0))
    rank_col = jnp.sum(earlier.astype(jnp.int32), axis=1, keepdims=True)
    target_col = jnp.where(owners_col >= 0, rank_col * owner_count + owners_col, -1)
    hit = target_col == iota((slots, rows), 1)
    return jnp.sum(jnp.where(hit, index_col + 1, 0), axis=0, keepdims=True) - 1


def pick_rows(tile, onehot_t, rows):
    picked = dot(tile, onehot_t).T
    return [picked[:rows, i : i + LANES] for i in range(0, tile.shape[0], LANES)]


def fetch(sources, stages, sems, tile, first=0):
    count = stages[0].shape[0] // tile

    def copies(i):
        at = pl.multiple_of(i * tile, tile)
        return [
            pltpu.make_async_copy(
                source.at[pl.ds(first + at, tile), :], stage.at[pl.ds(at, tile), :], sems.at[n, i]
            )
            for n, (source, stage) in enumerate(zip(sources, stages))
        ]

    def start(i):
        for copy in copies(i):
            copy.start()

    for i in range(min(AHEAD, count)):
        start(i)

    def wait(i):
        for copy in copies(i):
            copy.wait()

        @pl.when(i + AHEAD < count)
        def _():
            start(i + AHEAD)

        return pl.multiple_of(i * tile, tile)

    return wait, count


def pick_kernel(owner_count, slots, index, owners, gate, value, *refs):
    payload, picked, channels, onehot_t = refs[:4]
    acc, gate_stage, value_stage, lists, list_sems, sems = refs[4:]
    rows = owner_count * slots
    tile = gate_stage.shape[0] // sems.shape[1]
    list_copies = [
        pltpu.make_async_copy(source, lists.at[n], list_sems.at[n])
        for n, source in enumerate((index, owners))
    ]
    for copy in list_copies:
        copy.start()
    wait, count = fetch((gate, value), (gate_stage, value_stage), sems, tile)
    for copy in list_copies:
        copy.wait()
    row = channel_of_row(lists[0], lists[1], owner_count, onehot_t.shape[1])
    channels[...] = jnp.broadcast_to(row, channels.shape)
    onehot_t[...] = (iota(onehot_t.shape, 0) == row).astype(f32).astype(bf16)

    def step(i, _):
        at = pl.ds(wait(i), tile)
        gated = gate_stage[at, :] * value_stage[at, :]
        for n, block in enumerate(pick_rows(gated, onehot_t[...], rows)):
            acc[i * (tile // LANES) + n] = block
            picked[i * (tile // LANES) + n] = block.astype(bf16)
        return 0

    lax.fori_loop(0, count, step, 0)
    for s in range(slots):
        part = jnp.swapaxes(acc[:, s * owner_count : (s + 1) * owner_count, :], 0, 1)
        payload[:, :, s * LANES : (s + 1) * LANES] = part.astype(bf16)


def place_kernel(channels, skip, onehot, others, skip_wide):
    hit = iota(onehot.shape, 1) == to_column(channels[0:1, :])[: onehot.shape[0]]
    onehot[...] = hit.astype(f32).astype(bf16)
    others[...] = jnp.broadcast_to(1.0 - jnp.max(hit.astype(f32), axis=0, keepdims=True), others.shape)
    skip_col = jnp.sum(jnp.where(hit, skip[...], 0.0), axis=1, keepdims=True)
    skip_wide[...] = jnp.broadcast_to(skip_col, skip_wide.shape)


def base_kernel(first, onehot_t, others, skip, gate, value, out_gate, residual, *refs):
    base, sums, picked_gate, picked_res = refs[-12:-8]
    stages = refs[-8:-4]
    base_stage, partial, base_sems, sems = refs[-4:]
    gate_stage, value_stage, out_stage, res_stage = stages
    rows = picked_gate.shape[1]
    slab = gate_stage.shape[1]
    tile = partial.shape[0]
    wait, count = fetch((gate, value, out_gate, residual), stages, sems, tile, first)

    def copy(i):
        at = pl.multiple_of(i * tile, tile)
        return pltpu.make_async_copy(
            base_stage.at[pl.ds(at, tile), :], base.at[pl.ds(first + at, tile), :], base_sems.at[i]
        )

    def step(i, _):
        start = wait(i)
        for c in range(0, tile, CHUNK):
            at = pl.ds(start + c, CHUNK)
            total = jnp.zeros((CHUNK, LANES), f32)
            for j in range(0, slab, LANES):
                lanes = slice(j, j + LANES)
                gated = (gate_stage[at, lanes] * value_stage[at, lanes]).astype(f32)
                mixed = out_stage[at, lanes].astype(f32) * (skip[:, lanes] * gated)
                hidden = (res_stage[at, lanes].astype(f32) + mixed) * others[0:1, lanes]
                hidden = hidden.astype(bf16)
                base_stage[at, lanes] = hidden
                hidden = hidden.astype(f32)
                total = total + hidden * hidden
            partial[c : c + CHUNK, :] = total
        copy(i).start()
        total = jnp.sum(partial[...].T, axis=0, keepdims=True)
        at = pl.ds(start, tile)
        picks_gate = pick_rows(out_stage[at, :], onehot_t[...], rows)
        picks_res = pick_rows(res_stage[at, :], onehot_t[...], rows)
        for n in range(tile // LANES):
            block = i * (tile // LANES) + n
            sums[block] = total[:, n * LANES : (n + 1) * LANES]
            picked_gate[block] = picks_gate[n].astype(bf16)
            picked_res[block] = picks_res[n].astype(bf16)
        return 0

    lax.fori_loop(0, count, step, 0)
    lax.fori_loop(0, count, lambda i, _: (copy(i).wait(), 0)[1], 0)


def kept_kernel(halves, conv, picked, skip_wide, *refs):
    hidden, totals = refs[-2:]
    owner_count, blocks = conv.shape[:2]
    size = blocks // halves
    for h in range(halves):
        sums, picked_gate, picked_res = refs[3 * h : 3 * h + 3]
        at_h = slice(h * size, (h + 1) * size)
        total = jnp.zeros((size, LANES), f32)
        for s in range(conv.shape[2] // LANES):
            at = slice(s * owner_count, (s + 1) * owner_count)
            conv_rows = conv[:, at_h, s * LANES : (s + 1) * LANES].astype(f32)
            conv_rows = jnp.swapaxes(conv_rows, 0, 1)
            wide = conv_rows + skip_wide[at, :] * picked[at_h, at, :].astype(f32)
            value = picked_res[:, at, :].astype(f32) + picked_gate[:, at, :].astype(f32) * wide
            value = value.astype(bf16)
            hidden[at_h, at, :] = value
            value = value.astype(f32)
            total = total + jnp.sum(value * value, axis=1)
        for i in range(size):
            totals[h * size + i] = total[i : i + 1, :] + sums[i]


def hidden_kernel(base, hidden_kept, onehot, hidden, held, base_stage, base_sems, sems):
    slab = held.shape[1]
    wide = min(slab, 2 * LANES)
    wait, count = fetch((base,), (base_stage,), base_sems, LANES)

    def copy(i):
        rows = pl.ds(pl.multiple_of(i * LANES, LANES), LANES)
        return pltpu.make_async_copy(held.at[rows, :], hidden.at[rows, :], sems.at[i])

    def step(i, _):
        kept = hidden_kept[i].astype(f32).T.astype(bf16)
        rows = pl.ds(wait(i), LANES)
        for j in range(0, slab, wide):
            lanes = slice(j, j + wide)
            placed = dot(kept, onehot[:, lanes]).astype(bf16)
            held[rows, lanes] = base_stage[rows, lanes] + placed
        copy(i).start()
        return 0

    lax.fori_loop(0, count, step, 0)
    lax.fori_loop(0, count, lambda i, _: (copy(i).wait(), 0)[1], 0)


def norm_kernel(width, count, *refs):
    parts = refs[:count]
    held, gain, normed, stage, turned, sems = refs[count:]
    slab = held.shape[1]

    def copy(i):
        rows = pl.ds(pl.multiple_of(i * LANES, LANES), LANES)
        return pltpu.make_async_copy(stage.at[rows, :], normed.at[rows, :], sems.at[i])

    def step(i, _):
        total = parts[0][i]
        for part in parts[1:]:
            total = total + part[i]
        scale = lax.rsqrt(total / width + norm_eps)
        turned[...] = jnp.broadcast_to(scale, (LANES, LANES)).T
        first = pl.multiple_of(i * LANES, LANES)
        for c in range(0, LANES, CHUNK):
            at = pl.ds(first + c, CHUNK)
            scales = turned[c : c + CHUNK, :]
            for j in range(0, slab, LANES):
                lanes = slice(j, j + LANES)
                value = held[at, lanes].astype(f32) * scales * gain[:, lanes]
                stage[at, lanes] = value.astype(bf16)
        copy(i).start()
        return 0

    lax.fori_loop(0, sems.shape[0], step, 0)
    lax.fori_loop(0, sems.shape[0], lambda i, _: (copy(i).wait(), 0)[1], 0)


def in_hbm(x):
    return pltpu.with_memory_space_constraint(x, pltpu.HBM)


def in_vmem(x):
    return pltpu.with_memory_space_constraint(x, pltpu.VMEM)


def call(kernel, outs, ins, flops, moved, limit, scratch=(), far=(), far_outs=(), alias=None):
    near = pl.BlockSpec(memory_space=pltpu.VMEM)
    away = pl.BlockSpec(memory_space=pl.ANY)
    return pl.pallas_call(
        kernel,
        out_shape=outs,
        in_specs=[away if n in far else near for n in range(len(ins))],
        out_specs=[away if n in far_outs else near for n in range(len(outs))],
        scratch_shapes=list(scratch),
        input_output_aliases=alias or {},
        compiler_params=pltpu.CompilerParams(vmem_limit_bytes=limit),
        cost_estimate=pl.CostEstimate(flops=flops, bytes_accessed=moved, transcendentals=0),
    )(*ins)


def local(
    gate_in, value_in, out_gate, residual, filters, kept_index, kept_owner, skip_bias, norm_gain
):
    tok_rows, slab = gate_in.shape
    slots, length = filters.shape[2:]
    chan_devices = lax.axis_size("chan")
    owner_count = lax.axis_size("seqo") * lax.axis_size("seqi")
    rows = slots * owner_count
    lanes_rows = -(-rows // LANES) * LANES
    blocks = tok_rows // LANES
    outer = length // LANES
    tile = TILE if tok_rows % TILE == 0 else LANES
    dense = tok_rows * slab * 2
    sds = jax.ShapeDtypeStruct
    tables = [in_hbm(jnp.asarray(x)) for x in dft_tables(length)]
    outer_fwd, turn, inner, outer_back = tables
    skip_row = skip_bias[None, :]
    gain_row = norm_gain[None, :]
    gate_in, value_in, out_gate, residual = map(in_hbm, (gate_in, value_in, out_gate, residual))
    picks = sds((blocks, rows, LANES), bf16)
    row_sums = sds((blocks, 1, LANES), f32)
    buffer = (owner_count, blocks, slots * LANES)
    whole = (tok_rows, slab)

    payload, picked, channels, onehot_t = call(
        functools.partial(pick_kernel, owner_count, slots),
        [sds(buffer, bf16), picks, sds((8, lanes_rows), jnp.int32), sds((slab, lanes_rows), bf16)],
        [in_hbm(kept_index), in_hbm(kept_owner), gate_in, value_in],
        2 * tok_rows * slab * rows,
        2 * dense,
        24 * MIB,
        scratch=[
            pltpu.VMEM((blocks, rows, LANES), f32),
            pltpu.VMEM(whole, bf16),
            pltpu.VMEM(whole, bf16),
            pltpu.VMEM((2,) + kept_index.shape, jnp.int32),
            pltpu.SemaphoreType.DMA((2,)),
            pltpu.SemaphoreType.DMA((2, tok_rows // tile)),
        ],
        far=(0, 1, 2, 3),
    )

    incoming = lax.all_to_all(payload, ("seqo", "seqi"), split_axis=0, concat_axis=0, tiled=True)

    (spectra,) = call(
        filter_kernel,
        [sds((slots, outer, 2 * LANES), f32)],
        [filters[0, 0]] + [jnp.asarray(x) for x in dft_tables(length)[:3]],
        2 * slots * length * 2 * (2 * outer + 6 * LANES),
        8 * MIB,
        16 * MIB,
    )
    onehot, others, skip_wide = call(
        place_kernel,
        [sds((rows, slab), bf16), sds((8, slab), f32), sds((rows, LANES), f32)],
        [channels, skip_row],
        rows * slab * 8,
        rows * slab * 2,
        8 * MIB,
    )

    def base_half(h, onehot_t, base):
        part = tok_rows // HALVES
        count = part // LANES
        ins = [onehot_t, others, skip_row, gate_in, value_in, out_gate, residual]
        outs = [
            pltpu.HBM(whole, bf16),
            sds((count, 1, LANES), f32),
            sds((count, rows, LANES), bf16),
            sds((count, rows, LANES), bf16),
        ]
        if base is not None:
            ins.append(base)
        return call(
            functools.partial(base_kernel, h * part),
            outs,
            ins,
            4 * tok_rows * slab * rows // HALVES,
            5 * dense // HALVES,
            24 * MIB,
            scratch=[pltpu.VMEM((part, slab), bf16)] * 5
            + [
                pltpu.VMEM((LANES, LANES), f32),
                pltpu.SemaphoreType.DMA((count,)),
                pltpu.SemaphoreType.DMA((4, count)),
            ],
            far=(3, 4, 5, 6, 7),
            far_outs=(0,),
            alias={} if base is None else {7: 0},
        )

    base, *half_picks = base_half(0, onehot_t, None)
    spectra, base = lax.optimization_barrier((spectra, base))

    conv_ins = [in_hbm(incoming), outer_fwd, turn, inner, in_hbm(spectra), outer_back]
    (convolved,) = call(
        convolve_kernel,
        [sds(buffer, bf16)],
        conv_ins,
        2 * slots * length * 2 * (5 * outer + 12 * LANES),
        8 * MIB,
        20 * MIB,
        scratch=[pltpu.VMEM(x.shape, x.dtype) for x in conv_ins]
        + [pltpu.SemaphoreType.DMA((len(conv_ins),))],
        far=tuple(range(len(conv_ins))),
    )
    convolved, onehot_t = lax.optimization_barrier((convolved, onehot_t))

    returned = lax.all_to_all(convolved, ("seqo", "seqi"), split_axis=0, concat_axis=0, tiled=True)

    base, *more_picks = base_half(1, onehot_t, base)

    hidden_kept, totals = call(
        functools.partial(kept_kernel, HALVES),
        [picks, row_sums],
        [returned, picked, skip_wide, *half_picks, *more_picks],
        8 * rows * tok_rows,
        10 * rows * tok_rows,
        16 * MIB,
    )

    parts = [totals]
    for shift in range(1, chan_devices):
        ring = [(i, (i + shift) % chan_devices) for i in range(chan_devices)]
        parts.append(lax.ppermute(totals, "chan", ring))

    hidden, held = call(
        hidden_kernel,
        [pltpu.HBM(whole, bf16), pltpu.VMEM(whole, bf16)],
        [in_hbm(base), hidden_kept, onehot],
        2 * tok_rows * slab * rows,
        2 * dense,
        16 * MIB,
        scratch=[
            pltpu.VMEM(whole, bf16),
            pltpu.SemaphoreType.DMA((1, blocks)),
            pltpu.SemaphoreType.DMA((blocks,)),
        ],
        far=(0,),
        far_outs=(0,),
    )
    (normed,) = call(
        functools.partial(norm_kernel, float(slab * chan_devices), len(parts)),
        [pltpu.HBM(whole, bf16)],
        parts + [in_vmem(held), gain_row],
        4 * tok_rows * slab,
        2 * dense,
        16 * MIB,
        scratch=[
            pltpu.VMEM(whole, bf16),
            pltpu.VMEM((LANES, LANES), f32),
            pltpu.SemaphoreType.DMA((blocks,)),
        ],
        far_outs=(0,),
    )
    return (hidden, normed)


def solution(mesh):
    positions = P(("seqo", "seqi"), "chan")
    in_specs = (
        positions,
        positions,
        positions,
        positions,
        P("chan", ("seqo", "seqi"), None, None),
        P("chan", None),
        P("chan", None),
        P("chan"),
        P("chan"),
    )
    return jax.shard_map(
        local, mesh=mesh, in_specs=in_specs, out_specs=(positions, positions), check_vma=False
    )
```

time: 92.8 us -> 68.7 us (0.74)
  starting transfers between devices: 44.2 us -> 15 us
  Pallas kernels: 40.4 us -> 47.1 us
  waiting for transfers between devices: 7.29 us -> 3.4 us
  local copies, waits for them, and re-layouts: 0.04 us -> 1.92 us
    ppermute x30 -> x0, starting transfers between devices: 42.6 us -> none  [exchange(): result.append(lax.ppermute(pieces[d], ('seqo', 'seqi'), pairs))]
    all_to_all x0 -> x2, starting transfers between devices: none -> 13.4 us  [the longest x1 7.37 us: local(): lax.all_to_all(payload, ('seqo', 'seqi'), split_axis=0, concat_axis=0, ti...]
    ppermute x30 -> x0, waiting for transfers between devices: 7.29 us -> none  [exchange(): result.append(lax.ppermute(pieces[d], ('seqo', 'seqi'), pairs))]
    pallas_call x8 -> x9, Pallas kernels: 40.4 us -> 47.1 us  [call(): pl.pallas_call(kernel, out_shape=outs, in_specs=[away if n in far else ne...]
    all_to_all x0 -> x2, waiting for transfers between devices: none -> 3.4 us  [the longest x1 3.39 us: local(): lax.all_to_all(convolved, ('seqo', 'seqi'), split_axis=0, concat_axis=0,...]
    unnamed x16, local copies, waits for them, and re-layouts: 0.04 us -> 1.92 us
  transfers between devices with their start and end apart: 31 -> 3, of which waited for: 5 -> 1; matrix products, arithmetic and copies ran while one was open for 0% -> 0% of each run, Pallas kernels for 22% -> 42%
where the time goes in v4:
time: 68.7 us; the launch traced here: 68.2 us
  Pallas kernels  47.1 us (69%)
  starting transfers between devices  15 us (22%)
  waiting for transfers between devices  3.4 us (5%)
  local copies, waits for them, and re-layouts  1.92 us (3%)
  between operations  0.78 us (1%)
    pallas_call x9, Pallas kernels, call(): pl.pallas_call(kernel, out_shape=outs, in_specs=[away if n in far else ne...  47.1 us
    all_to_all x1, starting transfers between devices, local(): lax.all_to_all(payload, ('seqo', 'seqi'), split_axis=0, concat_axis=0, ti...  7.37 us
    all_to_all x1, starting transfers between devices, local(): lax.all_to_all(convolved, ('seqo', 'seqi'), split_axis=0, concat_axis=0,...  6.02 us
    all_to_all x1, waiting for transfers between devices, local(): lax.all_to_all(convolved, ('seqo', 'seqi'), split_axis=0, concat_axis=0,...  3.39 us
    unnamed x16, local copies, waits for them, and re-layouts  1.92 us
    ppermute x1, starting transfers between devices, local(): parts.append(lax.ppermute(totals, 'chan', ring))  1.57 us
  transfers between devices with their start and end apart: 3, of which 1 were waited for; matrix products, arithmetic and copies ran while one was open for 0% of the time, Pallas kernels for 42%

profile of v4, /device:TPU:0, one launch (start us, length us, event | category | flops | bytes accessed | tf_op | source)
XLA Modules:
  0.0 68.2 jit_solution(3353024070154485283)
XLA Ops:
  0.6 0.0 copy-start
  0.6 8.5 %shard_map.167 = (bf16[16,16,768]{2,1,0:T(8,128)(2,1)}, bf16[16,96,128]{2,1,0:T(8,128)(2,1)S(1)}, s32[8,128]{1,0:T(8,128)S(1)}, bf16[2048,128]{1,0:T(8,128)(2,1)S(1)}) custom-call(s32[1,64]{1,0:T(1,128)} %index.1, s32[1,64]{1,0:T(1,128)} %owners.1, bf16[2048,2048]{1,0:T(8,128)(2,1)} %gate.5, bf16[2048,2048]{1,0:T(8,128)(2,1)} %value.5), custom_call_target="tpu_custom_call" | custom-call | flops 805306368 | bytes 16777216 | tf_op jit(solution)/shard_map/pallas_call | solution.py:386
  9.1 7.4 %all-to-all-start = ((bf16[16,16,768]{2,1,0:T(8,128)(2,1)}), bf16[16,16,768]{2,1,0:T(8,128)(2,1)S(1)}, u32[]{:S(2)}, u32[]{:S(2)}) async-start(bf16[16,16,768]{2,1,0:T(8,128)(2,1)} %get-tuple-element.25), calls=%async_computation | async-start | bytes 786432 | tf_op jit(solution)/shard_map/all_to_all | solution.py:440
  16.5 0.0 copy-done
  16.5 0.4 shard_map.169
  16.9 0.0 copy-start.2
  16.9 0.0 copy-start.3
  16.9 0.0 copy-start.4
  16.9 0.0 copy-start.5
  16.9 9.4 %shard_map.170 = (bf16[2048,2048]{1,0:T(8,128)(2,1)}, f32[8,1,128]{2,1,0:T(1,128)S(1)}, bf16[8,96,128]{2,1,0:T(8,128)(2,1)S(1)}, bf16[8,96,128]{2,1,0:T(8,128)(2,1)S(1)}) custom-call(bf16[2048,128]{1,0:T(8,128)(2,1)S(1)} %get-tuple-element.31.onehot_t, f32[8,2048]{1,0:T(8,128)S(1)} %get-tuple-element.28.others, f32[1,2048]{1,0:T(1,128)S(1)} %bitcast.4, ...), custom_call_target="tpu_custom_call" | custom-call | flops 805306368 | bytes 20971520 | tf_op jit(solution)/shard_map/pallas_call | solution.py:386
  26.3 0.0 copy-done.2
  26.3 0.0 copy-done.3
  26.3 0.0 copy-done.4
  26.3 0.0 copy-done.5
  26.3 1.5 %shard_map.168.spectra_far = f32[6,256,256]{2,1,0:T(8,128)S(1)} custom-call(bf16[6,32768]{1,0:T(8,128)(2,1)S(1)} %bitcast.7, bf16[512,512]{1,0:T(8,128)(2,1)S(1)} %copy-done.4, f32[256,256]{1,0:T(8,128)S(1)} %copy-done.5, bf16[1024,256]{1,0:T(8,128)(2,1)S(1)} %copy-done.3), custom_call_target="tpu_custom_call" | custom-call | flops 1006632960 | bytes 8388608 | tf_op jit(solution)/shard_map/pallas_call | solution.py:386
  27.8 0.0 copy-start.6
  27.8 1.1 %copy-done.6 = f32[6,256,256]{2,1,0:T(8,128)} copy-done((f32[6,256,256]{2,1,0:T(8,128)}, f32[6,256,256]{2,1,0:T(8,128)S(1)}, u32[]{:S(2)}) %copy-start.6) | copy-done | bytes 1572888
  29.0 0.0 all-to-all-done.signals_far
  29.0 0.0 copy-start.7
  29.0 0.8 %copy-done.7 = bf16[16,16,768]{2,1,0:T(8,128)(2,1)} copy-done((bf16[16,16,768]{2,1,0:T(8,128)(2,1)}, bf16[16,16,768]{2,1,0:T(8,128)(2,1)S(1)}, u32[]{:S(2)}) %copy-start.7) | copy-done | bytes 393240
  29.7 5.3 %shard_map.171 = bf16[16,16,768]{2,1,0:T(8,128)(2,1)} custom-call(bf16[16,16,768]{2,1,0:T(8,128)(2,1)} %copy-done.7, bf16[512,512]{1,0:T(8,128)(2,1)} %constant.8.clone.outer_fwd.outer_fwd_far, f32[256,256]{1,0:T(8,128)} %constant.9.clone.turn.turn_far, bf16[1024,256]{1,0:T(8,128)(2,1)} %constant.10.clone.inner.inner_far, f32[6,256,256]{2,1,0:T(8,128)} %copy-done.6, ...), custom_call_target="tpu_custom_call" | custom-call | flops 2214592512 | bytes 8388608 | tf_op jit(solution)/shard_map/pallas_call | solution.py:386
  35.1 6.0 %all-to-all-start.1 = ((bf16[16,16,768]{2,1,0:T(8,128)(2,1)}), bf16[16,16,768]{2,1,0:T(8,128)(2,1)S(1)}, u32[]{:S(2)}, u32[]{:S(2)}) async-start(bf16[16,16,768]{2,1,0:T(8,128)(2,1)} %shard_map.171), calls=%async_computation.1 | async-start | bytes 786432 | tf_op jit(solution)/shard_map/all_to_all | solution.py:506
  41.1 8.8 %shard_map.172 = (bf16[2048,2048]{1,0:T(8,128)(2,1)}, f32[8,1,128]{2,1,0:T(1,128)S(1)}, bf16[8,96,128]{2,1,0:T(8,128)(2,1)S(1)}, bf16[8,96,128]{2,1,0:T(8,128)(2,1)S(1)}) custom-call(bf16[2048,128]{1,0:T(8,128)(2,1)S(1)} %get-tuple-element.31.onehot_t, f32[8,2048]{1,0:T(8,128)S(1)} %get-tuple-element.28.others, ...), custom_call_target="tpu_custom_call", output_to_operand_aliasing={{0}: (7, {})} | custom-call | flops 805306368 | bytes 20971520 | tf_op jit(solution)/shard_map/pallas_call | solution.py:386
  49.9 0.0 copy-start.1
  49.9 3.4 %all-to-all-done.1.conv = bf16[16,16,768]{2,1,0:T(8,128)(2,1)S(1)} async-done(((bf16[16,16,768]{2,1,0:T(8,128)(2,1)}), bf16[16,16,768]{2,1,0:T(8,128)(2,1)S(1)}, u32[]{:S(2)}, u32[]{:S(2)}) %all-to-all-start.1) | async-done | bytes 393248 | tf_op jit(solution)/shard_map/all_to_all | solution.py:506
  53.3 0.5 shard_map.173
  53.8 1.6 %collective-permute-start = (f32[16,1,128]{2,1,0:T(1,128)S(1)}, f32[16,1,128]{2,1,0:T(1,128)S(1)}, u32[]{:S(2)}, u32[]{:S(2)}) collective-permute-start(f32[16,1,128]{2,1,0:T(1,128)S(1)} %get-tuple-element.46.refs_0_), channel_id=1, source_target_pairs={{0,16},{16,0},{1,17},{17,1},{2,18},{18,2},{3,19},{19,3},{4,20},{20... | collective-permute-start | bytes 24584 | tf_op jit(solution)/shard_map/ppermute | solution.py:522
  55.4 8.4 %shard_map.174 = (bf16[2048,2048]{1,0:T(8,128)(2,1)}, bf16[2048,2048]{1,0:T(8,128)(2,1)S(1)}) custom-call(bf16[2048,2048]{1,0:T(8,128)(2,1)} %get-tuple-element.33.base, bf16[16,96,128]{2,1,0:T(8,128)(2,1)S(1)} %get-tuple-element.43.hidden_kept, bf16[96,2048]{1,0:T(8,128)(2,1)S(1)} %get-tuple-element.44.onehot), custom_call_target="tpu_custom_call" | custom-call | flops 805306368 | bytes 16777216 | tf_op jit(solution)/shard_map/pallas_call | solution.py:386
  63.8 0.0 collective-permute-done.refs_1_
  63.8 0.0 copy-done.1
  63.8 4.4 %shard_map.175 = bf16[2048,2048]{1,0:T(8,128)(2,1)} custom-call(f32[16,1,128]{2,1,0:T(1,128)S(1)} %get-tuple-element.46.refs_0_, f32[16,1,128]{2,1,0:T(1,128)S(1)} %collective-permute-done.refs_1_, bf16[2048,2048]{1,0:T(8,128)(2,1)S(1)} %get-tuple-element.47.refs_2_, f32[1,2048]{1,0:T(1,128)S(1)} %bitcast.6), custom_call_target="tpu_custom_call" | custom-call | flops 16777216 | bytes 16777216 | tf_op jit(solution)/shard_map/pallas_call | solution.py:386
Async XLA Ops:
  0.6 15.9 %copy-start = (f32[2048]{0:T(1024)S(1)}, f32[2048]{0:T(1024)}, u32[]{:S(2)}) copy-start(f32[2048]{0:T(1024)} %param.23) | copy-start | bytes 24580
  9.1 19.9 %all-to-all-start = ((bf16[16,16,768]{2,1,0:T(8,128)(2,1)}), bf16[16,16,768]{2,1,0:T(8,128)(2,1)S(1)}, u32[]{:S(2)}, u32[]{:S(2)}) async-start(bf16[16,16,768]{2,1,0:T(8,128)(2,1)} %get-tuple-element.25), calls=%async_computation | async-start | bytes 786432 | tf_op jit(solution)/shard_map/all_to_all | solution.py:440
  16.9 9.4 %copy-start.2 = (bf16[1,1,6,32768]{3,2,1,0:T(8,128)(2,1)S(1)}, bf16[1,1,6,32768]{3,2,1,0:T(8,128)(2,1)}, u32[]{:S(2)}) copy-start(bf16[1,1,6,32768]{3,2,1,0:T(8,128)(2,1)} %param.20) | copy-start | bytes 1179652
  16.9 9.4 %copy-start.3 = (bf16[1024,256]{1,0:T(8,128)(2,1)S(1)}, bf16[1024,256]{1,0:T(8,128)(2,1)}, u32[]{:S(2)}) copy-start(bf16[1024,256]{1,0:T(8,128)(2,1)} %constant.10.clone.inner.inner_far) | copy-start | bytes 1572868
  16.9 9.4 %copy-start.4 = (bf16[512,512]{1,0:T(8,128)(2,1)S(1)}, bf16[512,512]{1,0:T(8,128)(2,1)}, u32[]{:S(2)}) copy-start(bf16[512,512]{1,0:T(8,128)(2,1)} %constant.8.clone.outer_fwd.outer_fwd_far) | copy-start | bytes 1572868
  16.9 9.4 %copy-start.5 = (f32[256,256]{1,0:T(8,128)S(1)}, f32[256,256]{1,0:T(8,128)}, u32[]{:S(2)}) copy-start(f32[256,256]{1,0:T(8,128)} %constant.9.clone.turn.turn_far) | copy-start | bytes 786436
  27.8 1.1 %copy-start.6 = (f32[6,256,256]{2,1,0:T(8,128)}, f32[6,256,256]{2,1,0:T(8,128)S(1)}, u32[]{:S(2)}) copy-start(f32[6,256,256]{2,1,0:T(8,128)S(1)} %shard_map.168.spectra_far) | copy-start | bytes 4718596
  29.0 0.8 %copy-start.7 = (bf16[16,16,768]{2,1,0:T(8,128)(2,1)}, bf16[16,16,768]{2,1,0:T(8,128)(2,1)S(1)}, u32[]{:S(2)}) copy-start(bf16[16,16,768]{2,1,0:T(8,128)(2,1)S(1)} %all-to-all-done.signals_far) | copy-start | bytes 1179652
  35.1 18.2 %all-to-all-start.1 = ((bf16[16,16,768]{2,1,0:T(8,128)(2,1)}), bf16[16,16,768]{2,1,0:T(8,128)(2,1)S(1)}, u32[]{:S(2)}, u32[]{:S(2)}) async-start(bf16[16,16,768]{2,1,0:T(8,128)(2,1)} %shard_map.171), calls=%async_computation.1 | async-start | bytes 786432 | tf_op jit(solution)/shard_map/all_to_all | solution.py:506
  49.9 13.9 %copy-start.1 = (f32[2048]{0:T(1024)S(1)}, f32[2048]{0:T(1024)}, u32[]{:S(2)}) copy-start(f32[2048]{0:T(1024)} %param.24) | copy-start | bytes 24580
  53.8 9.9 %collective-permute-start = (f32[16,1,128]{2,1,0:T(1,128)S(1)}, f32[16,1,128]{2,1,0:T(1,128)S(1)}, u32[]{:S(2)}, u32[]{:S(2)}) collective-permute-start(f32[16,1,128]{2,1,0:T(1,128)S(1)} %get-tuple-element.46.refs_0_), channel_id=1, source_target_pairs={{0,16},{16,0},{1,17},{17,1},{2,18},{18,2},{3,19},{19,3},{4,20},{20... | collective-permute-start | bytes 24584 | tf_op jit(solution)/shard_map/ppermute | solution.py:522

commit v5 on v4

--- a/solution.py
+++ b/solution.py
@@ -12,7 +12,7 @@
 TILE = 256
 CHUNK = 16
 AHEAD = 3
-HALVES = 2
+EARLY = 7
 MIB = 1 << 20
 norm_eps = 1e-06
 f32 = jnp.float32
@@ -106,34 +106,33 @@
 
 
 def convolve_kernel(
-    signals_far, outer_fwd_far, turn_far, inner_far, spectra_far, outer_back_far, out, *scratch
+    signals, outer_fwd_far, turn_far, inner_far, spectra_far, outer_back_far, out, *scratch
 ):
-    sources = (signals_far, outer_fwd_far, turn_far, inner_far, spectra_far, outer_back_far)
-    signals, outer_fwd, turn_ref, inner, spectra, outer_back, sems = scratch
+    sources = (outer_fwd_far, turn_far, inner_far, spectra_far, outer_back_far)
+    outer_fwd, turn_ref, inner, spectra, outer_back, sems = scratch
     copies = [
         pltpu.make_async_copy(source, scratch[n], sems.at[n]) for n, source in enumerate(sources)
     ]
-    for copy in copies[:4]:
+    for copy in copies[:3]:
         copy.start()
     slots, outer = spectra.shape[:2]
 
     def turn_now():
+        copies[1].wait()
+        return turn_ref[...]
+
+    def inner_now():
         copies[2].wait()
-        return turn_ref[...]
-
-    def inner_now():
-        copies[3].wait()
         return inner[: 4 * LANES, :]
 
     copies[0].wait()
-    copies[1].wait()
-    for copy in copies[4:]:
+    for copy in copies[3:]:
         copy.start()
     blocks = signals[...].reshape(outer, slots * LANES)
     parts = to_spectrum(blocks, slots, outer_fwd[...], turn_now, inner_now)
     turn = turn_ref[...]
     cos, sin = turn[:, :LANES], turn[:, LANES:]
-    copies[4].wait()
+    copies[3].wait()
     turned = []
     for s in range(slots):
         sig_re, sig_im = parts[s][:, :LANES], parts[s][:, LANES:]
@@ -144,7 +143,7 @@
         back = times_table(joint, inner[4 * LANES :, :])
         re, im = back[:, :LANES], back[:, LANES:]
         turned.append(jnp.concatenate([re * cos - im * sin, im * cos + re * sin], axis=0))
-    copies[5].wait()
+    copies[4].wait()
     for s in range(0, slots, 2):
         pair = turned[s : s + 2]
         causal = table_times(outer_back[...], jnp.concatenate(pair, axis=1)).astype(bf16)
@@ -211,8 +210,8 @@
 
 
 def pick_kernel(owner_count, slots, index, owners, gate, value, *refs):
-    payload, picked, channels, onehot_t = refs[:4]
-    acc, gate_stage, value_stage, lists, list_sems, sems = refs[4:]
+    payload, channels, onehot_far = refs[:3]
+    acc, gate_stage, value_stage, onehot_t, lists, list_sems, sems = refs[3:]
     rows = owner_count * slots
     tile = gate_stage.shape[0] // sems.shape[1]
     list_copies = [
@@ -227,19 +226,21 @@
     row = channel_of_row(lists[0], lists[1], owner_count, onehot_t.shape[1])
     channels[...] = jnp.broadcast_to(row, channels.shape)
     onehot_t[...] = (iota(onehot_t.shape, 0) == row).astype(f32).astype(bf16)
+    onehot_copy = pltpu.make_async_copy(onehot_t, onehot_far, list_sems.at[2])
+    onehot_copy.start()
 
     def step(i, _):
         at = pl.ds(wait(i), tile)
         gated = gate_stage[at, :] * value_stage[at, :]
         for n, block in enumerate(pick_rows(gated, onehot_t[...], rows)):
             acc[i * (tile // LANES) + n] = block
-            picked[i * (tile // LANES) + n] = block.astype(bf16)
         return 0
 
     lax.fori_loop(0, count, step, 0)
     for s in range(slots):
         part = jnp.swapaxes(acc[:, s * owner_count : (s + 1) * owner_count, :], 0, 1)
         payload[:, :, s * LANES : (s + 1) * LANES] = part.astype(bf16)
+    onehot_copy.wait()
 
 
 def place_kernel(channels, skip, onehot, others, skip_wide):
@@ -297,40 +298,47 @@
     lax.fori_loop(0, count, lambda i, _: (copy(i).wait(), 0)[1], 0)
 
 
-def kept_kernel(halves, conv, picked, skip_wide, *refs):
+def kept_kernel(conv, payload, skip_wide, *refs):
     hidden, totals = refs[-2:]
     owner_count, blocks = conv.shape[:2]
-    size = blocks // halves
-    for h in range(halves):
-        sums, picked_gate, picked_res = refs[3 * h : 3 * h + 3]
-        at_h = slice(h * size, (h + 1) * size)
+    first = 0
+    for n in range(0, len(refs) - 2, 3):
+        sums, picked_gate, picked_res = refs[n : n + 3]
+        size = sums.shape[0]
+        at_h = slice(first, first + size)
         total = jnp.zeros((size, LANES), f32)
         for s in range(conv.shape[2] // LANES):
             at = slice(s * owner_count, (s + 1) * owner_count)
-            conv_rows = conv[:, at_h, s * LANES : (s + 1) * LANES].astype(f32)
-            conv_rows = jnp.swapaxes(conv_rows, 0, 1)
-            wide = conv_rows + skip_wide[at, :] * picked[at_h, at, :].astype(f32)
+            lanes = slice(s * LANES, (s + 1) * LANES)
+            gated = jnp.swapaxes(payload[:, at_h, lanes].astype(f32), 0, 1)
+            wide = jnp.swapaxes(conv[:, at_h, lanes].astype(f32), 0, 1)
+            wide = wide + skip_wide[at, :] * gated
             value = picked_res[:, at, :].astype(f32) + picked_gate[:, at, :].astype(f32) * wide
             value = value.astype(bf16)
             hidden[at_h, at, :] = value
             value = value.astype(f32)
             total = total + jnp.sum(value * value, axis=1)
         for i in range(size):
-            totals[h * size + i] = total[i : i + 1, :] + sums[i]
+            totals[first + i] = total[i : i + 1, :] + sums[i]
+        first = first + size
 
 
 def hidden_kernel(base, hidden_kept, onehot, hidden, held, base_stage, base_sems, sems):
     slab = held.shape[1]
     wide = min(slab, 2 * LANES)
-    wait, count = fetch((base,), (base_stage,), base_sems, LANES)
+    count = sems.shape[0]
+    tile = held.shape[0] // count
+    wait, _ = fetch((base,), (base_stage,), base_sems, tile)
 
     def copy(i):
-        rows = pl.ds(pl.multiple_of(i * LANES, LANES), LANES)
+        rows = pl.ds(pl.multiple_of(i * tile, tile), tile)
         return pltpu.make_async_copy(held.at[rows, :], hidden.at[rows, :], sems.at[i])
 
     def step(i, _):
-        kept = hidden_kept[i].astype(f32).T.astype(bf16)
-        rows = pl.ds(wait(i), LANES)
+        blocks = range(tile // LANES)
+        kept = [hidden_kept[i * (tile // LANES) + n].astype(f32).T.astype(bf16) for n in blocks]
+        kept = jnp.concatenate(kept, axis=0)
+        rows = pl.ds(wait(i), tile)
         for j in range(0, slab, wide):
             lanes = slice(j, j + wide)
             placed = dot(kept, onehot[:, lanes]).astype(bf16)
@@ -419,9 +427,13 @@
     buffer = (owner_count, blocks, slots * LANES)
     whole = (tok_rows, slab)
 
-    payload, picked, channels, onehot_t = call(
+    payload, channels, onehot_t = call(
         functools.partial(pick_kernel, owner_count, slots),
-        [sds(buffer, bf16), picks, sds((8, lanes_rows), jnp.int32), sds((slab, lanes_rows), bf16)],
+        [
+            sds(buffer, bf16),
+            sds((8, lanes_rows), jnp.int32),
+            pltpu.HBM((slab, lanes_rows), bf16),
+        ],
         [in_hbm(kept_index), in_hbm(kept_owner), gate_in, value_in],
         2 * tok_rows * slab * rows,
         2 * dense,
@@ -430,18 +442,20 @@
             pltpu.VMEM((blocks, rows, LANES), f32),
             pltpu.VMEM(whole, bf16),
             pltpu.VMEM(whole, bf16),
+            pltpu.VMEM((slab, lanes_rows), bf16),
             pltpu.VMEM((2,) + kept_index.shape, jnp.int32),
-            pltpu.SemaphoreType.DMA((2,)),
+            pltpu.SemaphoreType.DMA((3,)),
             pltpu.SemaphoreType.DMA((2, tok_rows // tile)),
         ],
         far=(0, 1, 2, 3),
+        far_outs=(2,),
     )
 
     incoming = lax.all_to_all(payload, ("seqo", "seqi"), split_axis=0, concat_axis=0, tiled=True)
 
     (spectra,) = call(
         filter_kernel,
-        [sds((slots, outer, 2 * LANES), f32)],
+        [pltpu.HBM((slots, outer, 2 * LANES), f32)],
         [filters[0, 0]] + [jnp.asarray(x) for x in dft_tables(length)[:3]],
         2 * slots * length * 2 * (2 * outer + 6 * LANES),
         8 * MIB,
@@ -456,9 +470,8 @@
         8 * MIB,
     )
 
-    def base_half(h, onehot_t, base):
-        part = tok_rows // HALVES
-        count = part // LANES
+    def base_part(first, count, onehot_t, base):
+        part = count * LANES
         ins = [onehot_t, others, skip_row, gate_in, value_in, out_gate, residual]
         outs = [
             pltpu.HBM(whole, bf16),
@@ -469,11 +482,11 @@
         if base is not None:
             ins.append(base)
         return call(
-            functools.partial(base_kernel, h * part),
+            functools.partial(base_kernel, first * LANES),
             outs,
             ins,
-            4 * tok_rows * slab * rows // HALVES,
-            5 * dense // HALVES,
+            4 * part * slab * rows,
+            10 * part * slab,
             24 * MIB,
             scratch=[pltpu.VMEM((part, slab), bf16)] * 5
             + [
@@ -486,10 +499,11 @@
             alias={} if base is None else {7: 0},
         )
 
-    base, *half_picks = base_half(0, onehot_t, None)
+    early = max(1, blocks * EARLY // 16)
+    base, *half_picks = base_part(0, early, onehot_t, None)
     spectra, base = lax.optimization_barrier((spectra, base))
 
-    conv_ins = [in_hbm(incoming), outer_fwd, turn, inner, in_hbm(spectra), outer_back]
+    conv_ins = [incoming, outer_fwd, turn, inner, in_hbm(spectra), outer_back]
     (convolved,) = call(
         convolve_kernel,
         [sds(buffer, bf16)],
@@ -497,20 +511,20 @@
         2 * slots * length * 2 * (5 * outer + 12 * LANES),
         8 * MIB,
         20 * MIB,
-        scratch=[pltpu.VMEM(x.shape, x.dtype) for x in conv_ins]
-        + [pltpu.SemaphoreType.DMA((len(conv_ins),))],
-        far=tuple(range(len(conv_ins))),
+        scratch=[pltpu.VMEM(x.shape, x.dtype) for x in conv_ins[1:]]
+        + [pltpu.SemaphoreType.DMA((len(conv_ins) - 1,))],
+        far=tuple(range(1, len(conv_ins))),
     )
     convolved, onehot_t = lax.optimization_barrier((convolved, onehot_t))
 
     returned = lax.all_to_all(convolved, ("seqo", "seqi"), split_axis=0, concat_axis=0, tiled=True)
 
-    base, *more_picks = base_half(1, onehot_t, base)
+    base, *more_picks = base_part(early, blocks - early, onehot_t, base)
 
     hidden_kept, totals = call(
-        functools.partial(kept_kernel, HALVES),
+        kept_kernel,
         [picks, row_sums],
-        [returned, picked, skip_wide, *half_picks, *more_picks],
+        [returned, payload, skip_wide, *half_picks, *more_picks],
         8 * rows * tok_rows,
         10 * rows * tok_rows,
         16 * MIB,
@@ -530,8 +544,8 @@
         16 * MIB,
         scratch=[
             pltpu.VMEM(whole, bf16),
-            pltpu.SemaphoreType.DMA((1, blocks)),
-            pltpu.SemaphoreType.DMA((blocks,)),
+            pltpu.SemaphoreType.DMA((1, tok_rows // tile)),
+            pltpu.SemaphoreType.DMA((tok_rows // tile,)),
         ],
         far=(0,),
         far_outs=(0,),

time: 68.7 us -> 68.6 us (level)
  Pallas kernels: 47.1 us -> 48.7 us
  local copies, waits for them, and re-layouts: 1.92 us -> 1.08 us
  waiting for transfers between devices: 3.4 us -> 2.56 us
    pallas_call x9, Pallas kernels: 47.1 us -> 48.7 us  [call(): pl.pallas_call(kernel, out_shape=outs, in_specs=[away if n in far else ne...]
    unnamed x16, local copies, waits for them, and re-layouts: 1.92 us -> 1.08 us
    all_to_all x1, waiting for transfers between devices: 3.39 us -> 2.56 us  [local(): lax.all_to_all(convolved, ('seqo', 'seqi'), split_axis=0, concat_axis=0,...]
where the time goes in v5:
time: 68.6 us; the launch traced here: 68.1 us
  Pallas kernels  48.7 us (71%)
  starting transfers between devices  15 us (22%)
  waiting for transfers between devices  2.56 us (4%)
  local copies, waits for them, and re-layouts  1.08 us (2%)
  between operations  0.78 us (1%)
    pallas_call x9, Pallas kernels, call(): pl.pallas_call(kernel, out_shape=outs, in_specs=[away if n in far else ne...  48.7 us
    all_to_all x1, starting transfers between devices, local(): lax.all_to_all(payload, ('seqo', 'seqi'), split_axis=0, concat_axis=0, ti...  7.37 us
    all_to_all x1, starting transfers between devices, local(): lax.all_to_all(convolved, ('seqo', 'seqi'), split_axis=0, concat_axis=0,...  6.03 us
    all_to_all x1, waiting for transfers between devices, local(): lax.all_to_all(convolved, ('seqo', 'seqi'), split_axis=0, concat_axis=0,...  2.56 us
    ppermute x1, starting transfers between devices, local(): parts.append(lax.ppermute(totals, 'chan', ring))  1.58 us
  transfers between devices with their start and end apart: 3, of which 1 were waited for; matrix products, arithmetic and copies ran while one was open for 0% of the time, Pallas kernels for 42%

profile of v5, /device:TPU:0, one launch (start us, length us, event | category | flops | bytes accessed | tf_op | source)
XLA Modules:
  0.0 68.1 jit_solution(5206997104980182671)
XLA Ops:
  0.6 0.0 copy-start.2
  0.6 8.6 %shard_map.167 = (bf16[16,16,768]{2,1,0:T(8,128)(2,1)}, s32[8,128]{1,0:T(8,128)S(1)}, bf16[2048,128]{1,0:T(8,128)(2,1)}) custom-call(s32[1,64]{1,0:T(1,128)} %index.1, s32[1,64]{1,0:T(1,128)} %owners.1, bf16[2048,2048]{1,0:T(8,128)(2,1)} %gate.5, bf16[2048,2048]{1,0:T(8,128)(2,1)} %value.5), custom_call_target="tpu_custom_call" | custom-call | flops 805306368 | bytes 16777216 | tf_op jit(solution)/shard_map/pallas_call | solution.py:394
  9.3 7.4 %all-to-all-start = ((bf16[16,16,768]{2,1,0:T(8,128)(2,1)}), bf16[16,16,768]{2,1,0:T(8,128)(2,1)S(1)}, u32[]{:S(2)}, u32[]{:S(2)}) async-start(bf16[16,16,768]{2,1,0:T(8,128)(2,1)} %get-tuple-element.24.payload), calls=%async_computation | async-start | bytes 786432 | tf_op jit(solution)/shard_map/all_to_all | solution.py:454
  16.7 0.0 copy-done.2
  16.7 0.4 shard_map.169
  17.1 0.0 copy-start
  17.1 1.0 %copy-done = bf16[2048,128]{1,0:T(8,128)(2,1)S(1)} copy-done((bf16[2048,128]{1,0:T(8,128)(2,1)S(1)}, bf16[2048,128]{1,0:T(8,128)(2,1)}, u32[]{:S(2)}) %copy-start) | copy-done | bytes 524312
  18.1 0.0 copy-start.4
  18.1 0.0 copy-start.5
  18.1 0.0 copy-start.6
  18.1 0.0 copy-start.7
  18.1 8.6 %shard_map.170 = (bf16[2048,2048]{1,0:T(8,128)(2,1)}, f32[7,1,128]{2,1,0:T(1,128)S(1)}, bf16[7,96,128]{2,1,0:T(8,128)(2,1)S(1)}, bf16[7,96,128]{2,1,0:T(8,128)(2,1)S(1)}) custom-call(bf16[2048,128]{1,0:T(8,128)(2,1)S(1)} %copy-done, f32[8,2048]{1,0:T(8,128)S(1)} %get-tuple-element.27.others, f32[1,2048]{1,0:T(1,128)S(1)} %bitcast.4, ...), custom_call_target="tpu_custom_call" | custom-call | flops 704643072 | bytes 18350080 | tf_op jit(solution)/shard_map/pallas_call | solution.py:394
  26.7 0.0 copy-start.1
  26.7 0.0 copy-done.4
  26.7 0.0 copy-done.5
  26.7 0.0 copy-done.6
  26.7 0.0 copy-done.7
  26.7 2.7 %shard_map.168.spectra_far = f32[6,256,256]{2,1,0:T(8,128)} custom-call(bf16[6,32768]{1,0:T(8,128)(2,1)S(1)} %bitcast.7, bf16[512,512]{1,0:T(8,128)(2,1)S(1)} %copy-done.6, f32[256,256]{1,0:T(8,128)S(1)} %copy-done.7, bf16[1024,256]{1,0:T(8,128)(2,1)S(1)} %copy-done.5), custom_call_target="tpu_custom_call" | custom-call | flops 1006632960 | bytes 8388608 | tf_op jit(solution)/shard_map/pallas_call | solution.py:394
  29.4 0.0 all-to-all-done.signals
  29.5 5.3 %shard_map.171 = bf16[16,16,768]{2,1,0:T(8,128)(2,1)} custom-call(bf16[16,16,768]{2,1,0:T(8,128)(2,1)S(1)} %all-to-all-done.signals, bf16[512,512]{1,0:T(8,128)(2,1)} %constant.8.clone.outer_fwd.outer_fwd_far, f32[256,256]{1,0:T(8,128)} %constant.9.clone.turn.turn_far, bf16[1024,256]{1,0:T(8,128)(2,1)} %constant.10.clone.inner.inner_far, ...), custom_call_target="tpu_custom_call" | custom-call | flops 2214592512 | bytes 8388608 | tf_op jit(solution)/shard_map/pallas_call | solution.py:394
  34.7 6.0 %all-to-all-start.1 = ((bf16[16,16,768]{2,1,0:T(8,128)(2,1)}), bf16[16,16,768]{2,1,0:T(8,128)(2,1)S(1)}, u32[]{:S(2)}, u32[]{:S(2)}) async-start(bf16[16,16,768]{2,1,0:T(8,128)(2,1)} %shard_map.171), calls=%async_computation.1 | async-start | bytes 786432 | tf_op jit(solution)/shard_map/all_to_all | solution.py:520
  40.7 0.0 copy-done.1
  40.8 9.6 %shard_map.172 = (bf16[2048,2048]{1,0:T(8,128)(2,1)}, f32[9,1,128]{2,1,0:T(1,128)S(1)}, bf16[9,96,128]{2,1,0:T(8,128)(2,1)S(1)}, bf16[9,96,128]{2,1,0:T(8,128)(2,1)S(1)}) custom-call(bf16[2048,128]{1,0:T(8,128)(2,1)S(1)} %copy-done.1, f32[8,2048]{1,0:T(8,128)S(1)} %get-tuple-element.27.others, ...), custom_call_target="tpu_custom_call", output_to_operand_aliasing={{0}: (7, {})} | custom-call | flops 905969664 | bytes 23592960 | tf_op jit(solution)/shard_map/pallas_call | solution.py:394
  50.4 0.0 copy-start.3
  50.4 2.6 %all-to-all-done.1.conv = bf16[16,16,768]{2,1,0:T(8,128)(2,1)S(1)} async-done(((bf16[16,16,768]{2,1,0:T(8,128)(2,1)}), bf16[16,16,768]{2,1,0:T(8,128)(2,1)S(1)}, u32[]{:S(2)}, u32[]{:S(2)}) %all-to-all-start.1) | async-done | bytes 393248 | tf_op jit(solution)/shard_map/all_to_all | solution.py:520
  52.9 1.8 %shard_map.173 = (bf16[16,96,128]{2,1,0:T(8,128)(2,1)S(1)}, f32[16,1,128]{2,1,0:T(1,128)S(1)}) custom-call(bf16[16,16,768]{2,1,0:T(8,128)(2,1)S(1)} %all-to-all-done.1.conv, bf16[16,16,768]{2,1,0:T(8,128)(2,1)} %get-tuple-element.24.payload, f32[96,128]{1,0:T(8,128)S(1)} %get-tuple-element.34.skip_wide, f32[7,1,128]{2,1,0:T(1,128)S(1)} %get-tuple-element.35.refs_0_, ...), custom_call_target="tpu_custom_call" | custom-call | flops 1572864 | bytes 1966080 | tf_op jit(solution)/shard_map/pallas_call | solution.py:394
  54.7 1.6 %collective-permute-start = (f32[16,1,128]{2,1,0:T(1,128)S(1)}, f32[16,1,128]{2,1,0:T(1,128)S(1)}, u32[]{:S(2)}, u32[]{:S(2)}) collective-permute-start(f32[16,1,128]{2,1,0:T(1,128)S(1)} %get-tuple-element.44.refs_0_), channel_id=1, source_target_pairs={{0,16},{16,0},{1,17},{17,1},{2,18},{18,2},{3,19},{19,3},{4,20},{20... | collective-permute-start | bytes 24584 | tf_op jit(solution)/shard_map/ppermute | solution.py:536
  56.3 7.4 %shard_map.174 = (bf16[2048,2048]{1,0:T(8,128)(2,1)}, bf16[2048,2048]{1,0:T(8,128)(2,1)S(1)}) custom-call(bf16[2048,2048]{1,0:T(8,128)(2,1)} %get-tuple-element.32.base, bf16[16,96,128]{2,1,0:T(8,128)(2,1)S(1)} %get-tuple-element.41.hidden_kept, bf16[96,2048]{1,0:T(8,128)(2,1)S(1)} %get-tuple-element.42.onehot), custom_call_target="tpu_custom_call" | custom-call | flops 805306368 | bytes 16777216 | tf_op jit(solution)/shard_map/pallas_call | solution.py:394
  63.7 0.0 collective-permute-done.refs_1_
  63.7 0.0 copy-done.3
  63.7 4.4 %shard_map.175 = bf16[2048,2048]{1,0:T(8,128)(2,1)} custom-call(f32[16,1,128]{2,1,0:T(1,128)S(1)} %get-tuple-element.44.refs_0_, f32[16,1,128]{2,1,0:T(1,128)S(1)} %collective-permute-done.refs_1_, bf16[2048,2048]{1,0:T(8,128)(2,1)S(1)} %get-tuple-element.45.refs_2_, f32[1,2048]{1,0:T(1,128)S(1)} %bitcast.6), custom_call_target="tpu_custom_call" | custom-call | flops 16777216 | bytes 16777216 | tf_op jit(solution)/shard_map/pallas_call | solution.py:394
Async XLA Ops:
  0.6 16.0 %copy-start.2 = (f32[2048]{0:T(1024)S(1)}, f32[2048]{0:T(1024)}, u32[]{:S(2)}) copy-start(f32[2048]{0:T(1024)} %param.23) | copy-start | bytes 24580
  9.3 20.2 %all-to-all-start = ((bf16[16,16,768]{2,1,0:T(8,128)(2,1)}), bf16[16,16,768]{2,1,0:T(8,128)(2,1)S(1)}, u32[]{:S(2)}, u32[]{:S(2)}) async-start(bf16[16,16,768]{2,1,0:T(8,128)(2,1)} %get-tuple-element.24.payload), calls=%async_computation | async-start | bytes 786432 | tf_op jit(solution)/shard_map/all_to_all | solution.py:454
  17.1 1.0 %copy-start = (bf16[2048,128]{1,0:T(8,128)(2,1)S(1)}, bf16[2048,128]{1,0:T(8,128)(2,1)}, u32[]{:S(2)}) copy-start(bf16[2048,128]{1,0:T(8,128)(2,1)} %get-tuple-element.30.onehot_t) | copy-start | bytes 1572868
  18.1 8.6 %copy-start.4 = (bf16[1,1,6,32768]{3,2,1,0:T(8,128)(2,1)S(1)}, bf16[1,1,6,32768]{3,2,1,0:T(8,128)(2,1)}, u32[]{:S(2)}) copy-start(bf16[1,1,6,32768]{3,2,1,0:T(8,128)(2,1)} %param.20) | copy-start | bytes 1179652
  18.1 8.6 %copy-start.5 = (bf16[1024,256]{1,0:T(8,128)(2,1)S(1)}, bf16[1024,256]{1,0:T(8,128)(2,1)}, u32[]{:S(2)}) copy-start(bf16[1024,256]{1,0:T(8,128)(2,1)} %constant.10.clone.inner.inner_far) | copy-start | bytes 1572868
  18.1 8.6 %copy-start.6 = (bf16[512,512]{1,0:T(8,128)(2,1)S(1)}, bf16[512,512]{1,0:T(8,128)(2,1)}, u32[]{:S(2)}) copy-start(bf16[512,512]{1,0:T(8,128)(2,1)} %constant.8.clone.outer_fwd.outer_fwd_far) | copy-start | bytes 1572868
  18.1 8.6 %copy-start.7 = (f32[256,256]{1,0:T(8,128)S(1)}, f32[256,256]{1,0:T(8,128)}, u32[]{:S(2)}) copy-start(f32[256,256]{1,0:T(8,128)} %constant.9.clone.turn.turn_far) | copy-start | bytes 786436
  26.7 14.1 %copy-start.1 = (bf16[2048,128]{1,0:T(8,128)(2,1)S(1)}, bf16[2048,128]{1,0:T(8,128)(2,1)}, u32[]{:S(2)}) copy-start(bf16[2048,128]{1,0:T(8,128)(2,1)} %get-tuple-element.30.onehot_t) | copy-start | bytes 1572868
  34.7 18.2 %all-to-all-start.1 = ((bf16[16,16,768]{2,1,0:T(8,128)(2,1)}), bf16[16,16,768]{2,1,0:T(8,128)(2,1)S(1)}, u32[]{:S(2)}, u32[]{:S(2)}) async-start(bf16[16,16,768]{2,1,0:T(8,128)(2,1)} %shard_map.171), calls=%async_computation.1 | async-start | bytes 786432 | tf_op jit(solution)/shard_map/all_to_all | solution.py:520
  50.4 13.3 %copy-start.3 = (f32[2048]{0:T(1024)S(1)}, f32[2048]{0:T(1024)}, u32[]{:S(2)}) copy-start(f32[2048]{0:T(1024)} %param.24) | copy-start | bytes 24580
  54.7 8.9 %collective-permute-start = (f32[16,1,128]{2,1,0:T(1,128)S(1)}, f32[16,1,128]{2,1,0:T(1,128)S(1)}, u32[]{:S(2)}, u32[]{:S(2)}) collective-permute-start(f32[16,1,128]{2,1,0:T(1,128)S(1)} %get-tuple-element.44.refs_0_), channel_id=1, source_target_pairs={{0,16},{16,0},{1,17},{17,1},{2,18},{18,2},{3,19},{19,3},{4,20},{20... | collective-permute-start | bytes 24584 | tf_op jit(solution)/shard_map/ppermute | solution.py:536

commit v6 on v5

--- a/solution.py
+++ b/solution.py
@@ -11,6 +11,7 @@
 LANES = 128
 TILE = 256
 CHUNK = 16
+GROUP = 3
 AHEAD = 3
 EARLY = 7
 MIB = 1 << 20
@@ -83,33 +84,40 @@
     first = dot(outer_fwd, jnp.concatenate([blocks, blocks], axis=0))
     turn, inner_fwd = turn(), inner_fwd()
     cos, sin = turn[:, :LANES], turn[:, LANES:]
-    result = []
+    turned = []
     for s in range(slots):
         re = first[:outer, s * LANES : (s + 1) * LANES]
         im = first[outer:, s * LANES : (s + 1) * LANES]
-        turned = jnp.concatenate([re * cos + im * sin, im * cos - re * sin], axis=1)
-        result.append(times_table(turned, inner_fwd))
+        turned.append(jnp.concatenate([re * cos + im * sin, im * cos - re * sin], axis=1))
+    return grouped(turned, inner_fwd)
+
+
+def grouped(values, table):
+    result = []
+    for s in range(0, len(values), GROUP):
+        part = values[s : s + GROUP]
+        size = part[0].shape[0]
+        product = times_table(jnp.concatenate(part, axis=0), table)
+        result += [product[n * size : (n + 1) * size] for n in range(len(part))]
     return result
 
 
-def filter_kernel(filters, outer_fwd, turn, inner, spectra):
+def filter_spectra(filters, outer_fwd, turn, inner):
     slots, length = filters.shape
     outer = length // LANES
     wide = filters[...].astype(f32)
     blocks = [wide[s].reshape(outer, LANES) for s in range(slots)]
     blocks = jnp.concatenate(blocks, axis=1).astype(bf16)
-    parts = to_spectrum(
+    return to_spectrum(
         blocks, slots, outer_fwd[...], lambda: turn[...], lambda: inner[: 4 * LANES, :]
     )
-    for s in range(slots):
-        spectra[s] = parts[s]
 
 
 def convolve_kernel(
     signals, outer_fwd_far, turn_far, inner_far, spectra_far, outer_back_far, out, *scratch
 ):
     sources = (outer_fwd_far, turn_far, inner_far, spectra_far, outer_back_far)
-    outer_fwd, turn_ref, inner, spectra, outer_back, sems = scratch
+    outer_fwd, turn_ref, inner, spectra, outer_back, result, sems = scratch
     copies = [
         pltpu.make_async_copy(source, scratch[n], sems.at[n]) for n, source in enumerate(sources)
     ]
@@ -133,22 +141,34 @@
     turn = turn_ref[...]
     cos, sin = turn[:, :LANES], turn[:, LANES:]
     copies[3].wait()
-    turned = []
+    joint = []
     for s in range(slots):
         sig_re, sig_im = parts[s][:, :LANES], parts[s][:, LANES:]
         ker_re, ker_im = spectra[s, :, :LANES], spectra[s, :, LANES:]
-        joint = jnp.concatenate(
-            [sig_re * ker_re - sig_im * ker_im, sig_re * ker_im + sig_im * ker_re], axis=1
+        joint.append(
+            jnp.concatenate(
+                [sig_re * ker_re - sig_im * ker_im, sig_re * ker_im + sig_im * ker_re], axis=1
+            )
         )
-        back = times_table(joint, inner[4 * LANES :, :])
+    turned = []
+    for back in grouped(joint, inner[4 * LANES :, :]):
         re, im = back[:, :LANES], back[:, LANES:]
         turned.append(jnp.concatenate([re * cos - im * sin, im * cos + re * sin], axis=0))
     copies[4].wait()
+    sends = []
     for s in range(0, slots, 2):
         pair = turned[s : s + 2]
         causal = table_times(outer_back[...], jnp.concatenate(pair, axis=1)).astype(bf16)
-        lanes = slice(s * LANES, (s + len(pair)) * LANES)
-        out[:, :, lanes] = causal.reshape(out.shape[:2] + (len(pair) * LANES,))
+        lanes = pl.ds(s * LANES, len(pair) * LANES)
+        result[:, :, lanes] = causal.reshape(out.shape[:2] + (len(pair) * LANES,))
+        sends.append(
+            pltpu.make_async_copy(
+                result.at[:, :, lanes], out.at[:, :, lanes], sems.at[len(copies) + len(sends)]
+            )
+        )
+        sends[-1].start()
+    for send in sends:
+        send.wait()
 
 
 def iota(shape, axis):
@@ -210,8 +230,8 @@
 
 
 def pick_kernel(owner_count, slots, index, owners, gate, value, *refs):
-    payload, channels, onehot_far = refs[:3]
-    acc, gate_stage, value_stage, onehot_t, lists, list_sems, sems = refs[3:]
+    payload, picked, channels, onehot_far = refs[:4]
+    acc, gate_stage, value_stage, onehot_t, lists, list_sems, sems = refs[4:]
     rows = owner_count * slots
     tile = gate_stage.shape[0] // sems.shape[1]
     list_copies = [
@@ -234,6 +254,7 @@
         gated = gate_stage[at, :] * value_stage[at, :]
         for n, block in enumerate(pick_rows(gated, onehot_t[...], rows)):
             acc[i * (tile // LANES) + n] = block
+            picked[i * (tile // LANES) + n] = block.astype(bf16)
         return 0
 
     lax.fori_loop(0, count, step, 0)
@@ -243,23 +264,62 @@
     onehot_copy.wait()
 
 
-def place_kernel(channels, skip, onehot, others, skip_wide):
-    hit = iota(onehot.shape, 1) == to_column(channels[0:1, :])[: onehot.shape[0]]
-    onehot[...] = hit.astype(f32).astype(bf16)
-    others[...] = jnp.broadcast_to(1.0 - jnp.max(hit.astype(f32), axis=0, keepdims=True), others.shape)
-    skip_col = jnp.sum(jnp.where(hit, skip[...], 0.0), axis=1, keepdims=True)
-    skip_wide[...] = jnp.broadcast_to(skip_col, skip_wide.shape)
-
-
-def base_kernel(first, onehot_t, others, skip, gate, value, out_gate, residual, *refs):
-    base, sums, picked_gate, picked_res = refs[-12:-8]
-    stages = refs[-8:-4]
-    base_stage, partial, base_sems, sems = refs[-4:]
+def first_kernel(channels, filters_far, outer_fwd_far, turn_far, inner_far, *refs):
+    onehot_t, skip, *dense = refs[:6]
+    onehot, others, skip_wide, spectra, *outs = refs[6:14]
+    filters, outer_fwd, turn, inner, spectra_stage, table_sems = refs[14:20]
+    tables = [
+        pltpu.make_async_copy(source, stage, table_sems.at[n])
+        for n, (source, stage) in enumerate(
+            (
+                (filters_far, filters),
+                (outer_fwd_far, outer_fwd),
+                (turn_far, turn),
+                (inner_far, inner),
+            )
+        )
+    ]
+    for copy in tables:
+        copy.start()
+
+    def beside():
+        hit = iota(onehot.shape, 1) == to_column(channels[0:1, :])[: onehot.shape[0]]
+        onehot[...] = hit.astype(f32).astype(bf16)
+        kept = jnp.max(hit.astype(f32), axis=0, keepdims=True)
+        others[...] = jnp.broadcast_to(1.0 - kept, others.shape)
+        skip_col = jnp.sum(jnp.where(hit, skip[...], 0.0), axis=1, keepdims=True)
+        skip_wide[...] = jnp.broadcast_to(skip_col, skip_wide.shape)
+        for copy in tables:
+            copy.wait()
+        for s, part in enumerate(filter_spectra(filters, outer_fwd, turn, inner)):
+            spectra_stage[s] = part
+            send(s).start()
+
+    def send(s):
+        return pltpu.make_async_copy(
+            spectra_stage.at[s], spectra.at[s], table_sems.at[len(tables) + s]
+        )
+
+    base_pass(0, onehot_t, others, skip, dense, outs, refs[20:], beside)
+    for s in range(spectra.shape[0]):
+        send(s).wait()
+
+
+def second_kernel(first, onehot_t, others, skip, *refs):
+    base_pass(first, onehot_t, others, skip, refs[:4], refs[5:9], refs[9:])
+
+
+def base_pass(first, onehot_t, others, skip, dense, outs, scratch, beside=None):
+    base, sums, picked_gate, picked_res = outs
+    stages = scratch[:4]
+    base_stage, partial, base_sems, sems = scratch[4:]
     gate_stage, value_stage, out_stage, res_stage = stages
     rows = picked_gate.shape[1]
     slab = gate_stage.shape[1]
     tile = partial.shape[0]
-    wait, count = fetch((gate, value, out_gate, residual), stages, sems, tile, first)
+    wait, count = fetch(dense, stages, sems, tile, first)
+    if beside is not None:
+        beside()
 
     def copy(i):
         at = pl.multiple_of(i * tile, tile)
@@ -298,7 +358,7 @@
     lax.fori_loop(0, count, lambda i, _: (copy(i).wait(), 0)[1], 0)
 
 
-def kept_kernel(conv, payload, skip_wide, *refs):
+def kept_kernel(conv, picked, skip_wide, *refs):
     hidden, totals = refs[-2:]
     owner_count, blocks = conv.shape[:2]
     first = 0
@@ -310,9 +370,8 @@
         for s in range(conv.shape[2] // LANES):
             at = slice(s * owner_count, (s + 1) * owner_count)
             lanes = slice(s * LANES, (s + 1) * LANES)
-            gated = jnp.swapaxes(payload[:, at_h, lanes].astype(f32), 0, 1)
             wide = jnp.swapaxes(conv[:, at_h, lanes].astype(f32), 0, 1)
-            wide = wide + skip_wide[at, :] * gated
+            wide = wide + skip_wide[at, :] * picked[at_h, at, :].astype(f32)
             value = picked_res[:, at, :].astype(f32) + picked_gate[:, at, :].astype(f32) * wide
             value = value.astype(bf16)
             hidden[at_h, at, :] = value
@@ -427,10 +486,11 @@
     buffer = (owner_count, blocks, slots * LANES)
     whole = (tok_rows, slab)
 
-    payload, channels, onehot_t = call(
+    payload, picked, channels, onehot_t = call(
         functools.partial(pick_kernel, owner_count, slots),
         [
             sds(buffer, bf16),
+            picks,
             sds((8, lanes_rows), jnp.int32),
             pltpu.HBM((slab, lanes_rows), bf16),
         ],
@@ -448,83 +508,87 @@
             pltpu.SemaphoreType.DMA((2, tok_rows // tile)),
         ],
         far=(0, 1, 2, 3),
-        far_outs=(2,),
+        far_outs=(3,),
     )
 
     incoming = lax.all_to_all(payload, ("seqo", "seqi"), split_axis=0, concat_axis=0, tiled=True)
 
-    (spectra,) = call(
-        filter_kernel,
-        [pltpu.HBM((slots, outer, 2 * LANES), f32)],
-        [filters[0, 0]] + [jnp.asarray(x) for x in dft_tables(length)[:3]],
-        2 * slots * length * 2 * (2 * outer + 6 * LANES),
-        8 * MIB,
-        16 * MIB,
-    )
-    onehot, others, skip_wide = call(
-        place_kernel,
-        [sds((rows, slab), bf16), sds((8, slab), f32), sds((rows, LANES), f32)],
-        [channels, skip_row],
-        rows * slab * 8,
-        rows * slab * 2,
-        8 * MIB,
-    )
-
-    def base_part(first, count, onehot_t, base):
+    dense_ins = [gate_in, value_in, out_gate, residual]
+
+    def base_parts(count):
         part = count * LANES
-        ins = [onehot_t, others, skip_row, gate_in, value_in, out_gate, residual]
         outs = [
             pltpu.HBM(whole, bf16),
             sds((count, 1, LANES), f32),
             sds((count, rows, LANES), bf16),
             sds((count, rows, LANES), bf16),
         ]
-        if base is not None:
-            ins.append(base)
-        return call(
-            functools.partial(base_kernel, first * LANES),
-            outs,
-            ins,
-            4 * part * slab * rows,
-            10 * part * slab,
-            24 * MIB,
-            scratch=[pltpu.VMEM((part, slab), bf16)] * 5
-            + [
-                pltpu.VMEM((LANES, LANES), f32),
-                pltpu.SemaphoreType.DMA((count,)),
-                pltpu.SemaphoreType.DMA((4, count)),
-            ],
-            far=(3, 4, 5, 6, 7),
-            far_outs=(0,),
-            alias={} if base is None else {7: 0},
-        )
+        scratch = [pltpu.VMEM((part, slab), bf16)] * 5 + [
+            pltpu.VMEM((LANES, LANES), f32),
+            pltpu.SemaphoreType.DMA((count,)),
+            pltpu.SemaphoreType.DMA((4, count)),
+        ]
+        return outs, scratch, 4 * part * slab * rows, 10 * part * slab
 
     early = max(1, blocks * EARLY // 16)
-    base, *half_picks = base_part(0, early, onehot_t, None)
-    spectra, base = lax.optimization_barrier((spectra, base))
+    outs, scratch, flops, moved = base_parts(early)
+    spectrum = (slots, outer, 2 * LANES)
+    table_ins = [in_hbm(filters[0, 0]), outer_fwd, turn, inner]
+    onehot, others, skip_wide, spectra, base, *first_picks = call(
+        first_kernel,
+        [
+            sds((rows, slab), bf16),
+            sds((8, slab), f32),
+            sds((rows, LANES), f32),
+            pltpu.HBM(spectrum, f32),
+        ]
+        + outs,
+        [channels] + table_ins + [onehot_t, skip_row] + dense_ins,
+        flops,
+        moved,
+        36 * MIB,
+        scratch=[pltpu.VMEM(x.shape, x.dtype) for x in table_ins]
+        + [pltpu.VMEM(spectrum, f32), pltpu.SemaphoreType.DMA((len(table_ins) + slots,))]
+        + scratch,
+        far=(1, 2, 3, 4, 7, 8, 9, 10),
+        far_outs=(3, 4),
+    )
 
     conv_ins = [incoming, outer_fwd, turn, inner, in_hbm(spectra), outer_back]
     (convolved,) = call(
         convolve_kernel,
-        [sds(buffer, bf16)],
+        [pltpu.HBM(buffer, bf16)],
         conv_ins,
         2 * slots * length * 2 * (5 * outer + 12 * LANES),
         8 * MIB,
         20 * MIB,
         scratch=[pltpu.VMEM(x.shape, x.dtype) for x in conv_ins[1:]]
-        + [pltpu.SemaphoreType.DMA((len(conv_ins) - 1,))],
+        + [pltpu.VMEM(buffer, bf16), pltpu.SemaphoreType.DMA((len(conv_ins) - 1 + slots,))],
         far=tuple(range(1, len(conv_ins))),
+        far_outs=(0,),
     )
     convolved, onehot_t = lax.optimization_barrier((convolved, onehot_t))
 
     returned = lax.all_to_all(convolved, ("seqo", "seqi"), split_axis=0, concat_axis=0, tiled=True)
 
-    base, *more_picks = base_part(early, blocks - early, onehot_t, base)
+    outs, scratch, flops, moved = base_parts(blocks - early)
+    base, *more_picks = call(
+        functools.partial(second_kernel, early * LANES),
+        outs,
+        [onehot_t, others, skip_row] + dense_ins + [base],
+        flops,
+        moved,
+        36 * MIB,
+        scratch=scratch,
+        far=(3, 4, 5, 6, 7),
+        far_outs=(0,),
+        alias={7: 0},
+    )
 
     hidden_kept, totals = call(
         kept_kernel,
         [picks, row_sums],
-        [returned, payload, skip_wide, *half_picks, *more_picks],
+        [returned, picked, skip_wide, *first_picks, *more_picks],
         8 * rows * tok_rows,
         10 * rows * tok_rows,
         16 * MIB,

time: 68.6 us -> 66.4 us (0.968)
  Pallas kernels: 48.7 us -> 46.6 us
    pallas_call x9 -> x7, Pallas kernels: 48.7 us -> 46.6 us  [call(): pl.pallas_call(kernel, out_shape=outs, in_specs=[away if n in far else ne...]
  transfers between devices with their start and end apart: 3 -> 3, of which waited for: 1 -> 2; matrix products, arithmetic and copies ran while one was open for 0% -> 0% of each run, Pallas kernels for 42% -> 42%
where the time goes in v6:
time: 66.4 us; the launch traced here: 66 us
  Pallas kernels  46.6 us (70%)
  starting transfers between devices  14.5 us (22%)
  waiting for transfers between devices  3.01 us (5%)
  local copies, waits for them, and re-layouts  1.05 us (2%)
  between operations  0.75 us (1%)
    pallas_call x7, Pallas kernels, call(): pl.pallas_call(kernel, out_shape=outs, in_specs=[away if n in far else ne...  46.6 us
    all_to_all x1, starting transfers between devices, local(): lax.all_to_all(payload, ('seqo', 'seqi'), split_axis=0, concat_axis=0, ti...  7.37 us
    all_to_all x1, starting transfers between devices, local(): lax.all_to_all(convolved, ('seqo', 'seqi'), split_axis=0, concat_axis=0,...  5.6 us
    all_to_all x1, waiting for transfers between devices, local(): lax.all_to_all(convolved, ('seqo', 'seqi'), split_axis=0, concat_axis=0,...  2.52 us
    ppermute x1, starting transfers between devices, local(): parts.append(lax.ppermute(totals, 'chan', ring))  1.58 us
  transfers between devices with their start and end apart: 3, of which 2 were waited for; matrix products, arithmetic and copies ran while one was open for 0% of the time, Pallas kernels for 42%

profile of v6, /device:TPU:0, one launch (start us, length us, event | category | flops | bytes accessed | tf_op | source)
XLA Modules:
  0.0 66.0 jit_solution(11735969826701478868)
XLA Ops:
  0.6 0.0 copy-start.2
  0.6 8.6 %shard_map.140 = (bf16[16,16,768]{2,1,0:T(8,128)(2,1)}, bf16[16,96,128]{2,1,0:T(8,128)(2,1)S(1)}, s32[8,128]{1,0:T(8,128)S(1)}, bf16[2048,128]{1,0:T(8,128)(2,1)}) custom-call(s32[1,64]{1,0:T(1,128)} %index.1, s32[1,64]{1,0:T(1,128)} %owners.1, bf16[2048,2048]{1,0:T(8,128)(2,1)} %refs_0_.1, bf16[2048,2048]{1,0:T(8,128)(2,1)} %refs_1_.1), custom_call_target="tpu_custom_call" | custom-call | flops 805306368 | bytes 16777216 | tf_op jit(solution)/shard_map/pallas_call | solution.py:453
  9.3 7.4 %all-to-all-start = ((bf16[16,16,768]{2,1,0:T(8,128)(2,1)}), bf16[16,16,768]{2,1,0:T(8,128)(2,1)S(1)}, u32[]{:S(2)}, u32[]{:S(2)}) async-start(bf16[16,16,768]{2,1,0:T(8,128)(2,1)} %get-tuple-element.24), calls=%async_computation | async-start | bytes 786432 | tf_op jit(solution)/shard_map/all_to_all | solution.py:514
  16.7 0.0 copy-done.2
  16.7 0.0 copy-start
  16.7 1.0 %copy-done = bf16[2048,128]{1,0:T(8,128)(2,1)S(1)} copy-done((bf16[2048,128]{1,0:T(8,128)(2,1)S(1)}, bf16[2048,128]{1,0:T(8,128)(2,1)}, u32[]{:S(2)}) %copy-start) | copy-done | bytes 524312
  17.7 10.6 %shard_map.141 = (bf16[96,2048]{1,0:T(8,128)(2,1)S(1)}, f32[8,2048]{1,0:T(8,128)S(1)}, f32[96,128]{1,0:T(8,128)S(1)}, f32[6,256,256]{2,1,0:T(8,128)}, bf16[2048,...) custom-call(s32[8,128]{1,0:T(8,128)S(1)} %get-tuple-element.25.chann, ...), custom_call_target="tpu_custom_call" | custom-call | flops 704643072 | bytes 18350080 | tf_op jit(solution)/shard_map/pallas_call | solution.py:453
  28.4 0.0 copy-start.1
  28.4 0.5 all-to-all-done.signals
  28.9 5.3 %shard_map.142 = bf16[16,16,768]{2,1,0:T(8,128)(2,1)} custom-call(bf16[16,16,768]{2,1,0:T(8,128)(2,1)S(1)} %all-to-all-done.signals, bf16[512,512]{1,0:T(8,128)(2,1)} %constant.8.clone.outer_fwd_far, f32[256,256]{1,0:T(8,128)} %constant.9.clone.turn_far, bf16[1024,256]{1,0:T(8,128)(2,1)} %constant.10.clone.inner_far, ...), custom_call_target="tpu_custom_call" | custom-call | flops 2214592512 | bytes 8388608 | tf_op jit(solution)/shard_map/pallas_call | solution.py:453
  34.2 5.6 %all-to-all-start.1 = ((bf16[16,16,768]{2,1,0:T(8,128)(2,1)}), bf16[16,16,768]{2,1,0:T(8,128)(2,1)S(1)}, u32[]{:S(2)}, u32[]{:S(2)}) async-start(bf16[16,16,768]{2,1,0:T(8,128)(2,1)} %shard_map.142), calls=%async_computation.1 | async-start | bytes 786432 | tf_op jit(solution)/shard_map/all_to_all | solution.py:572
  39.8 0.0 copy-done.1
  39.8 9.7 %shard_map.143 = (bf16[2048,2048]{1,0:T(8,128)(2,1)}, f32[9,1,128]{2,1,0:T(1,128)S(1)}, bf16[9,96,128]{2,1,0:T(8,128)(2,1)S(1)}, bf16[9,96,128]{2,1,0:T(8,128)(2,1)S(1)}) custom-call(bf16[2048,128]{1,0:T(8,128)(2,1)S(1)} %copy-done.1, f32[8,2048]{1,0:T(8,128)S(1)} %get-tuple-element.29.others, ...), custom_call_target="tpu_custom_call", output_to_operand_aliasing={{0}: (7, {})} | custom-call | flops 905969664 | bytes 23592960 | tf_op jit(solution)/shard_map/pallas_call | solution.py:453
  49.5 0.0 copy-start.3
  49.5 2.5 %all-to-all-done.1.conv = bf16[16,16,768]{2,1,0:T(8,128)(2,1)S(1)} async-done(((bf16[16,16,768]{2,1,0:T(8,128)(2,1)}), bf16[16,16,768]{2,1,0:T(8,128)(2,1)S(1)}, u32[]{:S(2)}, u32[]{:S(2)}) %all-to-all-start.1) | async-done | bytes 393248 | tf_op jit(solution)/shard_map/all_to_all | solution.py:572
  52.0 0.6 shard_map.144
  52.6 1.6 %collective-permute-start = (f32[16,1,128]{2,1,0:T(1,128)S(1)}, f32[16,1,128]{2,1,0:T(1,128)S(1)}, u32[]{:S(2)}, u32[]{:S(2)}) collective-permute-start(f32[16,1,128]{2,1,0:T(1,128)S(1)} %get-tuple-element.44.refs_0_), channel_id=1, source_target_pairs={{0,16},{16,0},{1,17},{17,1},{2,18},{18,2},{3,19},{19,3},{4,20},{20... | collective-permute-start | bytes 24584 | tf_op jit(solution)/shard_map/ppermute | solution.py:600
  54.2 7.4 %shard_map.145 = (bf16[2048,2048]{1,0:T(8,128)(2,1)}, bf16[2048,2048]{1,0:T(8,128)(2,1)S(1)}) custom-call(bf16[2048,2048]{1,0:T(8,128)(2,1)} %get-tuple-element.31.base, bf16[16,96,128]{2,1,0:T(8,128)(2,1)S(1)} %get-tuple-element.41.hidden_kept, bf16[96,2048]{1,0:T(8,128)(2,1)S(1)} %get-tuple-element.42.onehot), custom_call_target="tpu_custom_call" | custom-call | flops 805306368 | bytes 16777216 | tf_op jit(solution)/shard_map/pallas_call | solution.py:453
  61.6 0.0 collective-permute-done.refs_1_
  61.6 0.0 copy-done.3
  61.6 4.4 %shard_map.146 = bf16[2048,2048]{1,0:T(8,128)(2,1)} custom-call(f32[16,1,128]{2,1,0:T(1,128)S(1)} %get-tuple-element.44.refs_0_, f32[16,1,128]{2,1,0:T(1,128)S(1)} %collective-permute-done.refs_1_, bf16[2048,2048]{1,0:T(8,128)(2,1)S(1)} %get-tuple-element.45.refs_2_, f32[1,2048]{1,0:T(1,128)S(1)} %bitcast.5), custom_call_target="tpu_custom_call" | custom-call | flops 16777216 | bytes 16777216 | tf_op jit(solution)/shard_map/pallas_call | solution.py:453
Async XLA Ops:
  0.6 16.0 %copy-start.2 = (f32[2048]{0:T(1024)S(1)}, f32[2048]{0:T(1024)}, u32[]{:S(2)}) copy-start(f32[2048]{0:T(1024)} %param.20) | copy-start | bytes 24580
  9.3 19.6 %all-to-all-start = ((bf16[16,16,768]{2,1,0:T(8,128)(2,1)}), bf16[16,16,768]{2,1,0:T(8,128)(2,1)S(1)}, u32[]{:S(2)}, u32[]{:S(2)}) async-start(bf16[16,16,768]{2,1,0:T(8,128)(2,1)} %get-tuple-element.24), calls=%async_computation | async-start | bytes 786432 | tf_op jit(solution)/shard_map/all_to_all | solution.py:514
  16.7 1.0 %copy-start = (bf16[2048,128]{1,0:T(8,128)(2,1)S(1)}, bf16[2048,128]{1,0:T(8,128)(2,1)}, u32[]{:S(2)}) copy-start(bf16[2048,128]{1,0:T(8,128)(2,1)} %get-tuple-element.28.refs_0_.onehot_t) | copy-start | bytes 1572868
  28.4 11.5 %copy-start.1 = (bf16[2048,128]{1,0:T(8,128)(2,1)S(1)}, bf16[2048,128]{1,0:T(8,128)(2,1)}, u32[]{:S(2)}) copy-start(bf16[2048,128]{1,0:T(8,128)(2,1)} %get-tuple-element.28.refs_0_.onehot_t) | copy-start | bytes 1572868
  34.2 17.8 %all-to-all-start.1 = ((bf16[16,16,768]{2,1,0:T(8,128)(2,1)}), bf16[16,16,768]{2,1,0:T(8,128)(2,1)S(1)}, u32[]{:S(2)}, u32[]{:S(2)}) async-start(bf16[16,16,768]{2,1,0:T(8,128)(2,1)} %shard_map.142), calls=%async_computation.1 | async-start | bytes 786432 | tf_op jit(solution)/shard_map/all_to_all | solution.py:572
  49.5 12.1 %copy-start.3 = (f32[2048]{0:T(1024)S(1)}, f32[2048]{0:T(1024)}, u32[]{:S(2)}) copy-start(f32[2048]{0:T(1024)} %param.21) | copy-start | bytes 24580
  52.6 8.9 %collective-permute-start = (f32[16,1,128]{2,1,0:T(1,128)S(1)}, f32[16,1,128]{2,1,0:T(1,128)S(1)}, u32[]{:S(2)}, u32[]{:S(2)}) collective-permute-start(f32[16,1,128]{2,1,0:T(1,128)S(1)} %get-tuple-element.44.refs_0_), channel_id=1, source_target_pairs={{0,16},{16,0},{1,17},{17,1},{2,18},{18,2},{3,19},{19,3},{4,20},{20... | collective-permute-start | bytes 24584 | tf_op jit(solution)/shard_map/ppermute | solution.py:600

commit v7 on v6

--- a/solution.py
+++ b/solution.py
@@ -12,7 +12,6 @@
 TILE = 256
 CHUNK = 16
 GROUP = 3
-AHEAD = 3
 EARLY = 7
 MIB = 1 << 20
 norm_eps = 1e-06
@@ -121,8 +120,7 @@
     copies = [
         pltpu.make_async_copy(source, scratch[n], sems.at[n]) for n, source in enumerate(sources)
     ]
-    for copy in copies[:3]:
-        copy.start()
+    copies[0].start()
     slots, outer = spectra.shape[:2]
 
     def turn_now():
@@ -134,7 +132,7 @@
         return inner[: 4 * LANES, :]
 
     copies[0].wait()
-    for copy in copies[3:]:
+    for copy in copies[1:]:
         copy.start()
     blocks = signals[...].reshape(outer, slots * LANES)
     parts = to_spectrum(blocks, slots, outer_fwd[...], turn_now, inner_now)
@@ -197,7 +195,7 @@
     return [picked[:rows, i : i + LANES] for i in range(0, tile.shape[0], LANES)]
 
 
-def fetch(sources, stages, sems, tile, first=0):
+def fetch(sources, stages, sems, tile, first=0, ahead=2):
     count = stages[0].shape[0] // tile
 
     def copies(i):
@@ -213,16 +211,16 @@
         for copy in copies(i):
             copy.start()
 
-    for i in range(min(AHEAD, count)):
+    for i in range(min(ahead, count)):
         start(i)
 
     def wait(i):
         for copy in copies(i):
             copy.wait()
 
-        @pl.when(i + AHEAD < count)
+        @pl.when(i + ahead < count)
         def _():
-            start(i + AHEAD)
+            start(i + ahead)
 
         return pl.multiple_of(i * tile, tile)
 
@@ -265,51 +263,49 @@
 
 
 def first_kernel(channels, filters_far, outer_fwd_far, turn_far, inner_far, *refs):
-    onehot_t, skip, *dense = refs[:6]
+    onehot_far, skip, *dense = refs[:6]
     onehot, others, skip_wide, spectra, *outs = refs[6:14]
-    filters, outer_fwd, turn, inner, spectra_stage, table_sems = refs[14:20]
+    filters, outer_fwd, turn, inner, onehot_t, spectra_stage, table_sems = refs[14:21]
+    sources = (filters_far, outer_fwd_far, turn_far, inner_far, onehot_far)
+    stages = (filters, outer_fwd, turn, inner, onehot_t)
     tables = [
         pltpu.make_async_copy(source, stage, table_sems.at[n])
-        for n, (source, stage) in enumerate(
-            (
-                (filters_far, filters),
-                (outer_fwd_far, outer_fwd),
-                (turn_far, turn),
-                (inner_far, inner),
-            )
-        )
+        for n, (source, stage) in enumerate(zip(sources, stages))
     ]
     for copy in tables:
         copy.start()
+    hit = iota(onehot.shape, 1) == to_column(channels[0:1, :])[: onehot.shape[0]]
+    onehot[...] = hit.astype(f32).astype(bf16)
+    kept = jnp.max(hit.astype(f32), axis=0, keepdims=True)
+    others[...] = jnp.broadcast_to(1.0 - kept, others.shape)
+    skip_col = jnp.sum(jnp.where(hit, skip[...], 0.0), axis=1, keepdims=True)
+    skip_wide[...] = jnp.broadcast_to(skip_col, skip_wide.shape)
+
+    def send(s):
+        return pltpu.make_async_copy(
+            spectra_stage.at[s], spectra.at[s], table_sems.at[len(tables) + s]
+        )
 
     def beside():
-        hit = iota(onehot.shape, 1) == to_column(channels[0:1, :])[: onehot.shape[0]]
-        onehot[...] = hit.astype(f32).astype(bf16)
-        kept = jnp.max(hit.astype(f32), axis=0, keepdims=True)
-        others[...] = jnp.broadcast_to(1.0 - kept, others.shape)
-        skip_col = jnp.sum(jnp.where(hit, skip[...], 0.0), axis=1, keepdims=True)
-        skip_wide[...] = jnp.broadcast_to(skip_col, skip_wide.shape)
         for copy in tables:
             copy.wait()
         for s, part in enumerate(filter_spectra(filters, outer_fwd, turn, inner)):
             spectra_stage[s] = part
             send(s).start()
 
-    def send(s):
-        return pltpu.make_async_copy(
-            spectra_stage.at[s], spectra.at[s], table_sems.at[len(tables) + s]
-        )
-
-    base_pass(0, onehot_t, others, skip, dense, outs, refs[20:], beside)
+    base_pass(0, onehot_t, others, skip, dense, outs, refs[21:], beside, 3)
     for s in range(spectra.shape[0]):
         send(s).wait()
 
 
-def second_kernel(first, onehot_t, others, skip, *refs):
-    base_pass(first, onehot_t, others, skip, refs[:4], refs[5:9], refs[9:])
-
-
-def base_pass(first, onehot_t, others, skip, dense, outs, scratch, beside=None):
+def second_kernel(first, onehot_far, others, skip, *refs):
+    onehot_t, onehot_sem = refs[9:11]
+    copy = pltpu.make_async_copy(onehot_far, onehot_t, onehot_sem.at[0])
+    copy.start()
+    base_pass(first, onehot_t, others, skip, refs[:4], refs[5:9], refs[11:], copy.wait, 2)
+
+
+def base_pass(first, onehot_t, others, skip, dense, outs, scratch, beside, ahead):
     base, sums, picked_gate, picked_res = outs
     stages = scratch[:4]
     base_stage, partial, base_sems, sems = scratch[4:]
@@ -317,9 +313,8 @@
     rows = picked_gate.shape[1]
     slab = gate_stage.shape[1]
     tile = partial.shape[0]
-    wait, count = fetch(dense, stages, sems, tile, first)
-    if beside is not None:
-        beside()
+    wait, count = fetch(dense, stages, sems, tile, first, ahead)
+    beside()
 
     def copy(i):
         at = pl.multiple_of(i * tile, tile)
@@ -387,7 +382,7 @@
     wide = min(slab, 2 * LANES)
     count = sems.shape[0]
     tile = held.shape[0] // count
-    wait, _ = fetch((base,), (base_stage,), base_sems, tile)
+    wait, _ = fetch((base,), (base_stage,), base_sems, tile, 0, 3)
 
     def copy(i):
         rows = pl.ds(pl.multiple_of(i * tile, tile), tile)
@@ -533,7 +528,8 @@
     early = max(1, blocks * EARLY // 16)
     outs, scratch, flops, moved = base_parts(early)
     spectrum = (slots, outer, 2 * LANES)
-    table_ins = [in_hbm(filters[0, 0]), outer_fwd, turn, inner]
+    onehot_t = in_hbm(onehot_t)
+    table_ins = [in_hbm(filters[0, 0]), outer_fwd, turn, inner, onehot_t]
     onehot, others, skip_wide, spectra, base, *first_picks = call(
         first_kernel,
         [
@@ -543,14 +539,14 @@
             pltpu.HBM(spectrum, f32),
         ]
         + outs,
-        [channels] + table_ins + [onehot_t, skip_row] + dense_ins,
+        [channels] + table_ins + [skip_row] + dense_ins,
         flops,
         moved,
         36 * MIB,
         scratch=[pltpu.VMEM(x.shape, x.dtype) for x in table_ins]
         + [pltpu.VMEM(spectrum, f32), pltpu.SemaphoreType.DMA((len(table_ins) + slots,))]
         + scratch,
-        far=(1, 2, 3, 4, 7, 8, 9, 10),
+        far=(1, 2, 3, 4, 5, 7, 8, 9, 10),
         far_outs=(3, 4),
     )
 
@@ -575,12 +571,12 @@
     base, *more_picks = call(
         functools.partial(second_kernel, early * LANES),
         outs,
-        [onehot_t, others, skip_row] + dense_ins + [base],
+        [in_hbm(onehot_t), others, skip_row] + dense_ins + [base],
         flops,
         moved,
         36 * MIB,
-        scratch=scratch,
-        far=(3, 4, 5, 6, 7),
+        scratch=[pltpu.VMEM(onehot_t.shape, bf16), pltpu.SemaphoreType.DMA((1,))] + scratch,
+        far=(0, 3, 4, 5, 6, 7),
         far_outs=(0,),
         alias={7: 0},
     )

time: 66.4 us -> 67.3 us (1.014)
  Pallas kernels: 46.6 us -> 49.8 us
  local copies, waits for them, and re-layouts: 1.05 us -> 0.01 us
  waiting for transfers between devices: 3.01 us -> 2.15 us
    pallas_call x7, Pallas kernels: 46.6 us -> 49.8 us  [call(): pl.pallas_call(kernel, out_shape=outs, in_specs=[away if n in far else ne...]
    all_to_all x1, waiting for transfers between devices: 2.52 us -> 1.29 us  [local(): lax.all_to_all(convolved, ('seqo', 'seqi'), split_axis=0, concat_axis=0,...]
    unnamed x8 -> x4, local copies, waits for them, and re-layouts: 1.05 us -> 0.01 us
  transfers between devices with their start and end apart: 3 -> 3, of which waited for: 2 -> 2; matrix products, arithmetic and copies ran while one was open for 0% -> 0% of each run, Pallas kernels for 42% -> 44%
where the time goes in v7:
time: 67.3 us; the launch traced here: 66.8 us
  Pallas kernels  49.8 us (74%)
  starting transfers between devices  14.1 us (21%)
  waiting for transfers between devices  2.15 us (3%)
  between operations  0.73 us (1%)
    pallas_call x7, Pallas kernels, call(): pl.pallas_call(kernel, out_shape=outs, in_specs=[away if n in far else ne...  49.8 us
    all_to_all x1, starting transfers between devices, local(): lax.all_to_all(payload, ('seqo', 'seqi'), split_axis=0, concat_axis=0, ti...  7.37 us
    all_to_all x1, starting transfers between devices, local(): lax.all_to_all(convolved, ('seqo', 'seqi'), split_axis=0, concat_axis=0,...  5.17 us
    ppermute x1, starting transfers between devices, local(): parts.append(lax.ppermute(totals, 'chan', ring))  1.58 us
  transfers between devices with their start and end apart: 3, of which 2 were waited for; matrix products, arithmetic and copies ran while one was open for 0% of the time, Pallas kernels for 44%

profile of v7, /device:TPU:0, one launch (start us, length us, event | category | flops | bytes accessed | tf_op | source)
XLA Modules:
  0.0 66.8 jit_solution(13911978363299649241)
XLA Ops:
  0.6 0.0 copy-start
  0.6 9.4 %shard_map.140 = (bf16[16,16,768]{2,1,0:T(8,128)(2,1)}, bf16[16,96,128]{2,1,0:T(8,128)(2,1)S(1)}, s32[8,128]{1,0:T(8,128)S(1)}, bf16[2048,128]{1,0:T(8,128)(2,1)}) custom-call(s32[1,64]{1,0:T(1,128)} %index.1, s32[1,64]{1,0:T(1,128)} %owners.1, bf16[2048,2048]{1,0:T(8,128)(2,1)} %refs_0_.1, bf16[2048,2048]{1,0:T(8,128)(2,1)} %refs_1_.1), custom_call_target="tpu_custom_call" | custom-call | flops 805306368 | bytes 16777216 | tf_op jit(solution)/shard_map/pallas_call | solution.py:448
  10.0 7.4 %all-to-all-start = ((bf16[16,16,768]{2,1,0:T(8,128)(2,1)}), bf16[16,16,768]{2,1,0:T(8,128)(2,1)S(1)}, u32[]{:S(2)}, u32[]{:S(2)}) async-start(bf16[16,16,768]{2,1,0:T(8,128)(2,1)} %get-tuple-element.24), calls=%async_computation | async-start | bytes 786432 | tf_op jit(solution)/shard_map/all_to_all | solution.py:509
  17.4 0.0 copy-done
  17.4 11.3 %shard_map.141 = (bf16[96,2048]{1,0:T(8,128)(2,1)S(1)}, f32[8,2048]{1,0:T(8,128)S(1)}, f32[96,128]{1,0:T(8,128)S(1)}, f32[6,256,256]{2,1,0:T(8,128)}, bf16[2048,...) custom-call(s32[8,128]{1,0:T(8,128)S(1)} %get-tuple-element.25.chann, ...), custom_call_target="tpu_custom_call" | custom-call | flops 704643072 | bytes 18350080 | tf_op jit(solution)/shard_map/pallas_call | solution.py:448
  28.7 0.9 %all-to-all-done.signals = bf16[16,16,768]{2,1,0:T(8,128)(2,1)S(1)} async-done(((bf16[16,16,768]{2,1,0:T(8,128)(2,1)}), bf16[16,16,768]{2,1,0:T(8,128)(2,1)S(1)}, u32[]{:S(2)}, u32[]{:S(2)}) %all-to-all-start) | async-done | bytes 393248 | tf_op jit(solution)/shard_map/all_to_all | solution.py:509
  29.6 5.9 %shard_map.142 = bf16[16,16,768]{2,1,0:T(8,128)(2,1)} custom-call(bf16[16,16,768]{2,1,0:T(8,128)(2,1)S(1)} %all-to-all-done.signals, bf16[512,512]{1,0:T(8,128)(2,1)} %constant.8.clone.outer_fwd_far, f32[256,256]{1,0:T(8,128)} %constant.9.clone.turn_far, bf16[1024,256]{1,0:T(8,128)(2,1)} %constant.10.clone.inner_far, ...), custom_call_target="tpu_custom_call" | custom-call | flops 2214592512 | bytes 8388608 | tf_op jit(solution)/shard_map/pallas_call | solution.py:448
  35.5 5.2 %all-to-all-start.1 = ((bf16[16,16,768]{2,1,0:T(8,128)(2,1)}), bf16[16,16,768]{2,1,0:T(8,128)(2,1)S(1)}, u32[]{:S(2)}, u32[]{:S(2)}) async-start(bf16[16,16,768]{2,1,0:T(8,128)(2,1)} %shard_map.142), calls=%async_computation.1 | async-start | bytes 786432 | tf_op jit(solution)/shard_map/all_to_all | solution.py:568
  40.6 10.9 %shard_map.143 = (bf16[2048,2048]{1,0:T(8,128)(2,1)}, f32[9,1,128]{2,1,0:T(1,128)S(1)}, bf16[9,96,128]{2,1,0:T(8,128)(2,1)S(1)}, bf16[9,96,128]{2,1,0:T(8,128)(2,1)S(1)}) custom-call(bf16[2048,128]{1,0:T(8,128)(2,1)} %get-tuple-element.28.refs_0_.onehot_far, f32[8,2048]{1,0:T(8,128)S(1)} %get-tuple-element.29.others, ...), custom_call_target="tpu_custom_call", output_to_operand_aliasing={{0}: (7, {})} | custom-call | flops 905969664 | bytes 23592960 | tf_op jit(solution)/shard_map/pallas_call | solution.py:448
  51.5 0.0 copy-start.1
  51.6 1.3 %all-to-all-done.1.conv = bf16[16,16,768]{2,1,0:T(8,128)(2,1)S(1)} async-done(((bf16[16,16,768]{2,1,0:T(8,128)(2,1)}), bf16[16,16,768]{2,1,0:T(8,128)(2,1)S(1)}, u32[]{:S(2)}, u32[]{:S(2)}) %all-to-all-start.1) | async-done | bytes 393248 | tf_op jit(solution)/shard_map/all_to_all | solution.py:568
  52.8 0.6 shard_map.144
  53.4 1.6 %collective-permute-start = (f32[16,1,128]{2,1,0:T(1,128)S(1)}, f32[16,1,128]{2,1,0:T(1,128)S(1)}, u32[]{:S(2)}, u32[]{:S(2)}) collective-permute-start(f32[16,1,128]{2,1,0:T(1,128)S(1)} %get-tuple-element.44.refs_0_), channel_id=1, source_target_pairs={{0,16},{16,0},{1,17},{17,1},{2,18},{18,2},{3,19},{19,3},{4,20},{20... | collective-permute-start | bytes 24584 | tf_op jit(solution)/shard_map/ppermute | solution.py:596
  55.0 7.4 %shard_map.145 = (bf16[2048,2048]{1,0:T(8,128)(2,1)}, bf16[2048,2048]{1,0:T(8,128)(2,1)S(1)}) custom-call(bf16[2048,2048]{1,0:T(8,128)(2,1)} %get-tuple-element.31.base, bf16[16,96,128]{2,1,0:T(8,128)(2,1)S(1)} %get-tuple-element.41.hidden_kept, bf16[96,2048]{1,0:T(8,128)(2,1)S(1)} %get-tuple-element.42.onehot), custom_call_target="tpu_custom_call" | custom-call | flops 805306368 | bytes 16777216 | tf_op jit(solution)/shard_map/pallas_call | solution.py:448
  62.4 0.0 collective-permute-done.refs_1_
  62.4 0.0 copy-done.1
  62.4 4.4 %shard_map.146 = bf16[2048,2048]{1,0:T(8,128)(2,1)} custom-call(f32[16,1,128]{2,1,0:T(1,128)S(1)} %get-tuple-element.44.refs_0_, f32[16,1,128]{2,1,0:T(1,128)S(1)} %collective-permute-done.refs_1_, bf16[2048,2048]{1,0:T(8,128)(2,1)S(1)} %get-tuple-element.45.refs_2_, f32[1,2048]{1,0:T(1,128)S(1)} %bitcast.5), custom_call_target="tpu_custom_call" | custom-call | flops 16777216 | bytes 16777216 | tf_op jit(solution)/shard_map/pallas_call | solution.py:448
Async XLA Ops:
  0.6 16.8 %copy-start = (f32[2048]{0:T(1024)S(1)}, f32[2048]{0:T(1024)}, u32[]{:S(2)}) copy-start(f32[2048]{0:T(1024)} %param.20) | copy-start | bytes 24580
  10.0 19.6 %all-to-all-start = ((bf16[16,16,768]{2,1,0:T(8,128)(2,1)}), bf16[16,16,768]{2,1,0:T(8,128)(2,1)S(1)}, u32[]{:S(2)}, u32[]{:S(2)}) async-start(bf16[16,16,768]{2,1,0:T(8,128)(2,1)} %get-tuple-element.24), calls=%async_computation | async-start | bytes 786432 | tf_op jit(solution)/shard_map/all_to_all | solution.py:509
  35.5 17.4 %all-to-all-start.1 = ((bf16[16,16,768]{2,1,0:T(8,128)(2,1)}), bf16[16,16,768]{2,1,0:T(8,128)(2,1)S(1)}, u32[]{:S(2)}, u32[]{:S(2)}) async-start(bf16[16,16,768]{2,1,0:T(8,128)(2,1)} %shard_map.142), calls=%async_computation.1 | async-start | bytes 786432 | tf_op jit(solution)/shard_map/all_to_all | solution.py:568
  51.5 10.9 %copy-start.1 = (f32[2048]{0:T(1024)S(1)}, f32[2048]{0:T(1024)}, u32[]{:S(2)}) copy-start(f32[2048]{0:T(1024)} %param.21) | copy-start | bytes 24580
  53.4 8.9 %collective-permute-start = (f32[16,1,128]{2,1,0:T(1,128)S(1)}, f32[16,1,128]{2,1,0:T(1,128)S(1)}, u32[]{:S(2)}, u32[]{:S(2)}) collective-permute-start(f32[16,1,128]{2,1,0:T(1,128)S(1)} %get-tuple-element.44.refs_0_), channel_id=1, source_target_pairs={{0,16},{16,0},{1,17},{17,1},{2,18},{18,2},{3,19},{19,3},{4,20},{20... | collective-permute-start | bytes 24584 | tf_op jit(solution)/shard_map/ppermute | solution.py:596

commit v8 on v7

--- a/solution.py
+++ b/solution.py
@@ -120,7 +120,8 @@
     copies = [
         pltpu.make_async_copy(source, scratch[n], sems.at[n]) for n, source in enumerate(sources)
     ]
-    copies[0].start()
+    for copy in copies:
+        copy.start()
     slots, outer = spectra.shape[:2]
 
     def turn_now():
@@ -132,8 +133,6 @@
         return inner[: 4 * LANES, :]
 
     copies[0].wait()
-    for copy in copies[1:]:
-        copy.start()
     blocks = signals[...].reshape(outer, slots * LANES)
     parts = to_spectrum(blocks, slots, outer_fwd[...], turn_now, inner_now)
     turn = turn_ref[...]
@@ -195,7 +194,7 @@
     return [picked[:rows, i : i + LANES] for i in range(0, tile.shape[0], LANES)]
 
 
-def fetch(sources, stages, sems, tile, first=0, ahead=2):
+def fetch(sources, stages, sems, tile, first=0, ahead=4):
     count = stages[0].shape[0] // tile
 
     def copies(i):
@@ -293,7 +292,7 @@
             spectra_stage[s] = part
             send(s).start()
 
-    base_pass(0, onehot_t, others, skip, dense, outs, refs[21:], beside, 3)
+    base_pass(0, onehot_t, others, skip, dense, outs, refs[21:], beside, 4)
     for s in range(spectra.shape[0]):
         send(s).wait()
 
@@ -302,7 +301,7 @@
     onehot_t, onehot_sem = refs[9:11]
     copy = pltpu.make_async_copy(onehot_far, onehot_t, onehot_sem.at[0])
     copy.start()
-    base_pass(first, onehot_t, others, skip, refs[:4], refs[5:9], refs[11:], copy.wait, 2)
+    base_pass(first, onehot_t, others, skip, refs[:4], refs[5:9], refs[11:], copy.wait, 4)
 
 
 def base_pass(first, onehot_t, others, skip, dense, outs, scratch, beside, ahead):
@@ -382,7 +381,7 @@
     wide = min(slab, 2 * LANES)
     count = sems.shape[0]
     tile = held.shape[0] // count
-    wait, _ = fetch((base,), (base_stage,), base_sems, tile, 0, 3)
+    wait, _ = fetch((base,), (base_stage,), base_sems, tile)
 
     def copy(i):
         rows = pl.ds(pl.multiple_of(i * tile, tile), tile)

time: 67.3 us -> 66.3 us (0.985)
  waiting for transfers between devices: 2.15 us -> 1.06 us
  transfers between devices with their start and end apart: 3 -> 3, of which waited for: 2 -> 2; matrix products, arithmetic and copies ran while one was open for 0% -> 0% of each run, Pallas kernels for 44% -> 46%
where the time goes in v8:
time: 66.3 us; the launch traced here: 65.9 us
  Pallas kernels  49.4 us (75%)
  starting transfers between devices  14.7 us (22%)
  waiting for transfers between devices  1.06 us (2%)
  between operations  0.73 us (1%)
    pallas_call x7, Pallas kernels, call(): pl.pallas_call(kernel, out_shape=outs, in_specs=[away if n in far else ne...  49.4 us
    all_to_all x1, starting transfers between devices, local(): lax.all_to_all(payload, ('seqo', 'seqi'), split_axis=0, concat_axis=0, ti...  7.37 us
    all_to_all x1, starting transfers between devices, local(): lax.all_to_all(convolved, ('seqo', 'seqi'), split_axis=0, concat_axis=0,...  5.77 us
    ppermute x1, starting transfers between devices, local(): parts.append(lax.ppermute(totals, 'chan', ring))  1.58 us
  transfers between devices with their start and end apart: 3, of which 2 were waited for; matrix products, arithmetic and copies ran while one was open for 0% of the time, Pallas kernels for 46%

profile of v8, /device:TPU:0, one launch (start us, length us, event | category | flops | bytes accessed | tf_op | source)
XLA Modules:
  0.0 65.9 jit_solution(10041979248793835897)
XLA Ops:
  0.6 0.0 copy-start
  0.6 8.6 %shard_map.140 = (bf16[16,16,768]{2,1,0:T(8,128)(2,1)}, bf16[16,96,128]{2,1,0:T(8,128)(2,1)S(1)}, s32[8,128]{1,0:T(8,128)S(1)}, bf16[2048,128]{1,0:T(8,128)(2,1)}) custom-call(s32[1,64]{1,0:T(1,128)} %index.1, s32[1,64]{1,0:T(1,128)} %owners.1, bf16[2048,2048]{1,0:T(8,128)(2,1)} %refs_0_.1, bf16[2048,2048]{1,0:T(8,128)(2,1)} %refs_1_.1), custom_call_target="tpu_custom_call" | custom-call | flops 805306368 | bytes 16777216 | tf_op jit(solution)/shard_map/pallas_call | solution.py:447
  9.3 7.4 %all-to-all-start = ((bf16[16,16,768]{2,1,0:T(8,128)(2,1)}), bf16[16,16,768]{2,1,0:T(8,128)(2,1)S(1)}, u32[]{:S(2)}, u32[]{:S(2)}) async-start(bf16[16,16,768]{2,1,0:T(8,128)(2,1)} %get-tuple-element.24), calls=%async_computation | async-start | bytes 786432 | tf_op jit(solution)/shard_map/all_to_all | solution.py:508
  16.7 0.0 copy-done
  16.7 11.9 %shard_map.141 = (bf16[96,2048]{1,0:T(8,128)(2,1)S(1)}, f32[8,2048]{1,0:T(8,128)S(1)}, f32[96,128]{1,0:T(8,128)S(1)}, f32[6,256,256]{2,1,0:T(8,128)}, bf16[2048,...) custom-call(s32[8,128]{1,0:T(8,128)S(1)} %get-tuple-element.25.chann, ...), custom_call_target="tpu_custom_call" | custom-call | flops 704643072 | bytes 18350080 | tf_op jit(solution)/shard_map/pallas_call | solution.py:447
  28.6 0.3 all-to-all-done.signals
  28.9 5.2 %shard_map.142 = bf16[16,16,768]{2,1,0:T(8,128)(2,1)} custom-call(bf16[16,16,768]{2,1,0:T(8,128)(2,1)S(1)} %all-to-all-done.signals, bf16[512,512]{1,0:T(8,128)(2,1)} %constant.8.clone.outer_fwd_far, f32[256,256]{1,0:T(8,128)} %constant.9.clone.turn_far, bf16[1024,256]{1,0:T(8,128)(2,1)} %constant.10.clone.inner_far, ...), custom_call_target="tpu_custom_call" | custom-call | flops 2214592512 | bytes 8388608 | tf_op jit(solution)/shard_map/pallas_call | solution.py:447
  34.1 5.8 %all-to-all-start.1 = ((bf16[16,16,768]{2,1,0:T(8,128)(2,1)}), bf16[16,16,768]{2,1,0:T(8,128)(2,1)S(1)}, u32[]{:S(2)}, u32[]{:S(2)}) async-start(bf16[16,16,768]{2,1,0:T(8,128)(2,1)} %shard_map.142), calls=%async_computation.1 | async-start | bytes 786432 | tf_op jit(solution)/shard_map/all_to_all | solution.py:567
  39.9 11.4 %shard_map.143 = (bf16[2048,2048]{1,0:T(8,128)(2,1)}, f32[9,1,128]{2,1,0:T(1,128)S(1)}, bf16[9,96,128]{2,1,0:T(8,128)(2,1)S(1)}, bf16[9,96,128]{2,1,0:T(8,128)(2,1)S(1)}) custom-call(bf16[2048,128]{1,0:T(8,128)(2,1)} %get-tuple-element.28.refs_0_.onehot_far, f32[8,2048]{1,0:T(8,128)S(1)} %get-tuple-element.29.others, ...), custom_call_target="tpu_custom_call", output_to_operand_aliasing={{0}: (7, {})} | custom-call | flops 905969664 | bytes 23592960 | tf_op jit(solution)/shard_map/pallas_call | solution.py:447
  51.2 0.0 copy-start.1
  51.3 0.8 %all-to-all-done.1.conv = bf16[16,16,768]{2,1,0:T(8,128)(2,1)S(1)} async-done(((bf16[16,16,768]{2,1,0:T(8,128)(2,1)}), bf16[16,16,768]{2,1,0:T(8,128)(2,1)S(1)}, u32[]{:S(2)}, u32[]{:S(2)}) %all-to-all-start.1) | async-done | bytes 393248 | tf_op jit(solution)/shard_map/all_to_all | solution.py:567
  52.1 0.6 shard_map.144
  52.6 1.6 %collective-permute-start = (f32[16,1,128]{2,1,0:T(1,128)S(1)}, f32[16,1,128]{2,1,0:T(1,128)S(1)}, u32[]{:S(2)}, u32[]{:S(2)}) collective-permute-start(f32[16,1,128]{2,1,0:T(1,128)S(1)} %get-tuple-element.44.refs_0_), channel_id=1, source_target_pairs={{0,16},{16,0},{1,17},{17,1},{2,18},{18,2},{3,19},{19,3},{4,20},{20... | collective-permute-start | bytes 24584 | tf_op jit(solution)/shard_map/ppermute | solution.py:595
  54.2 7.3 %shard_map.145 = (bf16[2048,2048]{1,0:T(8,128)(2,1)}, bf16[2048,2048]{1,0:T(8,128)(2,1)S(1)}) custom-call(bf16[2048,2048]{1,0:T(8,128)(2,1)} %get-tuple-element.31.base, bf16[16,96,128]{2,1,0:T(8,128)(2,1)S(1)} %get-tuple-element.41.hidden_kept, bf16[96,2048]{1,0:T(8,128)(2,1)S(1)} %get-tuple-element.42.onehot), custom_call_target="tpu_custom_call" | custom-call | flops 805306368 | bytes 16777216 | tf_op jit(solution)/shard_map/pallas_call | solution.py:447
  61.5 0.0 collective-permute-done.refs_1_
  61.5 0.0 copy-done.1
  61.5 4.4 %shard_map.146 = bf16[2048,2048]{1,0:T(8,128)(2,1)} custom-call(f32[16,1,128]{2,1,0:T(1,128)S(1)} %get-tuple-element.44.refs_0_, f32[16,1,128]{2,1,0:T(1,128)S(1)} %collective-permute-done.refs_1_, bf16[2048,2048]{1,0:T(8,128)(2,1)S(1)} %get-tuple-element.45.refs_2_, f32[1,2048]{1,0:T(1,128)S(1)} %bitcast.5), custom_call_target="tpu_custom_call" | custom-call | flops 16777216 | bytes 16777216 | tf_op jit(solution)/shard_map/pallas_call | solution.py:447
Async XLA Ops:
  0.6 16.0 %copy-start = (f32[2048]{0:T(1024)S(1)}, f32[2048]{0:T(1024)}, u32[]{:S(2)}) copy-start(f32[2048]{0:T(1024)} %param.20) | copy-start | bytes 24580
  9.3 19.6 %all-to-all-start = ((bf16[16,16,768]{2,1,0:T(8,128)(2,1)}), bf16[16,16,768]{2,1,0:T(8,128)(2,1)S(1)}, u32[]{:S(2)}, u32[]{:S(2)}) async-start(bf16[16,16,768]{2,1,0:T(8,128)(2,1)} %get-tuple-element.24), calls=%async_computation | async-start | bytes 786432 | tf_op jit(solution)/shard_map/all_to_all | solution.py:508
  34.1 18.0 %all-to-all-start.1 = ((bf16[16,16,768]{2,1,0:T(8,128)(2,1)}), bf16[16,16,768]{2,1,0:T(8,128)(2,1)S(1)}, u32[]{:S(2)}, u32[]{:S(2)}) async-start(bf16[16,16,768]{2,1,0:T(8,128)(2,1)} %shard_map.142), calls=%async_computation.1 | async-start | bytes 786432 | tf_op jit(solution)/shard_map/all_to_all | solution.py:567
  51.2 10.3 %copy-start.1 = (f32[2048]{0:T(1024)S(1)}, f32[2048]{0:T(1024)}, u32[]{:S(2)}) copy-start(f32[2048]{0:T(1024)} %param.21) | copy-start | bytes 24580
  52.6 8.9 %collective-permute-start = (f32[16,1,128]{2,1,0:T(1,128)S(1)}, f32[16,1,128]{2,1,0:T(1,128)S(1)}, u32[]{:S(2)}, u32[]{:S(2)}) collective-permute-start(f32[16,1,128]{2,1,0:T(1,128)S(1)} %get-tuple-element.44.refs_0_), channel_id=1, source_target_pairs={{0,16},{16,0},{1,17},{17,1},{2,18},{18,2},{3,19},{19,3},{4,20},{20... | collective-permute-start | bytes 24584 | tf_op jit(solution)/shard_map/ppermute | solution.py:595

commit v9 on v8

--- a/solution.py
+++ b/solution.py
@@ -227,8 +227,8 @@
 
 
 def pick_kernel(owner_count, slots, index, owners, gate, value, *refs):
-    payload, picked, channels, onehot_far = refs[:4]
-    acc, gate_stage, value_stage, onehot_t, lists, list_sems, sems = refs[4:]
+    payload, picked, channels, onehot_t = refs[:4]
+    acc, gate_stage, value_stage, lists, list_sems, sems = refs[4:]
     rows = owner_count * slots
     tile = gate_stage.shape[0] // sems.shape[1]
     list_copies = [
@@ -243,8 +243,6 @@
     row = channel_of_row(lists[0], lists[1], owner_count, onehot_t.shape[1])
     channels[...] = jnp.broadcast_to(row, channels.shape)
     onehot_t[...] = (iota(onehot_t.shape, 0) == row).astype(f32).astype(bf16)
-    onehot_copy = pltpu.make_async_copy(onehot_t, onehot_far, list_sems.at[2])
-    onehot_copy.start()
 
     def step(i, _):
         at = pl.ds(wait(i), tile)
@@ -258,15 +256,14 @@
     for s in range(slots):
         part = jnp.swapaxes(acc[:, s * owner_count : (s + 1) * owner_count, :], 0, 1)
         payload[:, :, s * LANES : (s + 1) * LANES] = part.astype(bf16)
-    onehot_copy.wait()
 
 
 def first_kernel(channels, filters_far, outer_fwd_far, turn_far, inner_far, *refs):
-    onehot_far, skip, *dense = refs[:6]
+    onehot_t, skip, *dense = refs[:6]
     onehot, others, skip_wide, spectra, *outs = refs[6:14]
-    filters, outer_fwd, turn, inner, onehot_t, spectra_stage, table_sems = refs[14:21]
-    sources = (filters_far, outer_fwd_far, turn_far, inner_far, onehot_far)
-    stages = (filters, outer_fwd, turn, inner, onehot_t)
+    filters, outer_fwd, turn, inner, spectra_stage, table_sems = refs[14:20]
+    sources = (filters_far, outer_fwd_far, turn_far, inner_far)
+    stages = (filters, outer_fwd, turn, inner)
     tables = [
         pltpu.make_async_copy(source, stage, table_sems.at[n])
         for n, (source, stage) in enumerate(zip(sources, stages))
@@ -292,16 +289,13 @@
             spectra_stage[s] = part
             send(s).start()
 
-    base_pass(0, onehot_t, others, skip, dense, outs, refs[21:], beside, 4)
+    base_pass(0, onehot_t, others, skip, dense, outs, refs[20:], beside, 4)
     for s in range(spectra.shape[0]):
         send(s).wait()
 
 
-def second_kernel(first, onehot_far, others, skip, *refs):
-    onehot_t, onehot_sem = refs[9:11]
-    copy = pltpu.make_async_copy(onehot_far, onehot_t, onehot_sem.at[0])
-    copy.start()
-    base_pass(first, onehot_t, others, skip, refs[:4], refs[5:9], refs[11:], copy.wait, 4)
+def second_kernel(first, onehot_t, others, skip, *refs):
+    base_pass(first, onehot_t, others, skip, refs[:4], refs[5:9], refs[9:], None, 4)
 
 
 def base_pass(first, onehot_t, others, skip, dense, outs, scratch, beside, ahead):
@@ -313,7 +307,8 @@
     slab = gate_stage.shape[1]
     tile = partial.shape[0]
     wait, count = fetch(dense, stages, sems, tile, first, ahead)
-    beside()
+    if beside is not None:
+        beside()
 
     def copy(i):
         at = pl.multiple_of(i * tile, tile)
@@ -323,24 +318,28 @@
 
     def step(i, _):
         start = wait(i)
-        for c in range(0, tile, CHUNK):
-            at = pl.ds(start + c, CHUNK)
-            total = jnp.zeros((CHUNK, LANES), f32)
-            for j in range(0, slab, LANES):
-                lanes = slice(j, j + LANES)
+        chunks = range(0, tile, CHUNK)
+        totals = [jnp.zeros((CHUNK, LANES), f32) for _ in chunks]
+        for j in range(0, slab, LANES):
+            lanes = slice(j, j + LANES)
+            skips = skip[:, lanes]
+            mask = others[0:1, lanes].astype(bf16)
+            for n, c in enumerate(chunks):
+                at = pl.ds(start + c, CHUNK)
                 gated = (gate_stage[at, lanes] * value_stage[at, lanes]).astype(f32)
-                mixed = out_stage[at, lanes].astype(f32) * (skip[:, lanes] * gated)
-                hidden = (res_stage[at, lanes].astype(f32) + mixed) * others[0:1, lanes]
-                hidden = hidden.astype(bf16)
+                mixed = out_stage[at, lanes].astype(f32) * (skips * gated)
+                hidden = (res_stage[at, lanes].astype(f32) + mixed).astype(bf16) * mask
                 base_stage[at, lanes] = hidden
                 hidden = hidden.astype(f32)
-                total = total + hidden * hidden
-            partial[c : c + CHUNK, :] = total
+                totals[n] = totals[n] + hidden * hidden
         copy(i).start()
+        for n, c in enumerate(chunks):
+            partial[c : c + CHUNK, :] = totals[n]
         total = jnp.sum(partial[...].T, axis=0, keepdims=True)
         at = pl.ds(start, tile)
-        picks_gate = pick_rows(out_stage[at, :], onehot_t[...], rows)
-        picks_res = pick_rows(res_stage[at, :], onehot_t[...], rows)
+        both = jnp.concatenate([out_stage[at, :], res_stage[at, :]], axis=0)
+        both = pick_rows(both, onehot_t[...], rows)
+        picks_gate, picks_res = both[: tile // LANES], both[tile // LANES :]
         for n in range(tile // LANES):
             block = i * (tile // LANES) + n
             sums[block] = total[:, n * LANES : (n + 1) * LANES]
@@ -486,7 +485,7 @@
             sds(buffer, bf16),
             picks,
             sds((8, lanes_rows), jnp.int32),
-            pltpu.HBM((slab, lanes_rows), bf16),
+            sds((slab, lanes_rows), bf16),
         ],
         [in_hbm(kept_index), in_hbm(kept_owner), gate_in, value_in],
         2 * tok_rows * slab * rows,
@@ -496,13 +495,11 @@
             pltpu.VMEM((blocks, rows, LANES), f32),
             pltpu.VMEM(whole, bf16),
             pltpu.VMEM(whole, bf16),
-            pltpu.VMEM((slab, lanes_rows), bf16),
             pltpu.VMEM((2,) + kept_index.shape, jnp.int32),
-            pltpu.SemaphoreType.DMA((3,)),
+            pltpu.SemaphoreType.DMA((2,)),
             pltpu.SemaphoreType.DMA((2, tok_rows // tile)),
         ],
         far=(0, 1, 2, 3),
-        far_outs=(3,),
     )
 
     incoming = lax.all_to_all(payload, ("seqo", "seqi"), split_axis=0, concat_axis=0, tiled=True)
@@ -527,8 +524,7 @@
     early = max(1, blocks * EARLY // 16)
     outs, scratch, flops, moved = base_parts(early)
     spectrum = (slots, outer, 2 * LANES)
-    onehot_t = in_hbm(onehot_t)
-    table_ins = [in_hbm(filters[0, 0]), outer_fwd, turn, inner, onehot_t]
+    table_ins = [in_hbm(filters[0, 0]), outer_fwd, turn, inner]
     onehot, others, skip_wide, spectra, base, *first_picks = call(
         first_kernel,
         [
@@ -538,14 +534,14 @@
             pltpu.HBM(spectrum, f32),
         ]
         + outs,
-        [channels] + table_ins + [skip_row] + dense_ins,
+        [channels] + table_ins + [onehot_t, skip_row] + dense_ins,
         flops,
         moved,
         36 * MIB,
         scratch=[pltpu.VMEM(x.shape, x.dtype) for x in table_ins]
         + [pltpu.VMEM(spectrum, f32), pltpu.SemaphoreType.DMA((len(table_ins) + slots,))]
         + scratch,
-        far=(1, 2, 3, 4, 5, 7, 8, 9, 10),
+        far=(1, 2, 3, 4, 7, 8, 9, 10),
         far_outs=(3, 4),
     )
 
@@ -570,12 +566,12 @@
     base, *more_picks = call(
         functools.partial(second_kernel, early * LANES),
         outs,
-        [in_hbm(onehot_t), others, skip_row] + dense_ins + [base],
+        [onehot_t, others, skip_row] + dense_ins + [base],
         flops,
         moved,
         36 * MIB,
-        scratch=[pltpu.VMEM(onehot_t.shape, bf16), pltpu.SemaphoreType.DMA((1,))] + scratch,
-        far=(0, 3, 4, 5, 6, 7),
+        scratch=scratch,
+        far=(3, 4, 5, 6, 7),
         far_outs=(0,),
         alias={7: 0},
     )

time: 66.3 us -> 67.1 us (1.012)
  transfers between devices with their start and end apart: 3 -> 3, of which waited for: 2 -> 1; matrix products, arithmetic and copies ran while one was open for 0% -> 0% of each run, Pallas kernels for 46% -> 47%
where the time goes in v9:
time: 67.1 us; the launch traced here: 66.7 us
  Pallas kernels  49.9 us (74%)
  starting transfers between devices  15 us (22%)
  waiting for transfers between devices  1.08 us (2%)
  between operations  0.74 us (1%)
    pallas_call x7, Pallas kernels, call(): pl.pallas_call(kernel, out_shape=outs, in_specs=[away if n in far else ne...  49.9 us
    all_to_all x1, starting transfers between devices, local(): lax.all_to_all(payload, ('seqo', 'seqi'), split_axis=0, concat_axis=0, ti...  7.37 us
    all_to_all x1, starting transfers between devices, local(): lax.all_to_all(convolved, ('seqo', 'seqi'), split_axis=0, concat_axis=0,...  6.02 us
    ppermute x1, starting transfers between devices, local(): parts.append(lax.ppermute(totals, 'chan', ring))  1.58 us
  transfers between devices with their start and end apart: 3, of which 1 were waited for; matrix products, arithmetic and copies ran while one was open for 0% of the time, Pallas kernels for 47%

profile of v9, /device:TPU:0, one launch (start us, length us, event | category | flops | bytes accessed | tf_op | source)
XLA Modules:
  0.0 66.7 jit_solution(4146684166951637523)
XLA Ops:
  0.6 0.0 copy-start
  0.6 8.4 %shard_map.140 = (bf16[16,16,768]{2,1,0:T(8,128)(2,1)}, bf16[16,96,128]{2,1,0:T(8,128)(2,1)S(1)}, s32[8,128]{1,0:T(8,128)S(1)}, bf16[2048,128]{1,0:T(8,128)(2,1)S(1)}) custom-call(s32[1,64]{1,0:T(1,128)} %index.1, s32[1,64]{1,0:T(1,128)} %owners.1, bf16[2048,2048]{1,0:T(8,128)(2,1)} %refs_0_.1, bf16[2048,2048]{1,0:T(8,128)(2,1)} %refs_1_.1), custom_call_target="tpu_custom_call" | custom-call | flops 805306368 | bytes 16777216 | tf_op jit(solution)/shard_map/pallas_call | solution.py:446
  9.1 7.4 %all-to-all-start = ((bf16[16,16,768]{2,1,0:T(8,128)(2,1)}), bf16[16,16,768]{2,1,0:T(8,128)(2,1)S(1)}, u32[]{:S(2)}, u32[]{:S(2)}) async-start(bf16[16,16,768]{2,1,0:T(8,128)(2,1)} %get-tuple-element.24), calls=%async_computation | async-start | bytes 786432 | tf_op jit(solution)/shard_map/all_to_all | solution.py:505
  16.4 0.0 copy-done
  16.5 12.9 %shard_map.141 = (bf16[96,2048]{1,0:T(8,128)(2,1)S(1)}, f32[8,2048]{1,0:T(8,128)S(1)}, f32[96,128]{1,0:T(8,128)S(1)}, f32[6,256,256]{2,1,0:T(8,128)}, bf16[2048,...) custom-call(s32[8,128]{1,0:T(8,128)S(1)} %get-tuple-element.25.chann, ...), custom_call_target="tpu_custom_call" | custom-call | flops 704643072 | bytes 18350080 | tf_op jit(solution)/shard_map/pallas_call | solution.py:446
  29.4 0.0 all-to-all-done.signals
  29.4 5.2 %shard_map.142 = bf16[16,16,768]{2,1,0:T(8,128)(2,1)} custom-call(bf16[16,16,768]{2,1,0:T(8,128)(2,1)S(1)} %all-to-all-done.signals, bf16[512,512]{1,0:T(8,128)(2,1)} %constant.8.clone.outer_fwd_far, f32[256,256]{1,0:T(8,128)} %constant.9.clone.turn_far, bf16[1024,256]{1,0:T(8,128)(2,1)} %constant.10.clone.inner_far, ...), custom_call_target="tpu_custom_call" | custom-call | flops 2214592512 | bytes 8388608 | tf_op jit(solution)/shard_map/pallas_call | solution.py:446
  34.6 6.0 %all-to-all-start.1 = ((bf16[16,16,768]{2,1,0:T(8,128)(2,1)}), bf16[16,16,768]{2,1,0:T(8,128)(2,1)S(1)}, u32[]{:S(2)}, u32[]{:S(2)}) async-start(bf16[16,16,768]{2,1,0:T(8,128)(2,1)} %shard_map.142), calls=%async_computation.1 | async-start | bytes 786432 | tf_op jit(solution)/shard_map/all_to_all | solution.py:563
  40.6 11.1 %shard_map.143 = (bf16[2048,2048]{1,0:T(8,128)(2,1)}, f32[9,1,128]{2,1,0:T(1,128)S(1)}, bf16[9,96,128]{2,1,0:T(8,128)(2,1)S(1)}, bf16[9,96,128]{2,1,0:T(8,128)(2,1)S(1)}) custom-call(bf16[2048,128]{1,0:T(8,128)(2,1)S(1)} %get-tuple-element.28.refs_0_.onehot_t, f32[8,2048]{1,0:T(8,128)S(1)} %get-tuple-element.29.others, ...), custom_call_target="tpu_custom_call", output_to_operand_aliasing={{0}: (7, {})} | custom-call | flops 905969664 | bytes 23592960 | tf_op jit(solution)/shard_map/pallas_call | solution.py:446
  51.8 0.0 copy-start.1
  51.8 1.1 %all-to-all-done.1.conv = bf16[16,16,768]{2,1,0:T(8,128)(2,1)S(1)} async-done(((bf16[16,16,768]{2,1,0:T(8,128)(2,1)}), bf16[16,16,768]{2,1,0:T(8,128)(2,1)S(1)}, u32[]{:S(2)}, u32[]{:S(2)}) %all-to-all-start.1) | async-done | bytes 393248 | tf_op jit(solution)/shard_map/all_to_all | solution.py:563
  52.8 0.6 shard_map.144
  53.4 1.6 %collective-permute-start = (f32[16,1,128]{2,1,0:T(1,128)S(1)}, f32[16,1,128]{2,1,0:T(1,128)S(1)}, u32[]{:S(2)}, u32[]{:S(2)}) collective-permute-start(f32[16,1,128]{2,1,0:T(1,128)S(1)} %get-tuple-element.44.refs_0_), channel_id=1, source_target_pairs={{0,16},{16,0},{1,17},{17,1},{2,18},{18,2},{3,19},{19,3},{4,20},{20... | collective-permute-start | bytes 24584 | tf_op jit(solution)/shard_map/ppermute | solution.py:591
  55.0 7.3 %shard_map.145 = (bf16[2048,2048]{1,0:T(8,128)(2,1)}, bf16[2048,2048]{1,0:T(8,128)(2,1)S(1)}) custom-call(bf16[2048,2048]{1,0:T(8,128)(2,1)} %get-tuple-element.31.base, bf16[16,96,128]{2,1,0:T(8,128)(2,1)S(1)} %get-tuple-element.41.hidden_kept, bf16[96,2048]{1,0:T(8,128)(2,1)S(1)} %get-tuple-element.42.onehot), custom_call_target="tpu_custom_call" | custom-call | flops 805306368 | bytes 16777216 | tf_op jit(solution)/shard_map/pallas_call | solution.py:446
  62.3 0.0 collective-permute-done.refs_1_
  62.3 0.0 copy-done.1
  62.3 4.4 %shard_map.146 = bf16[2048,2048]{1,0:T(8,128)(2,1)} custom-call(f32[16,1,128]{2,1,0:T(1,128)S(1)} %get-tuple-element.44.refs_0_, f32[16,1,128]{2,1,0:T(1,128)S(1)} %collective-permute-done.refs_1_, bf16[2048,2048]{1,0:T(8,128)(2,1)S(1)} %get-tuple-element.45.refs_2_, f32[1,2048]{1,0:T(1,128)S(1)} %bitcast.5), custom_call_target="tpu_custom_call" | custom-call | flops 16777216 | bytes 16777216 | tf_op jit(solution)/shard_map/pallas_call | solution.py:446
Async XLA Ops:
  0.6 15.8 %copy-start = (f32[2048]{0:T(1024)S(1)}, f32[2048]{0:T(1024)}, u32[]{:S(2)}) copy-start(f32[2048]{0:T(1024)} %param.20) | copy-start | bytes 24580
  9.1 20.3 %all-to-all-start = ((bf16[16,16,768]{2,1,0:T(8,128)(2,1)}), bf16[16,16,768]{2,1,0:T(8,128)(2,1)S(1)}, u32[]{:S(2)}, u32[]{:S(2)}) async-start(bf16[16,16,768]{2,1,0:T(8,128)(2,1)} %get-tuple-element.24), calls=%async_computation | async-start | bytes 786432 | tf_op jit(solution)/shard_map/all_to_all | solution.py:505
  34.6 18.2 %all-to-all-start.1 = ((bf16[16,16,768]{2,1,0:T(8,128)(2,1)}), bf16[16,16,768]{2,1,0:T(8,128)(2,1)S(1)}, u32[]{:S(2)}, u32[]{:S(2)}) async-start(bf16[16,16,768]{2,1,0:T(8,128)(2,1)} %shard_map.142), calls=%async_computation.1 | async-start | bytes 786432 | tf_op jit(solution)/shard_map/all_to_all | solution.py:563
  51.8 10.6 %copy-start.1 = (f32[2048]{0:T(1024)S(1)}, f32[2048]{0:T(1024)}, u32[]{:S(2)}) copy-start(f32[2048]{0:T(1024)} %param.21) | copy-start | bytes 24580
  53.4 8.9 %collective-permute-start = (f32[16,1,128]{2,1,0:T(1,128)S(1)}, f32[16,1,128]{2,1,0:T(1,128)S(1)}, u32[]{:S(2)}, u32[]{:S(2)}) collective-permute-start(f32[16,1,128]{2,1,0:T(1,128)S(1)} %get-tuple-element.44.refs_0_), channel_id=1, source_target_pairs={{0,16},{16,0},{1,17},{17,1},{2,18},{18,2},{3,19},{19,3},{4,20},{20... | collective-permute-start | bytes 24584 | tf_op jit(solution)/shard_map/ppermute | solution.py:591

commit v10 on v9

--- a/solution.py
+++ b/solution.py
@@ -194,7 +194,7 @@
     return [picked[:rows, i : i + LANES] for i in range(0, tile.shape[0], LANES)]
 
 
-def fetch(sources, stages, sems, tile, first=0, ahead=4):
+def fetch(sources, stages, sems, tile, first=0, ahead=3):
     count = stages[0].shape[0] // tile
 
     def copies(i):
@@ -226,9 +226,14 @@
     return wait, count
 
 
+def build_onehot(onehot_t, row):
+    onehot_t[...] = (iota(onehot_t.shape, 0) == row).astype(f32).astype(bf16)
+
+
 def pick_kernel(owner_count, slots, index, owners, gate, value, *refs):
-    payload, picked, channels, onehot_t = refs[:4]
-    acc, gate_stage, value_stage, lists, list_sems, sems = refs[4:]
+    payload, picked, channels, gated_head = refs[:4]
+    acc, gate_stage, value_stage, onehot_t, lists, list_sems, sems = refs[4:]
+    head_tiles = gated_head.shape[0] // (gate_stage.shape[0] // sems.shape[1])
     rows = owner_count * slots
     tile = gate_stage.shape[0] // sems.shape[1]
     list_copies = [
@@ -237,16 +242,21 @@
     ]
     for copy in list_copies:
         copy.start()
-    wait, count = fetch((gate, value), (gate_stage, value_stage), sems, tile)
+    wait, count = fetch((gate, value), (gate_stage, value_stage), sems, tile, 0, 4)
     for copy in list_copies:
         copy.wait()
     row = channel_of_row(lists[0], lists[1], owner_count, onehot_t.shape[1])
     channels[...] = jnp.broadcast_to(row, channels.shape)
-    onehot_t[...] = (iota(onehot_t.shape, 0) == row).astype(f32).astype(bf16)
+    build_onehot(onehot_t, row)
 
     def step(i, _):
         at = pl.ds(wait(i), tile)
         gated = gate_stage[at, :] * value_stage[at, :]
+
+        @pl.when(i < head_tiles)
+        def _():
+            gated_head[at, :] = gated
+
         for n, block in enumerate(pick_rows(gated, onehot_t[...], rows)):
             acc[i * (tile // LANES) + n] = block
             picked[i * (tile // LANES) + n] = block.astype(bf16)
@@ -259,7 +269,7 @@
 
 
 def first_kernel(channels, filters_far, outer_fwd_far, turn_far, inner_far, *refs):
-    onehot_t, skip, *dense = refs[:6]
+    gated_head, skip, *dense = refs[:6]
     onehot, others, skip_wide, spectra, *outs = refs[6:14]
     filters, outer_fwd, turn, inner, spectra_stage, table_sems = refs[14:20]
     sources = (filters_far, outer_fwd_far, turn_far, inner_far)
@@ -270,6 +280,8 @@
     ]
     for copy in tables:
         copy.start()
+    scratch = refs[20:]
+    build_onehot(scratch[0], channels[0:1, :])
     hit = iota(onehot.shape, 1) == to_column(channels[0:1, :])[: onehot.shape[0]]
     onehot[...] = hit.astype(f32).astype(bf16)
     kept = jnp.max(hit.astype(f32), axis=0, keepdims=True)
@@ -289,26 +301,33 @@
             spectra_stage[s] = part
             send(s).start()
 
-    base_pass(0, onehot_t, others, skip, dense, outs, refs[20:], beside, 4)
+    base_pass(0, gated_head, others, skip, dense, outs, None, scratch, beside)
     for s in range(spectra.shape[0]):
         send(s).wait()
 
 
-def second_kernel(first, onehot_t, others, skip, *refs):
-    base_pass(first, onehot_t, others, skip, refs[:4], refs[5:9], refs[9:], None, 4)
-
-
-def base_pass(first, onehot_t, others, skip, dense, outs, scratch, beside, ahead):
+def second_kernel(first, channels, others, skip, *refs):
+    base, tail, *outs = refs[5:10]
+    build_onehot(refs[10], channels[0:1, :])
+    base_pass(first, None, others, skip, refs[:4], [base] + outs, tail, refs[10:], None)
+
+
+def base_pass(first, head, others, skip, dense, outs, tail, scratch, beside):
     base, sums, picked_gate, picked_res = outs
-    stages = scratch[:4]
-    base_stage, partial, base_sems, sems = scratch[4:]
-    gate_stage, value_stage, out_stage, res_stage = stages
+    onehot_t, gate_stage, value_stage, out_stage, res_stage, base_stage = scratch[:6]
+    partial, base_sems, gate_sems, sems = scratch[6:]
     rows = picked_gate.shape[1]
-    slab = gate_stage.shape[1]
+    slab = out_stage.shape[1]
     tile = partial.shape[0]
-    wait, count = fetch(dense, stages, sems, tile, first, ahead)
+    head_rows = 0 if head is None else head.shape[0]
+    wait, count = fetch(dense[2:], (out_stage, res_stage), sems, tile, first)
+    wait_gate, _ = fetch(
+        dense[:2], (gate_stage, value_stage), gate_sems, tile, first + head_rows
+    )
     if beside is not None:
         beside()
+    head_tiles = head_rows // tile
+    kept_tiles = base_stage.shape[0] // tile
 
     def copy(i):
         at = pl.multiple_of(i * tile, tile)
@@ -316,8 +335,10 @@
             base_stage.at[pl.ds(at, tile), :], base.at[pl.ds(first + at, tile), :], base_sems.at[i]
         )
 
-    def step(i, _):
+    def step(i, in_head, in_tail):
         start = wait(i)
+        gate_start = start if in_head else wait_gate(i - head_tiles)
+        target, target_start = (tail, start - kept_tiles * tile) if in_tail else (base_stage, start)
         chunks = range(0, tile, CHUNK)
         totals = [jnp.zeros((CHUNK, LANES), f32) for _ in chunks]
         for j in range(0, slab, LANES):
@@ -326,13 +347,18 @@
             mask = others[0:1, lanes].astype(bf16)
             for n, c in enumerate(chunks):
                 at = pl.ds(start + c, CHUNK)
-                gated = (gate_stage[at, lanes] * value_stage[at, lanes]).astype(f32)
-                mixed = out_stage[at, lanes].astype(f32) * (skips * gated)
+                gate_at = pl.ds(gate_start + c, CHUNK)
+                if in_head:
+                    gated = head[gate_at, lanes]
+                else:
+                    gated = gate_stage[gate_at, lanes] * value_stage[gate_at, lanes]
+                mixed = out_stage[at, lanes].astype(f32) * (skips * gated.astype(f32))
                 hidden = (res_stage[at, lanes].astype(f32) + mixed).astype(bf16) * mask
-                base_stage[at, lanes] = hidden
+                target[pl.ds(pl.multiple_of(target_start + c, CHUNK), CHUNK), lanes] = hidden
                 hidden = hidden.astype(f32)
                 totals[n] = totals[n] + hidden * hidden
-        copy(i).start()
+        if not in_tail:
+            copy(i).start()
         for n, c in enumerate(chunks):
             partial[c : c + CHUNK, :] = totals[n]
         total = jnp.sum(partial[...].T, axis=0, keepdims=True)
@@ -347,8 +373,12 @@
             picked_res[block] = picks_res[n].astype(bf16)
         return 0
 
-    lax.fori_loop(0, count, step, 0)
-    lax.fori_loop(0, count, lambda i, _: (copy(i).wait(), 0)[1], 0)
+    if head_tiles:
+        lax.fori_loop(0, head_tiles, lambda i, _: step(i, True, False), 0)
+    lax.fori_loop(head_tiles, kept_tiles, lambda i, _: step(i, False, False), 0)
+    if tail is not None:
+        lax.fori_loop(kept_tiles, count, lambda i, _: step(i, False, True), 0)
+    lax.fori_loop(0, kept_tiles, lambda i, _: (copy(i).wait(), 0)[1], 0)
 
 
 def kept_kernel(conv, picked, skip_wide, *refs):
@@ -375,30 +405,33 @@
         first = first + size
 
 
-def hidden_kernel(base, hidden_kept, onehot, hidden, held, base_stage, base_sems, sems):
+def hidden_kernel(base, tail, hidden_kept, onehot, hidden, held, base_stage, base_sems, sems):
     slab = held.shape[1]
     wide = min(slab, 2 * LANES)
     count = sems.shape[0]
     tile = held.shape[0] // count
-    wait, _ = fetch((base,), (base_stage,), base_sems, tile)
+    tail_tiles = tail.shape[0] // tile
+    wait, staged = fetch((base,), (base_stage,), base_sems, tile, 0, 4)
 
     def copy(i):
         rows = pl.ds(pl.multiple_of(i * tile, tile), tile)
         return pltpu.make_async_copy(held.at[rows, :], hidden.at[rows, :], sems.at[i])
 
-    def step(i, _):
+    def step(i, source, start):
         blocks = range(tile // LANES)
         kept = [hidden_kept[i * (tile // LANES) + n].astype(f32).T.astype(bf16) for n in blocks]
         kept = jnp.concatenate(kept, axis=0)
-        rows = pl.ds(wait(i), tile)
+        rows = pl.ds(pl.multiple_of(i * tile, tile), tile)
         for j in range(0, slab, wide):
             lanes = slice(j, j + wide)
             placed = dot(kept, onehot[:, lanes]).astype(bf16)
-            held[rows, lanes] = base_stage[rows, lanes] + placed
+            held[rows, lanes] = source[pl.ds(start, tile), lanes] + placed
         copy(i).start()
         return 0
 
-    lax.fori_loop(0, count, step, 0)
+    for n in range(tail_tiles):
+        step(staged + n, tail, n * tile)
+    lax.fori_loop(0, staged, lambda i, _: step(i, base_stage, wait(i)), 0)
     lax.fori_loop(0, count, lambda i, _: (copy(i).wait(), 0)[1], 0)
 
 
@@ -478,14 +511,16 @@
     row_sums = sds((blocks, 1, LANES), f32)
     buffer = (owner_count, blocks, slots * LANES)
     whole = (tok_rows, slab)
-
-    payload, picked, channels, onehot_t = call(
+    head_rows = tok_rows // 4 // tile * tile
+    tail_rows = tok_rows // 8 // tile * tile
+
+    payload, picked, channels, gated_head = call(
         functools.partial(pick_kernel, owner_count, slots),
         [
             sds(buffer, bf16),
             picks,
             sds((8, lanes_rows), jnp.int32),
-            sds((slab, lanes_rows), bf16),
+            pltpu.VMEM((head_rows, slab), bf16),
         ],
         [in_hbm(kept_index), in_hbm(kept_owner), gate_in, value_in],
         2 * tok_rows * slab * rows,
@@ -495,6 +530,7 @@
             pltpu.VMEM((blocks, rows, LANES), f32),
             pltpu.VMEM(whole, bf16),
             pltpu.VMEM(whole, bf16),
+            pltpu.VMEM((slab, lanes_rows), bf16),
             pltpu.VMEM((2,) + kept_index.shape, jnp.int32),
             pltpu.SemaphoreType.DMA((2,)),
             pltpu.SemaphoreType.DMA((2, tok_rows // tile)),
@@ -506,7 +542,7 @@
 
     dense_ins = [gate_in, value_in, out_gate, residual]
 
-    def base_parts(count):
+    def base_parts(count, head, tail):
         part = count * LANES
         outs = [
             pltpu.HBM(whole, bf16),
@@ -514,15 +550,22 @@
             sds((count, rows, LANES), bf16),
             sds((count, rows, LANES), bf16),
         ]
-        scratch = [pltpu.VMEM((part, slab), bf16)] * 5 + [
+        scratch = [
+            pltpu.VMEM((slab, lanes_rows), bf16),
+            pltpu.VMEM((part - head, slab), bf16),
+            pltpu.VMEM((part - head, slab), bf16),
+            pltpu.VMEM((part, slab), bf16),
+            pltpu.VMEM((part, slab), bf16),
+            pltpu.VMEM((part - tail, slab), bf16),
             pltpu.VMEM((LANES, LANES), f32),
-            pltpu.SemaphoreType.DMA((count,)),
-            pltpu.SemaphoreType.DMA((4, count)),
+            pltpu.SemaphoreType.DMA(((part - tail) // LANES,)),
+            pltpu.SemaphoreType.DMA((2, (part - head) // LANES)),
+            pltpu.SemaphoreType.DMA((2, count)),
         ]
         return outs, scratch, 4 * part * slab * rows, 10 * part * slab
 
-    early = max(1, blocks * EARLY // 16)
-    outs, scratch, flops, moved = base_parts(early)
+    early = max(head_rows // LANES + 1, blocks * EARLY // 16)
+    outs, scratch, flops, moved = base_parts(early, head_rows, 0)
     spectrum = (slots, outer, 2 * LANES)
     table_ins = [in_hbm(filters[0, 0]), outer_fwd, turn, inner]
     onehot, others, skip_wide, spectra, base, *first_picks = call(
@@ -534,7 +577,7 @@
             pltpu.HBM(spectrum, f32),
         ]
         + outs,
-        [channels] + table_ins + [onehot_t, skip_row] + dense_ins,
+        [channels] + table_ins + [in_vmem(gated_head), skip_row] + dense_ins,
         flops,
         moved,
         36 * MIB,
@@ -558,15 +601,15 @@
         far=tuple(range(1, len(conv_ins))),
         far_outs=(0,),
     )
-    convolved, onehot_t = lax.optimization_barrier((convolved, onehot_t))
+    convolved, channels = lax.optimization_barrier((convolved, channels))
 
     returned = lax.all_to_all(convolved, ("seqo", "seqi"), split_axis=0, concat_axis=0, tiled=True)
 
-    outs, scratch, flops, moved = base_parts(blocks - early)
-    base, *more_picks = call(
+    outs, scratch, flops, moved = base_parts(blocks - early, 0, tail_rows)
+    base, tail, *more_picks = call(
         functools.partial(second_kernel, early * LANES),
-        outs,
-        [onehot_t, others, skip_row] + dense_ins + [base],
+        [outs[0], pltpu.VMEM((tail_rows, slab), bf16)] + outs[1:],
+        [channels, others, skip_row] + dense_ins + [base],
         flops,
         moved,
         36 * MIB,
@@ -593,13 +636,13 @@
     hidden, held = call(
         hidden_kernel,
         [pltpu.HBM(whole, bf16), pltpu.VMEM(whole, bf16)],
-        [in_hbm(base), hidden_kept, onehot],
+        [in_hbm(base), in_vmem(tail), hidden_kept, onehot],
         2 * tok_rows * slab * rows,
         2 * dense,
         16 * MIB,
         scratch=[
-            pltpu.VMEM(whole, bf16),
-            pltpu.SemaphoreType.DMA((1, tok_rows // tile)),
+            pltpu.VMEM((tok_rows - tail_rows, slab), bf16),
+            pltpu.SemaphoreType.DMA((1, (tok_rows - tail_rows) // tile)),
             pltpu.SemaphoreType.DMA((tok_rows // tile,)),
         ],
         far=(0,),

time: 67.1 us -> 68.3 us (1.018)
  local copies, waits for them, and re-layouts: 0.01 us -> 2.07 us
  Pallas kernels: 49.9 us -> 48 us
  waiting for transfers between devices: 1.08 us -> 2.15 us
    unnamed x4 -> x12, local copies, waits for them, and re-layouts: 0.01 us -> 2.07 us
    pallas_call x7, Pallas kernels: 49.9 us -> 48 us  [call(): pl.pallas_call(kernel, out_shape=outs, in_specs=[away if n in far else ne...]
    all_to_all x1, waiting for transfers between devices: 1.08 us -> 2.15 us  [local(): lax.all_to_all(convolved, ('seqo', 'seqi'), split_axis=0, concat_axis=0,...]
  transfers between devices with their start and end apart: 3 -> 3, of which waited for: 1 -> 1; matrix products, arithmetic and copies ran while one was open for 0% -> 0% of each run, Pallas kernels for 47% -> 42%
where the time goes in v10:
time: 68.3 us; the launch traced here: 67.9 us
  Pallas kernels  48 us (70%)
  starting transfers between devices  15 us (22%)
  waiting for transfers between devices  2.15 us (3%)
  local copies, waits for them, and re-layouts  2.07 us (3%)
  between operations  0.75 us (1%)
    pallas_call x7, Pallas kernels, call(): pl.pallas_call(kernel, out_shape=outs, in_specs=[away if n in far else ne...  48 us
    all_to_all x1, starting transfers between devices, local(): lax.all_to_all(payload, ('seqo', 'seqi'), split_axis=0, concat_axis=0, ti...  7.37 us
    all_to_all x1, starting transfers between devices, local(): lax.all_to_all(convolved, ('seqo', 'seqi'), split_axis=0, concat_axis=0,...  6.02 us
    all_to_all x1, waiting for transfers between devices, local(): lax.all_to_all(convolved, ('seqo', 'seqi'), split_axis=0, concat_axis=0,...  2.15 us
    unnamed x12, local copies, waits for them, and re-layouts  2.07 us
    ppermute x1, starting transfers between devices, local(): parts.append(lax.ppermute(totals, 'chan', ring))  1.59 us
  transfers between devices with their start and end apart: 3, of which 1 were waited for; matrix products, arithmetic and copies ran while one was open for 0% of the time, Pallas kernels for 42%

profile of v10, /device:TPU:0, one launch (start us, length us, event | category | flops | bytes accessed | tf_op | source)
XLA Modules:
  0.0 67.9 jit_solution(9265396709787443417)
XLA Ops:
  0.6 0.0 copy-start.4
  0.6 9.2 %shard_map.140 = (bf16[16,16,768]{2,1,0:T(8,128)(2,1)}, bf16[16,96,128]{2,1,0:T(8,128)(2,1)S(1)}, s32[8,128]{1,0:T(8,128)S(1)}, bf16[512,2048]{1,0:T(8,128)(2,1)S(1)}) custom-call(s32[1,64]{1,0:T(1,128)} %index.1, s32[1,64]{1,0:T(1,128)} %owners.1, bf16[2048,2048]{1,0:T(8,128)(2,1)} %refs_0_.1, bf16[2048,2048]{1,0:T(8,128)(2,1)} %refs_1_.1), custom_call_target="tpu_custom_call" | custom-call | flops 805306368 | bytes 16777216 | tf_op jit(solution)/shard_map/pallas_call | solution.py:479
  9.8 7.4 %all-to-all-start = ((bf16[16,16,768]{2,1,0:T(8,128)(2,1)}), bf16[16,16,768]{2,1,0:T(8,128)(2,1)S(1)}, u32[]{:S(2)}, u32[]{:S(2)}) async-start(bf16[16,16,768]{2,1,0:T(8,128)(2,1)} %get-tuple-element.25), calls=%async_computation | async-start | bytes 786432 | tf_op jit(solution)/shard_map/all_to_all | solution.py:541
  17.2 0.0 copy-done.4
  17.2 11.5 %shard_map.141 = (bf16[96,2048]{1,0:T(8,128)(2,1)S(1)}, f32[8,2048]{1,0:T(8,128)S(1)}, f32[96,128]{1,0:T(8,128)S(1)}, f32[6,256,256]{2,1,0:T(8,128)}, bf16[2048,...) custom-call(s32[8,128]{1,0:T(8,128)S(1)} %get-tuple-element.29.chann, ...), custom_call_target="tpu_custom_call" | custom-call | flops 704643072 | bytes 18350080 | tf_op jit(solution)/shard_map/pallas_call | solution.py:479
  28.8 0.0 copy-start
  28.8 0.6 copy-done
  29.4 0.0 copy-start.2
  29.4 0.6 copy-done.2
  30.0 0.0 all-to-all-done.signals
  30.0 5.2 %shard_map.142 = bf16[16,16,768]{2,1,0:T(8,128)(2,1)} custom-call(bf16[16,16,768]{2,1,0:T(8,128)(2,1)S(1)} %all-to-all-done.signals, bf16[512,512]{1,0:T(8,128)(2,1)} %constant.8.clone.outer_fwd_far, f32[256,256]{1,0:T(8,128)} %constant.9.clone.turn_far, bf16[1024,256]{1,0:T(8,128)(2,1)} %constant.10.clone.inner_far, ...), custom_call_target="tpu_custom_call" | custom-call | flops 2214592512 | bytes 8388608 | tf_op jit(solution)/shard_map/pallas_call | solution.py:479
  35.3 6.0 %all-to-all-start.1 = ((bf16[16,16,768]{2,1,0:T(8,128)(2,1)}), bf16[16,16,768]{2,1,0:T(8,128)(2,1)S(1)}, u32[]{:S(2)}, u32[]{:S(2)}) async-start(bf16[16,16,768]{2,1,0:T(8,128)(2,1)} %shard_map.142), calls=%async_computation.1 | async-start | bytes 786432 | tf_op jit(solution)/shard_map/all_to_all | solution.py:606
  41.3 0.0 copy-start.1
  41.3 10.0 %shard_map.143 = (bf16[2048,2048]{1,0:T(8,128)(2,1)}, bf16[256,2048]{1,0:T(8,128)(2,1)S(1)}, f32[9,1,128]{2,1,0:T(1,128)S(1)}, bf16[9,96,128]{2,1,0:T(8,128)(2,1)S(1)}, bf16[9,96,128]{2,1,0:T(8,128)(2,1)S(1)}) custom-call(s32[8,128]{1,0:T(8,128)S(1)} %get-tuple-element.29.channels, ...), custom_call_target="tpu_custom_call", output_to_operand_aliasing={{0}: (7, {})} | custom-call | flops 905969664 | bytes 23592960 | tf_op jit(solution)/shard_map/pallas_call | solution.py:479
  51.3 0.0 copy-start.5
  51.3 2.1 %all-to-all-done.1.conv = bf16[16,16,768]{2,1,0:T(8,128)(2,1)S(1)} async-done(((bf16[16,16,768]{2,1,0:T(8,128)(2,1)}), bf16[16,16,768]{2,1,0:T(8,128)(2,1)S(1)}, u32[]{:S(2)}, u32[]{:S(2)}) %all-to-all-start.1) | async-done | bytes 393248 | tf_op jit(solution)/shard_map/all_to_all | solution.py:606
  53.5 0.0 copy-done.1
  53.5 0.0 copy-start.3
  53.5 0.8 %copy-done.3 = f32[96,128]{1,0:T(8,128)S(1)} copy-done((f32[96,128]{1,0:T(8,128)S(1)}, f32[96,128]{1,0:T(8,128)}, u32[]{:S(2)}) %copy-start.3) | copy-done | bytes 49176
  54.3 0.6 shard_map.144
  54.9 1.6 %collective-permute-start = (f32[16,1,128]{2,1,0:T(1,128)S(1)}, f32[16,1,128]{2,1,0:T(1,128)S(1)}, u32[]{:S(2)}, u32[]{:S(2)}) collective-permute-start(f32[16,1,128]{2,1,0:T(1,128)S(1)} %get-tuple-element.46.refs_0_), channel_id=1, source_target_pairs={{0,16},{16,0},{1,17},{17,1},{2,18},{18,2},{3,19},{19,3},{4,20},{20... | collective-permute-start | bytes 24584 | tf_op jit(solution)/shard_map/ppermute | solution.py:634
  56.5 7.0 %shard_map.145 = (bf16[2048,2048]{1,0:T(8,128)(2,1)}, bf16[2048,2048]{1,0:T(8,128)(2,1)S(1)}) custom-call(bf16[2048,2048]{1,0:T(8,128)(2,1)} %get-tuple-element.32.base, bf16[256,2048]{1,0:T(8,128)(2,1)S(1)} %get-tuple-element.33.tail, bf16[16,96,128]{2,1,0:T(8,128)(2,1)S(1)} %get-tuple-element.43.hidden_kept, bf16[96,2048]{1,0:T(8,128)(2,1)S(1)} %get-tuple-element.44.onehot), custom_call_target="tpu_custom_call" | custom-call | flops 805306368 | bytes 16777216 | tf_op jit(solution)/shard_map/pallas_call | solution.py:479
  63.5 0.0 collective-permute-done.refs_1_
  63.5 0.0 copy-done.5
  63.5 4.4 %shard_map.146 = bf16[2048,2048]{1,0:T(8,128)(2,1)} custom-call(f32[16,1,128]{2,1,0:T(1,128)S(1)} %get-tuple-element.46.refs_0_, f32[16,1,128]{2,1,0:T(1,128)S(1)} %collective-permute-done.refs_1_, bf16[2048,2048]{1,0:T(8,128)(2,1)S(1)} %get-tuple-element.47.refs_2_, f32[1,2048]{1,0:T(1,128)S(1)} %bitcast.5), custom_call_target="tpu_custom_call" | custom-call | flops 16777216 | bytes 16777216 | tf_op jit(solution)/shard_map/pallas_call | solution.py:479
Async XLA Ops:
  0.6 16.6 %copy-start.4 = (f32[2048]{0:T(1024)S(1)}, f32[2048]{0:T(1024)}, u32[]{:S(2)}) copy-start(f32[2048]{0:T(1024)} %param.20) | copy-start | bytes 24580
  9.8 20.2 %all-to-all-start = ((bf16[16,16,768]{2,1,0:T(8,128)(2,1)}), bf16[16,16,768]{2,1,0:T(8,128)(2,1)S(1)}, u32[]{:S(2)}, u32[]{:S(2)}) async-start(bf16[16,16,768]{2,1,0:T(8,128)(2,1)} %get-tuple-element.25), calls=%async_computation | async-start | bytes 786432 | tf_op jit(solution)/shard_map/all_to_all | solution.py:541
  28.8 0.7 copy-start
  29.4 0.6 copy-start.2
  35.3 18.2 %all-to-all-start.1 = ((bf16[16,16,768]{2,1,0:T(8,128)(2,1)}), bf16[16,16,768]{2,1,0:T(8,128)(2,1)S(1)}, u32[]{:S(2)}, u32[]{:S(2)}) async-start(bf16[16,16,768]{2,1,0:T(8,128)(2,1)} %shard_map.142), calls=%async_computation.1 | async-start | bytes 786432 | tf_op jit(solution)/shard_map/all_to_all | solution.py:606
  41.3 12.2 %copy-start.1 = (bf16[7,96,128]{2,1,0:T(8,128)(2,1)S(1)}, bf16[7,96,128]{2,1,0:T(8,128)(2,1)}, u32[]{:S(2)}) copy-start(bf16[7,96,128]{2,1,0:T(8,128)(2,1)} %copy-done) | copy-start | bytes 516100
  51.3 12.2 %copy-start.5 = (f32[2048]{0:T(1024)S(1)}, f32[2048]{0:T(1024)}, u32[]{:S(2)}) copy-start(f32[2048]{0:T(1024)} %param.21) | copy-start | bytes 24580
  53.5 0.8 %copy-start.3 = (f32[96,128]{1,0:T(8,128)S(1)}, f32[96,128]{1,0:T(8,128)}, u32[]{:S(2)}) copy-start(f32[96,128]{1,0:T(8,128)} %copy-done.2) | copy-start | bytes 147460
  54.9 8.6 %collective-permute-start = (f32[16,1,128]{2,1,0:T(1,128)S(1)}, f32[16,1,128]{2,1,0:T(1,128)S(1)}, u32[]{:S(2)}, u32[]{:S(2)}) collective-permute-start(f32[16,1,128]{2,1,0:T(1,128)S(1)} %get-tuple-element.46.refs_0_), channel_id=1, source_target_pairs={{0,16},{16,0},{1,17},{17,1},{2,18},{18,2},{3,19},{19,3},{4,20},{20... | collective-permute-start | bytes 24584 | tf_op jit(solution)/shard_map/ppermute | solution.py:634

commit v11 on v9

--- a/solution.py
+++ b/solution.py
@@ -12,7 +12,7 @@
 TILE = 256
 CHUNK = 16
 GROUP = 3
-EARLY = 7
+EARLY = 8
 MIB = 1 << 20
 norm_eps = 1e-06
 f32 = jnp.float32
@@ -113,10 +113,10 @@
 
 
 def convolve_kernel(
-    signals, outer_fwd_far, turn_far, inner_far, spectra_far, outer_back_far, out, *scratch
+    signals, spectra, outer_fwd_far, turn_far, inner_far, outer_back_far, out, *scratch
 ):
-    sources = (outer_fwd_far, turn_far, inner_far, spectra_far, outer_back_far)
-    outer_fwd, turn_ref, inner, spectra, outer_back, result, sems = scratch
+    sources = (outer_fwd_far, turn_far, inner_far, outer_back_far)
+    outer_fwd, turn_ref, inner, outer_back, result, sems = scratch
     copies = [
         pltpu.make_async_copy(source, scratch[n], sems.at[n]) for n, source in enumerate(sources)
     ]
@@ -137,7 +137,6 @@
     parts = to_spectrum(blocks, slots, outer_fwd[...], turn_now, inner_now)
     turn = turn_ref[...]
     cos, sin = turn[:, :LANES], turn[:, LANES:]
-    copies[3].wait()
     joint = []
     for s in range(slots):
         sig_re, sig_im = parts[s][:, :LANES], parts[s][:, LANES:]
@@ -151,7 +150,7 @@
     for back in grouped(joint, inner[4 * LANES :, :]):
         re, im = back[:, :LANES], back[:, LANES:]
         turned.append(jnp.concatenate([re * cos - im * sin, im * cos + re * sin], axis=0))
-    copies[4].wait()
+    copies[3].wait()
     sends = []
     for s in range(0, slots, 2):
         pair = turned[s : s + 2]
@@ -189,12 +188,14 @@
     return jnp.sum(jnp.where(hit, index_col + 1, 0), axis=0, keepdims=True) - 1
 
 
-def pick_rows(tile, onehot_t, rows):
-    picked = dot(tile, onehot_t).T
-    return [picked[:rows, i : i + LANES] for i in range(0, tile.shape[0], LANES)]
-
-
-def fetch(sources, stages, sems, tile, first=0, ahead=4):
+def pick_rows(onehot, tile):
+    picked = lax.dot_general(
+        onehot, tile, (((1,), (1,)), ((), ())), preferred_element_type=f32
+    )
+    return [picked[:, i : i + LANES] for i in range(0, tile.shape[0], LANES)]
+
+
+def fetch(sources, stages, sems, tile, first=0, ahead=3):
     count = stages[0].shape[0] // tile
 
     def copies(i):
@@ -226,10 +227,15 @@
     return wait, count
 
 
+def build_onehot(onehot, row):
+    hit = iota(onehot.shape, 1) == to_column(row)[: onehot.shape[0]]
+    onehot[...] = hit.astype(f32).astype(bf16)
+    return hit
+
+
 def pick_kernel(owner_count, slots, index, owners, gate, value, *refs):
-    payload, picked, channels, onehot_t = refs[:4]
-    acc, gate_stage, value_stage, lists, list_sems, sems = refs[4:]
-    rows = owner_count * slots
+    payload, picked, channels, gated_head = refs[:4]
+    acc, gate_stage, value_stage, onehot, lists, list_sems, sems = refs[4:]
     tile = gate_stage.shape[0] // sems.shape[1]
     list_copies = [
         pltpu.make_async_copy(source, lists.at[n], list_sems.at[n])
@@ -237,78 +243,67 @@
     ]
     for copy in list_copies:
         copy.start()
-    wait, count = fetch((gate, value), (gate_stage, value_stage), sems, tile)
+    wait, count = fetch((gate, value), (gate_stage, value_stage), sems, tile, 0, 4)
     for copy in list_copies:
         copy.wait()
-    row = channel_of_row(lists[0], lists[1], owner_count, onehot_t.shape[1])
+    row = channel_of_row(lists[0], lists[1], owner_count, channels.shape[1])
     channels[...] = jnp.broadcast_to(row, channels.shape)
-    onehot_t[...] = (iota(onehot_t.shape, 0) == row).astype(f32).astype(bf16)
-
-    def step(i, _):
+    build_onehot(onehot, row)
+
+    def step(i, in_head):
         at = pl.ds(wait(i), tile)
         gated = gate_stage[at, :] * value_stage[at, :]
-        for n, block in enumerate(pick_rows(gated, onehot_t[...], rows)):
+        if in_head:
+            gated_head[at, :] = gated
+        for n, block in enumerate(pick_rows(onehot[...], gated)):
             acc[i * (tile // LANES) + n] = block
             picked[i * (tile // LANES) + n] = block.astype(bf16)
         return 0
 
-    lax.fori_loop(0, count, step, 0)
+    head_tiles = gated_head.shape[0] // tile
+    lax.fori_loop(0, head_tiles, lambda i, _: step(i, True), 0)
+    lax.fori_loop(head_tiles, count, lambda i, _: step(i, False), 0)
     for s in range(slots):
         part = jnp.swapaxes(acc[:, s * owner_count : (s + 1) * owner_count, :], 0, 1)
         payload[:, :, s * LANES : (s + 1) * LANES] = part.astype(bf16)
 
 
-def first_kernel(channels, filters_far, outer_fwd_far, turn_far, inner_far, *refs):
-    onehot_t, skip, *dense = refs[:6]
-    onehot, others, skip_wide, spectra, *outs = refs[6:14]
-    filters, outer_fwd, turn, inner, spectra_stage, table_sems = refs[14:20]
-    sources = (filters_far, outer_fwd_far, turn_far, inner_far)
-    stages = (filters, outer_fwd, turn, inner)
-    tables = [
-        pltpu.make_async_copy(source, stage, table_sems.at[n])
-        for n, (source, stage) in enumerate(zip(sources, stages))
-    ]
-    for copy in tables:
-        copy.start()
-    hit = iota(onehot.shape, 1) == to_column(channels[0:1, :])[: onehot.shape[0]]
-    onehot[...] = hit.astype(f32).astype(bf16)
-    kept = jnp.max(hit.astype(f32), axis=0, keepdims=True)
-    others[...] = jnp.broadcast_to(1.0 - kept, others.shape)
-    skip_col = jnp.sum(jnp.where(hit, skip[...], 0.0), axis=1, keepdims=True)
-    skip_wide[...] = jnp.broadcast_to(skip_col, skip_wide.shape)
-
-    def send(s):
-        return pltpu.make_async_copy(
-            spectra_stage.at[s], spectra.at[s], table_sems.at[len(tables) + s]
-        )
+def filter_kernel(filters, outer_fwd, turn, inner, spectra):
+    for s, part in enumerate(filter_spectra(filters, outer_fwd, turn, inner)):
+        spectra[s] = part
+
+
+def first_kernel(channels, gated_head, skip, *refs):
+    onehot, others, skip_wide, *outs = refs[4:11]
 
     def beside():
-        for copy in tables:
-            copy.wait()
-        for s, part in enumerate(filter_spectra(filters, outer_fwd, turn, inner)):
-            spectra_stage[s] = part
-            send(s).start()
-
-    base_pass(0, onehot_t, others, skip, dense, outs, refs[20:], beside, 4)
-    for s in range(spectra.shape[0]):
-        send(s).wait()
-
-
-def second_kernel(first, onehot_t, others, skip, *refs):
-    base_pass(first, onehot_t, others, skip, refs[:4], refs[5:9], refs[9:], None, 4)
-
-
-def base_pass(first, onehot_t, others, skip, dense, outs, scratch, beside, ahead):
+        hit = build_onehot(onehot, channels[0:1, :])
+        kept = jnp.max(hit.astype(f32), axis=0, keepdims=True)
+        others[...] = jnp.broadcast_to(1.0 - kept, others.shape)
+        skip_col = jnp.sum(jnp.where(hit, skip[...], 0.0), axis=1, keepdims=True)
+        skip_wide[...] = jnp.broadcast_to(skip_col, skip_wide.shape)
+
+    base_pass(0, gated_head, onehot, others, skip, refs[:4], outs, refs[11:], beside)
+
+
+def second_kernel(first, onehot, others, skip, *refs):
+    base_pass(first, None, onehot, others, skip, refs[:4], refs[5:9], refs[9:], None)
+
+
+def base_pass(first, head, onehot, others, skip, dense, outs, scratch, beside):
     base, sums, picked_gate, picked_res = outs
-    stages = scratch[:4]
-    base_stage, partial, base_sems, sems = scratch[4:]
-    gate_stage, value_stage, out_stage, res_stage = stages
-    rows = picked_gate.shape[1]
-    slab = gate_stage.shape[1]
+    gate_stage, value_stage, out_stage, res_stage, base_stage = scratch[:5]
+    partial, base_sems, gate_sems, sems = scratch[5:]
+    slab = out_stage.shape[1]
     tile = partial.shape[0]
-    wait, count = fetch(dense, stages, sems, tile, first, ahead)
+    head_rows = 0 if head is None else head.shape[0]
+    wait, count = fetch(dense[2:], (out_stage, res_stage), sems, tile, first)
+    wait_gate, _ = fetch(
+        dense[:2], (gate_stage, value_stage), gate_sems, tile, first + head_rows
+    )
     if beside is not None:
         beside()
+    head_tiles = head_rows // tile
 
     def copy(i):
         at = pl.multiple_of(i * tile, tile)
@@ -316,8 +311,9 @@
             base_stage.at[pl.ds(at, tile), :], base.at[pl.ds(first + at, tile), :], base_sems.at[i]
         )
 
-    def step(i, _):
+    def step(i, in_head):
         start = wait(i)
+        gate_start = start if in_head else wait_gate(i - head_tiles)
         chunks = range(0, tile, CHUNK)
         totals = [jnp.zeros((CHUNK, LANES), f32) for _ in chunks]
         for j in range(0, slab, LANES):
@@ -326,8 +322,12 @@
             mask = others[0:1, lanes].astype(bf16)
             for n, c in enumerate(chunks):
                 at = pl.ds(start + c, CHUNK)
-                gated = (gate_stage[at, lanes] * value_stage[at, lanes]).astype(f32)
-                mixed = out_stage[at, lanes].astype(f32) * (skips * gated)
+                gate_at = pl.ds(gate_start + c, CHUNK)
+                if in_head:
+                    gated = head[gate_at, lanes]
+                else:
+                    gated = gate_stage[gate_at, lanes] * value_stage[gate_at, lanes]
+                mixed = out_stage[at, lanes].astype(f32) * (skips * gated.astype(f32))
                 hidden = (res_stage[at, lanes].astype(f32) + mixed).astype(bf16) * mask
                 base_stage[at, lanes] = hidden
                 hidden = hidden.astype(f32)
@@ -338,7 +338,7 @@
         total = jnp.sum(partial[...].T, axis=0, keepdims=True)
         at = pl.ds(start, tile)
         both = jnp.concatenate([out_stage[at, :], res_stage[at, :]], axis=0)
-        both = pick_rows(both, onehot_t[...], rows)
+        both = pick_rows(onehot[...], both)
         picks_gate, picks_res = both[: tile // LANES], both[tile // LANES :]
         for n in range(tile // LANES):
             block = i * (tile // LANES) + n
@@ -347,7 +347,9 @@
             picked_res[block] = picks_res[n].astype(bf16)
         return 0
 
-    lax.fori_loop(0, count, step, 0)
+    if head_tiles:
+        lax.fori_loop(0, head_tiles, lambda i, _: step(i, True), 0)
+    lax.fori_loop(head_tiles, count, lambda i, _: step(i, False), 0)
     lax.fori_loop(0, count, lambda i, _: (copy(i).wait(), 0)[1], 0)
 
 
@@ -380,7 +382,7 @@
     wide = min(slab, 2 * LANES)
     count = sems.shape[0]
     tile = held.shape[0] // count
-    wait, _ = fetch((base,), (base_stage,), base_sems, tile)
+    wait, _ = fetch((base,), (base_stage,), base_sems, tile, 0, 4)
 
     def copy(i):
         rows = pl.ds(pl.multiple_of(i * tile, tile), tile)
@@ -478,14 +480,15 @@
     row_sums = sds((blocks, 1, LANES), f32)
     buffer = (owner_count, blocks, slots * LANES)
     whole = (tok_rows, slab)
-
-    payload, picked, channels, onehot_t = call(
+    head_rows = tok_rows // 4 // tile * tile
+
+    payload, picked, channels, gated_head = call(
         functools.partial(pick_kernel, owner_count, slots),
         [
             sds(buffer, bf16),
             picks,
             sds((8, lanes_rows), jnp.int32),
-            sds((slab, lanes_rows), bf16),
+            pltpu.VMEM((head_rows, slab), bf16),
         ],
         [in_hbm(kept_index), in_hbm(kept_owner), gate_in, value_in],
         2 * tok_rows * slab * rows,
@@ -495,6 +498,7 @@
             pltpu.VMEM((blocks, rows, LANES), f32),
             pltpu.VMEM(whole, bf16),
             pltpu.VMEM(whole, bf16),
+            pltpu.VMEM((rows, slab), bf16),
             pltpu.VMEM((2,) + kept_index.shape, jnp.int32),
             pltpu.SemaphoreType.DMA((2,)),
             pltpu.SemaphoreType.DMA((2, tok_rows // tile)),
@@ -506,7 +510,7 @@
 
     dense_ins = [gate_in, value_in, out_gate, residual]
 
-    def base_parts(count):
+    def base_parts(count, head):
         part = count * LANES
         outs = [
             pltpu.HBM(whole, bf16),
@@ -514,38 +518,43 @@
             sds((count, rows, LANES), bf16),
             sds((count, rows, LANES), bf16),
         ]
-        scratch = [pltpu.VMEM((part, slab), bf16)] * 5 + [
+        scratch = [
+            pltpu.VMEM((part - head, slab), bf16),
+            pltpu.VMEM((part - head, slab), bf16),
+            pltpu.VMEM((part, slab), bf16),
+            pltpu.VMEM((part, slab), bf16),
+            pltpu.VMEM((part, slab), bf16),
             pltpu.VMEM((LANES, LANES), f32),
             pltpu.SemaphoreType.DMA((count,)),
-            pltpu.SemaphoreType.DMA((4, count)),
+            pltpu.SemaphoreType.DMA((2, (part - head) // LANES)),
+            pltpu.SemaphoreType.DMA((2, count)),
         ]
         return outs, scratch, 4 * part * slab * rows, 10 * part * slab
 
-    early = max(1, blocks * EARLY // 16)
-    outs, scratch, flops, moved = base_parts(early)
-    spectrum = (slots, outer, 2 * LANES)
-    table_ins = [in_hbm(filters[0, 0]), outer_fwd, turn, inner]
-    onehot, others, skip_wide, spectra, base, *first_picks = call(
+    early = max(head_rows // LANES + 1, blocks * EARLY // 16)
+    outs, scratch, flops, moved = base_parts(early, head_rows)
+    onehot, others, skip_wide, base, *first_picks = call(
         first_kernel,
-        [
-            sds((rows, slab), bf16),
-            sds((8, slab), f32),
-            sds((rows, LANES), f32),
-            pltpu.HBM(spectrum, f32),
-        ]
-        + outs,
-        [channels] + table_ins + [onehot_t, skip_row] + dense_ins,
+        [sds((rows, slab), bf16), sds((8, slab), f32), sds((rows, LANES), f32)] + outs,
+        [channels, in_vmem(gated_head), skip_row] + dense_ins,
         flops,
         moved,
         36 * MIB,
-        scratch=[pltpu.VMEM(x.shape, x.dtype) for x in table_ins]
-        + [pltpu.VMEM(spectrum, f32), pltpu.SemaphoreType.DMA((len(table_ins) + slots,))]
-        + scratch,
-        far=(1, 2, 3, 4, 7, 8, 9, 10),
-        far_outs=(3, 4),
-    )
-
-    conv_ins = [incoming, outer_fwd, turn, inner, in_hbm(spectra), outer_back]
+        scratch=scratch,
+        far=(3, 4, 5, 6),
+        far_outs=(3,),
+    )
+    (spectra,) = call(
+        filter_kernel,
+        [pltpu.VMEM((slots, outer, 2 * LANES), f32)],
+        [filters[0, 0]] + [jnp.asarray(x) for x in dft_tables(length)[:3]],
+        2 * slots * length * 2 * (2 * outer + 6 * LANES),
+        4 * MIB,
+        16 * MIB,
+    )
+    spectra, base = lax.optimization_barrier((spectra, base))
+
+    conv_ins = [incoming, in_vmem(spectra), outer_fwd, turn, inner, outer_back]
     (convolved,) = call(
         convolve_kernel,
         [pltpu.HBM(buffer, bf16)],
@@ -553,20 +562,20 @@
         2 * slots * length * 2 * (5 * outer + 12 * LANES),
         8 * MIB,
         20 * MIB,
-        scratch=[pltpu.VMEM(x.shape, x.dtype) for x in conv_ins[1:]]
-        + [pltpu.VMEM(buffer, bf16), pltpu.SemaphoreType.DMA((len(conv_ins) - 1 + slots,))],
-        far=tuple(range(1, len(conv_ins))),
+        scratch=[pltpu.VMEM(x.shape, x.dtype) for x in conv_ins[2:]]
+        + [pltpu.VMEM(buffer, bf16), pltpu.SemaphoreType.DMA((len(conv_ins) + slots,))],
+        far=tuple(range(2, len(conv_ins))),
         far_outs=(0,),
     )
-    convolved, onehot_t = lax.optimization_barrier((convolved, onehot_t))
+    convolved, onehot = lax.optimization_barrier((convolved, onehot))
 
     returned = lax.all_to_all(convolved, ("seqo", "seqi"), split_axis=0, concat_axis=0, tiled=True)
 
-    outs, scratch, flops, moved = base_parts(blocks - early)
+    outs, scratch, flops, moved = base_parts(blocks - early, 0)
     base, *more_picks = call(
         functools.partial(second_kernel, early * LANES),
         outs,
-        [onehot_t, others, skip_row] + dense_ins + [base],
+        [onehot, others, skip_row] + dense_ins + [base],
         flops,
         moved,
         36 * MIB,

time: 67.1 us -> 64.5 us (0.961)
  Pallas kernels: 49.9 us -> 45.5 us
  waiting for transfers between devices: 1.08 us -> 4.33 us
  starting transfers between devices: 15 us -> 13.4 us
    pallas_call x7 -> x8, Pallas kernels: 49.9 us -> 45.5 us  [call(): pl.pallas_call(kernel, out_shape=outs, in_specs=[away if n in far else ne...]
    all_to_all x1, waiting for transfers between devices: 1.08 us -> 2.73 us  [local(): lax.all_to_all(convolved, ('seqo', 'seqi'), split_axis=0, concat_axis=0,...]
    all_to_all x1, waiting for transfers between devices: 0.01 us -> 1.59 us  [local(): lax.all_to_all(payload, ('seqo', 'seqi'), split_axis=0, concat_axis=0, ti...]
    all_to_all x1, starting transfers between devices: 6.02 us -> 4.44 us  [local(): lax.all_to_all(convolved, ('seqo', 'seqi'), split_axis=0, concat_axis=0,...]
  transfers between devices with their start and end apart: 3 -> 3, of which waited for: 1 -> 2; matrix products, arithmetic and copies ran while one was open for 0% -> 0% of each run, Pallas kernels for 47% -> 42%
where the time goes in v11:
time: 64.5 us; the launch traced here: 64.1 us
  Pallas kernels  45.5 us (71%)
  starting transfers between devices  13.4 us (21%)
  waiting for transfers between devices  4.33 us (7%)
  between operations  0.84 us (1%)
    pallas_call x8, Pallas kernels, call(): pl.pallas_call(kernel, out_shape=outs, in_specs=[away if n in far else ne...  45.5 us
    all_to_all x1, starting transfers between devices, local(): lax.all_to_all(payload, ('seqo', 'seqi'), split_axis=0, concat_axis=0, ti...  7.37 us
    all_to_all x1, starting transfers between devices, local(): lax.all_to_all(convolved, ('seqo', 'seqi'), split_axis=0, concat_axis=0,...  4.44 us
    all_to_all x1, waiting for transfers between devices, local(): lax.all_to_all(convolved, ('seqo', 'seqi'), split_axis=0, concat_axis=0,...  2.73 us
    all_to_all x1, waiting for transfers between devices, local(): lax.all_to_all(payload, ('seqo', 'seqi'), split_axis=0, concat_axis=0, ti...  1.59 us
    ppermute x1, starting transfers between devices, local(): parts.append(lax.ppermute(totals, 'chan', ring))  1.58 us
  transfers between devices with their start and end apart: 3, of which 2 were waited for; matrix products, arithmetic and copies ran while one was open for 0% of the time, Pallas kernels for 42%

profile of v11, /device:TPU:0, one launch (start us, length us, event | category | flops | bytes accessed | tf_op | source)
XLA Modules:
  0.0 64.1 jit_solution(10099031243646663375)
XLA Ops:
  0.6 0.0 copy-start.4
  0.6 8.3 %shard_map.167 = (bf16[16,16,768]{2,1,0:T(8,128)(2,1)}, bf16[16,96,128]{2,1,0:T(8,128)(2,1)S(1)}, s32[8,128]{1,0:T(8,128)S(1)}, bf16[512,2048]{1,0:T(8,128)(2,1)S(1)}) custom-call(s32[1,64]{1,0:T(1,128)} %index.1, s32[1,64]{1,0:T(1,128)} %owners.1, bf16[2048,2048]{1,0:T(8,128)(2,1)} %refs_0_.3, bf16[2048,2048]{1,0:T(8,128)(2,1)} %refs_1_.3), custom_call_target="tpu_custom_call" | custom-call | flops 805306368 | bytes 16777216 | tf_op jit(solution)/shard_map/pallas_call | solution.py:448
  9.0 7.4 %all-to-all-start = ((bf16[16,16,768]{2,1,0:T(8,128)(2,1)}), bf16[16,16,768]{2,1,0:T(8,128)(2,1)S(1)}, u32[]{:S(2)}, u32[]{:S(2)}) async-start(bf16[16,16,768]{2,1,0:T(8,128)(2,1)} %get-tuple-element.25), calls=%async_computation | async-start | bytes 786432 | tf_op jit(solution)/shard_map/all_to_all | solution.py:509
  16.4 0.0 copy-done.4
  16.4 0.0 copy-start.6
  16.4 0.0 copy-start.7
  16.4 0.0 copy-start.8
  16.4 0.0 copy-start.9
  16.4 9.0 %shard_map.169 = (bf16[96,2048]{1,0:T(8,128)(2,1)S(1)}, f32[8,2048]{1,0:T(8,128)S(1)}, f32[96,128]{1,0:T(8,128)S(1)}, bf16[2048,2048]{1,0:T(8,128)(2,1)}, f32[8,...) custom-call(s32[8,128]{1,0:T(8,128)S(1)} %get-tuple-element.26.channels, ...), custom_call_target="tpu_custom_call" | custom-call | flops 805306368 | bytes 20971520 | tf_op jit(solution)/shard_map/pallas_call | solution.py:448
  25.4 0.0 copy-start
  25.4 0.0 copy-start.2
  25.4 0.0 copy-done.6
  25.4 0.0 copy-done.7
  25.5 0.0 copy-done.8
  25.5 0.0 copy-done.9
  25.5 1.5 %shard_map.168.spectra = f32[6,256,256]{2,1,0:T(8,128)S(1)} custom-call(bf16[6,32768]{1,0:T(8,128)(2,1)S(1)} %bitcast.6, bf16[512,512]{1,0:T(8,128)(2,1)S(1)} %copy-done.8, f32[256,256]{1,0:T(8,128)S(1)} %copy-done.9, bf16[1024,256]{1,0:T(8,128)(2,1)S(1)} %copy-done.7), custom_call_target="tpu_custom_call" | custom-call | flops 1006632960 | bytes 4194304 | tf_op jit(solution)/shard_map/pallas_call | solution.py:448
  27.0 0.0 copy-done
  27.0 0.0 copy-done.2
  27.0 1.6 %all-to-all-done.signals = bf16[16,16,768]{2,1,0:T(8,128)(2,1)S(1)} async-done(((bf16[16,16,768]{2,1,0:T(8,128)(2,1)}), bf16[16,16,768]{2,1,0:T(8,128)(2,1)S(1)}, u32[]{:S(2)}, u32[]{:S(2)}) %all-to-all-start) | async-done | bytes 393248 | tf_op jit(solution)/shard_map/all_to_all | solution.py:509
  28.6 5.1 %shard_map.170 = bf16[16,16,768]{2,1,0:T(8,128)(2,1)} custom-call(bf16[16,16,768]{2,1,0:T(8,128)(2,1)S(1)} %all-to-all-done.signals, f32[6,256,256]{2,1,0:T(8,128)S(1)} %shard_map.168.spectra, bf16[512,512]{1,0:T(8,128)(2,1)} %constant.8.clone.outer_fwd.outer_fwd_far, f32[256,256]{1,0:T(8,128)} %constant.9.clone.turn.turn_far, ...), custom_call_target="tpu_custom_call" | custom-call | flops 2214592512 | bytes 8388608 | tf_op jit(solution)/shard_map/pallas_call | solution.py:448
  33.7 4.4 %all-to-all-start.1 = ((bf16[16,16,768]{2,1,0:T(8,128)(2,1)}), bf16[16,16,768]{2,1,0:T(8,128)(2,1)S(1)}, u32[]{:S(2)}, u32[]{:S(2)}) async-start(bf16[16,16,768]{2,1,0:T(8,128)(2,1)} %shard_map.170), calls=%async_computation.1 | async-start | bytes 786432 | tf_op jit(solution)/shard_map/all_to_all | solution.py:572
  38.1 0.0 copy-start.1
  38.2 0.0 copy-start.3
  38.2 9.4 %shard_map.171 = (bf16[2048,2048]{1,0:T(8,128)(2,1)}, f32[8,1,128]{2,1,0:T(1,128)S(1)}, bf16[8,96,128]{2,1,0:T(8,128)(2,1)S(1)}, bf16[8,96,128]{2,1,0:T(8,128)(2,1)S(1)}) custom-call(bf16[96,2048]{1,0:T(8,128)(2,1)S(1)} %get-tuple-element.31.onehot, f32[8,2048]{1,0:T(8,128)S(1)} %get-tuple-element.32.others, ...), custom_call_target="tpu_custom_call", output_to_operand_aliasing={{0}: (7, {})} | custom-call | flops 805306368 | bytes 20971520 | tf_op jit(solution)/shard_map/pallas_call | solution.py:448
  47.6 0.0 copy-start.5
  47.6 2.7 %all-to-all-done.1.conv = bf16[16,16,768]{2,1,0:T(8,128)(2,1)S(1)} async-done(((bf16[16,16,768]{2,1,0:T(8,128)(2,1)}), bf16[16,16,768]{2,1,0:T(8,128)(2,1)S(1)}, u32[]{:S(2)}, u32[]{:S(2)}) %all-to-all-start.1) | async-done | bytes 393248 | tf_op jit(solution)/shard_map/all_to_all | solution.py:572
  50.3 0.0 copy-done.1
  50.3 0.0 copy-done.3
  50.3 0.5 shard_map.172
  50.9 1.6 %collective-permute-start = (f32[16,1,128]{2,1,0:T(1,128)S(1)}, f32[16,1,128]{2,1,0:T(1,128)S(1)}, u32[]{:S(2)}, u32[]{:S(2)}) collective-permute-start(f32[16,1,128]{2,1,0:T(1,128)S(1)} %get-tuple-element.46.refs_0_), channel_id=1, source_target_pairs={{0,16},{16,0},{1,17},{17,1},{2,18},{18,2},{3,19},{19,3},{4,20},{20... | collective-permute-start | bytes 24584 | tf_op jit(solution)/shard_map/ppermute | solution.py:600
  52.5 7.3 %shard_map.173 = (bf16[2048,2048]{1,0:T(8,128)(2,1)}, bf16[2048,2048]{1,0:T(8,128)(2,1)S(1)}) custom-call(bf16[2048,2048]{1,0:T(8,128)(2,1)} %get-tuple-element.34.base, bf16[16,96,128]{2,1,0:T(8,128)(2,1)S(1)} %get-tuple-element.44.hidden_kept, bf16[96,2048]{1,0:T(8,128)(2,1)S(1)} %get-tuple-element.31.onehot), custom_call_target="tpu_custom_call" | custom-call | flops 805306368 | bytes 16777216 | tf_op jit(solution)/shard_map/pallas_call | solution.py:448
  59.7 0.0 collective-permute-done.refs_1_
  59.7 0.0 copy-done.5
  59.8 4.4 %shard_map.174 = bf16[2048,2048]{1,0:T(8,128)(2,1)} custom-call(f32[16,1,128]{2,1,0:T(1,128)S(1)} %get-tuple-element.46.refs_0_, f32[16,1,128]{2,1,0:T(1,128)S(1)} %collective-permute-done.refs_1_, bf16[2048,2048]{1,0:T(8,128)(2,1)S(1)} %get-tuple-element.47.refs_2_, f32[1,2048]{1,0:T(1,128)S(1)} %bitcast.5), custom_call_target="tpu_custom_call" | custom-call | flops 16777216 | bytes 16777216 | tf_op jit(solution)/shard_map/pallas_call | solution.py:448
Async XLA Ops:
  0.6 15.7 %copy-start.4 = (f32[2048]{0:T(1024)S(1)}, f32[2048]{0:T(1024)}, u32[]{:S(2)}) copy-start(f32[2048]{0:T(1024)} %param.23) | copy-start | bytes 24580
  9.0 19.6 %all-to-all-start = ((bf16[16,16,768]{2,1,0:T(8,128)(2,1)}), bf16[16,16,768]{2,1,0:T(8,128)(2,1)S(1)}, u32[]{:S(2)}, u32[]{:S(2)}) async-start(bf16[16,16,768]{2,1,0:T(8,128)(2,1)} %get-tuple-element.25), calls=%async_computation | async-start | bytes 786432 | tf_op jit(solution)/shard_map/all_to_all | solution.py:509
  16.4 9.1 %copy-start.6 = (bf16[1,1,6,32768]{3,2,1,0:T(8,128)(2,1)S(1)}, bf16[1,1,6,32768]{3,2,1,0:T(8,128)(2,1)}, u32[]{:S(2)}) copy-start(bf16[1,1,6,32768]{3,2,1,0:T(8,128)(2,1)} %param.20) | copy-start | bytes 1179652
  16.4 9.1 %copy-start.7 = (bf16[1024,256]{1,0:T(8,128)(2,1)S(1)}, bf16[1024,256]{1,0:T(8,128)(2,1)}, u32[]{:S(2)}) copy-start(bf16[1024,256]{1,0:T(8,128)(2,1)} %constant.10.clone.inner.inner_far) | copy-start | bytes 1572868
  16.4 9.1 %copy-start.8 = (bf16[512,512]{1,0:T(8,128)(2,1)S(1)}, bf16[512,512]{1,0:T(8,128)(2,1)}, u32[]{:S(2)}) copy-start(bf16[512,512]{1,0:T(8,128)(2,1)} %constant.8.clone.outer_fwd.outer_fwd_far) | copy-start | bytes 1572868
  16.4 9.0 %copy-start.9 = (f32[256,256]{1,0:T(8,128)S(1)}, f32[256,256]{1,0:T(8,128)}, u32[]{:S(2)}) copy-start(f32[256,256]{1,0:T(8,128)} %constant.9.clone.turn.turn_far) | copy-start | bytes 786436
  25.4 1.5 %copy-start = (bf16[8,96,128]{2,1,0:T(8,128)(2,1)}, bf16[8,96,128]{2,1,0:T(8,128)(2,1)S(1)}, u32[]{:S(2)}) copy-start(bf16[8,96,128]{2,1,0:T(8,128)(2,1)S(1)} %get-tuple-element.40.refs_2_) | copy-start | bytes 589828
  25.4 1.5 %copy-start.2 = (f32[96,128]{1,0:T(8,128)}, f32[96,128]{1,0:T(8,128)S(1)}, u32[]{:S(2)}) copy-start(f32[96,128]{1,0:T(8,128)S(1)} %get-tuple-element.37.skip_wide) | copy-start | bytes 147460
  33.7 16.6 %all-to-all-start.1 = ((bf16[16,16,768]{2,1,0:T(8,128)(2,1)}), bf16[16,16,768]{2,1,0:T(8,128)(2,1)S(1)}, u32[]{:S(2)}, u32[]{:S(2)}) async-start(bf16[16,16,768]{2,1,0:T(8,128)(2,1)} %shard_map.170), calls=%async_computation.1 | async-start | bytes 786432 | tf_op jit(solution)/shard_map/all_to_all | solution.py:572
  38.1 12.2 %copy-start.1 = (bf16[8,96,128]{2,1,0:T(8,128)(2,1)S(1)}, bf16[8,96,128]{2,1,0:T(8,128)(2,1)}, u32[]{:S(2)}) copy-start(bf16[8,96,128]{2,1,0:T(8,128)(2,1)} %copy-done) | copy-start | bytes 589828
  38.2 12.2 %copy-start.3 = (f32[96,128]{1,0:T(8,128)S(1)}, f32[96,128]{1,0:T(8,128)}, u32[]{:S(2)}) copy-start(f32[96,128]{1,0:T(8,128)} %copy-done.2) | copy-start | bytes 147460
  47.6 12.2 %copy-start.5 = (f32[2048]{0:T(1024)S(1)}, f32[2048]{0:T(1024)}, u32[]{:S(2)}) copy-start(f32[2048]{0:T(1024)} %param.24) | copy-start | bytes 24580
  50.9 8.9 %collective-permute-start = (f32[16,1,128]{2,1,0:T(1,128)S(1)}, f32[16,1,128]{2,1,0:T(1,128)S(1)}, u32[]{:S(2)}, u32[]{:S(2)}) collective-permute-start(f32[16,1,128]{2,1,0:T(1,128)S(1)} %get-tuple-element.46.refs_0_), channel_id=1, source_target_pairs={{0,16},{16,0},{1,17},{17,1},{2,18},{18,2},{3,19},{19,3},{4,20},{20... | collective-permute-start | bytes 24584 | tf_op jit(solution)/shard_map/ppermute | solution.py:600

commit v12 on v11

--- a/solution.py
+++ b/solution.py
@@ -12,6 +12,7 @@
 TILE = 256
 CHUNK = 16
 GROUP = 3
+AHEAD = 3
 EARLY = 8
 MIB = 1 << 20
 norm_eps = 1e-06
@@ -44,7 +45,7 @@
     )
     outer_back = np.concatenate([np.cos(outer_angle).T, -np.sin(outer_angle).T], axis=1) / length
     turn = np.concatenate([np.cos(turn_angle), np.sin(turn_angle)], axis=1).astype(np.float32)
-    outer_fwd = np.concatenate(split_np(outer_fwd), axis=1)
+    outer_fwd = np.concatenate(split_np(outer_fwd), axis=0)
     inner = np.concatenate(split_np(inner_fwd) + split_np(inner_back), axis=0)
     outer_back = np.concatenate(split_np(outer_back), axis=1)
     return outer_fwd, turn, inner, outer_back
@@ -80,7 +81,8 @@
 
 def to_spectrum(blocks, slots, outer_fwd, turn, inner_fwd):
     outer = blocks.shape[0]
-    first = dot(outer_fwd, jnp.concatenate([blocks, blocks], axis=0))
+    first = dot(outer_fwd(0), blocks)
+    first = first + dot(outer_fwd(1), blocks)
     turn, inner_fwd = turn(), inner_fwd()
     cos, sin = turn[:, :LANES], turn[:, LANES:]
     turned = []
@@ -108,7 +110,11 @@
     blocks = [wide[s].reshape(outer, LANES) for s in range(slots)]
     blocks = jnp.concatenate(blocks, axis=1).astype(bf16)
     return to_spectrum(
-        blocks, slots, outer_fwd[...], lambda: turn[...], lambda: inner[: 4 * LANES, :]
+        blocks,
+        slots,
+        lambda n: outer_fwd[2 * outer * n : 2 * outer * (n + 1), :],
+        lambda: turn[...],
+        lambda: inner[: 4 * LANES, :],
     )
 
 
@@ -117,24 +123,33 @@
 ):
     sources = (outer_fwd_far, turn_far, inner_far, outer_back_far)
     outer_fwd, turn_ref, inner, outer_back, result, sems = scratch
+    slots, outer = spectra.shape[:2]
+    halves = [pl.ds(2 * outer * n, 2 * outer) for n in range(2)]
     copies = [
-        pltpu.make_async_copy(source, scratch[n], sems.at[n]) for n, source in enumerate(sources)
+        pltpu.make_async_copy(outer_fwd_far.at[half, :], outer_fwd.at[half, :], sems.at[n])
+        for n, half in enumerate(halves)
+    ] + [
+        pltpu.make_async_copy(source, scratch[n], sems.at[n + 1])
+        for n, source in enumerate(sources)
+        if n > 0
     ]
     for copy in copies:
         copy.start()
-    slots, outer = spectra.shape[:2]
+
+    def outer_now(n):
+        copies[n].wait()
+        return outer_fwd[halves[n], :]
 
     def turn_now():
-        copies[1].wait()
+        copies[2].wait()
         return turn_ref[...]
 
     def inner_now():
-        copies[2].wait()
+        copies[3].wait()
         return inner[: 4 * LANES, :]
 
-    copies[0].wait()
     blocks = signals[...].reshape(outer, slots * LANES)
-    parts = to_spectrum(blocks, slots, outer_fwd[...], turn_now, inner_now)
+    parts = to_spectrum(blocks, slots, outer_now, turn_now, inner_now)
     turn = turn_ref[...]
     cos, sin = turn[:, :LANES], turn[:, LANES:]
     joint = []
@@ -150,7 +165,7 @@
     for back in grouped(joint, inner[4 * LANES :, :]):
         re, im = back[:, :LANES], back[:, LANES:]
         turned.append(jnp.concatenate([re * cos - im * sin, im * cos + re * sin], axis=0))
-    copies[3].wait()
+    copies[4].wait()
     sends = []
     for s in range(0, slots, 2):
         pair = turned[s : s + 2]
@@ -195,7 +210,7 @@
     return [picked[:, i : i + LANES] for i in range(0, tile.shape[0], LANES)]
 
 
-def fetch(sources, stages, sems, tile, first=0, ahead=3):
+def fetch(sources, stages, sems, tile, first=0, ahead=3, begin=True):
     count = stages[0].shape[0] // tile
 
     def copies(i):
@@ -211,8 +226,10 @@
         for copy in copies(i):
             copy.start()
 
-    for i in range(min(ahead, count)):
-        start(i)
+    ahead = min(ahead, count)
+    if begin:
+        for i in range(ahead):
+            start(i)
 
     def wait(i):
         for copy in copies(i):
@@ -224,7 +241,7 @@
 
         return pl.multiple_of(i * tile, tile)
 
-    return wait, count
+    return start, wait, ahead
 
 
 def build_onehot(onehot, row):
@@ -243,7 +260,8 @@
     ]
     for copy in list_copies:
         copy.start()
-    wait, count = fetch((gate, value), (gate_stage, value_stage), sems, tile, 0, 4)
+    count = sems.shape[1]
+    _, wait, _ = fetch((gate, value), (gate_stage, value_stage), sems, tile, 0, 4)
     for copy in list_copies:
         copy.wait()
     row = channel_of_row(lists[0], lists[1], owner_count, channels.shape[1])
@@ -297,13 +315,15 @@
     slab = out_stage.shape[1]
     tile = partial.shape[0]
     head_rows = 0 if head is None else head.shape[0]
-    wait, count = fetch(dense[2:], (out_stage, res_stage), sems, tile, first)
-    wait_gate, _ = fetch(
-        dense[:2], (gate_stage, value_stage), gate_sems, tile, first + head_rows
+    head_tiles = head_rows // tile
+    count = sems.shape[1]
+    late = head_tiles > AHEAD
+    _, wait, _ = fetch(dense[2:], (out_stage, res_stage), sems, tile, first, AHEAD)
+    start_gate, wait_gate, early = fetch(
+        dense[:2], (gate_stage, value_stage), gate_sems, tile, first + head_rows, AHEAD, not late
     )
     if beside is not None:
         beside()
-    head_tiles = head_rows // tile
 
     def copy(i):
         at = pl.multiple_of(i * tile, tile)
@@ -313,6 +333,12 @@
 
     def step(i, in_head):
         start = wait(i)
+        if in_head and late:
+
+            @pl.when((i > 0) & (i <= early))
+            def _():
+                start_gate(i - 1)
+
         gate_start = start if in_head else wait_gate(i - head_tiles)
         chunks = range(0, tile, CHUNK)
         totals = [jnp.zeros((CHUNK, LANES), f32) for _ in chunks]
@@ -382,7 +408,7 @@
     wide = min(slab, 2 * LANES)
     count = sems.shape[0]
     tile = held.shape[0] // count
-    wait, _ = fetch((base,), (base_stage,), base_sems, tile, 0, 4)
+    _, wait, _ = fetch((base,), (base_stage,), base_sems, tile, 0, 4)
 
     def copy(i):
         rows = pl.ds(pl.multiple_of(i * tile, tile), tile)

time: 64.5 us -> 64.3 us (level)
  no operation moved by 1% of the time
where the time goes in v12:
time: 64.3 us; the launch traced here: 63.9 us
  Pallas kernels  45.3 us (70%)
  starting transfers between devices  13.2 us (21%)
  waiting for transfers between devices  4.52 us (7%)
  between operations  0.84 us (1%)
    pallas_call x8, Pallas kernels, call(): pl.pallas_call(kernel, out_shape=outs, in_specs=[away if n in far else ne...  45.3 us
    all_to_all x1, starting transfers between devices, local(): lax.all_to_all(payload, ('seqo', 'seqi'), split_axis=0, concat_axis=0, ti...  7.37 us
    all_to_all x1, starting transfers between devices, local(): lax.all_to_all(convolved, ('seqo', 'seqi'), split_axis=0, concat_axis=0,...  4.24 us
    all_to_all x1, waiting for transfers between devices, local(): lax.all_to_all(convolved, ('seqo', 'seqi'), split_axis=0, concat_axis=0,...  2.73 us
    all_to_all x1, waiting for transfers between devices, local(): lax.all_to_all(payload, ('seqo', 'seqi'), split_axis=0, concat_axis=0, ti...  1.79 us
    ppermute x1, starting transfers between devices, local(): parts.append(lax.ppermute(totals, 'chan', ring))  1.58 us
  transfers between devices with their start and end apart: 3, of which 2 were waited for; matrix products, arithmetic and copies ran while one was open for 0% of the time, Pallas kernels for 42%

profile of v12, /device:TPU:0, one launch (start us, length us, event | category | flops | bytes accessed | tf_op | source)
XLA Modules:
  0.0 63.9 jit_solution(6936113889210192181)
XLA Ops:
  0.6 0.0 copy-start.4
  0.6 8.3 %shard_map.167 = (bf16[16,16,768]{2,1,0:T(8,128)(2,1)}, bf16[16,96,128]{2,1,0:T(8,128)(2,1)S(1)}, s32[8,128]{1,0:T(8,128)S(1)}, bf16[512,2048]{1,0:T(8,128)(2,1)S(1)}) custom-call(s32[1,64]{1,0:T(1,128)} %index.1, s32[1,64]{1,0:T(1,128)} %owners.1, bf16[2048,2048]{1,0:T(8,128)(2,1)} %refs_0_.3, bf16[2048,2048]{1,0:T(8,128)(2,1)} %refs_1_.3), custom_call_target="tpu_custom_call" | custom-call | flops 805306368 | bytes 16777216 | tf_op jit(solution)/shard_map/pallas_call | solution.py:474
  9.0 7.4 %all-to-all-start = ((bf16[16,16,768]{2,1,0:T(8,128)(2,1)}), bf16[16,16,768]{2,1,0:T(8,128)(2,1)S(1)}, u32[]{:S(2)}, u32[]{:S(2)}) async-start(bf16[16,16,768]{2,1,0:T(8,128)(2,1)} %get-tuple-element.25), calls=%async_computation | async-start | bytes 786432 | tf_op jit(solution)/shard_map/all_to_all | solution.py:535
  16.4 0.0 copy-done.4
  16.4 0.0 copy-start.6
  16.4 0.0 copy-start.7
  16.4 0.0 copy-start.8
  16.4 0.0 copy-start.9
  16.4 8.7 %shard_map.169 = (bf16[96,2048]{1,0:T(8,128)(2,1)S(1)}, f32[8,2048]{1,0:T(8,128)S(1)}, f32[96,128]{1,0:T(8,128)S(1)}, bf16[2048,2048]{1,0:T(8,128)(2,1)}, f32[8,...) custom-call(s32[8,128]{1,0:T(8,128)S(1)} %get-tuple-element.26.channels, ...), custom_call_target="tpu_custom_call" | custom-call | flops 805306368 | bytes 20971520 | tf_op jit(solution)/shard_map/pallas_call | solution.py:474
  25.2 0.0 copy-start
  25.2 0.0 copy-start.2
  25.2 0.0 copy-done.6
  25.2 0.0 copy-done.7
  25.2 0.0 copy-done.8
  25.2 0.0 copy-done.9
  25.2 1.5 %shard_map.168.spectra = f32[6,256,256]{2,1,0:T(8,128)S(1)} custom-call(bf16[6,32768]{1,0:T(8,128)(2,1)S(1)} %bitcast.6, bf16[1024,256]{1,0:T(8,128)(2,1)S(1)} %copy-done.8, f32[256,256]{1,0:T(8,128)S(1)} %copy-done.9, bf16[1024,256]{1,0:T(8,128)(2,1)S(1)} %copy-done.7), custom_call_target="tpu_custom_call" | custom-call | flops 1006632960 | bytes 4194304 | tf_op jit(solution)/shard_map/pallas_call | solution.py:474
  26.8 0.0 copy-done
  26.8 0.0 copy-done.2
  26.8 1.8 %all-to-all-done.signals = bf16[16,16,768]{2,1,0:T(8,128)(2,1)S(1)} async-done(((bf16[16,16,768]{2,1,0:T(8,128)(2,1)}), bf16[16,16,768]{2,1,0:T(8,128)(2,1)S(1)}, u32[]{:S(2)}, u32[]{:S(2)}) %all-to-all-start) | async-done | bytes 393248 | tf_op jit(solution)/shard_map/all_to_all | solution.py:535
  28.6 5.1 %shard_map.170 = bf16[16,16,768]{2,1,0:T(8,128)(2,1)} custom-call(bf16[16,16,768]{2,1,0:T(8,128)(2,1)S(1)} %all-to-all-done.signals, f32[6,256,256]{2,1,0:T(8,128)S(1)} %shard_map.168.spectra, bf16[1024,256]{1,0:T(8,128)(2,1)} %constant.8.clone.outer_fwd.outer_fwd_far, f32[256,256]{1,0:T(8,128)} %constant.9.clone.turn.turn_far, ...), custom_call_target="tpu_custom_call" | custom-call | flops 2214592512 | bytes 8388608 | tf_op jit(solution)/shard_map/pallas_call | solution.py:474
  33.7 4.2 %all-to-all-start.1 = ((bf16[16,16,768]{2,1,0:T(8,128)(2,1)}), bf16[16,16,768]{2,1,0:T(8,128)(2,1)S(1)}, u32[]{:S(2)}, u32[]{:S(2)}) async-start(bf16[16,16,768]{2,1,0:T(8,128)(2,1)} %shard_map.170), calls=%async_computation.1 | async-start | bytes 786432 | tf_op jit(solution)/shard_map/all_to_all | solution.py:598
  37.9 0.0 copy-start.1
  38.0 0.0 copy-start.3
  38.0 9.4 %shard_map.171 = (bf16[2048,2048]{1,0:T(8,128)(2,1)}, f32[8,1,128]{2,1,0:T(1,128)S(1)}, bf16[8,96,128]{2,1,0:T(8,128)(2,1)S(1)}, bf16[8,96,128]{2,1,0:T(8,128)(2,1)S(1)}) custom-call(bf16[96,2048]{1,0:T(8,128)(2,1)S(1)} %get-tuple-element.31.onehot, f32[8,2048]{1,0:T(8,128)S(1)} %get-tuple-element.32.others, ...), custom_call_target="tpu_custom_call", output_to_operand_aliasing={{0}: (7, {})} | custom-call | flops 805306368 | bytes 20971520 | tf_op jit(solution)/shard_map/pallas_call | solution.py:474
  47.4 0.0 copy-start.5
  47.4 2.7 %all-to-all-done.1.conv = bf16[16,16,768]{2,1,0:T(8,128)(2,1)S(1)} async-done(((bf16[16,16,768]{2,1,0:T(8,128)(2,1)}), bf16[16,16,768]{2,1,0:T(8,128)(2,1)S(1)}, u32[]{:S(2)}, u32[]{:S(2)}) %all-to-all-start.1) | async-done | bytes 393248 | tf_op jit(solution)/shard_map/all_to_all | solution.py:598
  50.1 0.0 copy-done.1
  50.1 0.0 copy-done.3
  50.1 0.5 shard_map.172
  50.7 1.6 %collective-permute-start = (f32[16,1,128]{2,1,0:T(1,128)S(1)}, f32[16,1,128]{2,1,0:T(1,128)S(1)}, u32[]{:S(2)}, u32[]{:S(2)}) collective-permute-start(f32[16,1,128]{2,1,0:T(1,128)S(1)} %get-tuple-element.46.refs_0_), channel_id=1, source_target_pairs={{0,16},{16,0},{1,17},{17,1},{2,18},{18,2},{3,19},{19,3},{4,20},{20... | collective-permute-start | bytes 24584 | tf_op jit(solution)/shard_map/ppermute | solution.py:626
  52.3 7.3 %shard_map.173 = (bf16[2048,2048]{1,0:T(8,128)(2,1)}, bf16[2048,2048]{1,0:T(8,128)(2,1)S(1)}) custom-call(bf16[2048,2048]{1,0:T(8,128)(2,1)} %get-tuple-element.34.base, bf16[16,96,128]{2,1,0:T(8,128)(2,1)S(1)} %get-tuple-element.44.hidden_kept, bf16[96,2048]{1,0:T(8,128)(2,1)S(1)} %get-tuple-element.31.onehot), custom_call_target="tpu_custom_call" | custom-call | flops 805306368 | bytes 16777216 | tf_op jit(solution)/shard_map/pallas_call | solution.py:474
  59.5 0.0 collective-permute-done.refs_1_
  59.6 0.0 copy-done.5
  59.6 4.4 %shard_map.174 = bf16[2048,2048]{1,0:T(8,128)(2,1)} custom-call(f32[16,1,128]{2,1,0:T(1,128)S(1)} %get-tuple-element.46.refs_0_, f32[16,1,128]{2,1,0:T(1,128)S(1)} %collective-permute-done.refs_1_, bf16[2048,2048]{1,0:T(8,128)(2,1)S(1)} %get-tuple-element.47.refs_2_, f32[1,2048]{1,0:T(1,128)S(1)} %bitcast.5), custom_call_target="tpu_custom_call" | custom-call | flops 16777216 | bytes 16777216 | tf_op jit(solution)/shard_map/pallas_call | solution.py:474
Async XLA Ops:
  0.6 15.7 %copy-start.4 = (f32[2048]{0:T(1024)S(1)}, f32[2048]{0:T(1024)}, u32[]{:S(2)}) copy-start(f32[2048]{0:T(1024)} %param.23) | copy-start | bytes 24580
  9.0 19.6 %all-to-all-start = ((bf16[16,16,768]{2,1,0:T(8,128)(2,1)}), bf16[16,16,768]{2,1,0:T(8,128)(2,1)S(1)}, u32[]{:S(2)}, u32[]{:S(2)}) async-start(bf16[16,16,768]{2,1,0:T(8,128)(2,1)} %get-tuple-element.25), calls=%async_computation | async-start | bytes 786432 | tf_op jit(solution)/shard_map/all_to_all | solution.py:535
  16.4 8.8 %copy-start.6 = (bf16[1,1,6,32768]{3,2,1,0:T(8,128)(2,1)S(1)}, bf16[1,1,6,32768]{3,2,1,0:T(8,128)(2,1)}, u32[]{:S(2)}) copy-start(bf16[1,1,6,32768]{3,2,1,0:T(8,128)(2,1)} %param.20) | copy-start | bytes 1179652
  16.4 8.8 %copy-start.7 = (bf16[1024,256]{1,0:T(8,128)(2,1)S(1)}, bf16[1024,256]{1,0:T(8,128)(2,1)}, u32[]{:S(2)}) copy-start(bf16[1024,256]{1,0:T(8,128)(2,1)} %constant.10.clone.inner.inner_far) | copy-start | bytes 1572868
  16.4 8.8 %copy-start.8 = (bf16[1024,256]{1,0:T(8,128)(2,1)S(1)}, bf16[1024,256]{1,0:T(8,128)(2,1)}, u32[]{:S(2)}) copy-start(bf16[1024,256]{1,0:T(8,128)(2,1)} %constant.8.clone.outer_fwd.outer_fwd_far) | copy-start | bytes 1572868
  16.4 8.8 %copy-start.9 = (f32[256,256]{1,0:T(8,128)S(1)}, f32[256,256]{1,0:T(8,128)}, u32[]{:S(2)}) copy-start(f32[256,256]{1,0:T(8,128)} %constant.9.clone.turn.turn_far) | copy-start | bytes 786436
  25.2 1.6 %copy-start = (bf16[8,96,128]{2,1,0:T(8,128)(2,1)}, bf16[8,96,128]{2,1,0:T(8,128)(2,1)S(1)}, u32[]{:S(2)}) copy-start(bf16[8,96,128]{2,1,0:T(8,128)(2,1)S(1)} %get-tuple-element.40.refs_2_) | copy-start | bytes 589828
  25.2 1.6 %copy-start.2 = (f32[96,128]{1,0:T(8,128)}, f32[96,128]{1,0:T(8,128)S(1)}, u32[]{:S(2)}) copy-start(f32[96,128]{1,0:T(8,128)S(1)} %get-tuple-element.37.skip_wide) | copy-start | bytes 147460
  33.7 16.4 %all-to-all-start.1 = ((bf16[16,16,768]{2,1,0:T(8,128)(2,1)}), bf16[16,16,768]{2,1,0:T(8,128)(2,1)S(1)}, u32[]{:S(2)}, u32[]{:S(2)}) async-start(bf16[16,16,768]{2,1,0:T(8,128)(2,1)} %shard_map.170), calls=%async_computation.1 | async-start | bytes 786432 | tf_op jit(solution)/shard_map/all_to_all | solution.py:598
  37.9 12.2 %copy-start.1 = (bf16[8,96,128]{2,1,0:T(8,128)(2,1)S(1)}, bf16[8,96,128]{2,1,0:T(8,128)(2,1)}, u32[]{:S(2)}) copy-start(bf16[8,96,128]{2,1,0:T(8,128)(2,1)} %copy-done) | copy-start | bytes 589828
  38.0 12.2 %copy-start.3 = (f32[96,128]{1,0:T(8,128)S(1)}, f32[96,128]{1,0:T(8,128)}, u32[]{:S(2)}) copy-start(f32[96,128]{1,0:T(8,128)} %copy-done.2) | copy-start | bytes 147460
  47.4 12.2 %copy-start.5 = (f32[2048]{0:T(1024)S(1)}, f32[2048]{0:T(1024)}, u32[]{:S(2)}) copy-start(f32[2048]{0:T(1024)} %param.24) | copy-start | bytes 24580
  50.7 8.9 %collective-permute-start = (f32[16,1,128]{2,1,0:T(1,128)S(1)}, f32[16,1,128]{2,1,0:T(1,128)S(1)}, u32[]{:S(2)}, u32[]{:S(2)}) collective-permute-start(f32[16,1,128]{2,1,0:T(1,128)S(1)} %get-tuple-element.46.refs_0_), channel_id=1, source_target_pairs={{0,16},{16,0},{1,17},{17,1},{2,18},{18,2},{3,19},{19,3},{4,20},{20... | collective-permute-start | bytes 24584 | tf_op jit(solution)/shard_map/ppermute | solution.py:626

commit v13 on v12

--- a/solution.py
+++ b/solution.py
@@ -119,7 +119,7 @@
 
 
 def convolve_kernel(
-    signals, spectra, outer_fwd_far, turn_far, inner_far, outer_back_far, out, *scratch
+    outer_devices, inner_devices, signals, spectra, outer_fwd_far, turn_far, inner_far, outer_back_far, out, *scratch
 ):
     sources = (outer_fwd_far, turn_far, inner_far, outer_back_far)
     outer_fwd, turn_ref, inner, outer_back, result, sems = scratch
@@ -148,7 +148,11 @@
         copies[3].wait()
         return inner[: 4 * LANES, :]
 
-    blocks = signals[...].reshape(outer, slots * LANES)
+    places = [
+        place_of(n, outer_devices, inner_devices) for n in range(outer_devices * inner_devices)
+    ]
+    piece = signals.shape[1]
+    blocks = jnp.concatenate([signals[place] for place in places], axis=0)
     parts = to_spectrum(blocks, slots, outer_now, turn_now, inner_now)
     turn = turn_ref[...]
     cos, sin = turn[:, :LANES], turn[:, LANES:]
@@ -171,7 +175,8 @@
         pair = turned[s : s + 2]
         causal = table_times(outer_back[...], jnp.concatenate(pair, axis=1)).astype(bf16)
         lanes = pl.ds(s * LANES, len(pair) * LANES)
-        result[:, :, lanes] = causal.reshape(out.shape[:2] + (len(pair) * LANES,))
+        for n, place in enumerate(places):
+            result[place, :, lanes] = causal[n * piece : (n + 1) * piece]
         sends.append(
             pltpu.make_async_copy(
                 result.at[:, :, lanes], out.at[:, :, lanes], sems.at[len(copies) + len(sends)]
@@ -182,6 +187,10 @@
         send.wait()
 
 
+def place_of(owner, outer_devices, inner_devices):
+    return owner % inner_devices * outer_devices + owner // inner_devices
+
+
 def iota(shape, axis):
     return lax.broadcasted_iota(jnp.int32, shape, axis)
 
@@ -192,13 +201,18 @@
     return jnp.sum(jnp.where(same, row, 0), axis=1, keepdims=True)
 
 
-def channel_of_row(index_row, owners_row, owner_count, rows):
+def channel_of_row(index_row, owners_row, outer_devices, inner_devices, rows):
     slots = owners_row.shape[1]
     owners_col = to_column(owners_row)
     index_col = to_column(index_row)
     earlier = (owners_col == owners_row) & (iota((slots, slots), 1) < iota((slots, slots), 0))
     rank_col = jnp.sum(earlier.astype(jnp.int32), axis=1, keepdims=True)
-    target_col = jnp.where(owners_col >= 0, rank_col * owner_count + owners_col, -1)
+    outer_col = jnp.zeros_like(owners_col)
+    for n in range(1, outer_devices):
+        outer_col = outer_col + (owners_col >= n * inner_devices).astype(jnp.int32)
+    place_col = (owners_col - outer_col * inner_devices) * outer_devices + outer_col
+    owner_count = outer_devices * inner_devices
+    target_col = jnp.where(owners_col >= 0, rank_col * owner_count + place_col, -1)
     hit = target_col == iota((slots, rows), 1)
     return jnp.sum(jnp.where(hit, index_col + 1, 0), axis=0, keepdims=True) - 1
 
@@ -250,7 +264,7 @@
     return hit
 
 
-def pick_kernel(owner_count, slots, index, owners, gate, value, *refs):
+def pick_kernel(outer_devices, inner_devices, slots, index, owners, gate, value, *refs):
     payload, picked, channels, gated_head = refs[:4]
     acc, gate_stage, value_stage, onehot, lists, list_sems, sems = refs[4:]
     tile = gate_stage.shape[0] // sems.shape[1]
@@ -264,7 +278,8 @@
     _, wait, _ = fetch((gate, value), (gate_stage, value_stage), sems, tile, 0, 4)
     for copy in list_copies:
         copy.wait()
-    row = channel_of_row(lists[0], lists[1], owner_count, channels.shape[1])
+    owner_count = outer_devices * inner_devices
+    row = channel_of_row(lists[0], lists[1], outer_devices, inner_devices, channels.shape[1])
     channels[...] = jnp.broadcast_to(row, channels.shape)
     build_onehot(onehot, row)
 
@@ -489,7 +504,8 @@
     tok_rows, slab = gate_in.shape
     slots, length = filters.shape[2:]
     chan_devices = lax.axis_size("chan")
-    owner_count = lax.axis_size("seqo") * lax.axis_size("seqi")
+    outer_devices, inner_devices = lax.axis_size("seqo"), lax.axis_size("seqi")
+    owner_count = outer_devices * inner_devices
     rows = slots * owner_count
     lanes_rows = -(-rows // LANES) * LANES
     blocks = tok_rows // LANES
@@ -509,7 +525,7 @@
     head_rows = tok_rows // 4 // tile * tile
 
     payload, picked, channels, gated_head = call(
-        functools.partial(pick_kernel, owner_count, slots),
+        functools.partial(pick_kernel, outer_devices, inner_devices, slots),
         [
             sds(buffer, bf16),
             picks,
@@ -532,7 +548,7 @@
         far=(0, 1, 2, 3),
     )
 
-    incoming = lax.all_to_all(payload, ("seqo", "seqi"), split_axis=0, concat_axis=0, tiled=True)
+    incoming = lax.all_to_all(payload, ("seqi", "seqo"), split_axis=0, concat_axis=0, tiled=True)
 
     dense_ins = [gate_in, value_in, out_gate, residual]
 
@@ -582,7 +598,7 @@
 
     conv_ins = [incoming, in_vmem(spectra), outer_fwd, turn, inner, outer_back]
     (convolved,) = call(
-        convolve_kernel,
+        functools.partial(convolve_kernel, outer_devices, inner_devices),
         [pltpu.HBM(buffer, bf16)],
         conv_ins,
         2 * slots * length * 2 * (5 * outer + 12 * LANES),
@@ -595,7 +611,7 @@
     )
     convolved, onehot = lax.optimization_barrier((convolved, onehot))
 
-    returned = lax.all_to_all(convolved, ("seqo", "seqi"), split_axis=0, concat_axis=0, tiled=True)
+    returned = lax.all_to_all(convolved, ("seqi", "seqo"), split_axis=0, concat_axis=0, tiled=True)
 
     outs, scratch, flops, moved = base_parts(blocks - early, 0)
     base, *more_picks = call(

time: 64.3 us -> 65 us (1.011)
  waiting for transfers between devices: 4.52 us -> 5.87 us
  starting transfers between devices: 13.2 us -> 12.5 us
    all_to_all x2, waiting for transfers between devices: 4.52 us -> 5.87 us  [the longest x1 3.4 us: local(): lax.all_to_all(convolved, ('seqi', 'seqo'), split_axis=0, concat_axis=0,...]
    all_to_all x2, starting transfers between devices: 11.6 us -> 10.9 us  [the longest x1 7.37 us: local(): lax.all_to_all(payload, ('seqi', 'seqo'), split_axis=0, concat_axis=0, ti...]
where the time goes in v13:
time: 65 us; the launch traced here: 64.6 us
  Pallas kernels  45.3 us (70%)
  starting transfers between devices  12.5 us (19%)
  waiting for transfers between devices  5.87 us (9%)
  between operations  0.84 us (1%)
    pallas_call x8, Pallas kernels, call(): pl.pallas_call(kernel, out_shape=outs, in_specs=[away if n in far else ne...  45.3 us
    all_to_all x1, starting transfers between devices, local(): lax.all_to_all(payload, ('seqi', 'seqo'), split_axis=0, concat_axis=0, ti...  7.37 us
    all_to_all x1, starting transfers between devices, local(): lax.all_to_all(convolved, ('seqi', 'seqo'), split_axis=0, concat_axis=0,...  3.57 us
    all_to_all x1, waiting for transfers between devices, local(): lax.all_to_all(convolved, ('seqi', 'seqo'), split_axis=0, concat_axis=0,...  3.4 us
    all_to_all x1, waiting for transfers between devices, local(): lax.all_to_all(payload, ('seqi', 'seqo'), split_axis=0, concat_axis=0, ti...  2.47 us
    ppermute x1, starting transfers between devices, local(): parts.append(lax.ppermute(totals, 'chan', ring))  1.58 us
  transfers between devices with their start and end apart: 3, of which 2 were waited for; matrix products, arithmetic and copies ran while one was open for 0% of the time, Pallas kernels for 42%

profile of v13, /device:TPU:0, one launch (start us, length us, event | category | flops | bytes accessed | tf_op | source)
XLA Modules:
  0.0 64.6 jit_solution(17409898816264406914)
XLA Ops:
  0.6 0.0 copy-start.4
  0.6 8.3 %shard_map.167 = (bf16[16,16,768]{2,1,0:T(8,128)(2,1)}, bf16[16,96,128]{2,1,0:T(8,128)(2,1)S(1)}, s32[8,128]{1,0:T(8,128)S(1)}, bf16[512,2048]{1,0:T(8,128)(2,1)S(1)}) custom-call(s32[1,64]{1,0:T(1,128)} %index.1, s32[1,64]{1,0:T(1,128)} %owners.1, bf16[2048,2048]{1,0:T(8,128)(2,1)} %refs_0_.3, bf16[2048,2048]{1,0:T(8,128)(2,1)} %refs_1_.3), custom_call_target="tpu_custom_call" | custom-call | flops 805306368 | bytes 16777216 | tf_op jit(solution)/shard_map/pallas_call | solution.py:489
  9.0 7.4 %all-to-all-start = ((bf16[16,16,768]{2,1,0:T(8,128)(2,1)}), bf16[16,16,768]{2,1,0:T(8,128)(2,1)S(1)}, u32[]{:S(2)}, u32[]{:S(2)}) async-start(bf16[16,16,768]{2,1,0:T(8,128)(2,1)} %get-tuple-element.25), calls=%async_computation | async-start | bytes 786432 | tf_op jit(solution)/shard_map/all_to_all | solution.py:551
  16.4 0.0 copy-done.4
  16.4 0.0 copy-start.6
  16.4 0.0 copy-start.7
  16.4 0.0 copy-start.8
  16.4 0.0 copy-start.9
  16.4 8.7 %shard_map.169 = (bf16[96,2048]{1,0:T(8,128)(2,1)S(1)}, f32[8,2048]{1,0:T(8,128)S(1)}, f32[96,128]{1,0:T(8,128)S(1)}, bf16[2048,2048]{1,0:T(8,128)(2,1)}, f32[8,...) custom-call(s32[8,128]{1,0:T(8,128)S(1)} %get-tuple-element.26.channels, ...), custom_call_target="tpu_custom_call" | custom-call | flops 805306368 | bytes 20971520 | tf_op jit(solution)/shard_map/pallas_call | solution.py:489
  25.2 0.0 copy-start
  25.2 0.0 copy-start.2
  25.2 0.0 copy-done.6
  25.2 0.0 copy-done.7
  25.2 0.0 copy-done.8
  25.2 0.0 copy-done.9
  25.2 1.5 %shard_map.168.spectra = f32[6,256,256]{2,1,0:T(8,128)S(1)} custom-call(bf16[6,32768]{1,0:T(8,128)(2,1)S(1)} %bitcast.6, bf16[1024,256]{1,0:T(8,128)(2,1)S(1)} %copy-done.8, f32[256,256]{1,0:T(8,128)S(1)} %copy-done.9, bf16[1024,256]{1,0:T(8,128)(2,1)S(1)} %copy-done.7), custom_call_target="tpu_custom_call" | custom-call | flops 1006632960 | bytes 4194304 | tf_op jit(solution)/shard_map/pallas_call | solution.py:489
  26.8 0.0 copy-done
  26.8 0.0 copy-done.2
  26.8 2.5 %all-to-all-done.signals = bf16[16,16,768]{2,1,0:T(8,128)(2,1)S(1)} async-done(((bf16[16,16,768]{2,1,0:T(8,128)(2,1)}), bf16[16,16,768]{2,1,0:T(8,128)(2,1)S(1)}, u32[]{:S(2)}, u32[]{:S(2)}) %all-to-all-start) | async-done | bytes 393248 | tf_op jit(solution)/shard_map/all_to_all | solution.py:551
  29.2 5.1 %shard_map.170 = bf16[16,16,768]{2,1,0:T(8,128)(2,1)} custom-call(bf16[16,16,768]{2,1,0:T(8,128)(2,1)S(1)} %all-to-all-done.signals, f32[6,256,256]{2,1,0:T(8,128)S(1)} %shard_map.168.spectra, bf16[1024,256]{1,0:T(8,128)(2,1)} %constant.8.clone.outer_fwd.outer_fwd_far, f32[256,256]{1,0:T(8,128)} %constant.9.clone.turn.turn_far, ...), custom_call_target="tpu_custom_call" | custom-call | flops 2214592512 | bytes 8388608 | tf_op jit(solution)/shard_map/pallas_call | solution.py:489
  34.4 3.6 %all-to-all-start.1 = ((bf16[16,16,768]{2,1,0:T(8,128)(2,1)}), bf16[16,16,768]{2,1,0:T(8,128)(2,1)S(1)}, u32[]{:S(2)}, u32[]{:S(2)}) async-start(bf16[16,16,768]{2,1,0:T(8,128)(2,1)} %shard_map.170), calls=%async_computation.1 | async-start | bytes 786432 | tf_op jit(solution)/shard_map/all_to_all | solution.py:614
  38.0 0.0 copy-start.1
  38.0 0.0 copy-start.3
  38.0 9.4 %shard_map.171 = (bf16[2048,2048]{1,0:T(8,128)(2,1)}, f32[8,1,128]{2,1,0:T(1,128)S(1)}, bf16[8,96,128]{2,1,0:T(8,128)(2,1)S(1)}, bf16[8,96,128]{2,1,0:T(8,128)(2,1)S(1)}) custom-call(bf16[96,2048]{1,0:T(8,128)(2,1)S(1)} %get-tuple-element.31.onehot, f32[8,2048]{1,0:T(8,128)S(1)} %get-tuple-element.32.others, ...), custom_call_target="tpu_custom_call", output_to_operand_aliasing={{0}: (7, {})} | custom-call | flops 805306368 | bytes 20971520 | tf_op jit(solution)/shard_map/pallas_call | solution.py:489
  47.4 0.0 copy-start.5
  47.4 3.4 %all-to-all-done.1.conv = bf16[16,16,768]{2,1,0:T(8,128)(2,1)S(1)} async-done(((bf16[16,16,768]{2,1,0:T(8,128)(2,1)}), bf16[16,16,768]{2,1,0:T(8,128)(2,1)S(1)}, u32[]{:S(2)}, u32[]{:S(2)}) %all-to-all-start.1) | async-done | bytes 393248 | tf_op jit(solution)/shard_map/all_to_all | solution.py:614
  50.8 0.0 copy-done.1
  50.8 0.0 copy-done.3
  50.8 0.5 shard_map.172
  51.4 1.6 %collective-permute-start = (f32[16,1,128]{2,1,0:T(1,128)S(1)}, f32[16,1,128]{2,1,0:T(1,128)S(1)}, u32[]{:S(2)}, u32[]{:S(2)}) collective-permute-start(f32[16,1,128]{2,1,0:T(1,128)S(1)} %get-tuple-element.46.refs_0_), channel_id=1, source_target_pairs={{0,16},{16,0},{1,17},{17,1},{2,18},{18,2},{3,19},{19,3},{4,20},{20... | collective-permute-start | bytes 24584 | tf_op jit(solution)/shard_map/ppermute | solution.py:642
  52.9 7.3 %shard_map.173 = (bf16[2048,2048]{1,0:T(8,128)(2,1)}, bf16[2048,2048]{1,0:T(8,128)(2,1)S(1)}) custom-call(bf16[2048,2048]{1,0:T(8,128)(2,1)} %get-tuple-element.34.base, bf16[16,96,128]{2,1,0:T(8,128)(2,1)S(1)} %get-tuple-element.44.hidden_kept, bf16[96,2048]{1,0:T(8,128)(2,1)S(1)} %get-tuple-element.31.onehot), custom_call_target="tpu_custom_call" | custom-call | flops 805306368 | bytes 16777216 | tf_op jit(solution)/shard_map/pallas_call | solution.py:489
  60.2 0.0 collective-permute-done.refs_1_
  60.2 0.0 copy-done.5
  60.2 4.4 %shard_map.174 = bf16[2048,2048]{1,0:T(8,128)(2,1)} custom-call(f32[16,1,128]{2,1,0:T(1,128)S(1)} %get-tuple-element.46.refs_0_, f32[16,1,128]{2,1,0:T(1,128)S(1)} %collective-permute-done.refs_1_, bf16[2048,2048]{1,0:T(8,128)(2,1)S(1)} %get-tuple-element.47.refs_2_, f32[1,2048]{1,0:T(1,128)S(1)} %bitcast.5), custom_call_target="tpu_custom_call" | custom-call | flops 16777216 | bytes 16777216 | tf_op jit(solution)/shard_map/pallas_call | solution.py:489
Async XLA Ops:
  0.6 15.7 %copy-start.4 = (f32[2048]{0:T(1024)S(1)}, f32[2048]{0:T(1024)}, u32[]{:S(2)}) copy-start(f32[2048]{0:T(1024)} %param.23) | copy-start | bytes 24580
  9.0 20.3 %all-to-all-start = ((bf16[16,16,768]{2,1,0:T(8,128)(2,1)}), bf16[16,16,768]{2,1,0:T(8,128)(2,1)S(1)}, u32[]{:S(2)}, u32[]{:S(2)}) async-start(bf16[16,16,768]{2,1,0:T(8,128)(2,1)} %get-tuple-element.25), calls=%async_computation | async-start | bytes 786432 | tf_op jit(solution)/shard_map/all_to_all | solution.py:551
  16.4 8.8 %copy-start.6 = (bf16[1,1,6,32768]{3,2,1,0:T(8,128)(2,1)S(1)}, bf16[1,1,6,32768]{3,2,1,0:T(8,128)(2,1)}, u32[]{:S(2)}) copy-start(bf16[1,1,6,32768]{3,2,1,0:T(8,128)(2,1)} %param.20) | copy-start | bytes 1179652
  16.4 8.8 %copy-start.7 = (bf16[1024,256]{1,0:T(8,128)(2,1)S(1)}, bf16[1024,256]{1,0:T(8,128)(2,1)}, u32[]{:S(2)}) copy-start(bf16[1024,256]{1,0:T(8,128)(2,1)} %constant.10.clone.inner.inner_far) | copy-start | bytes 1572868
  16.4 8.8 %copy-start.8 = (bf16[1024,256]{1,0:T(8,128)(2,1)S(1)}, bf16[1024,256]{1,0:T(8,128)(2,1)}, u32[]{:S(2)}) copy-start(bf16[1024,256]{1,0:T(8,128)(2,1)} %constant.8.clone.outer_fwd.outer_fwd_far) | copy-start | bytes 1572868
  16.4 8.8 %copy-start.9 = (f32[256,256]{1,0:T(8,128)S(1)}, f32[256,256]{1,0:T(8,128)}, u32[]{:S(2)}) copy-start(f32[256,256]{1,0:T(8,128)} %constant.9.clone.turn.turn_far) | copy-start | bytes 786436
  25.2 1.6 %copy-start = (bf16[8,96,128]{2,1,0:T(8,128)(2,1)}, bf16[8,96,128]{2,1,0:T(8,128)(2,1)S(1)}, u32[]{:S(2)}) copy-start(bf16[8,96,128]{2,1,0:T(8,128)(2,1)S(1)} %get-tuple-element.40.refs_2_) | copy-start | bytes 589828
  25.2 1.6 %copy-start.2 = (f32[96,128]{1,0:T(8,128)}, f32[96,128]{1,0:T(8,128)S(1)}, u32[]{:S(2)}) copy-start(f32[96,128]{1,0:T(8,128)S(1)} %get-tuple-element.37.skip_wide) | copy-start | bytes 147460
  34.4 16.4 %all-to-all-start.1 = ((bf16[16,16,768]{2,1,0:T(8,128)(2,1)}), bf16[16,16,768]{2,1,0:T(8,128)(2,1)S(1)}, u32[]{:S(2)}, u32[]{:S(2)}) async-start(bf16[16,16,768]{2,1,0:T(8,128)(2,1)} %shard_map.170), calls=%async_computation.1 | async-start | bytes 786432 | tf_op jit(solution)/shard_map/all_to_all | solution.py:614
  38.0 12.9 %copy-start.1 = (bf16[8,96,128]{2,1,0:T(8,128)(2,1)S(1)}, bf16[8,96,128]{2,1,0:T(8,128)(2,1)}, u32[]{:S(2)}) copy-start(bf16[8,96,128]{2,1,0:T(8,128)(2,1)} %copy-done) | copy-start | bytes 589828
  38.0 12.9 %copy-start.3 = (f32[96,128]{1,0:T(8,128)S(1)}, f32[96,128]{1,0:T(8,128)}, u32[]{:S(2)}) copy-start(f32[96,128]{1,0:T(8,128)} %copy-done.2) | copy-start | bytes 147460
  47.4 12.8 %copy-start.5 = (f32[2048]{0:T(1024)S(1)}, f32[2048]{0:T(1024)}, u32[]{:S(2)}) copy-start(f32[2048]{0:T(1024)} %param.24) | copy-start | bytes 24580
  51.4 8.9 %collective-permute-start = (f32[16,1,128]{2,1,0:T(1,128)S(1)}, f32[16,1,128]{2,1,0:T(1,128)S(1)}, u32[]{:S(2)}, u32[]{:S(2)}) collective-permute-start(f32[16,1,128]{2,1,0:T(1,128)S(1)} %get-tuple-element.46.refs_0_), channel_id=1, source_target_pairs={{0,16},{16,0},{1,17},{17,1},{2,18},{18,2},{3,19},{19,3},{4,20},{20... | collective-permute-start | bytes 24584 | tf_op jit(solution)/shard_map/ppermute | solution.py:642

commit v14 on v12

--- a/solution.py
+++ b/solution.py
@@ -252,7 +252,7 @@
 
 def pick_kernel(owner_count, slots, index, owners, gate, value, *refs):
     payload, picked, channels, gated_head = refs[:4]
-    acc, gate_stage, value_stage, onehot, lists, list_sems, sems = refs[4:]
+    acc, gate_stage, value_stage, onehot, payload_stage, lists, list_sems, sems = refs[4:]
     tile = gate_stage.shape[0] // sems.shape[1]
     list_copies = [
         pltpu.make_async_copy(source, lists.at[n], list_sems.at[n])
@@ -281,9 +281,19 @@
     head_tiles = gated_head.shape[0] // tile
     lax.fori_loop(0, head_tiles, lambda i, _: step(i, True), 0)
     lax.fori_loop(head_tiles, count, lambda i, _: step(i, False), 0)
+    sends = []
     for s in range(slots):
         part = jnp.swapaxes(acc[:, s * owner_count : (s + 1) * owner_count, :], 0, 1)
-        payload[:, :, s * LANES : (s + 1) * LANES] = part.astype(bf16)
+        lanes = pl.ds(s * LANES, LANES)
+        payload_stage[:, :, lanes] = part.astype(bf16)
+        sends.append(
+            pltpu.make_async_copy(
+                payload_stage.at[:, :, lanes], payload.at[:, :, lanes], list_sems.at[2 + s]
+            )
+        )
+        sends[-1].start()
+    for send in sends:
+        send.wait()
 
 
 def filter_kernel(filters, outer_fwd, turn, inner, spectra):
@@ -430,9 +440,7 @@
     lax.fori_loop(0, count, lambda i, _: (copy(i).wait(), 0)[1], 0)
 
 
-def norm_kernel(width, count, *refs):
-    parts = refs[:count]
-    held, gain, normed, stage, turned, sems = refs[count:]
+def norm_kernel(width, gathered, held, gain, normed, stage, turned, sems):
     slab = held.shape[1]
 
     def copy(i):
@@ -440,9 +448,9 @@
         return pltpu.make_async_copy(stage.at[rows, :], normed.at[rows, :], sems.at[i])
 
     def step(i, _):
-        total = parts[0][i]
-        for part in parts[1:]:
-            total = total + part[i]
+        total = gathered[0, i]
+        for n in range(1, gathered.shape[0]):
+            total = total + gathered[n, i]
         scale = lax.rsqrt(total / width + norm_eps)
         turned[...] = jnp.broadcast_to(scale, (LANES, LANES)).T
         first = pl.multiple_of(i * LANES, LANES)
@@ -511,7 +519,7 @@
     payload, picked, channels, gated_head = call(
         functools.partial(pick_kernel, owner_count, slots),
         [
-            sds(buffer, bf16),
+            pltpu.HBM(buffer, bf16),
             picks,
             sds((8, lanes_rows), jnp.int32),
             pltpu.VMEM((head_rows, slab), bf16),
@@ -525,11 +533,13 @@
             pltpu.VMEM(whole, bf16),
             pltpu.VMEM(whole, bf16),
             pltpu.VMEM((rows, slab), bf16),
+            pltpu.VMEM(buffer, bf16),
             pltpu.VMEM((2,) + kept_index.shape, jnp.int32),
-            pltpu.SemaphoreType.DMA((2,)),
+            pltpu.SemaphoreType.DMA((2 + slots,)),
             pltpu.SemaphoreType.DMA((2, tok_rows // tile)),
         ],
         far=(0, 1, 2, 3),
+        far_outs=(0,),
     )
 
     incoming = lax.all_to_all(payload, ("seqo", "seqi"), split_axis=0, concat_axis=0, tiled=True)
@@ -620,10 +630,7 @@
         16 * MIB,
     )
 
-    parts = [totals]
-    for shift in range(1, chan_devices):
-        ring = [(i, (i + shift) % chan_devices) for i in range(chan_devices)]
-        parts.append(lax.ppermute(totals, "chan", ring))
+    gathered = lax.all_gather(totals, "chan")
 
     hidden, held = call(
         hidden_kernel,
@@ -641,9 +648,9 @@
         far_outs=(0,),
     )
     (normed,) = call(
-        functools.partial(norm_kernel, float(slab * chan_devices), len(parts)),
+        functools.partial(norm_kernel, float(slab * chan_devices)),
         [pltpu.HBM(whole, bf16)],
-        parts + [in_vmem(held), gain_row],
+        [gathered, in_vmem(held), gain_row],
         4 * tok_rows * slab,
         2 * dense,
         16 * MIB,

time: 64.3 us -> 67 us (1.042)
  blocking collectives: 0 us -> 4.36 us
  starting transfers between devices: 13.2 us -> 11.6 us
    all_gather x0 -> x1, blocking collectives: none -> 4.36 us  [local(): gathered = lax.all_gather(totals, 'chan')]
    ppermute x1 -> x0, starting transfers between devices: 1.58 us -> none  [local(): parts.append(lax.ppermute(totals, 'chan', ring))]
  transfers between devices with their start and end apart: 3 -> 2, of which waited for: 2 -> 2; matrix products, arithmetic and copies ran while one was open for 0% -> 0% of each run, Pallas kernels for 42% -> 30%
where the time goes in v14:
time: 67 us; the launch traced here: 66.6 us
  Pallas kernels  45.3 us (68%)
  starting transfers between devices  11.6 us (17%)
  waiting for transfers between devices  4.52 us (7%)
  blocking collectives  4.36 us (7%)
  between operations  0.84 us (1%)
    pallas_call x8, Pallas kernels, call(): pl.pallas_call(kernel, out_shape=outs, in_specs=[away if n in far else ne...  45.3 us
    all_to_all x1, starting transfers between devices, local(): lax.all_to_all(payload, ('seqo', 'seqi'), split_axis=0, concat_axis=0, ti...  7.37 us
    all_gather x1, blocking collectives, local(): gathered = lax.all_gather(totals, 'chan')  4.36 us
    all_to_all x1, starting transfers between devices, local(): lax.all_to_all(convolved, ('seqo', 'seqi'), split_axis=0, concat_axis=0,...  4.22 us
    all_to_all x1, waiting for transfers between devices, local(): lax.all_to_all(convolved, ('seqo', 'seqi'), split_axis=0, concat_axis=0,...  2.73 us
    all_to_all x1, waiting for transfers between devices, local(): lax.all_to_all(payload, ('seqo', 'seqi'), split_axis=0, concat_axis=0, ti...  1.79 us
  transfers between devices with their start and end apart: 2, of which 2 were waited for; matrix products, arithmetic and copies ran while one was open for 0% of the time, Pallas kernels for 30%

profile of v14, /device:TPU:0, one launch (start us, length us, event | category | flops | bytes accessed | tf_op | source)
XLA Modules:
  0.0 66.6 jit_solution(6194644728305911913)
XLA Ops:
  0.6 0.0 copy-start.4
  0.6 8.3 %shard_map.167 = (bf16[16,16,768]{2,1,0:T(8,128)(2,1)}, bf16[16,96,128]{2,1,0:T(8,128)(2,1)S(1)}, s32[8,128]{1,0:T(8,128)S(1)}, bf16[512,2048]{1,0:T(8,128)(2,1)S(1)}) custom-call(s32[1,64]{1,0:T(1,128)} %index.1, s32[1,64]{1,0:T(1,128)} %owners.1, bf16[2048,2048]{1,0:T(8,128)(2,1)} %refs_0_.3, bf16[2048,2048]{1,0:T(8,128)(2,1)} %refs_1_.3), custom_call_target="tpu_custom_call" | custom-call | flops 805306368 | bytes 16777216 | tf_op jit(solution)/shard_map/pallas_call | solution.py:482
  8.9 7.4 %all-to-all-start = ((bf16[16,16,768]{2,1,0:T(8,128)(2,1)}), bf16[16,16,768]{2,1,0:T(8,128)(2,1)S(1)}, u32[]{:S(2)}, u32[]{:S(2)}) async-start(bf16[16,16,768]{2,1,0:T(8,128)(2,1)} %get-tuple-element.25), calls=%async_computation | async-start | bytes 786432 | tf_op jit(solution)/shard_map/all_to_all | solution.py:545
  16.3 0.0 copy-done.4
  16.3 0.0 copy-start.6
  16.3 0.0 copy-start.7
  16.3 0.0 copy-start.8
  16.4 0.0 copy-start.9
  16.4 8.7 %shard_map.169 = (bf16[96,2048]{1,0:T(8,128)(2,1)S(1)}, f32[8,2048]{1,0:T(8,128)S(1)}, f32[96,128]{1,0:T(8,128)S(1)}, bf16[2048,2048]{1,0:T(8,128)(2,1)}, f32[8,...) custom-call(s32[8,128]{1,0:T(8,128)S(1)} %get-tuple-element.26.channels, ...), custom_call_target="tpu_custom_call" | custom-call | flops 805306368 | bytes 20971520 | tf_op jit(solution)/shard_map/pallas_call | solution.py:482
  25.1 0.0 copy-start
  25.1 0.0 copy-start.2
  25.1 0.0 copy-done.6
  25.1 0.0 copy-done.7
  25.1 0.0 copy-done.8
  25.2 0.0 copy-done.9
  25.2 1.5 %shard_map.168.spectra = f32[6,256,256]{2,1,0:T(8,128)S(1)} custom-call(bf16[6,32768]{1,0:T(8,128)(2,1)S(1)} %bitcast.8, bf16[1024,256]{1,0:T(8,128)(2,1)S(1)} %copy-done.8, f32[256,256]{1,0:T(8,128)S(1)} %copy-done.9, bf16[1024,256]{1,0:T(8,128)(2,1)S(1)} %copy-done.7), custom_call_target="tpu_custom_call" | custom-call | flops 1006632960 | bytes 4194304 | tf_op jit(solution)/shard_map/pallas_call | solution.py:482
  26.7 0.0 copy-done
  26.7 0.0 copy-done.2
  26.7 1.8 %all-to-all-done.signals = bf16[16,16,768]{2,1,0:T(8,128)(2,1)S(1)} async-done(((bf16[16,16,768]{2,1,0:T(8,128)(2,1)}), bf16[16,16,768]{2,1,0:T(8,128)(2,1)S(1)}, u32[]{:S(2)}, u32[]{:S(2)}) %all-to-all-start) | async-done | bytes 393248 | tf_op jit(solution)/shard_map/all_to_all | solution.py:545
  28.5 5.1 %shard_map.170 = bf16[16,16,768]{2,1,0:T(8,128)(2,1)} custom-call(bf16[16,16,768]{2,1,0:T(8,128)(2,1)S(1)} %all-to-all-done.signals, f32[6,256,256]{2,1,0:T(8,128)S(1)} %shard_map.168.spectra, bf16[1024,256]{1,0:T(8,128)(2,1)} %constant.8.clone.outer_fwd.outer_fwd_far, f32[256,256]{1,0:T(8,128)} %constant.9.clone.turn.turn_far, ...), custom_call_target="tpu_custom_call" | custom-call | flops 2214592512 | bytes 8388608 | tf_op jit(solution)/shard_map/pallas_call | solution.py:482
  33.6 4.2 %all-to-all-start.1 = ((bf16[16,16,768]{2,1,0:T(8,128)(2,1)}), bf16[16,16,768]{2,1,0:T(8,128)(2,1)S(1)}, u32[]{:S(2)}, u32[]{:S(2)}) async-start(bf16[16,16,768]{2,1,0:T(8,128)(2,1)} %shard_map.170), calls=%async_computation.1 | async-start | bytes 786432 | tf_op jit(solution)/shard_map/all_to_all | solution.py:608
  37.9 0.0 copy-start.1
  37.9 0.0 copy-start.3
  37.9 9.4 %shard_map.171 = (bf16[2048,2048]{1,0:T(8,128)(2,1)}, f32[8,1,128]{2,1,0:T(1,128)S(1)}, bf16[8,96,128]{2,1,0:T(8,128)(2,1)S(1)}, bf16[8,96,128]{2,1,0:T(8,128)(2,1)S(1)}) custom-call(bf16[96,2048]{1,0:T(8,128)(2,1)S(1)} %get-tuple-element.31.onehot, f32[8,2048]{1,0:T(8,128)S(1)} %get-tuple-element.32.others, ...), custom_call_target="tpu_custom_call", output_to_operand_aliasing={{0}: (7, {})} | custom-call | flops 805306368 | bytes 20971520 | tf_op jit(solution)/shard_map/pallas_call | solution.py:482
  47.3 0.0 copy-start.5
  47.3 2.7 %all-to-all-done.1.conv = bf16[16,16,768]{2,1,0:T(8,128)(2,1)S(1)} async-done(((bf16[16,16,768]{2,1,0:T(8,128)(2,1)}), bf16[16,16,768]{2,1,0:T(8,128)(2,1)S(1)}, u32[]{:S(2)}, u32[]{:S(2)}) %all-to-all-start.1) | async-done | bytes 393248 | tf_op jit(solution)/shard_map/all_to_all | solution.py:608
  50.1 0.0 copy-done.1
  50.1 0.0 copy-done.3
  50.1 0.5 shard_map.172
  50.6 4.4 %all-gather = f32[32,1,128]{2,1,0:T(1,128)S(1)} all-gather(f32[16,1,128]{2,1,0:T(1,128)S(1)} %get-tuple-element.46), channel_id=2, replica_groups=mesh['chan'=2,'seqo'=4,'seqi'=4] {'chan'}, dimensions={0}, use_global_device_ids=true | all-gather | bytes 24576 | tf_op jit(solution)/shard_map/all_gather | solution.py:633
  55.0 7.3 %shard_map.173 = (bf16[2048,2048]{1,0:T(8,128)(2,1)}, bf16[2048,2048]{1,0:T(8,128)(2,1)S(1)}) custom-call(bf16[2048,2048]{1,0:T(8,128)(2,1)} %get-tuple-element.34.base, bf16[16,96,128]{2,1,0:T(8,128)(2,1)S(1)} %get-tuple-element.44.hidden_kept, bf16[96,2048]{1,0:T(8,128)(2,1)S(1)} %get-tuple-element.31.onehot), custom_call_target="tpu_custom_call" | custom-call | flops 805306368 | bytes 16777216 | tf_op jit(solution)/shard_map/pallas_call | solution.py:482
  62.3 0.0 copy-done.5
  62.3 4.4 %shard_map.174 = bf16[2048,2048]{1,0:T(8,128)(2,1)} custom-call(f32[2,16,1,128]{3,2,1,0:T(1,128)S(1)} %bitcast.4, bf16[2048,2048]{1,0:T(8,128)(2,1)S(1)} %get-tuple-element.47.held, f32[1,2048]{1,0:T(1,128)S(1)} %bitcast.7), custom_call_target="tpu_custom_call" | custom-call | flops 16777216 | bytes 16777216 | tf_op jit(solution)/shard_map/pallas_call | solution.py:482
Async XLA Ops:
  0.6 15.7 %copy-start.4 = (f32[2048]{0:T(1024)S(1)}, f32[2048]{0:T(1024)}, u32[]{:S(2)}) copy-start(f32[2048]{0:T(1024)} %param.23) | copy-start | bytes 24580
  8.9 19.6 %all-to-all-start = ((bf16[16,16,768]{2,1,0:T(8,128)(2,1)}), bf16[16,16,768]{2,1,0:T(8,128)(2,1)S(1)}, u32[]{:S(2)}, u32[]{:S(2)}) async-start(bf16[16,16,768]{2,1,0:T(8,128)(2,1)} %get-tuple-element.25), calls=%async_computation | async-start | bytes 786432 | tf_op jit(solution)/shard_map/all_to_all | solution.py:545
  16.3 8.8 %copy-start.6 = (bf16[1,1,6,32768]{3,2,1,0:T(8,128)(2,1)S(1)}, bf16[1,1,6,32768]{3,2,1,0:T(8,128)(2,1)}, u32[]{:S(2)}) copy-start(bf16[1,1,6,32768]{3,2,1,0:T(8,128)(2,1)} %param.20) | copy-start | bytes 1179652
  16.3 8.8 %copy-start.7 = (bf16[1024,256]{1,0:T(8,128)(2,1)S(1)}, bf16[1024,256]{1,0:T(8,128)(2,1)}, u32[]{:S(2)}) copy-start(bf16[1024,256]{1,0:T(8,128)(2,1)} %constant.10.clone.inner.inner_far) | copy-start | bytes 1572868
  16.3 8.8 %copy-start.8 = (bf16[1024,256]{1,0:T(8,128)(2,1)S(1)}, bf16[1024,256]{1,0:T(8,128)(2,1)}, u32[]{:S(2)}) copy-start(bf16[1024,256]{1,0:T(8,128)(2,1)} %constant.8.clone.outer_fwd.outer_fwd_far) | copy-start | bytes 1572868
  16.4 8.8 %copy-start.9 = (f32[256,256]{1,0:T(8,128)S(1)}, f32[256,256]{1,0:T(8,128)}, u32[]{:S(2)}) copy-start(f32[256,256]{1,0:T(8,128)} %constant.9.clone.turn.turn_far) | copy-start | bytes 786436
  25.1 1.6 %copy-start = (bf16[8,96,128]{2,1,0:T(8,128)(2,1)}, bf16[8,96,128]{2,1,0:T(8,128)(2,1)S(1)}, u32[]{:S(2)}) copy-start(bf16[8,96,128]{2,1,0:T(8,128)(2,1)S(1)} %get-tuple-element.40.refs_2_) | copy-start | bytes 589828
  25.1 1.6 %copy-start.2 = (f32[96,128]{1,0:T(8,128)}, f32[96,128]{1,0:T(8,128)S(1)}, u32[]{:S(2)}) copy-start(f32[96,128]{1,0:T(8,128)S(1)} %get-tuple-element.37.skip_wide) | copy-start | bytes 147460
  33.6 16.4 %all-to-all-start.1 = ((bf16[16,16,768]{2,1,0:T(8,128)(2,1)}), bf16[16,16,768]{2,1,0:T(8,128)(2,1)S(1)}, u32[]{:S(2)}, u32[]{:S(2)}) async-start(bf16[16,16,768]{2,1,0:T(8,128)(2,1)} %shard_map.170), calls=%async_computation.1 | async-start | bytes 786432 | tf_op jit(solution)/shard_map/all_to_all | solution.py:608
  37.9 12.2 %copy-start.1 = (bf16[8,96,128]{2,1,0:T(8,128)(2,1)S(1)}, bf16[8,96,128]{2,1,0:T(8,128)(2,1)}, u32[]{:S(2)}) copy-start(bf16[8,96,128]{2,1,0:T(8,128)(2,1)} %copy-done) | copy-start | bytes 589828
  37.9 12.2 %copy-start.3 = (f32[96,128]{1,0:T(8,128)S(1)}, f32[96,128]{1,0:T(8,128)}, u32[]{:S(2)}) copy-start(f32[96,128]{1,0:T(8,128)} %copy-done.2) | copy-start | bytes 147460
  47.3 14.9 %copy-start.5 = (f32[2048]{0:T(1024)S(1)}, f32[2048]{0:T(1024)}, u32[]{:S(2)}) copy-start(f32[2048]{0:T(1024)} %param.24) | copy-start | bytes 24580

commit v15 on v14

--- a/solution.py
+++ b/solution.py
@@ -261,7 +261,7 @@
     for copy in list_copies:
         copy.start()
     count = sems.shape[1]
-    _, wait, _ = fetch((gate, value), (gate_stage, value_stage), sems, tile, 0, 4)
+    _, wait, _ = fetch((gate, value), (gate_stage, value_stage), sems, tile, 0, 5)
     for copy in list_copies:
         copy.wait()
     row = channel_of_row(lists[0], lists[1], owner_count, channels.shape[1])
@@ -440,7 +440,9 @@
     lax.fori_loop(0, count, lambda i, _: (copy(i).wait(), 0)[1], 0)
 
 
-def norm_kernel(width, gathered, held, gain, normed, stage, turned, sems):
+def norm_kernel(width, count, *refs):
+    parts = refs[:count]
+    held, gain, normed, stage, turned, sems = refs[count:]
     slab = held.shape[1]
 
     def copy(i):
@@ -448,9 +450,9 @@
         return pltpu.make_async_copy(stage.at[rows, :], normed.at[rows, :], sems.at[i])
 
     def step(i, _):
-        total = gathered[0, i]
-        for n in range(1, gathered.shape[0]):
-            total = total + gathered[n, i]
+        total = parts[0][i]
+        for part in parts[1:]:
+            total = total + part[i]
         scale = lax.rsqrt(total / width + norm_eps)
         turned[...] = jnp.broadcast_to(scale, (LANES, LANES)).T
         first = pl.multiple_of(i * LANES, LANES)
@@ -630,7 +632,10 @@
         16 * MIB,
     )
 
-    gathered = lax.all_gather(totals, "chan")
+    parts = [totals]
+    for shift in range(1, chan_devices):
+        ring = [(i, (i + shift) % chan_devices) for i in range(chan_devices)]
+        parts.append(lax.ppermute(totals, "chan", ring))
 
     hidden, held = call(
         hidden_kernel,
@@ -648,9 +653,9 @@
         far_outs=(0,),
     )
     (normed,) = call(
-        functools.partial(norm_kernel, float(slab * chan_devices)),
+        functools.partial(norm_kernel, float(slab * chan_devices), len(parts)),
         [pltpu.HBM(whole, bf16)],
-        [gathered, in_vmem(held), gain_row],
+        parts + [in_vmem(held), gain_row],
         4 * tok_rows * slab,
         2 * dense,
         16 * MIB,

time: 67 us -> 64.7 us (0.966)
  blocking collectives: 4.36 us -> 0 us
  starting transfers between devices: 11.6 us -> 13.2 us
    all_gather x1 -> x0, blocking collectives: 4.36 us -> none  [local(): gathered = lax.all_gather(totals, 'chan')]
    ppermute x0 -> x1, starting transfers between devices: none -> 1.58 us  [local(): parts.append(lax.ppermute(totals, 'chan', ring))]
  transfers between devices with their start and end apart: 2 -> 3, of which waited for: 2 -> 2; matrix products, arithmetic and copies ran while one was open for 0% -> 0% of each run, Pallas kernels for 30% -> 42%
where the time goes in v15:
time: 64.7 us; the launch traced here: 64.3 us
  Pallas kernels  45.7 us (71%)
  starting transfers between devices  13.2 us (20%)
  waiting for transfers between devices  4.52 us (7%)
  between operations  0.84 us (1%)
    pallas_call x8, Pallas kernels, call(): pl.pallas_call(kernel, out_shape=outs, in_specs=[away if n in far else ne...  45.7 us
    all_to_all x1, starting transfers between devices, local(): lax.all_to_all(payload, ('seqo', 'seqi'), split_axis=0, concat_axis=0, ti...  7.37 us
    all_to_all x1, starting transfers between devices, local(): lax.all_to_all(convolved, ('seqo', 'seqi'), split_axis=0, concat_axis=0,...  4.23 us
    all_to_all x1, waiting for transfers between devices, local(): lax.all_to_all(convolved, ('seqo', 'seqi'), split_axis=0, concat_axis=0,...  2.73 us
    all_to_all x1, waiting for transfers between devices, local(): lax.all_to_all(payload, ('seqo', 'seqi'), split_axis=0, concat_axis=0, ti...  1.79 us
    ppermute x1, starting transfers between devices, local(): parts.append(lax.ppermute(totals, 'chan', ring))  1.58 us
  transfers between devices with their start and end apart: 3, of which 2 were waited for; matrix products, arithmetic and copies ran while one was open for 0% of the time, Pallas kernels for 42%

profile of v15, /device:TPU:0, one launch (start us, length us, event | category | flops | bytes accessed | tf_op | source)
XLA Modules:
  0.0 64.3 jit_solution(9407140391704593134)
XLA Ops:
  0.6 0.0 copy-start.4
  0.6 8.7 %shard_map.167 = (bf16[16,16,768]{2,1,0:T(8,128)(2,1)}, bf16[16,96,128]{2,1,0:T(8,128)(2,1)S(1)}, s32[8,128]{1,0:T(8,128)S(1)}, bf16[512,2048]{1,0:T(8,128)(2,1)S(1)}) custom-call(s32[1,64]{1,0:T(1,128)} %index.1, s32[1,64]{1,0:T(1,128)} %owners.1, bf16[2048,2048]{1,0:T(8,128)(2,1)} %refs_0_.3, bf16[2048,2048]{1,0:T(8,128)(2,1)} %refs_1_.3), custom_call_target="tpu_custom_call" | custom-call | flops 805306368 | bytes 16777216 | tf_op jit(solution)/shard_map/pallas_call | solution.py:484
  9.4 7.4 %all-to-all-start = ((bf16[16,16,768]{2,1,0:T(8,128)(2,1)}), bf16[16,16,768]{2,1,0:T(8,128)(2,1)S(1)}, u32[]{:S(2)}, u32[]{:S(2)}) async-start(bf16[16,16,768]{2,1,0:T(8,128)(2,1)} %get-tuple-element.25), calls=%async_computation | async-start | bytes 786432 | tf_op jit(solution)/shard_map/all_to_all | solution.py:547
  16.7 0.0 copy-done.4
  16.8 0.0 copy-start.6
  16.8 0.0 copy-start.7
  16.8 0.0 copy-start.8
  16.8 0.0 copy-start.9
  16.8 8.7 %shard_map.169 = (bf16[96,2048]{1,0:T(8,128)(2,1)S(1)}, f32[8,2048]{1,0:T(8,128)S(1)}, f32[96,128]{1,0:T(8,128)S(1)}, bf16[2048,2048]{1,0:T(8,128)(2,1)}, f32[8,...) custom-call(s32[8,128]{1,0:T(8,128)S(1)} %get-tuple-element.26.channels, ...), custom_call_target="tpu_custom_call" | custom-call | flops 805306368 | bytes 20971520 | tf_op jit(solution)/shard_map/pallas_call | solution.py:484
  25.5 0.0 copy-start
  25.5 0.0 copy-start.2
  25.6 0.0 copy-done.6
  25.6 0.0 copy-done.7
  25.6 0.0 copy-done.8
  25.6 0.0 copy-done.9
  25.6 1.5 %shard_map.168.spectra = f32[6,256,256]{2,1,0:T(8,128)S(1)} custom-call(bf16[6,32768]{1,0:T(8,128)(2,1)S(1)} %bitcast.6, bf16[1024,256]{1,0:T(8,128)(2,1)S(1)} %copy-done.8, f32[256,256]{1,0:T(8,128)S(1)} %copy-done.9, bf16[1024,256]{1,0:T(8,128)(2,1)S(1)} %copy-done.7), custom_call_target="tpu_custom_call" | custom-call | flops 1006632960 | bytes 4194304 | tf_op jit(solution)/shard_map/pallas_call | solution.py:484
  27.1 0.0 copy-done
  27.1 0.0 copy-done.2
  27.2 1.8 %all-to-all-done.signals = bf16[16,16,768]{2,1,0:T(8,128)(2,1)S(1)} async-done(((bf16[16,16,768]{2,1,0:T(8,128)(2,1)}), bf16[16,16,768]{2,1,0:T(8,128)(2,1)S(1)}, u32[]{:S(2)}, u32[]{:S(2)}) %all-to-all-start) | async-done | bytes 393248 | tf_op jit(solution)/shard_map/all_to_all | solution.py:547
  28.9 5.1 %shard_map.170 = bf16[16,16,768]{2,1,0:T(8,128)(2,1)} custom-call(bf16[16,16,768]{2,1,0:T(8,128)(2,1)S(1)} %all-to-all-done.signals, f32[6,256,256]{2,1,0:T(8,128)S(1)} %shard_map.168.spectra, bf16[1024,256]{1,0:T(8,128)(2,1)} %constant.8.clone.outer_fwd.outer_fwd_far, f32[256,256]{1,0:T(8,128)} %constant.9.clone.turn.turn_far, ...), custom_call_target="tpu_custom_call" | custom-call | flops 2214592512 | bytes 8388608 | tf_op jit(solution)/shard_map/pallas_call | solution.py:484
  34.1 4.2 %all-to-all-start.1 = ((bf16[16,16,768]{2,1,0:T(8,128)(2,1)}), bf16[16,16,768]{2,1,0:T(8,128)(2,1)S(1)}, u32[]{:S(2)}, u32[]{:S(2)}) async-start(bf16[16,16,768]{2,1,0:T(8,128)(2,1)} %shard_map.170), calls=%async_computation.1 | async-start | bytes 786432 | tf_op jit(solution)/shard_map/all_to_all | solution.py:610
  38.3 0.0 copy-start.1
  38.3 0.0 copy-start.3
  38.3 9.4 %shard_map.171 = (bf16[2048,2048]{1,0:T(8,128)(2,1)}, f32[8,1,128]{2,1,0:T(1,128)S(1)}, bf16[8,96,128]{2,1,0:T(8,128)(2,1)S(1)}, bf16[8,96,128]{2,1,0:T(8,128)(2,1)S(1)}) custom-call(bf16[96,2048]{1,0:T(8,128)(2,1)S(1)} %get-tuple-element.31.onehot, f32[8,2048]{1,0:T(8,128)S(1)} %get-tuple-element.32.others, ...), custom_call_target="tpu_custom_call", output_to_operand_aliasing={{0}: (7, {})} | custom-call | flops 805306368 | bytes 20971520 | tf_op jit(solution)/shard_map/pallas_call | solution.py:484
  47.8 0.0 copy-start.5
  47.8 2.7 %all-to-all-done.1.conv = bf16[16,16,768]{2,1,0:T(8,128)(2,1)S(1)} async-done(((bf16[16,16,768]{2,1,0:T(8,128)(2,1)}), bf16[16,16,768]{2,1,0:T(8,128)(2,1)S(1)}, u32[]{:S(2)}, u32[]{:S(2)}) %all-to-all-start.1) | async-done | bytes 393248 | tf_op jit(solution)/shard_map/all_to_all | solution.py:610
  50.5 0.0 copy-done.1
  50.5 0.0 copy-done.3
  50.5 0.5 shard_map.172
  51.0 1.6 %collective-permute-start = (f32[16,1,128]{2,1,0:T(1,128)S(1)}, f32[16,1,128]{2,1,0:T(1,128)S(1)}, u32[]{:S(2)}, u32[]{:S(2)}) collective-permute-start(f32[16,1,128]{2,1,0:T(1,128)S(1)} %get-tuple-element.46.refs_0_), channel_id=1, source_target_pairs={{0,16},{16,0},{1,17},{17,1},{2,18},{18,2},{3,19},{19,3},{4,20},{20... | collective-permute-start | bytes 24584 | tf_op jit(solution)/shard_map/ppermute | solution.py:638
  52.6 7.3 %shard_map.173 = (bf16[2048,2048]{1,0:T(8,128)(2,1)}, bf16[2048,2048]{1,0:T(8,128)(2,1)S(1)}) custom-call(bf16[2048,2048]{1,0:T(8,128)(2,1)} %get-tuple-element.34.base, bf16[16,96,128]{2,1,0:T(8,128)(2,1)S(1)} %get-tuple-element.44.hidden_kept, bf16[96,2048]{1,0:T(8,128)(2,1)S(1)} %get-tuple-element.31.onehot), custom_call_target="tpu_custom_call" | custom-call | flops 805306368 | bytes 16777216 | tf_op jit(solution)/shard_map/pallas_call | solution.py:484
  59.9 0.0 collective-permute-done.refs_1_
  59.9 0.0 copy-done.5
  59.9 4.4 %shard_map.174 = bf16[2048,2048]{1,0:T(8,128)(2,1)} custom-call(f32[16,1,128]{2,1,0:T(1,128)S(1)} %get-tuple-element.46.refs_0_, f32[16,1,128]{2,1,0:T(1,128)S(1)} %collective-permute-done.refs_1_, bf16[2048,2048]{1,0:T(8,128)(2,1)S(1)} %get-tuple-element.47.refs_2_, f32[1,2048]{1,0:T(1,128)S(1)} %bitcast.5), custom_call_target="tpu_custom_call" | custom-call | flops 16777216 | bytes 16777216 | tf_op jit(solution)/shard_map/pallas_call | solution.py:484
Async XLA Ops:
  0.6 16.1 %copy-start.4 = (f32[2048]{0:T(1024)S(1)}, f32[2048]{0:T(1024)}, u32[]{:S(2)}) copy-start(f32[2048]{0:T(1024)} %param.23) | copy-start | bytes 24580
  9.4 19.6 %all-to-all-start = ((bf16[16,16,768]{2,1,0:T(8,128)(2,1)}), bf16[16,16,768]{2,1,0:T(8,128)(2,1)S(1)}, u32[]{:S(2)}, u32[]{:S(2)}) async-start(bf16[16,16,768]{2,1,0:T(8,128)(2,1)} %get-tuple-element.25), calls=%async_computation | async-start | bytes 786432 | tf_op jit(solution)/shard_map/all_to_all | solution.py:547
  16.8 8.8 %copy-start.6 = (bf16[1,1,6,32768]{3,2,1,0:T(8,128)(2,1)S(1)}, bf16[1,1,6,32768]{3,2,1,0:T(8,128)(2,1)}, u32[]{:S(2)}) copy-start(bf16[1,1,6,32768]{3,2,1,0:T(8,128)(2,1)} %param.20) | copy-start | bytes 1179652
  16.8 8.8 %copy-start.7 = (bf16[1024,256]{1,0:T(8,128)(2,1)S(1)}, bf16[1024,256]{1,0:T(8,128)(2,1)}, u32[]{:S(2)}) copy-start(bf16[1024,256]{1,0:T(8,128)(2,1)} %constant.10.clone.inner.inner_far) | copy-start | bytes 1572868
  16.8 8.8 %copy-start.8 = (bf16[1024,256]{1,0:T(8,128)(2,1)S(1)}, bf16[1024,256]{1,0:T(8,128)(2,1)}, u32[]{:S(2)}) copy-start(bf16[1024,256]{1,0:T(8,128)(2,1)} %constant.8.clone.outer_fwd.outer_fwd_far) | copy-start | bytes 1572868
  16.8 8.8 %copy-start.9 = (f32[256,256]{1,0:T(8,128)S(1)}, f32[256,256]{1,0:T(8,128)}, u32[]{:S(2)}) copy-start(f32[256,256]{1,0:T(8,128)} %constant.9.clone.turn.turn_far) | copy-start | bytes 786436
  25.5 1.6 %copy-start = (bf16[8,96,128]{2,1,0:T(8,128)(2,1)}, bf16[8,96,128]{2,1,0:T(8,128)(2,1)S(1)}, u32[]{:S(2)}) copy-start(bf16[8,96,128]{2,1,0:T(8,128)(2,1)S(1)} %get-tuple-element.40.refs_2_) | copy-start | bytes 589828
  25.5 1.6 %copy-start.2 = (f32[96,128]{1,0:T(8,128)}, f32[96,128]{1,0:T(8,128)S(1)}, u32[]{:S(2)}) copy-start(f32[96,128]{1,0:T(8,128)S(1)} %get-tuple-element.37.skip_wide) | copy-start | bytes 147460
  34.1 16.4 %all-to-all-start.1 = ((bf16[16,16,768]{2,1,0:T(8,128)(2,1)}), bf16[16,16,768]{2,1,0:T(8,128)(2,1)S(1)}, u32[]{:S(2)}, u32[]{:S(2)}) async-start(bf16[16,16,768]{2,1,0:T(8,128)(2,1)} %shard_map.170), calls=%async_computation.1 | async-start | bytes 786432 | tf_op jit(solution)/shard_map/all_to_all | solution.py:610
  38.3 12.2 %copy-start.1 = (bf16[8,96,128]{2,1,0:T(8,128)(2,1)S(1)}, bf16[8,96,128]{2,1,0:T(8,128)(2,1)}, u32[]{:S(2)}) copy-start(bf16[8,96,128]{2,1,0:T(8,128)(2,1)} %copy-done) | copy-start | bytes 589828
  38.3 12.2 %copy-start.3 = (f32[96,128]{1,0:T(8,128)S(1)}, f32[96,128]{1,0:T(8,128)}, u32[]{:S(2)}) copy-start(f32[96,128]{1,0:T(8,128)} %copy-done.2) | copy-start | bytes 147460
  47.8 12.2 %copy-start.5 = (f32[2048]{0:T(1024)S(1)}, f32[2048]{0:T(1024)}, u32[]{:S(2)}) copy-start(f32[2048]{0:T(1024)} %param.24) | copy-start | bytes 24580
  51.0 8.9 %collective-permute-start = (f32[16,1,128]{2,1,0:T(1,128)S(1)}, f32[16,1,128]{2,1,0:T(1,128)S(1)}, u32[]{:S(2)}, u32[]{:S(2)}) collective-permute-start(f32[16,1,128]{2,1,0:T(1,128)S(1)} %get-tuple-element.46.refs_0_), channel_id=1, source_target_pairs={{0,16},{16,0},{1,17},{17,1},{2,18},{18,2},{3,19},{19,3},{4,20},{20... | collective-permute-start | bytes 24584 | tf_op jit(solution)/shard_map/ppermute | solution.py:638

commit v16 on v15

--- a/solution.py
+++ b/solution.py
@@ -261,7 +261,7 @@
     for copy in list_copies:
         copy.start()
     count = sems.shape[1]
-    _, wait, _ = fetch((gate, value), (gate_stage, value_stage), sems, tile, 0, 5)
+    _, wait, _ = fetch((gate, value), (gate_stage, value_stage), sems, tile, 0, 4)
     for copy in list_copies:
         copy.wait()
     row = channel_of_row(lists[0], lists[1], owner_count, channels.shape[1])

time: 64.7 us -> 64.3 us (level)
  no operation moved by 1% of the time
where the time goes in v16:
time: 64.3 us; the launch traced here: 63.9 us
  Pallas kernels  45.3 us (70%)
  starting transfers between devices  13.2 us (21%)
  waiting for transfers between devices  4.52 us (7%)
  between operations  0.84 us (1%)
    pallas_call x8, Pallas kernels, call(): pl.pallas_call(kernel, out_shape=outs, in_specs=[away if n in far else ne...  45.3 us
    all_to_all x1, starting transfers between devices, local(): lax.all_to_all(payload, ('seqo', 'seqi'), split_axis=0, concat_axis=0, ti...  7.37 us
    all_to_all x1, starting transfers between devices, local(): lax.all_to_all(convolved, ('seqo', 'seqi'), split_axis=0, concat_axis=0,...  4.22 us
    all_to_all x1, waiting for transfers between devices, local(): lax.all_to_all(convolved, ('seqo', 'seqi'), split_axis=0, concat_axis=0,...  2.73 us
    all_to_all x1, waiting for transfers between devices, local(): lax.all_to_all(payload, ('seqo', 'seqi'), split_axis=0, concat_axis=0, ti...  1.79 us
    ppermute x1, starting transfers between devices, local(): parts.append(lax.ppermute(totals, 'chan', ring))  1.59 us
  transfers between devices with their start and end apart: 3, of which 2 were waited for; matrix products, arithmetic and copies ran while one was open for 0% of the time, Pallas kernels for 42%

profile of v16, /device:TPU:0, one launch (start us, length us, event | category | flops | bytes accessed | tf_op | source)
XLA Modules:
  0.0 63.9 jit_solution(15745734926756263781)
XLA Ops:
  0.6 0.0 copy-start.4
  0.6 8.3 %shard_map.167 = (bf16[16,16,768]{2,1,0:T(8,128)(2,1)}, bf16[16,96,128]{2,1,0:T(8,128)(2,1)S(1)}, s32[8,128]{1,0:T(8,128)S(1)}, bf16[512,2048]{1,0:T(8,128)(2,1)S(1)}) custom-call(s32[1,64]{1,0:T(1,128)} %index.1, s32[1,64]{1,0:T(1,128)} %owners.1, bf16[2048,2048]{1,0:T(8,128)(2,1)} %refs_0_.3, bf16[2048,2048]{1,0:T(8,128)(2,1)} %refs_1_.3), custom_call_target="tpu_custom_call" | custom-call | flops 805306368 | bytes 16777216 | tf_op jit(solution)/shard_map/pallas_call | solution.py:484
  8.9 7.4 %all-to-all-start = ((bf16[16,16,768]{2,1,0:T(8,128)(2,1)}), bf16[16,16,768]{2,1,0:T(8,128)(2,1)S(1)}, u32[]{:S(2)}, u32[]{:S(2)}) async-start(bf16[16,16,768]{2,1,0:T(8,128)(2,1)} %get-tuple-element.25), calls=%async_computation | async-start | bytes 786432 | tf_op jit(solution)/shard_map/all_to_all | solution.py:547
  16.3 0.0 copy-done.4
  16.3 0.0 copy-start.6
  16.3 0.0 copy-start.7
  16.3 0.0 copy-start.8
  16.4 0.0 copy-start.9
  16.4 8.7 %shard_map.169 = (bf16[96,2048]{1,0:T(8,128)(2,1)S(1)}, f32[8,2048]{1,0:T(8,128)S(1)}, f32[96,128]{1,0:T(8,128)S(1)}, bf16[2048,2048]{1,0:T(8,128)(2,1)}, f32[8,...) custom-call(s32[8,128]{1,0:T(8,128)S(1)} %get-tuple-element.26.channels, ...), custom_call_target="tpu_custom_call" | custom-call | flops 805306368 | bytes 20971520 | tf_op jit(solution)/shard_map/pallas_call | solution.py:484
  25.1 0.0 copy-start
  25.1 0.0 copy-start.2
  25.1 0.0 copy-done.6
  25.1 0.0 copy-done.7
  25.1 0.0 copy-done.8
  25.2 0.0 copy-done.9
  25.2 1.5 %shard_map.168.spectra = f32[6,256,256]{2,1,0:T(8,128)S(1)} custom-call(bf16[6,32768]{1,0:T(8,128)(2,1)S(1)} %bitcast.6, bf16[1024,256]{1,0:T(8,128)(2,1)S(1)} %copy-done.8, f32[256,256]{1,0:T(8,128)S(1)} %copy-done.9, bf16[1024,256]{1,0:T(8,128)(2,1)S(1)} %copy-done.7), custom_call_target="tpu_custom_call" | custom-call | flops 1006632960 | bytes 4194304 | tf_op jit(solution)/shard_map/pallas_call | solution.py:484
  26.7 0.0 copy-done
  26.7 0.0 copy-done.2
  26.7 1.8 %all-to-all-done.signals = bf16[16,16,768]{2,1,0:T(8,128)(2,1)S(1)} async-done(((bf16[16,16,768]{2,1,0:T(8,128)(2,1)}), bf16[16,16,768]{2,1,0:T(8,128)(2,1)S(1)}, u32[]{:S(2)}, u32[]{:S(2)}) %all-to-all-start) | async-done | bytes 393248 | tf_op jit(solution)/shard_map/all_to_all | solution.py:547
  28.5 5.1 %shard_map.170 = bf16[16,16,768]{2,1,0:T(8,128)(2,1)} custom-call(bf16[16,16,768]{2,1,0:T(8,128)(2,1)S(1)} %all-to-all-done.signals, f32[6,256,256]{2,1,0:T(8,128)S(1)} %shard_map.168.spectra, bf16[1024,256]{1,0:T(8,128)(2,1)} %constant.8.clone.outer_fwd.outer_fwd_far, f32[256,256]{1,0:T(8,128)} %constant.9.clone.turn.turn_far, ...), custom_call_target="tpu_custom_call" | custom-call | flops 2214592512 | bytes 8388608 | tf_op jit(solution)/shard_map/pallas_call | solution.py:484
  33.6 4.2 %all-to-all-start.1 = ((bf16[16,16,768]{2,1,0:T(8,128)(2,1)}), bf16[16,16,768]{2,1,0:T(8,128)(2,1)S(1)}, u32[]{:S(2)}, u32[]{:S(2)}) async-start(bf16[16,16,768]{2,1,0:T(8,128)(2,1)} %shard_map.170), calls=%async_computation.1 | async-start | bytes 786432 | tf_op jit(solution)/shard_map/all_to_all | solution.py:610
  37.9 0.0 copy-start.1
  37.9 0.0 copy-start.3
  37.9 9.4 %shard_map.171 = (bf16[2048,2048]{1,0:T(8,128)(2,1)}, f32[8,1,128]{2,1,0:T(1,128)S(1)}, bf16[8,96,128]{2,1,0:T(8,128)(2,1)S(1)}, bf16[8,96,128]{2,1,0:T(8,128)(2,1)S(1)}) custom-call(bf16[96,2048]{1,0:T(8,128)(2,1)S(1)} %get-tuple-element.31.onehot, f32[8,2048]{1,0:T(8,128)S(1)} %get-tuple-element.32.others, ...), custom_call_target="tpu_custom_call", output_to_operand_aliasing={{0}: (7, {})} | custom-call | flops 805306368 | bytes 20971520 | tf_op jit(solution)/shard_map/pallas_call | solution.py:484
  47.3 0.0 copy-start.5
  47.3 2.7 %all-to-all-done.1.conv = bf16[16,16,768]{2,1,0:T(8,128)(2,1)S(1)} async-done(((bf16[16,16,768]{2,1,0:T(8,128)(2,1)}), bf16[16,16,768]{2,1,0:T(8,128)(2,1)S(1)}, u32[]{:S(2)}, u32[]{:S(2)}) %all-to-all-start.1) | async-done | bytes 393248 | tf_op jit(solution)/shard_map/all_to_all | solution.py:610
  50.1 0.0 copy-done.1
  50.1 0.0 copy-done.3
  50.1 0.5 shard_map.172
  50.6 1.6 %collective-permute-start = (f32[16,1,128]{2,1,0:T(1,128)S(1)}, f32[16,1,128]{2,1,0:T(1,128)S(1)}, u32[]{:S(2)}, u32[]{:S(2)}) collective-permute-start(f32[16,1,128]{2,1,0:T(1,128)S(1)} %get-tuple-element.46.refs_0_), channel_id=1, source_target_pairs={{0,16},{16,0},{1,17},{17,1},{2,18},{18,2},{3,19},{19,3},{4,20},{20... | collective-permute-start | bytes 24584 | tf_op jit(solution)/shard_map/ppermute | solution.py:638
  52.2 7.3 %shard_map.173 = (bf16[2048,2048]{1,0:T(8,128)(2,1)}, bf16[2048,2048]{1,0:T(8,128)(2,1)S(1)}) custom-call(bf16[2048,2048]{1,0:T(8,128)(2,1)} %get-tuple-element.34.base, bf16[16,96,128]{2,1,0:T(8,128)(2,1)S(1)} %get-tuple-element.44.hidden_kept, bf16[96,2048]{1,0:T(8,128)(2,1)S(1)} %get-tuple-element.31.onehot), custom_call_target="tpu_custom_call" | custom-call | flops 805306368 | bytes 16777216 | tf_op jit(solution)/shard_map/pallas_call | solution.py:484
  59.5 0.0 collective-permute-done.refs_1_
  59.5 0.0 copy-done.5
  59.5 4.4 %shard_map.174 = bf16[2048,2048]{1,0:T(8,128)(2,1)} custom-call(f32[16,1,128]{2,1,0:T(1,128)S(1)} %get-tuple-element.46.refs_0_, f32[16,1,128]{2,1,0:T(1,128)S(1)} %collective-permute-done.refs_1_, bf16[2048,2048]{1,0:T(8,128)(2,1)S(1)} %get-tuple-element.47.refs_2_, f32[1,2048]{1,0:T(1,128)S(1)} %bitcast.5), custom_call_target="tpu_custom_call" | custom-call | flops 16777216 | bytes 16777216 | tf_op jit(solution)/shard_map/pallas_call | solution.py:484
Async XLA Ops:
  0.6 15.7 %copy-start.4 = (f32[2048]{0:T(1024)S(1)}, f32[2048]{0:T(1024)}, u32[]{:S(2)}) copy-start(f32[2048]{0:T(1024)} %param.23) | copy-start | bytes 24580
  8.9 19.6 %all-to-all-start = ((bf16[16,16,768]{2,1,0:T(8,128)(2,1)}), bf16[16,16,768]{2,1,0:T(8,128)(2,1)S(1)}, u32[]{:S(2)}, u32[]{:S(2)}) async-start(bf16[16,16,768]{2,1,0:T(8,128)(2,1)} %get-tuple-element.25), calls=%async_computation | async-start | bytes 786432 | tf_op jit(solution)/shard_map/all_to_all | solution.py:547
  16.3 8.8 %copy-start.6 = (bf16[1,1,6,32768]{3,2,1,0:T(8,128)(2,1)S(1)}, bf16[1,1,6,32768]{3,2,1,0:T(8,128)(2,1)}, u32[]{:S(2)}) copy-start(bf16[1,1,6,32768]{3,2,1,0:T(8,128)(2,1)} %param.20) | copy-start | bytes 1179652
  16.3 8.8 %copy-start.7 = (bf16[1024,256]{1,0:T(8,128)(2,1)S(1)}, bf16[1024,256]{1,0:T(8,128)(2,1)}, u32[]{:S(2)}) copy-start(bf16[1024,256]{1,0:T(8,128)(2,1)} %constant.10.clone.inner.inner_far) | copy-start | bytes 1572868
  16.3 8.8 %copy-start.8 = (bf16[1024,256]{1,0:T(8,128)(2,1)S(1)}, bf16[1024,256]{1,0:T(8,128)(2,1)}, u32[]{:S(2)}) copy-start(bf16[1024,256]{1,0:T(8,128)(2,1)} %constant.8.clone.outer_fwd.outer_fwd_far) | copy-start | bytes 1572868
  16.4 8.8 %copy-start.9 = (f32[256,256]{1,0:T(8,128)S(1)}, f32[256,256]{1,0:T(8,128)}, u32[]{:S(2)}) copy-start(f32[256,256]{1,0:T(8,128)} %constant.9.clone.turn.turn_far) | copy-start | bytes 786436
  25.1 1.6 %copy-start = (bf16[8,96,128]{2,1,0:T(8,128)(2,1)}, bf16[8,96,128]{2,1,0:T(8,128)(2,1)S(1)}, u32[]{:S(2)}) copy-start(bf16[8,96,128]{2,1,0:T(8,128)(2,1)S(1)} %get-tuple-element.40.refs_2_) | copy-start | bytes 589828
  25.1 1.6 %copy-start.2 = (f32[96,128]{1,0:T(8,128)}, f32[96,128]{1,0:T(8,128)S(1)}, u32[]{:S(2)}) copy-start(f32[96,128]{1,0:T(8,128)S(1)} %get-tuple-element.37.skip_wide) | copy-start | bytes 147460
  33.6 16.4 %all-to-all-start.1 = ((bf16[16,16,768]{2,1,0:T(8,128)(2,1)}), bf16[16,16,768]{2,1,0:T(8,128)(2,1)S(1)}, u32[]{:S(2)}, u32[]{:S(2)}) async-start(bf16[16,16,768]{2,1,0:T(8,128)(2,1)} %shard_map.170), calls=%async_computation.1 | async-start | bytes 786432 | tf_op jit(solution)/shard_map/all_to_all | solution.py:610
  37.9 12.2 %copy-start.1 = (bf16[8,96,128]{2,1,0:T(8,128)(2,1)S(1)}, bf16[8,96,128]{2,1,0:T(8,128)(2,1)}, u32[]{:S(2)}) copy-start(bf16[8,96,128]{2,1,0:T(8,128)(2,1)} %copy-done) | copy-start | bytes 589828
  37.9 12.2 %copy-start.3 = (f32[96,128]{1,0:T(8,128)S(1)}, f32[96,128]{1,0:T(8,128)}, u32[]{:S(2)}) copy-start(f32[96,128]{1,0:T(8,128)} %copy-done.2) | copy-start | bytes 147460
  47.3 12.2 %copy-start.5 = (f32[2048]{0:T(1024)S(1)}, f32[2048]{0:T(1024)}, u32[]{:S(2)}) copy-start(f32[2048]{0:T(1024)} %param.24) | copy-start | bytes 24580
  50.6 8.9 %collective-permute-start = (f32[16,1,128]{2,1,0:T(1,128)S(1)}, f32[16,1,128]{2,1,0:T(1,128)S(1)}, u32[]{:S(2)}, u32[]{:S(2)}) collective-permute-start(f32[16,1,128]{2,1,0:T(1,128)S(1)} %get-tuple-element.46.refs_0_), channel_id=1, source_target_pairs={{0,16},{16,0},{1,17},{17,1},{2,18},{18,2},{3,19},{19,3},{4,20},{20... | collective-permute-start | bytes 24584 | tf_op jit(solution)/shard_map/ppermute | solution.py:638
